TPU v7x, 32 devices: a whole 2x2x4 slice. The times are simulated.
32 devices in a mesh: fsdp: 4 (over z), context: 2 (over x), tensor: 4 (over y, core).
Axes of the slice: x: 2, y: 2, z: 4, core: 2. Of those that a mesh axis runs over, the one named last changes fastest.
Arguments:
- hidden_in: bfloat16 [8, 1024, 2048], P('fsdp', 'context'), may hold values from -6 to 6
- norm_gains: bfloat16 [2, 2048], P(None, 'fsdp'), may hold values from 0.5 to 1.5
- norm_biases: bfloat16 [2, 2048], P(None, 'fsdp'), may hold values from -3 to 3
- qkv_weight: bfloat16 [3, 2048, 2048], P(None, 'fsdp', 'tensor'), may hold values from -0.1875 to 0.1875
- qkv_bias: bfloat16 [3, 2048], P(None, 'tensor'), may hold values from -3 to 3
- out_weight: bfloat16 [2048, 2048], P('tensor', 'fsdp'), may hold values from -0.25 to 0.25
- gate_up_weight: bfloat16 [2, 2048, 5632], P(None, 'fsdp', 'tensor'), may hold values from -0.125 to 0.125
- down_weight: bfloat16 [5632, 2048], P('tensor', 'fsdp'), may hold values from -0.109375 to 0.109375
- cotangent: bfloat16 [8, 1024, 2048], P('fsdp', 'context'), may hold values from -6 to 6
Outputs:
- layer_out: bfloat16 [8, 1024, 2048], P('fsdp', 'context')
- input_grad: float32 [8, 1024, 2048], P('fsdp', 'context')
- grad_norm_gains: float32 [2, 2048], P(None, 'fsdp')
- grad_norm_biases: float32 [2, 2048], P(None, 'fsdp')
- grad_qkv_weight: float32 [3, 2048, 2048], P(None, 'fsdp', 'tensor')
- grad_qkv_bias: float32 [3, 2048], P(None, 'tensor')
- grad_out_weight: float32 [2048, 2048], P('tensor', 'fsdp')
- grad_gate_up: float32 [2, 2048, 5632], P(None, 'fsdp', 'tensor')
- grad_down: float32 [5632, 2048], P('tensor', 'fsdp')
All inputs are finite; a program needn't handle non-finite values.
Results may differ from a plain program's by a relative error of at most 0.022.
Values may be sent and summed in bfloat16 or wider, within the bound.
No kernel may reach another device: no remote copies, remote signals or barrier semaphores. Data moves between devices by JAX's collectives and lax.ppermute only.
A program may use at most 320 MiB of HBM per device.

v0:
```python
import math

import jax
import jax.numpy as jnp
from jax import lax
from jax.sharding import PartitionSpec as P

HEAD_DIM = 64
ROT = 16


EPSILON = 1e-05
NEG_HUGE = -1e30


def norm_forward(values, gain, shift):
    row_mean = jnp.mean(values, axis=-1, keepdims=True)
    centred = values - row_mean
    variance = jnp.mean(centred * centred, axis=-1, keepdims=True)
    inv_std = lax.rsqrt(variance + EPSILON)
    scaled = centred * inv_std
    return (scaled * gain + shift, scaled, inv_std)


def norm_backward(grad_out, scaled, inv_std, gain):
    grad_scaled = grad_out * gain
    first_mean = jnp.mean(grad_scaled, axis=-1, keepdims=True)
    second_mean = jnp.mean(grad_scaled * scaled, axis=-1, keepdims=True)
    grad_in = inv_std * (grad_scaled - first_mean - scaled * second_mean)
    return (grad_in, jnp.sum(grad_out * scaled, axis=0), jnp.sum(grad_out, axis=0))


def rotary_tables(positions, feat_width):
    column = jnp.arange(feat_width, dtype=jnp.int32) % HEAD_DIM
    half_rot = ROT // 2
    freq_index = (column % half_rot).astype(jnp.float32)
    frequency = jnp.power(10000.0, -2.0 * freq_index / ROT)
    angles = positions.astype(jnp.float32)[:, None] * frequency[None, :]
    inside = column < ROT
    lower_half = column < half_rot
    cosine = jnp.where(inside, jnp.cos(angles), 1.0)
    sine_tab = jnp.sin(angles)
    minus_sine = jnp.where(lower_half, -sine_tab, 0.0)
    plus_sine = jnp.where(inside & jnp.logical_not(lower_half), sine_tab, 0.0)
    return (cosine, minus_sine, plus_sine)


def rotate(values, tables):
    cosine, minus_sine, plus_sine = tables
    half_rot = ROT // 2
    shifted_up = jnp.roll(values, -half_rot, axis=-1)
    behind = jnp.roll(values, half_rot, axis=-1)
    return values * cosine + shifted_up * minus_sine + behind * plus_sine


def rotate_back(grads_in, tables):
    cosine, minus_sine, plus_sine = tables
    half_rot = ROT // 2
    return (
        grads_in * cosine
        + jnp.roll(grads_in * minus_sine, half_rot, axis=-1)
        + jnp.roll(grads_in * plus_sine, -half_rot, axis=-1)
    )


def to_groups(values, group_count):
    seq_count, row_count, feat_width = values.shape
    return values.reshape(seq_count, row_count, group_count, feat_width // group_count).transpose(
        2, 0, 1, 3
    )


def from_groups(values):
    group_count, seq_count, row_count, feat_width = values.shape
    return values.transpose(1, 2, 0, 3).reshape(seq_count, row_count, group_count * feat_width)


def split_heads(values):
    seq_count, row_count, feat_width = values.shape
    return values.reshape(seq_count, row_count, feat_width // HEAD_DIM, HEAD_DIM)


def causal_scores(queries, key_rows, q_pos, k_pos):
    scores = jnp.einsum(
        "sqhd,skhd->shqk",
        split_heads(queries),
        split_heads(key_rows),
        preferred_element_type=jnp.float32,
    )
    scores = scores * (1.0 / math.sqrt(HEAD_DIM))
    allowed = q_pos[:, None] >= k_pos[None, :]
    return jnp.where(allowed, scores, NEG_HUGE)


def attend_forward(queries, key_rows, value_rows, q_pos, k_pos):
    scores = causal_scores(queries, key_rows, q_pos, k_pos)
    row_max = jnp.max(scores, axis=-1, keepdims=True)
    row_total = jnp.sum(jnp.exp(scores - row_max), axis=-1, keepdims=True)
    log_total = row_max + jnp.log(row_total)
    probs_low = jnp.exp(scores - log_total).astype(jnp.bfloat16)
    attended = jnp.einsum(
        "shqk,skhd->sqhd", probs_low, split_heads(value_rows), preferred_element_type=jnp.float32
    )
    return (
        attended.reshape(queries.shape).astype(jnp.bfloat16),
        jnp.transpose(log_total[..., 0], (0, 2, 1)),
    )


def attend_back_rows(queries, key_rows, value_rows, grad_att, log_total, q_pos, k_pos):
    score_scale = 1.0 / math.sqrt(HEAD_DIM)
    scores = causal_scores(queries, key_rows, q_pos, k_pos)
    attn_probs = jnp.exp(scores - jnp.transpose(log_total, (0, 2, 1))[..., None])
    grad_probs = jnp.einsum(
        "sqhd,skhd->shqk",
        split_heads(grad_att),
        split_heads(value_rows),
        preferred_element_type=jnp.float32,
    )
    delta_row = jnp.sum(attn_probs * grad_probs, axis=-1, keepdims=True)
    grad_scores = (attn_probs * (grad_probs - delta_row)).astype(jnp.bfloat16)
    grad_query = (
        jnp.einsum(
            "shqk,skhd->sqhd",
            grad_scores,
            split_heads(key_rows),
            preferred_element_type=jnp.float32,
        )
        * score_scale
    )
    results = (grad_query.reshape(queries.shape), jnp.transpose(delta_row[..., 0], (0, 2, 1)))
    grad_keys = (
        jnp.einsum(
            "shqk,sqhd->skhd", grad_scores, split_heads(queries), preferred_element_type=jnp.float32
        )
        * score_scale
    )
    grad_values = jnp.einsum(
        "shqk,sqhd->skhd",
        attn_probs.astype(jnp.bfloat16),
        split_heads(grad_att),
        preferred_element_type=jnp.float32,
    )
    results = results + (grad_keys.reshape(key_rows.shape), grad_values.reshape(value_rows.shape))
    return results


def branch_total(values):
    return lax.psum(values, "tensor")


def input_total(values):
    return lax.psum(values.astype(jnp.bfloat16), "tensor").astype(jnp.float32)


def local(
    hidden_in,
    norm_gains,
    norm_biases,
    qkv_weight,
    qkv_bias,
    out_weight,
    gate_up_weight,
    down_weight,
    cotangent,
):
    seq_count, row_count, feat_width = hidden_in.shape
    tok_rows = seq_count * row_count
    local_width = qkv_bias.shape[1]
    head_count = local_width // HEAD_DIM
    group_size = min(head_count, max(1, 128 // HEAD_DIM))
    group_count = head_count // group_size
    q_pos = lax.axis_index("context") * row_count + jnp.arange(row_count, dtype=jnp.int32)
    k_pos = jnp.arange(row_count * lax.axis_size("context"), dtype=jnp.int32)
    gain_rows, shift_rows, w_qkv, w_out = (
        lax.all_gather(norm_gains, "fsdp", axis=1, tiled=True),
        lax.all_gather(norm_biases, "fsdp", axis=1, tiled=True),
        lax.all_gather(qkv_weight, "fsdp", axis=1, tiled=True),
        lax.all_gather(out_weight, "fsdp", axis=1, tiled=True),
    )
    w_gate_up, w_down = (
        lax.all_gather(gate_up_weight, "fsdp", axis=1, tiled=True),
        lax.all_gather(down_weight, "fsdp", axis=1, tiled=True),
    )
    gain_rows = gain_rows.astype(jnp.float32)
    shift_rows = shift_rows.astype(jnp.float32)
    inputs = hidden_in.astype(jnp.float32).reshape(tok_rows, feat_width)
    normed, scaled_one, inv_one = norm_forward(inputs, gain_rows[0], shift_rows[0])
    normed_low = normed.astype(jnp.bfloat16)
    mixed_qkv = jnp.einsum("rd,cde->cre", normed_low, w_qkv, preferred_element_type=jnp.float32)
    mixed_qkv = (mixed_qkv + qkv_bias.astype(jnp.float32)[:, None, :]).reshape(
        3, seq_count, row_count, local_width
    )
    tables = rotary_tables(q_pos, local_width)
    query_grp = to_groups(rotate(mixed_qkv[0], tables).astype(jnp.bfloat16), group_count)
    key_grp = to_groups(rotate(mixed_qkv[1], tables).astype(jnp.bfloat16), group_count)
    value_grp = to_groups(mixed_qkv[2].astype(jnp.bfloat16), group_count)
    key_whole, value_whole = (
        lax.all_gather(key_grp, "context", axis=2, tiled=True),
        lax.all_gather(value_grp, "context", axis=2, tiled=True),
    )

    def forward_group(operands):
        return attend_forward(operands[0], operands[1], operands[2], q_pos, k_pos)

    att_grp, log_total = lax.map(forward_group, (query_grp, key_whole, value_whole))
    att_low = from_groups(att_grp).reshape(tok_rows, local_width)
    attn_term = jnp.dot(att_low, w_out, preferred_element_type=jnp.float32)
    middle = inputs + branch_total(attn_term)
    normed_two, scaled_two, inv_two = norm_forward(middle, gain_rows[1], shift_rows[1])
    normed_two_low = normed_two.astype(jnp.bfloat16)
    gate_up = jnp.einsum(
        "rd,cdf->crf", normed_two_low, w_gate_up, preferred_element_type=jnp.float32
    )
    gate_act = jax.nn.silu(gate_up[0])
    hidden = (gate_act * gate_up[1]).astype(jnp.bfloat16)
    down_term = jnp.dot(hidden, w_down, preferred_element_type=jnp.float32)
    final_out = (middle + branch_total(down_term)).astype(jnp.bfloat16)
    grad_top = cotangent.astype(jnp.float32).reshape(tok_rows, feat_width)
    grad_top_low = grad_top.astype(jnp.bfloat16)
    grad_w_down = jnp.einsum("rf,rd->fd", hidden, grad_top_low, preferred_element_type=jnp.float32)
    grad_hidden = jnp.einsum("rd,fd->rf", grad_top_low, w_down, preferred_element_type=jnp.float32)
    sig_gate = jax.nn.sigmoid(gate_up[0])
    grad_gate = grad_hidden * gate_up[1] * (sig_gate * (1.0 + gate_up[0] * (1.0 - sig_gate)))
    grad_up = grad_hidden * gate_act
    grad_gu_low = jnp.stack([grad_gate, grad_up]).astype(jnp.bfloat16)
    grad_w_gate_up = jnp.einsum(
        "rd,crf->cdf", normed_two_low, grad_gu_low, preferred_element_type=jnp.float32
    )
    grad_two_term = jnp.einsum(
        "crf,cdf->rd", grad_gu_low, w_gate_up, preferred_element_type=jnp.float32
    )
    grad_mid, gain_two, shift_two = norm_backward(
        input_total(grad_two_term), scaled_two, inv_two, gain_rows[1]
    )
    grad_middle = grad_top + grad_mid
    grad_mid_low = grad_middle.astype(jnp.bfloat16)
    grad_w_out = jnp.einsum("re,rd->ed", att_low, grad_mid_low, preferred_element_type=jnp.float32)
    grad_att = jnp.einsum(
        "rd,ed->re", grad_mid_low, w_out, preferred_element_type=jnp.float32
    ).astype(jnp.bfloat16)
    grad_att_grp = to_groups(grad_att.reshape(seq_count, row_count, local_width), group_count)

    def back_group(operands):
        return attend_back_rows(
            operands[0], operands[1], operands[2], operands[3], operands[4], q_pos, k_pos
        )

    grad_q_grp, delta_grp, grad_k_whole, grad_v_whole = lax.map(
        back_group, (query_grp, key_whole, value_whole, grad_att_grp, log_total)
    )
    grad_k_grp, grad_v_grp = (
        lax.psum_scatter(
            grad_k_whole.astype(jnp.bfloat16), "context", scatter_dimension=2, tiled=True
        ).astype(jnp.float32),
        lax.psum_scatter(
            grad_v_whole.astype(jnp.bfloat16), "context", scatter_dimension=2, tiled=True
        ).astype(jnp.float32),
    )
    grad_query = rotate_back(from_groups(grad_q_grp), tables)
    grad_key = rotate_back(from_groups(grad_k_grp), tables)
    grad_value = from_groups(grad_v_grp)
    grad_mixed_low = (
        jnp.stack([grad_query, grad_key, grad_value])
        .reshape(3, tok_rows, local_width)
        .astype(jnp.bfloat16)
    )
    grad_bias = lax.psum(jnp.sum(grad_mixed_low, axis=1, dtype=jnp.float32), ("fsdp", "context"))
    grad_w_qkv = jnp.einsum(
        "rd,cre->cde", normed_low, grad_mixed_low, preferred_element_type=jnp.float32
    )
    grad_one_term = jnp.einsum(
        "cre,cde->rd", grad_mixed_low, w_qkv, preferred_element_type=jnp.float32
    )
    grad_first, gain_one, shift_one = norm_backward(
        input_total(grad_one_term), scaled_one, inv_one, gain_rows[0]
    )
    input_grad = grad_middle + grad_first
    grad_gains = jnp.stack([gain_one, gain_two])
    grad_shifts = jnp.stack([shift_one, shift_two])
    input_grad = input_grad.reshape(seq_count, row_count, feat_width)
    part_gains, part_shifts, part_qkv, part_out, part_gate_up, part_down = (
        lax.psum_scatter(
            grad_gains.astype(jnp.bfloat16), ("fsdp", "context"), scatter_dimension=1, tiled=True
        ).astype(jnp.float32),
        lax.psum_scatter(
            grad_shifts.astype(jnp.bfloat16), ("fsdp", "context"), scatter_dimension=1, tiled=True
        ).astype(jnp.float32),
        lax.psum_scatter(
            grad_w_qkv.astype(jnp.bfloat16), ("fsdp", "context"), scatter_dimension=1, tiled=True
        ).astype(jnp.float32),
        lax.psum_scatter(
            grad_w_out.astype(jnp.bfloat16), ("fsdp", "context"), scatter_dimension=1, tiled=True
        ).astype(jnp.float32),
        lax.psum_scatter(
            grad_w_gate_up.astype(jnp.bfloat16),
            ("fsdp", "context"),
            scatter_dimension=1,
            tiled=True,
        ).astype(jnp.float32),
        lax.psum_scatter(
            grad_w_down.astype(jnp.bfloat16), ("fsdp", "context"), scatter_dimension=1, tiled=True
        ).astype(jnp.float32),
    )
    out_gains, out_shifts, out_qkv, out_proj, out_gate_up, out_down = (
        lax.all_gather(part_gains.astype(jnp.bfloat16), "context", axis=1, tiled=True).astype(
            part_gains.dtype
        ),
        lax.all_gather(part_shifts.astype(jnp.bfloat16), "context", axis=1, tiled=True).astype(
            part_shifts.dtype
        ),
        lax.all_gather(part_qkv.astype(jnp.bfloat16), "context", axis=1, tiled=True).astype(
            part_qkv.dtype
        ),
        lax.all_gather(part_out.astype(jnp.bfloat16), "context", axis=1, tiled=True).astype(
            part_out.dtype
        ),
        lax.all_gather(part_gate_up.astype(jnp.bfloat16), "context", axis=1, tiled=True).astype(
            part_gate_up.dtype
        ),
        lax.all_gather(part_down.astype(jnp.bfloat16), "context", axis=1, tiled=True).astype(
            part_down.dtype
        ),
    )
    final_out = final_out.reshape(seq_count, row_count, feat_width)
    return (
        final_out,
        input_grad,
        out_gains,
        out_shifts,
        out_qkv,
        grad_bias,
        out_proj,
        out_gate_up,
        out_down,
    )


def solution(mesh):
    placed = (
        P("fsdp", "context", None),
        P(None, "fsdp"),
        P(None, "fsdp"),
        P(None, "fsdp", "tensor"),
        P(None, "tensor"),
        P("tensor", "fsdp"),
        P(None, "fsdp", "tensor"),
        P("tensor", "fsdp"),
        P("fsdp", "context", None),
    )
    return jax.shard_map(
        local,
        mesh=mesh,
        in_specs=placed,
        out_specs=(
            P("fsdp", "context", None),
            P("fsdp", "context", None),
            P(None, "fsdp"),
            P(None, "fsdp"),
            P(None, "fsdp", "tensor"),
            P(None, "tensor"),
            P("tensor", "fsdp"),
            P(None, "fsdp", "tensor"),
            P("tensor", "fsdp"),
        ),
        check_vma=False,
    )
```

profile of v0, /device:TPU:0, one launch (start us, length us, event | category | flops | bytes accessed | tf_op | source)
XLA Modules:
  0.0 2046.5 jit_solution(1666081161307357533)
XLA Ops:
  8.0 3.0 convert_reduce_fusion
  12.7 13.6 all_gather.42
  26.3 17.7 all_gather.43
  44.2 5.5 fusion.80
  50.3 4.6 fusion.42
  55.0 72.9 %all-gather.10.cloned.1.call-done = bf16[3,2048,512]{2,1,0:T(8,128)(2,1)} async-done(((bf16[3,512,512]{2,1,0:T(8,128)(2,1)}), bf16[3,2048,512]{2,1,0:T(8,128)(2,1)}) %all-gather.10.cloned.1.call-update) | async-done | bytes 6291472 | tf_op jit(solution)/shard_map/all_gather | solution.py:178
  127.8 10.2 add_bitcast_fusion
  153.2 3.0 copy.108
  156.3 3.1 copy.111
  169.6 3.0 copy.70
  177.2 4.9 fusion.83
  186.5 27.1 %all-gather.14.cloned.1.call-done = bf16[4,2,1024,128]{2,3,0,1:T(8,128)(2,1)} async-done(((bf16[4,2,512,128]{2,3,0,1:T(8,128)(2,1)}), bf16[4,2,1024,128]{2,3,0,1:T(8,128)(2,1)}) %all-gather.14.cloned.1.call-update) | async-done | bytes 2097168 | tf_op jit(solution)/shard_map/all_gather | solution.py:199
  215.4 33.4 %all-gather.12.cloned.1.call-done = bf16[4,2,1024,128]{2,3,1,0:T(8,128)(2,1)} async-done(((bf16[4,2,512,128]{2,3,1,0:T(8,128)(2,1)}), bf16[4,2,1024,128]{2,3,1,0:T(8,128)(2,1)}) %all-gather.12.cloned.1.call-update) | async-done | bytes 2097168 | tf_op jit(solution)/shard_map/all_gather | solution.py:200
  248.8 35.2 %while.28 = (s32[]{:T(128)}, bf16[4,2,512,128]{2,3,1,0:T(8,128)(2,1)}, f32[4,2,512,2]{2,3,1,0:T(2,128)S(1)}, bf16[4,2,1024,128]{2,3,1,0:T(8,128)(2,1)}, bf16[4,2...) while((s32[]{:T(128)}, ...), condition=%wide.region_5.6_spmd.clone, body=%wide.region_2.5_spmd.clone.sunk | while | flops 560593408 | bytes 32051812 | solution.py:206
  286.5 9.7 all-gather.16.cloned.1.call-done
  296.2 7.7 fusion.85
  305.3 150.4 %all-reduce.5.cloned.1.call-done = f32[1024,2048]{1,0:T(8,128)} async-done(((f32[1024,2048]{1,0:T(8,128)}), f32[1024,2048]{1,0:T(8,128)}) %all-reduce.5.cloned.1.call-update) | async-done | bytes 8388624 | tf_op jit(solution)/shard_map/psum | solution.py:149
  455.7 5.5 fusion.112
  464.5 193.8 %all-gather.18.cloned.1.call-done = bf16[2,2048,1408]{2,1,0:T(8,128)(2,1)} async-done(((bf16[2,512,1408]{2,1,0:T(8,128)(2,1)}), bf16[2,2048,1408]{2,1,0:T(8,128)(2,1)}) %all-gather.18.cloned.1.call-update) | async-done | bytes 11534352 | tf_op jit(solution)/shard_map/all_gather | solution.py:182
  658.3 20.3 convolution_bitcast_fusion
  678.6 86.2 %all-gather.20.cloned.1.call-done = bf16[1408,2048]{1,0:T(8,128)(2,1)} async-done(((bf16[1408,512]{1,0:T(8,128)(2,1)}), bf16[1408,2048]{1,0:T(8,128)(2,1)}) %all-gather.20.cloned.1.call-update) | async-done | bytes 5767184 | tf_op jit(solution)/shard_map/all_gather | solution.py:183
  764.8 14.2 fusion.59
  781.6 16.3 bitcast_convert_fusion.1
  798.0 14.4 fusion.56
  812.5 69.3 %all-reduce.9.cloned.1.call-done = bf16[1024,2048]{1,0:T(8,128)(2,1)} async-done(((bf16[1024,2048]{1,0:T(8,128)(2,1)}), bf16[1024,2048]{1,0:T(8,128)(2,1)}) %all-reduce.9.cloned.1.call-update) | async-done | bytes 4194320 | tf_op jit(solution)/shard_map/psum | solution.py:153
  881.9 7.0 fusion.30
  888.9 148.6 %all-reduce.7.cloned.1.call-done = f32[1024,2048]{1,0:T(8,128)} async-done(((f32[1024,2048]{1,0:T(8,128)}), f32[1024,2048]{1,0:T(8,128)}) %all-reduce.7.cloned.1.call-update) | async-done | bytes 8388624 | tf_op jit(solution)/shard_map/psum | solution.py:149
  1037.5 12.4 fusion.28
  1050.0 3.2 copy-done.2
  1053.2 3.3 fusion.71
  1061.1 66.4 %while.29 = (s32[]{:T(128)}, f32[4,2,512,128]{2,3,1,0:T(8,128)}, bf16[4,2,1024,128]{2,3,0,1:T(8,128)(2,1)}, bf16[4,2,1024,128]{2,3,1,0:T(8,128)(2,1)}, bf16[4,2,...) while((s32[]{:T(128)}, f32[4,2,512,128]{2,3,1,0:T(8,128)}, ...), condition=%wide.region_15.16_spmd.clone, body=%wide.region_13.15_spmd.clone.sunk | while | flops 1374812672 | bytes 75560576 | solution.py:249
  1068.4 3.2 multiply_reduce_fusion.3
  1084.9 3.2 multiply_reduce_fusion.3
  1101.5 3.2 multiply_reduce_fusion.3
  1118.1 3.2 multiply_reduce_fusion.3
  1128.4 5.9 fusion.76
  1141.4 18.3 reduce-scatter.13.cloned.1.call-done
  1159.6 3.8 bitcast_multiply_fusion.8
  1190.9 3.1 reshape.579
  1200.3 5.2 fusion.64
  1206.4 11.1 bitcast_convert_fusion
  1217.6 13.6 convolution_convert_fusion
  1232.8 10.8 convert_bitcast_fusion.1
  1244.3 19.7 convert_bitcast_fusion
  1264.1 8.1 convolution_convert_fusion.1
  1275.3 28.0 %all-reduce.11.cloned.1.call-done = bf16[1024,2048]{1,0:T(8,128)(2,1)} async-done(((bf16[1024,2048]{1,0:T(8,128)(2,1)}), bf16[1024,2048]{1,0:T(8,128)(2,1)}) %all-reduce.11.cloned.1.call-update) | async-done | bytes 4194320 | tf_op jit(solution)/shard_map/psum | solution.py:153
  1307.2 6.2 fusion.35
  1314.7 103.3 %reduce-scatter.23.cloned.1.call-done = bf16[1408,256]{1,0:T(8,128)(2,1)} async-done(((bf16[1408,2048]{1,0:T(8,128)(2,1)}), bf16[1408,256]{1,0:T(8,128)(2,1)}) %reduce-scatter.23.cloned.1.call-update) | async-done | bytes 720912 | tf_op jit(solution)/shard_map/reduce_scatter | solution.py:301
  1418.1 121.6 %reduce-scatter.17.cloned.1.call-done = bf16[3,256,512]{1,2,0:T(8,128)(2,1)} async-done(((bf16[3,2048,512]{1,2,0:T(8,128)(2,1)}), bf16[3,256,512]{1,2,0:T(8,128)(2,1)}) %reduce-scatter.17.cloned.1.call-update) | async-done | bytes 786448 | tf_op jit(solution)/shard_map/reduce_scatter | solution.py:289
  1539.8 195.5 %reduce-scatter.21.cloned.1.call-done = bf16[2,256,1408]{1,2,0:T(8,128)(2,1)} async-done(((bf16[2,2048,1408]{1,2,0:T(8,128)(2,1)}), bf16[2,256,1408]{1,2,0:T(8,128)(2,1)}) %reduce-scatter.21.cloned.1.call-update) | async-done | bytes 1441808 | tf_op jit(solution)/shard_map/reduce_scatter | solution.py:295
  1735.3 71.3 %reduce-scatter.19.cloned.1.call-done = bf16[512,256]{1,0:T(8,128)(2,1)} async-done(((bf16[512,2048]{1,0:T(8,128)(2,1)}), bf16[512,256]{1,0:T(8,128)(2,1)}) %reduce-scatter.19.cloned.1.call-update) | async-done | bytes 262160 | tf_op jit(solution)/shard_map/reduce_scatter | solution.py:292
  1806.6 7.2 all_gather.53
  1815.4 20.9 %psum.39 = f32[3,512]{1,0:T(4,128)} all-reduce(f32[3,512]{1,0:T(4,128)S(1)} %convert_reduce_fusion.1), channel_id=1, replica_groups=mesh['fsdp'=4,'context'=2,'tensor'=4] {'fsdp','context'}, use_global_device_ids=true, to_apply=%region_29.30 | all-reduce | flops 1536 | bytes 12288 | tf_op jit(solution)/shard_map/psum | solution.py:268
  1836.3 9.4 fusion.33
  1845.7 25.0 %reduce-scatter.27.cloned.1.call-done = bf16[256,2]{1,0:T(8,128)(2,1)} async-done(((bf16[2048,2]{1,0:T(8,128)(2,1)}), bf16[256,2]{1,0:T(8,128)(2,1)}) %reduce-scatter.27.cloned.1.call-update) | async-done | bytes 1040
  1871.7 4.3 all_gather.51
  1876.5 59.3 %reduce-scatter.25.cloned.1.call-done = bf16[256,2]{1,0:T(8,128)(2,1)} async-done(((bf16[2048,2]{1,0:T(8,128)(2,1)}), bf16[256,2]{1,0:T(8,128)(2,1)}) %reduce-scatter.25.cloned.1.call-update) | async-done | bytes 1040
  1936.8 4.3 all_gather.50
  1941.6 20.5 %all-gather.26.cloned.1.call-done = bf16[1408,512]{1,0:T(8,128)(2,1)} async-done(((bf16[1408,256]{1,0:T(8,128)(2,1)}), bf16[1408,512]{1,0:T(8,128)(2,1)}) %all-gather.26.cloned.1.call-update) | async-done | bytes 1441808 | tf_op jit(solution)/shard_map/all_gather | solution.py:321
  1962.1 3.3 convert_element_type.204
  1965.5 25.2 %all-gather.22.cloned.1.call-done = bf16[3,512,512]{1,2,0:T(8,128)(2,1)} async-done(((bf16[3,256,512]{1,2,0:T(8,128)(2,1)}), bf16[3,512,512]{1,2,0:T(8,128)(2,1)}) %all-gather.22.cloned.1.call-update) | async-done | bytes 1572880 | tf_op jit(solution)/shard_map/all_gather | solution.py:312
  1990.7 3.1 copy.97
  1993.8 40.5 %all-gather.24.cloned.1.call-done = bf16[2,512,1408]{1,2,0:T(8,128)(2,1)} async-done(((bf16[2,256,1408]{1,2,0:T(8,128)(2,1)}), bf16[2,512,1408]{1,2,0:T(8,128)(2,1)}) %all-gather.24.cloned.1.call-update) | async-done | bytes 2883600 | tf_op jit(solution)/shard_map/all_gather | solution.py:318
  2034.3 5.1 copy.98
  (310 shorter events, 200.0 us)
Async XLA Ops:
  7.2 120.6 %all-gather.10.cloned.1.call-start = ((), (), s32[]{:S(2)}) async-start(), calls=%async_computation.8 | async-start | bytes 7864320 | tf_op jit(solution)/shard_map/all_gather | solution.py:178
  7.9 205.6 %all-gather.14.cloned.1.call-start = ((), (), s32[]{:S(2)}) async-start(), calls=%async_computation.10 | async-start | bytes 3145728 | tf_op jit(solution)/shard_map/all_gather | solution.py:199
  8.0 3.5 copy-start
  8.0 4.7 copy-start.35
  8.0 4.7 copy-start.36
  8.0 18.4 copy-start.37
  12.7 42.3 %copy-start.24 = (f32[1,4,2,128]{3,1,2,0:T(4,128)}, f32[1,4,2,128]{3,1,2,0:T(4,128)S(1)}, u32[]{:S(2)}) copy-start(f32[1,4,2,128]{3,1,2,0:T(4,128)S(1)} %copy.128) | copy-start | bytes 12292
  12.7 42.3 %copy-start.26 = (f32[1,4,2,128]{3,1,2,0:T(4,128)}, f32[1,4,2,128]{3,1,2,0:T(4,128)S(1)}, u32[]{:S(2)}) copy-start(f32[1,4,2,128]{3,1,2,0:T(4,128)S(1)} %copy.127) | copy-start | bytes 12292
  44.2 5.6 copy-start.30
  49.7 0.6 copy-start.18
  49.7 987.8 %copy-start.20 = (f32[1,2048]{1,0:T(1,128)}, f32[1,2048]{1,0:T(1,128)S(1)}, u32[]{:S(2)}) copy-start(f32[1,2048]{1,0:T(1,128)S(1)} %get-tuple-element.293) | copy-start | bytes 24580
  49.8 608.5 %copy-start.33 = (f32[1,2048]{1,0:T(1,128)}, f32[1,2048]{1,0:T(1,128)S(1)}, u32[]{:S(2)}) copy-start(f32[1,2048]{1,0:T(1,128)S(1)} %get-tuple-element.295) | copy-start | bytes 24580
  138.0 2.7 copy-start.11
  140.7 2.8 copy-start.3
  153.2 3.0 copy-start.17
  156.3 8.3 copy-start.7
  172.6 2.2 copy-start.8
  172.6 2.8 copy-start.9
  174.8 1.7 copy-start.10
  175.5 1.7 copy-start.5
  182.1 4.3 copy-start.16
  182.1 66.7 %all-gather.12.cloned.1.call-start = ((), (), s32[]{:S(2)}) async-start(), calls=%async_computation.9 | async-start | bytes 3145728 | tf_op jit(solution)/shard_map/all_gather | solution.py:200
  185.8 110.5 %all-gather.16.cloned.1.call-start = ((), (), s32[]{:S(2)}) async-start(), calls=%async_computation.11 | async-start | bytes 2621440 | tf_op jit(solution)/shard_map/all_gather | solution.py:179
  186.3 269.3 %all-reduce.5.cloned.1.call-start = ((), (), s32[]{:S(2)}) async-start(), calls=%async_computation.12 | async-start | bytes 16777216 | tf_op jit(solution)/shard_map/psum | solution.py:149
  303.9 354.4 %all-gather.18.cloned.1.call-start = ((), (), s32[]{:S(2)}) async-start(), calls=%async_computation.13 | async-start | bytes 14417920 | tf_op jit(solution)/shard_map/all_gather | solution.py:182
  304.5 460.4 %all-gather.20.cloned.1.call-start = ((), (), s32[]{:S(2)}) async-start(), calls=%async_computation.14 | async-start | bytes 7208960 | tf_op jit(solution)/shard_map/all_gather | solution.py:183
  305.2 576.6 %all-reduce.9.cloned.1.call-start = ((), (), s32[]{:S(2)}) async-start(), calls=%async_computation.16 | async-start | bytes 8388608 | tf_op jit(solution)/shard_map/psum | solution.py:153
  461.1 3.4 copy-start.1
  461.1 576.4 %copy-start.22 = (f32[1024]{0:T(1024)}, f32[1024]{0:T(1024)S(1)}, u32[]{:S(2)}) copy-start(f32[1024]{0:T(1024)S(1)} %broadcast_multiply_fusion.4) | copy-start | bytes 12292
  464.5 573.0 %copy-start.28 = (f32[1024]{0:T(1024)}, f32[1024]{0:T(1024)S(1)}, u32[]{:S(2)}) copy-start(f32[1024]{0:T(1024)S(1)} %add_rsqrt_fusion) | copy-start | bytes 12292
  779.1 1.6 copy-start.39
  779.1 2.5 copy-start.40
  797.9 239.6 %all-reduce.7.cloned.1.call-start = ((), (), s32[]{:S(2)}) async-start(), calls=%async_computation.15 | async-start | bytes 16777216 | tf_op jit(solution)/shard_map/psum | solution.py:149
  812.4 347.2 %reduce-scatter.13.cloned.1.call-start = ((), (), s32[]{:S(2)}) async-start(), calls=%async_computation.17 | async-start | bytes 3145728 | tf_op jit(solution)/shard_map/reduce_scatter | solution.py:253
  1037.5 15.7 copy-start.38
  1050.0 3.2 copy-start.2
  1127.5 0.9 copy-start.31
  1127.5 8.3 copy-start.6
  1127.5 66.4 %reduce-scatter.15.cloned.1.call-start = ((), (), s32[]{:S(2)}) async-start(), calls=%async_computation.18 | async-start | bytes 3145728 | tf_op jit(solution)/shard_map/reduce_scatter | solution.py:256
  1128.3 174.9 %all-reduce.11.cloned.1.call-start = ((), (), s32[]{:S(2)}) async-start(), calls=%async_computation.19 | async-start | bytes 8388608 | tf_op jit(solution)/shard_map/psum | solution.py:153
  1198.7 1.6 copy-start.4
  1200.3 6.2 copy-start.14
  1205.4 1.0 copy-start.12
  1217.5 200.5 %reduce-scatter.23.cloned.1.call-start = ((), (), s32[]{:S(2)}) async-start(), calls=%async_computation.25 | async-start | bytes 6488064 | tf_op jit(solution)/shard_map/reduce_scatter | solution.py:301
  1231.2 1.2 copy-start.13
  1231.2 1.6 copy-start.15
  1231.2 308.5 %reduce-scatter.17.cloned.1.call-start = ((), (), s32[]{:S(2)}) async-start(), calls=%async_computation.20 | async-start | bytes 7077888 | tf_op jit(solution)/shard_map/reduce_scatter | solution.py:289
  1243.6 0.7 copy-start.21
  1243.6 0.7 copy-start.23
  1243.6 0.7 copy-start.29
  1243.6 0.7 copy-start.34
  1243.7 491.6 %reduce-scatter.21.cloned.1.call-start = ((), (), s32[]{:S(2)}) async-start(), calls=%async_computation.23 | async-start | bytes 12976128 | tf_op jit(solution)/shard_map/reduce_scatter | solution.py:295
  1264.1 542.5 %reduce-scatter.19.cloned.1.call-start = ((), (), s32[]{:S(2)}) async-start(), calls=%async_computation.22 | async-start | bytes 2359296 | tf_op jit(solution)/shard_map/reduce_scatter | solution.py:292
  1272.2 3.0 copy-start.32
  1272.2 35.0 %copy-start.19 = (f32[1,2048]{1,0:T(1,128)S(1)}, f32[1,2048]{1,0:T(1,128)}, u32[]{:S(2)}) copy-start(f32[1,2048]{1,0:T(1,128)} %copy-done.18) | copy-start | bytes 24580
  1272.3 34.9 %copy-start.25 = (f32[1,4,2,128]{3,1,2,0:T(4,128)S(1)}, f32[1,4,2,128]{3,1,2,0:T(4,128)}, u32[]{:S(2)}) copy-start(f32[1,4,2,128]{3,1,2,0:T(4,128)} %copy-done.24) | copy-start | bytes 12292
  1272.3 34.9 %copy-start.27 = (f32[1,4,2,128]{3,1,2,0:T(4,128)S(1)}, f32[1,4,2,128]{3,1,2,0:T(4,128)}, u32[]{:S(2)}) copy-start(f32[1,4,2,128]{3,1,2,0:T(4,128)} %copy-done.26) | copy-start | bytes 12292
  1272.3 598.5 %reduce-scatter.27.cloned.1.call-start = ((), (), s32[]{:S(2)}) async-start(), calls=%async_computation.28 | async-start | bytes 589824
  1313.5 622.4 %reduce-scatter.25.cloned.1.call-start = ((), (), s32[]{:S(2)}) async-start(), calls=%async_computation.27 | async-start | bytes 589824
  1314.6 647.5 %all-gather.26.cloned.1.call-start = ((), (), s32[]{:S(2)}) async-start(), calls=%async_computation.26 | async-start | bytes 2162688 | tf_op jit(solution)/shard_map/all_gather | solution.py:321
  1418.1 572.7 %all-gather.22.cloned.1.call-start = ((), (), s32[]{:S(2)}) async-start(), calls=%async_computation.21 | async-start | bytes 2359296 | tf_op jit(solution)/shard_map/all_gather | solution.py:312
  1539.7 494.5 %all-gather.24.cloned.1.call-start = ((), (), s32[]{:S(2)}) async-start(), calls=%async_computation.24 | async-start | bytes 4325376 | tf_op jit(solution)/shard_map/all_gather | solution.py:318
Sparse Core Ops, SparseCore 0:
  9.6 118.1 all-gather.9
  182.2 31.2 all-gather.13
  215.7 33.1 all-gather.11
  250.3 45.9 all-gather.15
  304.0 151.5 all-reduce.4
  457.1 201.1 all-gather.17
  659.9 104.8 all-gather.19
  798.1 83.7 all-reduce.8
  884.5 152.9 all-reduce.6
  1127.7 31.9 reduce-scatter.12
  1161.9 31.8 reduce-scatter.14
  1217.6 85.5 all-reduce.10
  1307.5 110.5 reduce-scatter.22
  1421.5 118.1 reduce-scatter.16
  1543.1 192.0 reduce-scatter.20
  1739.2 67.3 reduce-scatter.18
  1809.8 60.9 reduce-scatter.26
  1874.9 60.9 reduce-scatter.24
  1937.4 24.6 all-gather.25
  1963.5 27.1 all-gather.21
  1992.3 41.9 all-gather.23
where the time goes:
time: 2050 us
  waiting for transfers between devices  1500 us (73%)
  matrix products  202 us (10%)
  local copies, waits for them, and re-layouts  141 us (7%)
  other arithmetic  115 us (6%)
  blocking collectives  68 us (3%)
    psum x2, waiting for transfers between devices, branch_total(): return lax.psum(values, 'tensor')  299 us
    reduce_scatter x1, waiting for transfers between devices, local(): lax.psum_scatter(grad_w_gate_up.astype(jnp.bfloat16), ('fsdp', 'context')...  195 us
    all_gather x1, waiting for transfers between devices, local(): lax.all_gather(gate_up_weight, 'fsdp', axis=1, tiled=True)  194 us
    reduce_scatter x1, waiting for transfers between devices, local(): lax.psum_scatter(grad_w_qkv.astype(jnp.bfloat16), ('fsdp', 'context'), sc...  122 us
    reduce_scatter x1, waiting for transfers between devices, local(): lax.psum_scatter(grad_w_down.astype(jnp.bfloat16), ('fsdp', 'context'), s...  103 us
    psum x2, waiting for transfers between devices, input_total(): return lax.psum(values.astype(jnp.bfloat16), 'tensor').astype(jnp.float32)  97.3 us
    unnamed x23, waiting for transfers between devices  87.7 us
    all_gather x1, waiting for transfers between devices, local(): lax.all_gather(down_weight, 'fsdp', axis=1, tiled=True)  86.2 us
  transfers between devices with their start and end apart: 21, of which 20 were waited for; matrix products, arithmetic and copies ran while one was open for 12% of the time, Pallas kernels for 0%

commit v1 on v0

v1 whole, which is shorter than its diff:
```python
import math

import jax
import jax.numpy as jnp
import numpy as np
from jax import lax
from jax.experimental import pallas as pl
from jax.experimental.pallas import tpu as pltpu
from jax.sharding import PartitionSpec as P

HEAD_DIM = 64
ROT = 16
EPSILON = 1e-05
F32 = jnp.float32
LOW = jnp.bfloat16


def rotary_tables(length, width):
    column = np.arange(width) % HEAD_DIM
    half = ROT // 2
    frequency = np.power(10000.0, -2.0 * (column % half) / ROT).astype(np.float32)
    angles = np.arange(length, dtype=np.float32)[:, None] * frequency[None, :]
    inside = column < ROT
    lower = column < half
    sine = np.sin(angles)
    cosine = np.where(inside, np.cos(angles), 1.0)
    minus = np.where(lower, -sine, 0.0)
    plus = np.where(inside & ~lower, sine, 0.0)
    return jnp.asarray(np.stack([cosine, minus, plus]).astype(np.float32))

def dot_nt(a,b): return lax.dot_general(a,b,(((1,),(1,)),((),())),preferred_element_type=F32)
def dot_nn(a,b): return lax.dot_general(a,b,(((1,),(0,)),((),())),preferred_element_type=F32)
def dot_tn(a,b): return lax.dot_general(a,b,(((0,),(0,)),((),())),preferred_element_type=F32)

def head_masks(width):
    lane=lax.broadcasted_iota(jnp.int32,(1,width),1)
    return [ (lane//HEAD_DIM)==h for h in range(width//HEAD_DIM)]

def fwd_kernel(block, mixed_ref, bias_ref, table_ref, q_ref, k_ref, v_ref, att_ref, lse_ref):
    length, width = q_ref.shape
    half=ROT//2
    def rotated(c):
        v=mixed_ref[c]+bias_ref[c]
        return v*table_ref[0]+pltpu.roll(v,width-half,1)*table_ref[1]+pltpu.roll(v,half,1)*table_ref[2]
    q_ref[...]=(rotated(0)*(1.0/math.sqrt(HEAD_DIM))).astype(LOW)
    k_ref[...]=rotated(1).astype(LOW)
    v_ref[...]=(mixed_ref[2]+bias_ref[2]).astype(LOW)
    masks=head_masks(width)
    row=lax.broadcasted_iota(jnp.int32,(block,block),0)
    col=lax.broadcasted_iota(jnp.int32,(block,block),1)
    for i in range(length//block):
        rows=pl.ds(i*block,block)
        q=q_ref[rows,:]
        out=jnp.zeros((block,width),F32); lse=jnp.zeros((block,width),F32)
        for mask in masks:
            qh=jnp.where(mask,q,jnp.zeros_like(q))
            diag=jnp.where(row>=col,dot_nt(qh,k_ref[rows,:]),-1e30)
            top=jnp.max(diag,axis=1,keepdims=True)
            if i>0:
                rest=dot_nt(qh,k_ref[pl.ds(0,i*block),:])
                top=jnp.maximum(top,jnp.max(rest,axis=1,keepdims=True))
            diag=jnp.exp(diag-top)
            total=jnp.sum(diag,axis=1,keepdims=True)
            acc=dot_nn(diag.astype(LOW),v_ref[rows,:])
            if i>0:
                rest=jnp.exp(rest-top)
                total=total+jnp.sum(rest,axis=1,keepdims=True)
                acc=acc+dot_nn(rest.astype(LOW),v_ref[pl.ds(0,i*block),:])
            out=jnp.where(mask,acc/total,out)
            lse=jnp.where(mask,top+jnp.log(total),lse)
        att_ref[rows,:]=out.astype(LOW)
        lse_ref[rows,:]=lse

def attend_forward(mixed,bias,tables,seqs,length,block=256):
    pair,_,rows,cols=mixed.shape
    width=min(cols,128); groups=cols//width
    tok=lambda o,s,g:(o,s,g)
    spec=pl.BlockSpec((None,length,width),tok)
    shape=lambda d:jax.ShapeDtypeStruct((pair,rows,cols),d)
    return pl.pallas_call(
        lambda *r: fwd_kernel(block,*r),
        grid=(pair,seqs,groups),
        in_specs=[pl.BlockSpec((None,3,length,width),lambda o,s,g:(o,0,s,g)),
                  pl.BlockSpec((None,3,1,width),lambda o,s,g:(o,0,0,g)),
                  pl.BlockSpec((3,length,width),lambda o,s,g:(0,0,0))],
        out_specs=[spec]*5,
        out_shape=[shape(LOW)]*4+[shape(F32)],
        compiler_params=pltpu.CompilerParams(vmem_limit_bytes=48<<20),
        cost_estimate=pl.CostEstimate(flops=int(4*pair*rows*length*cols*0.6),bytes_accessed=pair*rows*cols*26,transcendentals=pair*rows*length*cols//128),
        name="attend_forward",
    )(mixed,bias,tables)

def bwd_kernel(block,q_ref,k_ref,v_ref,att_ref,lse_ref,do_ref,table_ref,out_ref,dk_acc,dv_acc,dq_acc):
    length,width=q_ref.shape
    half=ROT//2
    masks=head_masks(width)
    row=lax.broadcasted_iota(jnp.int32,(block,block),0)
    col=lax.broadcasted_iota(jnp.int32,(block,block),1)
    count=length//block
    for i in reversed(range(count)):
        rows=pl.ds(i*block,block)
        q=q_ref[rows,:]; do=do_ref[rows,:]; lse=lse_ref[rows,:]
        prod=do.astype(F32)*att_ref[rows,:].astype(F32)
        n=(i+1)*block
        keys=k_ref[pl.ds(0,n),:]; vals=v_ref[pl.ds(0,n),:]
        dq=jnp.zeros((block,width),F32)
        dk=None
        for h,mask in enumerate(masks):
            qh=jnp.where(mask,q,jnp.zeros_like(q)); dh=jnp.where(mask,do,jnp.zeros_like(do))
            delta=jnp.sum(jnp.where(mask,prod,0.0),axis=1,keepdims=True)
            lse_h=lse[:,h*HEAD_DIM:h*HEAD_DIM+1]
            s=dot_nt(qh,keys)
            p=jnp.exp(s-lse_h)
            if i==0:
                p=jnp.where(row>=col,p,0.0)
            else:
                p=jnp.concatenate([p[:,:n-block],jnp.where(row>=col,p[:,n-block:],0.0)],axis=1)
            dp=dot_nt(dh,vals)
            ds=(p*(dp-delta)).astype(LOW)
            pl_low=p.astype(LOW)
            dq=jnp.where(mask,dot_nn(ds,keys),dq)
            tk=dot_tn(ds,qh); tv=dot_tn(pl_low,dh)
            dk=tk if dk is None else dk+tk
            dv=tv if h==0 else dv+tv
        dq_acc[rows,:]=dq*(1.0/math.sqrt(HEAD_DIM))
        if i==count-1:
            dk_acc[...]=dk; dv_acc[...]=dv
        else:
            dk_acc[pl.ds(0,n),:]+=dk; dv_acc[pl.ds(0,n),:]+=dv
    def back(v):
        return v*table_ref[0]+pltpu.roll(v*table_ref[1],half,1)+pltpu.roll(v*table_ref[2],width-half,1)
    out_ref[0]=back(dq_acc[...]).astype(LOW)
    out_ref[1]=back(dk_acc[...]).astype(LOW)
    out_ref[2]=dv_acc[...].astype(LOW)

def attend_back(q,k,v,att,lse,grad,tables,seqs,length,block=256):
    pair,rows,cols=q.shape
    width=min(cols,128); groups=cols//width
    spec=pl.BlockSpec((None,length,width),lambda o,s,g:(o,s,g))
    return pl.pallas_call(
        lambda *r: bwd_kernel(block,*r),
        grid=(pair,seqs,groups),
        in_specs=[spec]*6+[pl.BlockSpec((3,length,width),lambda o,s,g:(0,0,0))],
        out_specs=pl.BlockSpec((None,3,length,width),lambda o,s,g:(o,0,s,g)),
        out_shape=jax.ShapeDtypeStruct((pair,3,rows,cols),LOW),
        scratch_shapes=[pltpu.VMEM((length,width),F32)]*3,
        compiler_params=pltpu.CompilerParams(vmem_limit_bytes=48<<20),
        cost_estimate=pl.CostEstimate(flops=int(10*pair*rows*length*cols*0.6),bytes_accessed=pair*rows*cols*20,transcendentals=pair*rows*length*cols//128),
        name="attend_back",
    )(q,k,v,att,lse,grad,tables)


class Place:
    def __init__(self):
        self.fsdp = lax.axis_size("fsdp")
        self.context = lax.axis_size("context")
        self.tensor = lax.axis_size("tensor")
        self.pairs = self.tensor // 2
        self.z = lax.axis_index("fsdp")
        self.x = lax.axis_index("context")
        self.t = lax.axis_index("tensor")
        self.y = self.t // 2
        self.core = self.t % 2

    def size(self, which):
        return self.context if which == "x" else self.pairs

    def at(self, which):
        return self.x if which == "x" else self.y

    def shift(self, value, which, step):
        if which == "z":
            n = self.fsdp
            return lax.ppermute(value, "fsdp", [(i, (i + step) % n) for i in range(n)])
        if which == "x":
            n = self.context
            return lax.ppermute(value, "context", [(i, (i + step) % n) for i in range(n)])
        n = self.tensor
        return lax.ppermute(value, "tensor", [(i, (i + 2 * step) % n) for i in range(n)])

    def swap(self, value):
        return lax.ppermute(value, "tensor", [(i, i ^ 1) for i in range(self.tensor)])


def pick(value, index, axis):
    return lax.dynamic_index_in_dim(value, index, axis, keepdims=False)


def scatter_stage(place, value, axis, which):
    n, at = place.size(which), place.at(which)
    total = pick(value, at, axis).astype(F32)
    for step in range(1, n):
        sent = pick(value, (at + step) % n, axis)
        total = total + place.shift(sent, which, step).astype(F32)
    return total


def gather_stage(place, value, axis, which):
    n, at = place.size(which), place.at(which)
    if n == 1:
        return jnp.expand_dims(value, axis)
    if n == 2:
        other = place.shift(value, which, 1)
        return jnp.where(at == 0, jnp.stack([value, other], axis), jnp.stack([other, value], axis))
    parts = [value] + [place.shift(value, which, step) for step in range(1, n)]
    order = (at - jnp.arange(n)) % n
    return jnp.take(jnp.stack(parts, axis), order, axis=axis)


def sum_rows(place, value, seqs):
    feat = value.shape[1]
    value = value.reshape(seqs, place.context, place.pairs, -1, feat)
    first, second = value[..., : feat // 2], value[..., feat // 2 :]
    first = scatter_stage(place, first, 1, "x").astype(LOW)
    second = scatter_stage(place, second, 2, "y").astype(LOW)
    first = scatter_stage(place, first, 1, "y")
    second = scatter_stage(place, second, 1, "x")
    return jnp.concatenate([first, second], axis=-1)


def spread_rows(place, value):
    feat = value.shape[-1]
    first, second = value[..., : feat // 2], value[..., feat // 2 :]
    first = gather_stage(place, first, 1, "y")
    second = gather_stage(place, second, 1, "x")
    first = gather_stage(place, first, 1, "x")
    second = gather_stage(place, second, 2, "y")
    return jnp.concatenate([first, second], axis=-1).reshape(-1, feat)


def whole_rows(place, value):
    value = gather_stage(place, value, 1, "y")
    seqs, pairs, rows, feat = value.shape
    value = value.reshape(seqs, pairs * rows, feat)
    other = place.swap(value)
    return jnp.where(
        place.core == 0,
        jnp.concatenate([value, other]),
        jnp.concatenate([other, value]),
    )


def gather_weight(place, shard, axis):
    n, z = place.fsdp, place.z
    size = shard.shape[axis]
    if n != 4:
        mine = lax.all_gather(shard, "fsdp", axis=axis, tiled=True)
        return jnp.stack([mine, place.swap(mine)])
    half = size // 2
    before = place.shift(shard, "z", 1)
    after = place.shift(shard, "z", -1)
    low = place.shift(lax.slice_in_dim(before, 0, half, axis=axis), "z", 1)
    high = place.shift(lax.slice_in_dim(after, half, size, axis=axis), "z", -1)
    shape = list(shard.shape)
    shape[axis] = n * size
    whole = jnp.zeros([2] + shape, shard.dtype)
    parts = [
        (shard, z * size),
        (before, (z + 3) % n * size),
        (after, (z + 1) % n * size),
        (low, (z + 2) % n * size),
        (high, (z + 2) % n * size + half),
    ]
    for part, start in parts:
        for slot, piece in enumerate((part, place.swap(part))):
            where = [0] * (shard.ndim + 1)
            where[0], where[axis + 1] = slot, start
            whole = lax.dynamic_update_slice(whole, piece[None], where)
    return whole


def scatter_grad(place, grad, axis):
    n, z = place.fsdp, place.z
    if n != 4:
        return lax.psum_scatter(grad, "fsdp", scatter_dimension=axis, tiled=True)
    size = grad.shape[axis] // n
    half = size // 2

    def part(ahead, start, count):
        return lax.dynamic_slice_in_dim(grad, (z + ahead) % n * size + start, count, axis)

    def added(one, two):
        return (one.astype(F32) + two.astype(F32)).astype(LOW)

    from_left = place.shift(part(2, half, half), "z", 1)
    from_right = place.shift(part(2, 0, half), "z", -1)
    left_low = place.shift(part(1, 0, half), "z", 1)
    right_high = place.shift(part(3, half, half), "z", -1)
    left_high = place.shift(added(part(1, half, half), from_left), "z", 1)
    right_low = place.shift(added(part(3, 0, half), from_right), "z", -1)
    low = part(0, 0, half).astype(F32) + left_low.astype(F32) + right_low.astype(F32)
    high = part(0, half, half).astype(F32) + left_high.astype(F32) + right_high.astype(F32)
    return jnp.concatenate([low, high], axis=axis).astype(LOW)


def join_context(place, value, axis):
    value = gather_stage(place, value, axis, "x")
    shape = list(value.shape)
    shape[axis : axis + 2] = [shape[axis] * shape[axis + 1]]
    return value.reshape(shape).astype(F32)


def product_grad(mine, theirs, my_grad, their_grad):
    total = dot_tn(mine, my_grad) + dot_tn(theirs, their_grad)
    return total.astype(LOW)


def norm_forward(values, gain, shift):
    row_mean = jnp.mean(values, axis=-1, keepdims=True)
    centred = values - row_mean
    variance = jnp.mean(centred * centred, axis=-1, keepdims=True)
    inv_std = lax.rsqrt(variance + EPSILON)
    scaled = centred * inv_std
    return scaled * gain + shift, scaled, inv_std


def norm_backward(grad_out, scaled, inv_std, gain):
    grad_scaled = grad_out * gain
    first_mean = jnp.mean(grad_scaled, axis=-1, keepdims=True)
    second_mean = jnp.mean(grad_scaled * scaled, axis=-1, keepdims=True)
    grad_in = inv_std * (grad_scaled - first_mean - scaled * second_mean)
    sums = jnp.stack([jnp.sum(grad_out * scaled, axis=(0, 1)), jnp.sum(grad_out, axis=(0, 1))])
    return grad_in, sums


def local(
    hidden_in,
    norm_gains,
    norm_biases,
    qkv_weight,
    qkv_bias,
    out_weight,
    gate_up_weight,
    down_weight,
    cotangent,
):
    place = Place()
    all_seqs, part_rows, feat = hidden_in.shape
    seqs = all_seqs // 2
    length = part_rows * place.context
    own_rows = part_rows // place.pairs
    head_cols = qkv_bias.shape[1] // place.context
    hidden_cols = down_weight.shape[0] // place.context

    def columns(value, count, axis):
        return lax.dynamic_slice_in_dim(value, place.x * count, count, axis)

    def own_sequences(value):
        return lax.dynamic_slice_in_dim(value, place.core * seqs, seqs, 0)

    def own_piece(value):
        return lax.dynamic_slice_in_dim(value, place.y * own_rows, own_rows, 1)

    norms = lax.all_gather(jnp.stack([norm_gains, norm_biases]), "fsdp", axis=2, tiled=True).astype(F32)
    gain_rows, shift_rows = norms[0], norms[1]
    w_qkv = gather_weight(place, columns(qkv_weight, head_cols, 2), 1)
    hidden_mine = own_sequences(hidden_in)
    hidden_full = gather_stage(place, hidden_mine, 1, "x").reshape(seqs * length, feat)
    w_out = gather_weight(place, columns(out_weight, head_cols, 0), 1)
    w_gate_up = gather_weight(place, columns(gate_up_weight, hidden_cols, 2), 1)
    w_down = gather_weight(place, columns(down_weight, hidden_cols, 0), 1)
    grad_top_mine = own_sequences(cotangent)
    grad_top = gather_stage(place, grad_top_mine, 1, "x").reshape(seqs * length, feat)
    bias = columns(qkv_bias, head_cols, 1)
    bias = jnp.stack([bias, place.swap(bias)]).astype(F32)[:, :, None, :]

    normed = norm_forward(hidden_full.astype(F32), gain_rows[0], shift_rows[0])[0].astype(LOW)
    mixed = jnp.einsum("rd,ocde->ocre", normed, w_qkv, preferred_element_type=F32)
    tables = rotary_tables(length, min(head_cols, 128))
    query, keys, values, attended, log_total = attend_forward(mixed, bias, tables, seqs, length)
    attn_term = jnp.einsum("ore,oed->rd", attended, w_out, preferred_element_type=F32).astype(LOW)
    inputs = own_piece(hidden_mine).astype(F32)
    middle = inputs + sum_rows(place, attn_term, seqs)
    normed_two, scaled_two, inv_two = norm_forward(middle, gain_rows[1], shift_rows[1])
    normed_two = spread_rows(place, normed_two.astype(LOW))
    gate_up = jnp.einsum("rd,ocdf->ocrf", normed_two, w_gate_up, preferred_element_type=F32)
    gate, up = gate_up[:, 0], gate_up[:, 1]
    sig = jax.nn.sigmoid(gate)
    act = gate * sig
    hidden = (act * up).astype(LOW)
    down_term = jnp.einsum("orf,ofd->rd", hidden, w_down, preferred_element_type=F32).astype(LOW)
    final_out = (middle + sum_rows(place, down_term, seqs)).astype(LOW)
    layer_out = whole_rows(place, final_out)

    grad_down = product_grad(hidden[0], place.swap(hidden[1]), grad_top, place.swap(grad_top))
    grad_hidden = jnp.einsum("rd,ofd->orf", grad_top, w_down, preferred_element_type=F32)
    grad_gate = grad_hidden * up * (sig * (1.0 + gate * (1.0 - sig)))
    grad_up = grad_hidden * act
    grad_gu = jnp.stack([grad_gate, grad_up], axis=1).astype(LOW)
    grad_two = jnp.einsum("ocrf,ocdf->rd", grad_gu, w_gate_up, preferred_element_type=F32).astype(LOW)
    theirs_two, theirs_gu = place.swap(normed_two), place.swap(grad_gu[1])
    grad_gate_up = jnp.stack(
        [product_grad(normed_two, theirs_two, grad_gu[0, c], theirs_gu[c]) for c in range(2)]
    )
    grad_mid, sums_two = norm_backward(sum_rows(place, grad_two, seqs), scaled_two, inv_two, gain_rows[1])
    grad_middle = own_piece(grad_top_mine).astype(F32) + grad_mid
    grad_mid_low = spread_rows(place, grad_middle.astype(LOW))
    grad_out = product_grad(
        attended[0], place.swap(attended[1]), grad_mid_low, place.swap(grad_mid_low)
    )
    grad_att = jnp.einsum("rd,oed->ore", grad_mid_low, w_out, preferred_element_type=F32).astype(LOW)
    grad_mixed = attend_back(query, keys, values, attended, log_total, grad_att, tables, seqs, length)
    theirs_one, theirs_mixed = place.swap(normed), place.swap(grad_mixed[1])
    grad_qkv = jnp.stack(
        [product_grad(normed, theirs_one, grad_mixed[0, c], theirs_mixed[c]) for c in range(3)]
    )
    grad_one = jnp.einsum("ocre,ocde->rd", grad_mixed, w_qkv, preferred_element_type=F32).astype(LOW)
    _, scaled_one, inv_one = norm_forward(inputs, gain_rows[0], shift_rows[0])
    grad_first, sums_one = norm_backward(sum_rows(place, grad_one, seqs), scaled_one, inv_one, gain_rows[0])
    input_grad = whole_rows(place, (grad_middle + grad_first).astype(LOW)).astype(F32)

    sums = lax.psum(jnp.stack([sums_one, sums_two], axis=1), ("fsdp", "context", "tensor"))
    sums = lax.dynamic_slice_in_dim(sums, place.z * norm_gains.shape[1], norm_gains.shape[1], 2)
    bias_part = jnp.sum(grad_mixed.astype(F32), axis=2)
    bias_part = bias_part[0] + place.swap(bias_part[1])
    grad_bias = lax.dynamic_update_slice(
        jnp.zeros(qkv_bias.shape, F32), bias_part, (0, place.x * head_cols)
    )
    grad_bias = lax.psum(grad_bias, ("fsdp", "context"))

    return (
        layer_out,
        input_grad,
        sums[0],
        sums[1],
        join_context(place, scatter_grad(place, grad_qkv, 1), 2),
        grad_bias,
        join_context(place, scatter_grad(place, grad_out, 1), 0),
        join_context(place, scatter_grad(place, grad_gate_up, 1), 2),
        join_context(place, scatter_grad(place, grad_down, 1), 0),
    )


def solution(mesh):
    placed = (
        P("fsdp", "context", None),
        P(None, "fsdp"),
        P(None, "fsdp"),
        P(None, "fsdp", "tensor"),
        P(None, "tensor"),
        P("tensor", "fsdp"),
        P(None, "fsdp", "tensor"),
        P("tensor", "fsdp"),
        P("fsdp", "context", None),
    )
    return jax.shard_map(
        local,
        mesh=mesh,
        in_specs=placed,
        out_specs=(
            P("fsdp", "context", None),
            P("fsdp", "context", None),
            P(None, "fsdp"),
            P(None, "fsdp"),
            P(None, "fsdp", "tensor"),
            P(None, "tensor"),
            P("tensor", "fsdp"),
            P(None, "fsdp", "tensor"),
            P("tensor", "fsdp"),
        ),
        check_vma=False,
    )
```

time: 2050 us -> 956 us (0.47)
  waiting for transfers between devices: 1500 us -> 383 us
  starting transfers between devices: 0.85 us -> 88.1 us
  matrix products: 202 us -> 146 us
  Pallas kernels: 0 us -> 39.4 us
  local copies, waits for them, and re-layouts: 141 us -> 106 us
  blocking collectives: 68 us -> 98.5 us
  other arithmetic: 115 us -> 85.2 us
    reduce_scatter x6 -> x0, waiting for transfers between devices: 510 us -> none  [the longest x1 195 us: local(): lax.psum_scatter(grad_w_gate_up.astype(jnp.bfloat16), ('fsdp', 'context')...]
    all_gather x9 -> x0, waiting for transfers between devices: 509 us -> none  [the longest x1 194 us: local(): lax.all_gather(gate_up_weight, 'fsdp', axis=1, tiled=True)]
    psum x4 -> x0, waiting for transfers between devices: 396 us -> none  [the longest x2 299 us: branch_total(): return lax.psum(values, 'tensor')]
    ppermute x0 -> x104, waiting for transfers between devices: none -> 383 us  [the longest x40 277 us: shift(): return lax.ppermute(value, 'fsdp', [(i, (i + step) % n) for i in range(n)])]
    ppermute x0 -> x104, starting transfers between devices: none -> 88.1 us  [the longest x40 50.8 us: shift(): return lax.ppermute(value, 'fsdp', [(i, (i + step) % n) for i in range(n)])]
    unnamed x23 -> x0, waiting for transfers between devices: 87.7 us -> none
    psum x1 -> x2, blocking collectives: 20.9 us -> 86.6 us  [the longest x1 63.9 us: local(): lax.psum(jnp.stack([sums_one, sums_two], axis=1), ('fsdp', 'context', 'te...]
    dot_general x40 -> x22, matrix products: 202 us -> 146 us  [the longest x14 56.9 us: dot_tn(): lax.dot_general(a, b, (((0,), (0,)), ((), ())), preferred_element_type=F32)]
  transfers between devices with their start and end apart: 21 -> 104, of which waited for: 20 -> 38; matrix products, arithmetic and copies ran while one was open for 12% -> 35% of each run, Pallas kernels for 0% -> 4%
where the time goes in v1:
time: 956 us; the launch traced here: 948 us
  waiting for transfers between devices  383 us (40%)
  matrix products  146 us (15%)
  local copies, waits for them, and re-layouts  106 us (11%)
  blocking collectives  98.5 us (10%)
  starting transfers between devices  88.1 us (9%)
  other arithmetic  85.2 us (9%)
  Pallas kernels  39.4 us (4%)
    ppermute x40, waiting for transfers between devices, shift(): return lax.ppermute(value, 'fsdp', [(i, (i + step) % n) for i in range(n)])  277 us
    psum x1, blocking collectives, local(): lax.psum(jnp.stack([sums_one, sums_two], axis=1), ('fsdp', 'context', 'te...  63.9 us
    ppermute x14, waiting for transfers between devices, shift(): lax.ppermute(value, 'tensor', [(i, (i + 2 * step) % n) for i in range(n)])  59.7 us
    dot_general x14, matrix products, dot_tn(): lax.dot_general(a, b, (((0,), (0,)), ((), ())), preferred_element_type=F32)  56.9 us
    ppermute x40, starting transfers between devices, shift(): return lax.ppermute(value, 'fsdp', [(i, (i + step) % n) for i in range(n)])  50.8 us
    ppermute x18, waiting for transfers between devices, shift(): lax.ppermute(value, 'context', [(i, (i + step) % n) for i in range(n)])  45.1 us
    dynamic_update_slice x40, local copies, waits for them, and re-layouts, gather_weight(): whole = lax.dynamic_update_slice(whole, piece[None], where)  44.6 us
    psum x1, blocking collectives, local(): grad_bias = lax.psum(grad_bias, ('fsdp', 'context'))  22.7 us
  transfers between devices with their start and end apart: 104, of which 38 were waited for; matrix products, arithmetic and copies ran while one was open for 35% of the time, Pallas kernels for 4%

profile of v1, /device:TPU:0, one launch (start us, length us, event | category | flops | bytes accessed | tf_op | source)
XLA Modules:
  0.0 948.0 jit_solution(4512397092180269957)
XLA Ops:
  23.7 11.9 %all_gather.3 = bf16[2,2,2048]{2,1,0:T(2,128)(2,1)S(1)} all-gather(bf16[2,2,512]{2,1,0:T(2,128)(2,1)S(1)} %pad_maximum_fusion.12), channel_id=1, replica_groups=mesh['fsdp'=4,'context'=2,'tensor'=4] {'fsdp'}, dimensions={2}, use_global_device_ids=true | all-gather | bytes 20480 | tf_op jit(solution)/shard_map/all_gather | solution.py:354
  40.8 5.7 broadcast_in_dim.168
  52.4 3.7 collective-permute-start.40
  60.7 29.0 %collective-permute-done.16 = bf16[256,256]{1,0:T(8,128)(2,1)S(1)} collective-permute-done((bf16[256,256]{1,0:T(8,128)(2,1)S(1)}, bf16[256,256]{1,0:T(8,128)(2,1)S(1)}, u32[]{:S(2)}, u32[]{:S(2)}) %collective-permute-start.16) | collective-permute-done | bytes 131104 | tf_op jit(solution)/shard_map/ppermute | solution.py:174
  91.2 3.5 collective-permute-done.18
  97.2 3.8 collective-permute-start.3
  106.0 13.4 %collective-permute-done.1 = bf16[3,512,256]{2,1,0:T(8,128)(2,1)S(1)} collective-permute-done((bf16[3,512,256]{2,1,0:T(8,128)(2,1)S(1)}, bf16[3,512,256]{2,1,0:T(8,128)(2,1)S(1)}, u32[]{:S(2)}, u32[]{:S(2)}) %collective-permute-start.1) | collective-permute-done | bytes 786464 | tf_op jit(solution)/shard_map/ppermute | solution.py:174
  119.4 14.2 %collective-permute-done.3 = bf16[3,512,256]{2,1,0:T(8,128)(2,1)S(1)} collective-permute-done((bf16[3,512,256]{2,1,0:T(8,128)(2,1)S(1)}, bf16[3,512,256]{2,1,0:T(8,128)(2,1)S(1)}, u32[]{:S(2)}, u32[]{:S(2)}) %collective-permute-start.3) | collective-permute-done | bytes 786464 | tf_op jit(solution)/shard_map/ppermute | solution.py:174
  140.0 65.0 %collective-permute-done.42 = bf16[704,256]{1,0:T(8,128)(2,1)S(1)} collective-permute-done((bf16[704,256]{1,0:T(8,128)(2,1)S(1)}, bf16[704,256]{1,0:T(8,128)(2,1)S(1)}, u32[]{:S(2)}, u32[]{:S(2)}) %collective-permute-start.42) | collective-permute-done | bytes 360480 | tf_op jit(solution)/shard_map/ppermute | solution.py:174
  209.8 4.9 collective-permute-done.44
  218.6 3.8 collective-permute-start.7
  225.1 4.6 collective-permute-done.5
  231.3 5.9 collective-permute-done.7
  247.5 7.8 collective-permute-done.9
  258.4 7.3 fusion.5
  265.7 11.8 %fusion.32.r_0_ = f32[2,3,1024,256]{3,2,1,0:T(8,128)} fusion(bf16[2,3,2048,256]{3,2,0,1:T(8,128)(2,1)} %bitcast_dynamic-update-slice_fusion.22, bf16[1024,2048]{1,0:T(8,128)(2,1)} %fusion.5), kind=kOutput, calls=%fused_computation.72 | convolution fusion | flops 6442450944 | bytes 16777216 | tf_op jit(solution)/shard_map/rd,ocde->ocre/dot_general | solution.py:368
  277.6 17.7 %attend_forward.1 = (bf16[2,1024,256]{2,1,0:T(8,128)(2,1)S(1)}, bf16[2,1024,256]{2,1,0:T(8,128)(2,1)S(1)}, bf16[2,1024,256]{2,1,0:T(8,128)(2,1)S(1)}, bf16[2,1024,256]{2,1,0:T(8,128)(2,1)S(1)}, f32[2,1024,256]{2,1,0:T(8,128)}) custom-call(f32[2,3,1024,256]{3,2,1,0:T(8,128)} %fusion.32.r_0_, f32[2,3,1,256]{3,2,1,0:T(1,128)S(1)} %maximum_convert_fusion.r_1_, ...), custom_call_target="tpu_custom_call" | custom-call | flops 1288490240 | bytes 13631488 | tf_op jit(solution)/shard_map/attend_forward/pallas_call | solution.py:80
  295.3 4.3 bitcast_convert_fusion.3
  301.9 3.9 add_convert_fusion
  313.8 11.1 %collective-permute-done.22 = bf16[1,2,256,1024]{3,2,1,0:T(8,128)(2,1)S(1)} collective-permute-done((bf16[1,2,256,1024]{3,2,1,0:T(8,128)(2,1)S(1)}, bf16[1,2,256,1024]{3,2,1,0:T(8,128)(2,1)S(1)}, u32[]{:S(2)}, u32[]{:S(2)}) %collective-permute-start.22) | collective-permute-done | bytes 1048608 | tf_op jit(solution)/shard_map/ppermute | solution.py:179
  326.9 5.9 collective-permute-done.20
  335.6 6.6 collective-permute-done.23
  353.2 6.9 collective-permute-done.35
  368.0 17.1 %collective-permute-done.36 = bf16[1,2,256,1024]{3,2,1,0:T(8,128)(2,1)S(1)} collective-permute-done((bf16[1,2,256,1024]{3,2,1,0:T(8,128)(2,1)S(1)}, bf16[1,2,256,1024]{3,2,1,0:T(8,128)(2,1)S(1)}, u32[]{:S(2)}, u32[]{:S(2)}) %collective-permute-start.36) | collective-permute-done | bytes 1048608 | tf_op jit(solution)/shard_map/ppermute | solution.py:179
  386.4 17.2 %fusion.21 = f32[2,2,1024,704]{2,3,1,0:T(8,128)} fusion(bf16[2,2,2048,704]{2,3,0,1:T(8,128)(2,1)} %bitcast_dynamic-update-slice_fusion.12, bf16[1024,1024]{1,0:T(8,128)(2,1)S(1)} %bitcast.497, bf16[1024,1024]{1,0:T(8,128)(2,1)S(1)} %bitcast.501), kind=kOutput, calls=%fused_computation.61 | convolution fusion | flops 11819548672 | bytes 27262976 | tf_op jit(solution)/shard_map/rd,ocdf->ocrf/dot_general | solution.py:376
  403.6 15.5 %fusion.13 = (bf16[2,1024,704]{1,2,0:T(8,128)(2,1)}, bf16[2,1024,704]{1,2,0:T(8,128)(2,1)}, bf16[2,1024,704]{1,2,0:T(8,128)(2,1)}) fusion(f32[2,2,1024,704]{2,3,1,0:T(8,128)} %fusion.21, bf16[2,704,2048]{2,1,0:T(8,128)(2,1)} %bitcast_dynamic-update-slice_fusion.26, bf16[1024,2048,1]{1,0,2:T(8,128)(2,1)S(1)} %bitcast.518), kind=kOutput, calls=%fused_computation.42 | convolution fusion | flops 5927206912 | bytes 30146560 | tf_op jit(solution)/shard_map/rd,ofd->orf/dot_general | solution.py:386
  419.1 18.4 %bitcast_convert_fusion.1 = bf16[1024,2048]{1,0:T(8,128)(2,1)} fusion(bf16[2,2,2048,704]{2,3,0,1:T(8,128)(2,1)} %bitcast_dynamic-update-slice_fusion.12, bf16[2,1,1024,704]{2,3,0,1:T(8,128)(2,1)} %bitcast.531, bf16[2,1,1024,704]{2,3,0,1:T(8,128)(2,1)} %bitcast.529), kind=kOutput, calls=%fused_computation.19 | convolution fusion | flops 11816140800 | bytes 21495808 | tf_op jit(solution)/shard_map/ocrf,ocdf->rd/dot_general | solution.py:390
  441.9 9.1 bitcast_convert_fusion.2
  451.1 5.1 fusion.65
  456.2 5.5 fusion.64
  473.0 13.3 %collective-permute-done.48 = bf16[1,2,256,1024]{3,2,1,0:T(8,128)(2,1)} collective-permute-done((bf16[1,2,256,1024]{3,2,1,0:T(8,128)(2,1)S(1)}, bf16[1,2,256,1024]{3,2,1,0:T(8,128)(2,1)}, u32[]{:S(2)}, u32[]{:S(2)}) %collective-permute-start.48) | collective-permute-done | bytes 1048608 | tf_op jit(solution)/shard_map/ppermute | solution.py:179
  493.5 7.3 fusion.105
  500.8 5.2 add_convert_fusion.1
  509.4 3.7 fusion.98
  525.5 4.4 collective-permute-done.97
  531.4 6.1 collective-permute-done.100
  539.1 3.8 collective-permute-done.99
  544.4 7.6 collective-permute-done.102
  552.0 4.8 collective-permute-done.101
  560.1 14.2 %collective-permute-done.60 = bf16[1,2,256,1024]{3,2,1,0:T(8,128)(2,1)S(1)} collective-permute-done((bf16[1,2,256,1024]{3,2,1,0:T(8,128)(2,1)S(1)}, bf16[1,2,256,1024]{3,2,1,0:T(8,128)(2,1)S(1)}, u32[]{:S(2)}, u32[]{:S(2)}) %collective-permute-start.60) | collective-permute-done | bytes 1048608 | tf_op jit(solution)/shard_map/ppermute | solution.py:179
  575.6 4.0 fusion.66.r_5_
  579.6 21.7 %attend_back.1 = bf16[2,3,1024,256]{3,2,1,0:T(8,128)(2,1)} custom-call(bf16[2,1024,256]{2,1,0:T(8,128)(2,1)S(1)} %get-tuple-element.15.r_0_, bf16[2,1024,256]{2,1,0:T(8,128)(2,1)S(1)} %get-tuple-element.16.r_1_, bf16[2,1024,256]{2,1,0:T(8,128)(2,1)S(1)} %get-tuple-element.17.r_2_, bf16[2,1024,256]{2,1,0:T(8,128)(2,1)S(1)} %copy-done.3, ...), custom_call_target="tpu_custom_call" | custom-call | flops 3221225472 | bytes 10485760 | tf_op jit(solution)/shard_map/attend_back/pallas_call | solution.py:140
  604.2 8.8 bitcast_convert_fusion
  623.7 22.7 %psum.15 = f32[3,512]{1,0:T(4,128)} all-reduce(f32[3,512]{1,0:T(4,128)S(1)} %constant_dynamic-update-slice_fusion), channel_id=1, replica_groups=mesh['fsdp'=4,'context'=2,'tensor'=4] {'fsdp','context'}, use_global_device_ids=true, to_apply=%region_16.17 | all-reduce | flops 1536 | bytes 12288 | tf_op jit(solution)/shard_map/psum | solution.py:419
  653.2 7.5 fusion.29
  660.7 15.1 %collective-permute-done.61 = bf16[1,2,256,1024]{3,2,1,0:T(8,128)(2,1)S(1)} collective-permute-done((bf16[1,2,256,1024]{3,2,1,0:T(8,128)(2,1)S(1)}, bf16[1,2,256,1024]{3,2,1,0:T(8,128)(2,1)S(1)}, u32[]{:S(2)}, u32[]{:S(2)}) %collective-permute-start.61) | collective-permute-done | bytes 1048608 | tf_op jit(solution)/shard_map/ppermute | solution.py:177
  676.5 7.5 fusion.30
  687.7 3.5 fusion.83
  692.7 3.5 fusion.85
  697.7 3.5 fusion.87
  706.8 3.9 collective-permute-start.70
  711.8 35.6 %collective-permute-done.70 = bf16[3,256,256]{2,1,0:T(8,128)(2,1)S(1)} collective-permute-done((bf16[3,256,256]{2,1,0:T(8,128)(2,1)S(1)}, bf16[3,256,256]{2,1,0:T(8,128)(2,1)S(1)}, u32[]{:S(2)}, u32[]{:S(2)}) %collective-permute-start.70) | collective-permute-done | bytes 393248 | tf_op jit(solution)/shard_map/ppermute | solution.py:174
  754.7 8.2 collective-permute-done.72
  763.0 7.1 collective-permute-done.71
  773.6 12.0 %collective-permute-done.93 = bf16[2,256,704]{1,2,0:T(8,128)(2,1)S(1)} collective-permute-done((bf16[2,256,704]{1,2,0:T(8,128)(2,1)S(1)}, bf16[2,256,704]{1,2,0:T(8,128)(2,1)S(1)}, u32[]{:S(2)}, u32[]{:S(2)}) %collective-permute-start.93) | collective-permute-done | bytes 720928 | tf_op jit(solution)/shard_map/ppermute | solution.py:174
  785.6 16.7 %collective-permute-done.90 = bf16[2,256,704]{1,2,0:T(8,128)(2,1)S(1)} collective-permute-done((bf16[2,256,704]{1,2,0:T(8,128)(2,1)S(1)}, bf16[2,256,704]{1,2,0:T(8,128)(2,1)S(1)}, u32[]{:S(2)}, u32[]{:S(2)}) %collective-permute-start.90) | collective-permute-done | bytes 720928 | tf_op jit(solution)/shard_map/ppermute | solution.py:174
  802.7 15.1 %collective-permute-done.92 = bf16[2,256,704]{1,2,0:T(8,128)(2,1)S(1)} collective-permute-done((bf16[2,256,704]{1,2,0:T(8,128)(2,1)S(1)}, bf16[2,256,704]{1,2,0:T(8,128)(2,1)S(1)}, u32[]{:S(2)}, u32[]{:S(2)}) %collective-permute-start.92) | collective-permute-done | bytes 720928 | tf_op jit(solution)/shard_map/ppermute | solution.py:174
  820.9 5.2 collective-permute-done.74
  826.1 7.1 collective-permute-done.73
  838.7 63.9 %psum.14 = f32[2,2,2048]{2,1,0:T(2,128)S(1)} all-reduce(f32[2,2,2048]{2,1,0:T(2,128)S(1)} %pad_maximum_fusion.9), channel_id=1, replica_groups=mesh['fsdp'=4,'context'=2,'tensor'=4] {'fsdp','context','tensor'}, use_global_device_ids=true, to_apply=%region_14.15 | all-reduce | flops 8192 | bytes 65536 | tf_op jit(solution)/shard_map/psum | solution.py:412
  913.0 3.5 copy.87
  916.5 3.6 copy.89
  929.7 6.2 copy.90
  939.3 7.3 fusion.16
  (454 shorter events, 241.6 us)
Async XLA Ops:
  4.1 48.3 %collective-permute-start.11 = (bf16[256,512]{1,0:T(8,128)(2,1)}, bf16[256,512]{1,0:T(8,128)(2,1)}, u32[]{:S(2)}, u32[]{:S(2)}) collective-permute-start(bf16[256,512]{1,0:T(8,128)(2,1)} %get-tuple-element.43), channel_id=1, source_target_pairs={{0,1},{1,0},{2,3},{3,2},{4,5},{5,4},{6,7},{7,6},{8,9},{9,8},{10,11... | collective-permute-start | bytes 786440 | tf_op jit(solution)/shard_map/ppermute | solution.py:182
  4.6 51.6 %collective-permute-start.12 = (bf16[256,512]{1,0:T(8,128)(2,1)}, bf16[256,512]{1,0:T(8,128)(2,1)S(1)}, u32[]{:S(2)}, u32[]{:S(2)}) collective-permute-start(bf16[256,512]{1,0:T(8,128)(2,1)} %get-tuple-element.43), channel_id=1, source_target_pairs={{0,8},{8,16},{16,24},{24,0},{1,9},{9,17},{17,25},{25,1},{2,10},{10... | collective-permute-start | bytes 786440 | tf_op jit(solution)/shard_map/ppermute | solution.py:174
  7.1 50.7 %collective-permute-start.14 = (bf16[256,512]{1,0:T(8,128)(2,1)}, bf16[256,512]{1,0:T(8,128)(2,1)S(1)}, u32[]{:S(2)}, u32[]{:S(2)}) collective-permute-start(bf16[256,512]{1,0:T(8,128)(2,1)} %get-tuple-element.43), channel_id=1, source_target_pairs={{0,24},{8,0},{16,8},{24,16},{1,25},{9,1},{17,9},{25,17},{2,26},{10... | collective-permute-start | bytes 786440 | tf_op jit(solution)/shard_map/ppermute | solution.py:174
  9.2 43.0 %collective-permute-start.10 = (bf16[3,256]{1,0:T(4,128)(2,1)S(1)}, bf16[3,256]{1,0:T(4,128)(2,1)S(1)}, u32[]{:S(2)}, u32[]{:S(2)}) collective-permute-start(bf16[3,256]{1,0:T(4,128)(2,1)S(1)} %constant_dynamic-slice_fusion.18), channel_id=1, source_target_pairs={{0,1},{1,0},{2,3},{3,2},{4,5},{5,4},{6,7},{7,6},{8,9},{9,8},{10,11... | collective-permute-start | bytes 4616 | tf_op jit(solution)/shard_map/ppermute | solution.py:182
  13.8 88.7 %collective-permute-start.37 = (bf16[704,512]{1,0:T(8,128)(2,1)}, bf16[704,512]{1,0:T(8,128)(2,1)}, u32[]{:S(2)}, u32[]{:S(2)}) collective-permute-start(bf16[704,512]{1,0:T(8,128)(2,1)} %get-tuple-element.39), channel_id=1, source_target_pairs={{0,1},{1,0},{2,3},{3,2},{4,5},{5,4},{6,7},{7,6},{8,9},{9,8},{10,11... | collective-permute-start | bytes 2162696 | tf_op jit(solution)/shard_map/ppermute | solution.py:182
  52.2 45.0 %collective-permute-start.38 = (bf16[704,512]{1,0:T(8,128)(2,1)}, bf16[704,512]{1,0:T(8,128)(2,1)S(1)}, u32[]{:S(2)}, u32[]{:S(2)}) collective-permute-start(bf16[704,512]{1,0:T(8,128)(2,1)} %get-tuple-element.39), channel_id=1, source_target_pairs={{0,8},{8,16},{16,24},{24,0},{1,9},{9,17},{17,25},{25,1},{2,10},{10... | collective-permute-start | bytes 2162696 | tf_op jit(solution)/shard_map/ppermute | solution.py:174
  52.4 49.9 %collective-permute-start.40 = (bf16[704,512]{1,0:T(8,128)(2,1)}, bf16[704,512]{1,0:T(8,128)(2,1)S(1)}, u32[]{:S(2)}, u32[]{:S(2)}) collective-permute-start(bf16[704,512]{1,0:T(8,128)(2,1)} %get-tuple-element.39), channel_id=1, source_target_pairs={{0,24},{8,0},{16,8},{24,16},{1,25},{9,1},{17,9},{25,17},{2,26},{10... | collective-permute-start | bytes 2162696 | tf_op jit(solution)/shard_map/ppermute | solution.py:174
  57.9 31.8 %collective-permute-start.16 = (bf16[256,256]{1,0:T(8,128)(2,1)S(1)}, bf16[256,256]{1,0:T(8,128)(2,1)S(1)}, u32[]{:S(2)}, u32[]{:S(2)}) collective-permute-start(bf16[256,256]{1,0:T(8,128)(2,1)S(1)} %slice.204), channel_id=1, source_target_pairs={{0,8},{8,16},{16,24},{24,0},{1,9},{9,17},{17,25},{25,1},{2,10},{10... | collective-permute-start | bytes 393224 | tf_op jit(solution)/shard_map/ppermute | solution.py:174
  58.7 31.0 %collective-permute-start.15 = (bf16[256,512]{1,0:T(8,128)(2,1)S(1)}, bf16[256,512]{1,0:T(8,128)(2,1)S(1)}, u32[]{:S(2)}, u32[]{:S(2)}) collective-permute-start(bf16[256,512]{1,0:T(8,128)(2,1)S(1)} %collective-permute-done.14), channel_id=1, source_target_pairs={{0,1},{1,0},{2,3},{3,2},{4,5},{5,4},{6,7},{7,6},{8,9},{9,8},{10,11... | collective-permute-start | bytes 786440 | tf_op jit(solution)/shard_map/ppermute | solution.py:182
  94.7 41.6 %collective-permute-start = (bf16[3,512,256]{2,1,0:T(8,128)(2,1)S(1)}, bf16[3,512,256]{2,1,0:T(8,128)(2,1)S(1)}, u32[]{:S(2)}, u32[]{:S(2)}) collective-permute-start(bf16[3,512,256]{2,1,0:T(8,128)(2,1)S(1)} %copy-done.31), channel_id=1, source_target_pairs={{0,1},{1,0},{2,3},{3,2},{4,5},{5,4},{6,7},{7,6},{8,9},{9,8},{10,11... | collective-permute-start | bytes 2359304 | tf_op jit(solution)/shard_map/ppermute | solution.py:182
  97.2 36.4 %collective-permute-start.3 = (bf16[3,512,256]{2,1,0:T(8,128)(2,1)S(1)}, bf16[3,512,256]{2,1,0:T(8,128)(2,1)S(1)}, u32[]{:S(2)}, u32[]{:S(2)}) collective-permute-start(bf16[3,512,256]{2,1,0:T(8,128)(2,1)S(1)} %copy-done.31), channel_id=1, source_target_pairs={{0,24},{8,0},{16,8},{24,16},{1,25},{9,1},{17,9},{25,17},{2,26},{10... | collective-permute-start | bytes 2359304 | tf_op jit(solution)/shard_map/ppermute | solution.py:174
  102.4 104.5 %collective-permute-start.24 = (bf16[2,512,704]{1,2,0:T(8,128)(2,1)S(1)}, bf16[2,512,704]{1,2,0:T(8,128)(2,1)S(1)}, u32[]{:S(2)}, u32[]{:S(2)}) collective-permute-start(bf16[2,512,704]{1,2,0:T(8,128)(2,1)S(1)} %copy.102), channel_id=1, source_target_pairs={{0,1},{1,0},{2,3},{3,2},{4,5},{5,4},{6,7},{7,6},{8,9},{9,8},{10,11... | collective-permute-start | bytes 4325384 | tf_op jit(solution)/shard_map/ppermute | solution.py:182
  102.5 35.7 %collective-permute-start.39 = (bf16[704,512]{1,0:T(8,128)(2,1)S(1)}, bf16[704,512]{1,0:T(8,128)(2,1)S(1)}, u32[]{:S(2)}, u32[]{:S(2)}) collective-permute-start(bf16[704,512]{1,0:T(8,128)(2,1)S(1)} %collective-permute-done.38), channel_id=1, source_target_pairs={{0,1},{1,0},{2,3},{3,2},{4,5},{5,4},{6,7},{7,6},{8,9},{9,8},{10,11... | collective-permute-start | bytes 2162696 | tf_op jit(solution)/shard_map/ppermute | solution.py:182
  119.4 96.5 %collective-permute-start.25 = (bf16[2,512,704]{1,2,0:T(8,128)(2,1)S(1)}, bf16[2,512,704]{1,2,0:T(8,128)(2,1)}, u32[]{:S(2)}, u32[]{:S(2)}) collective-permute-start(bf16[2,512,704]{1,2,0:T(8,128)(2,1)S(1)} %copy.102), channel_id=1, source_target_pairs={{0,8},{8,16},{16,24},{24,0},{1,9},{9,17},{17,25},{25,1},{2,10},{10... | collective-permute-start | bytes 4325384 | tf_op jit(solution)/shard_map/ppermute | solution.py:174
  133.6 85.0 %collective-permute-start.27 = (bf16[2,512,704]{1,2,0:T(8,128)(2,1)S(1)}, bf16[2,512,704]{1,2,0:T(8,128)(2,1)S(1)}, u32[]{:S(2)}, u32[]{:S(2)}) collective-permute-start(bf16[2,512,704]{1,2,0:T(8,128)(2,1)S(1)} %copy.102), channel_id=1, source_target_pairs={{0,24},{8,0},{16,8},{24,16},{1,25},{9,1},{17,9},{25,17},{2,26},{10... | collective-permute-start | bytes 4325384 | tf_op jit(solution)/shard_map/ppermute | solution.py:174
  136.2 69.0 %collective-permute-start.41 = (bf16[704,512]{1,0:T(8,128)(2,1)S(1)}, bf16[704,512]{1,0:T(8,128)(2,1)S(1)}, u32[]{:S(2)}, u32[]{:S(2)}) collective-permute-start(bf16[704,512]{1,0:T(8,128)(2,1)S(1)} %collective-permute-done.40), channel_id=1, source_target_pairs={{0,1},{1,0},{2,3},{3,2},{4,5},{5,4},{6,7},{7,6},{8,9},{9,8},{10,11... | collective-permute-start | bytes 2162696 | tf_op jit(solution)/shard_map/ppermute | solution.py:182
  138.2 66.8 %collective-permute-start.42 = (bf16[704,256]{1,0:T(8,128)(2,1)S(1)}, bf16[704,256]{1,0:T(8,128)(2,1)S(1)}, u32[]{:S(2)}, u32[]{:S(2)}) collective-permute-start(bf16[704,256]{1,0:T(8,128)(2,1)S(1)} %slice.216), channel_id=1, source_target_pairs={{0,8},{8,16},{16,24},{24,0},{1,9},{9,17},{17,25},{25,1},{2,10},{10... | collective-permute-start | bytes 1081352 | tf_op jit(solution)/shard_map/ppermute | solution.py:174
  206.9 48.4 %collective-permute-start.9 = (bf16[1,512,2048]{2,1,0:T(8,128)(2,1)S(1)}, bf16[1,512,2048]{2,1,0:T(8,128)(2,1)S(1)}, u32[]{:S(2)}, u32[]{:S(2)}) collective-permute-start(bf16[1,512,2048]{2,1,0:T(8,128)(2,1)S(1)} %copy-done.27), channel_id=1, source_target_pairs={{0,4},{4,0},{1,5},{5,1},{2,6},{6,2},{3,7},{7,3},{8,12},{12,8},{9,1... | collective-permute-start | bytes 6291464 | tf_op jit(solution)/shard_map/ppermute | solution.py:177
  229.7 77.0 %collective-permute-start.52 = (bf16[1,512,2048]{2,1,0:T(8,128)(2,1)S(1)}, bf16[1,512,2048]{2,1,0:T(8,128)(2,1)}, u32[]{:S(2)}, u32[]{:S(2)}) collective-permute-start(bf16[1,512,2048]{2,1,0:T(8,128)(2,1)S(1)} %copy-done.26), channel_id=1, source_target_pairs={{0,4},{4,0},{1,5},{5,1},{2,6},{6,2},{3,7},{7,3},{8,12},{12,8},{9,1... | collective-permute-start | bytes 6291464 | tf_op jit(solution)/shard_map/ppermute | solution.py:177
  239.5 95.6 %collective-permute-start.29 = (bf16[2,256,704]{1,2,0:T(8,128)(2,1)S(1)}, bf16[2,256,704]{1,2,0:T(8,128)(2,1)}, u32[]{:S(2)}, u32[]{:S(2)}) collective-permute-start(bf16[2,256,704]{1,2,0:T(8,128)(2,1)S(1)} %slice.208), channel_id=1, source_target_pairs={{0,8},{8,16},{16,24},{24,0},{1,9},{9,17},{17,25},{25,1},{2,10},{10... | collective-permute-start | bytes 2162696 | tf_op jit(solution)/shard_map/ppermute | solution.py:174
  241.8 93.3 %collective-permute-start.31 = (bf16[2,256,704]{1,2,0:T(8,128)(2,1)S(1)}, bf16[2,256,704]{1,2,0:T(8,128)(2,1)}, u32[]{:S(2)}, u32[]{:S(2)}) collective-permute-start(bf16[2,256,704]{1,2,0:T(8,128)(2,1)S(1)} %slice.209), channel_id=1, source_target_pairs={{0,24},{8,0},{16,8},{24,16},{1,25},{9,1},{17,9},{25,17},{2,26},{10... | collective-permute-start | bytes 2162696 | tf_op jit(solution)/shard_map/ppermute | solution.py:174
  246.7 64.3 %collective-permute-start.26 = (bf16[2,512,704]{1,2,0:T(8,128)(2,1)}, bf16[2,512,704]{1,2,0:T(8,128)(2,1)}, u32[]{:S(2)}, u32[]{:S(2)}) collective-permute-start(bf16[2,512,704]{1,2,0:T(8,128)(2,1)} %collective-permute-done.25), channel_id=1, source_target_pairs={{0,1},{1,0},{2,3},{3,2},{4,5},{5,4},{6,7},{7,6},{8,9},{9,8},{10,11... | collective-permute-start | bytes 4325384 | tf_op jit(solution)/shard_map/ppermute | solution.py:182
  300.3 24.6 %collective-permute-start.22 = (bf16[1,2,256,1024]{3,2,1,0:T(8,128)(2,1)S(1)}, bf16[1,2,256,1024]{3,2,1,0:T(8,128)(2,1)S(1)}, u32[]{:S(2)}, u32[]{:S(2)}) collective-permute-start(bf16[1,2,256,1024]{3,2,1,0:T(8,128)(2,1)S(1)} %dynamic-slice_bitcast_fusion.6), channel_id=1, source_target_pairs={{0,2},{1,3},{2,0},{3,1},{4,6},{5,7},{6,4},{7,5},{8,10},{9,11},{10,... | collective-permute-start | bytes 3145736 | tf_op jit(solution)/shard_map/ppermute | solution.py:179
  306.7 26.1 %collective-permute-start.20 = (bf16[1,2,256,1024]{3,2,1,0:T(8,128)(2,1)S(1)}, bf16[1,2,256,1024]{3,2,1,0:T(8,128)(2,1)S(1)}, u32[]{:S(2)}, u32[]{:S(2)}) collective-permute-start(bf16[1,2,256,1024]{3,2,1,0:T(8,128)(2,1)S(1)} %dynamic-slice_bitcast_fusion.7), channel_id=1, source_target_pairs={{0,4},{4,0},{1,5},{5,1},{2,6},{6,2},{3,7},{7,3},{8,12},{12,8},{9,1... | collective-permute-start | bytes 3145736 | tf_op jit(solution)/shard_map/ppermute | solution.py:177
  311.1 37.4 %collective-permute-start.28 = (bf16[2,512,704]{1,2,0:T(8,128)(2,1)S(1)}, bf16[2,512,704]{1,2,0:T(8,128)(2,1)S(1)}, u32[]{:S(2)}, u32[]{:S(2)}) collective-permute-start(bf16[2,512,704]{1,2,0:T(8,128)(2,1)S(1)} %collective-permute-done.27), channel_id=1, source_target_pairs={{0,1},{1,0},{2,3},{3,2},{4,5},{5,4},{6,7},{7,6},{8,9},{9,8},{10,11... | collective-permute-start | bytes 4325384 | tf_op jit(solution)/shard_map/ppermute | solution.py:182
  335.1 157.8 %collective-permute-start.96 = (bf16[1024,2048]{1,0:T(8,128)(2,1)S(1)}, bf16[1024,2048]{1,0:T(8,128)(2,1)}, u32[]{:S(2)}, u32[]{:S(2)}) collective-permute-start(bf16[1024,2048]{1,0:T(8,128)(2,1)S(1)} %bitcast.517), channel_id=1, source_target_pairs={{0,1},{1,0},{2,3},{3,2},{4,5},{5,4},{6,7},{7,6},{8,9},{9,8},{10,11... | collective-permute-start | bytes 12582920 | tf_op jit(solution)/shard_map/ppermute | solution.py:182
  342.2 23.9 %collective-permute-start.32 = (bf16[2,256,704]{1,2,0:T(8,128)(2,1)}, bf16[2,256,704]{1,2,0:T(8,128)(2,1)S(1)}, u32[]{:S(2)}, u32[]{:S(2)}) collective-permute-start(bf16[2,256,704]{1,2,0:T(8,128)(2,1)} %collective-permute-done.31), channel_id=1, source_target_pairs={{0,1},{1,0},{2,3},{3,2},{4,5},{5,4},{6,7},{7,6},{8,9},{9,8},{10,11... | collective-permute-start | bytes 2162696 | tf_op jit(solution)/shard_map/ppermute | solution.py:182
  360.3 24.8 %collective-permute-start.36 = (bf16[1,2,256,1024]{3,2,1,0:T(8,128)(2,1)S(1)}, bf16[1,2,256,1024]{3,2,1,0:T(8,128)(2,1)S(1)}, u32[]{:S(2)}, u32[]{:S(2)}) collective-permute-start(bf16[1,2,256,1024]{3,2,1,0:T(8,128)(2,1)S(1)} %maximum_select_fusion.16), channel_id=1, source_target_pairs={{0,2},{1,3},{2,0},{3,1},{4,6},{5,7},{6,4},{7,5},{8,10},{9,11},{10,... | collective-permute-start | bytes 3145736 | tf_op jit(solution)/shard_map/ppermute | solution.py:179
  440.2 28.7 %collective-permute-start.55 = (bf16[1,2,256,1024]{3,2,1,0:T(8,128)(2,1)S(1)}, bf16[1,2,256,1024]{3,2,1,0:T(8,128)(2,1)}, u32[]{:S(2)}, u32[]{:S(2)}) collective-permute-start(bf16[1,2,256,1024]{3,2,1,0:T(8,128)(2,1)S(1)} %dynamic-slice_bitcast_fusion.2), channel_id=1, source_target_pairs={{0,2},{1,3},{2,0},{3,1},{4,6},{5,7},{6,4},{7,5},{8,10},{9,11},{10,... | collective-permute-start | bytes 3145736 | tf_op jit(solution)/shard_map/ppermute | solution.py:179
  440.9 29.8 %collective-permute-start.53 = (bf16[1,2,256,1024]{3,2,1,0:T(8,128)(2,1)S(1)}, bf16[1,2,256,1024]{3,2,1,0:T(8,128)(2,1)}, u32[]{:S(2)}, u32[]{:S(2)}) collective-permute-start(bf16[1,2,256,1024]{3,2,1,0:T(8,128)(2,1)S(1)} %dynamic-slice_bitcast_fusion.3), channel_id=1, source_target_pairs={{0,4},{4,0},{1,5},{5,1},{2,6},{6,2},{3,7},{7,3},{8,12},{12,8},{9,1... | collective-permute-start | bytes 3145736 | tf_op jit(solution)/shard_map/ppermute | solution.py:177
  462.3 24.0 %collective-permute-start.48 = (bf16[1,2,256,1024]{3,2,1,0:T(8,128)(2,1)S(1)}, bf16[1,2,256,1024]{3,2,1,0:T(8,128)(2,1)}, u32[]{:S(2)}, u32[]{:S(2)}) collective-permute-start(bf16[1,2,256,1024]{3,2,1,0:T(8,128)(2,1)S(1)} %dynamic-slice_bitcast_fusion.4), channel_id=1, source_target_pairs={{0,2},{1,3},{2,0},{3,1},{4,6},{5,7},{6,4},{7,5},{8,10},{9,11},{10,... | collective-permute-start | bytes 3145736 | tf_op jit(solution)/shard_map/ppermute | solution.py:179
  463.4 26.3 %collective-permute-start.46 = (bf16[1,2,256,1024]{3,2,1,0:T(8,128)(2,1)S(1)}, bf16[1,2,256,1024]{3,2,1,0:T(8,128)(2,1)}, u32[]{:S(2)}, u32[]{:S(2)}) collective-permute-start(bf16[1,2,256,1024]{3,2,1,0:T(8,128)(2,1)S(1)} %dynamic-slice_bitcast_fusion.5), channel_id=1, source_target_pairs={{0,4},{4,0},{1,5},{5,1},{2,6},{6,2},{3,7},{7,3},{8,12},{12,8},{9,1... | collective-permute-start | bytes 3145736 | tf_op jit(solution)/shard_map/ppermute | solution.py:177
  468.9 24.6 %collective-permute-start.95 = (bf16[1024,704]{0,1:T(8,128)(2,1)S(1)}, bf16[1024,704]{0,1:T(8,128)(2,1)S(1)}, u32[]{:S(2)}, u32[]{:S(2)}) collective-permute-start(bf16[1024,704]{0,1:T(8,128)(2,1)S(1)} %slice_bitcast_fusion.3), channel_id=1, source_target_pairs={{0,1},{1,0},{2,3},{3,2},{4,5},{5,4},{6,7},{7,6},{8,9},{9,8},{10,11... | collective-permute-start | bytes 4325384 | tf_op jit(solution)/shard_map/ppermute | solution.py:182
  470.7 36.2 %collective-permute-start.56 = (bf16[1,256,1024]{2,1,0:T(8,128)(2,1)S(1)}, bf16[1,256,1024]{2,1,0:T(8,128)(2,1)S(1)}, u32[]{:S(2)}, u32[]{:S(2)}) collective-permute-start(bf16[1,256,1024]{2,1,0:T(8,128)(2,1)S(1)} %dynamic-slice_bitcast_fusion.10), channel_id=1, source_target_pairs={{0,4},{4,0},{1,5},{5,1},{2,6},{6,2},{3,7},{7,3},{8,12},{12,8},{9,1... | collective-permute-start | bytes 1572872 | tf_op jit(solution)/shard_map/ppermute | solution.py:177
  519.2 24.0 %collective-permute-start.57 = (bf16[1,256,1024]{2,1,0:T(8,128)(2,1)S(1)}, bf16[1,256,1024]{2,1,0:T(8,128)(2,1)S(1)}, u32[]{:S(2)}, u32[]{:S(2)}) collective-permute-start(bf16[1,256,1024]{2,1,0:T(8,128)(2,1)S(1)} %get-tuple-element.90), channel_id=1, source_target_pairs={{0,2},{1,3},{2,0},{3,1},{4,6},{5,7},{6,4},{7,5},{8,10},{9,11},{10,... | collective-permute-start | bytes 1572872 | tf_op jit(solution)/shard_map/ppermute | solution.py:179
  524.4 27.6 %collective-permute-start.102 = (bf16[704,256]{1,0:T(8,128)(2,1)S(1)}, bf16[704,256]{1,0:T(8,128)(2,1)S(1)}, u32[]{:S(2)}, u32[]{:S(2)}) collective-permute-start(bf16[704,256]{1,0:T(8,128)(2,1)S(1)} %get-tuple-element.75), channel_id=1, source_target_pairs={{0,24},{8,0},{16,8},{24,16},{1,25},{9,1},{17,9},{25,17},{2,26},{10... | collective-permute-start | bytes 1081352 | tf_op jit(solution)/shard_map/ppermute | solution.py:174
  529.9 28.0 %collective-permute-start.50 = (bf16[1,256,2048]{2,1,0:T(8,128)(2,1)S(1)}, bf16[1,256,2048]{2,1,0:T(8,128)(2,1)S(1)}, u32[]{:S(2)}, u32[]{:S(2)}) collective-permute-start(bf16[1,256,2048]{2,1,0:T(8,128)(2,1)S(1)} %get-tuple-element.78), channel_id=1, source_target_pairs={{0,2},{1,3},{2,0},{3,1},{4,6},{5,7},{6,4},{7,5},{8,10},{9,11},{10,... | collective-permute-start | bytes 3145736 | tf_op jit(solution)/shard_map/ppermute | solution.py:179
  537.6 36.7 %collective-permute-start.60 = (bf16[1,2,256,1024]{3,2,1,0:T(8,128)(2,1)S(1)}, bf16[1,2,256,1024]{3,2,1,0:T(8,128)(2,1)S(1)}, u32[]{:S(2)}, u32[]{:S(2)}) collective-permute-start(bf16[1,2,256,1024]{3,2,1,0:T(8,128)(2,1)S(1)} %maximum_select_fusion.19), channel_id=1, source_target_pairs={{0,2},{1,3},{2,0},{3,1},{4,6},{5,7},{6,4},{7,5},{8,10},{9,11},{10,... | collective-permute-start | bytes 3145736 | tf_op jit(solution)/shard_map/ppermute | solution.py:179
  543.4 31.8 %collective-permute-start.58 = (bf16[1,2,256,1024]{3,2,1,0:T(8,128)(2,1)S(1)}, bf16[1,2,256,1024]{3,2,1,0:T(8,128)(2,1)S(1)}, u32[]{:S(2)}, u32[]{:S(2)}) collective-permute-start(bf16[1,2,256,1024]{3,2,1,0:T(8,128)(2,1)S(1)} %maximum_select_fusion.18), channel_id=1, source_target_pairs={{0,4},{4,0},{1,5},{5,1},{2,6},{6,2},{3,7},{7,3},{8,12},{12,8},{9,1... | collective-permute-start | bytes 3145736 | tf_op jit(solution)/shard_map/ppermute | solution.py:177
  552.0 132.5 %collective-permute-start.67 = (bf16[1024,2048]{1,0:T(8,128)(2,1)}, bf16[1024,2048]{1,0:T(8,128)(2,1)}, u32[]{:S(2)}, u32[]{:S(2)}) collective-permute-start(bf16[1024,2048]{1,0:T(8,128)(2,1)} %fusion.5), channel_id=1, source_target_pairs={{0,1},{1,0},{2,3},{3,2},{4,5},{5,4},{6,7},{7,6},{8,9},{9,8},{10,11... | collective-permute-start | bytes 12582920 | tf_op jit(solution)/shard_map/ppermute | solution.py:182
  556.8 96.3 %collective-permute-start.86 = (bf16[1024,2048]{1,0:T(8,128)(2,1)}, bf16[1024,2048]{1,0:T(8,128)(2,1)}, u32[]{:S(2)}, u32[]{:S(2)}) collective-permute-start(bf16[1024,2048]{1,0:T(8,128)(2,1)} %pad_maximum_fusion), channel_id=1, source_target_pairs={{0,1},{1,0},{2,3},{3,2},{4,5},{5,4},{6,7},{7,6},{8,9},{9,8},{10,11... | collective-permute-start | bytes 12582920 | tf_op jit(solution)/shard_map/ppermute | solution.py:182
  557.9 94.6 %collective-permute-start.87 = (bf16[2,1024,704]{1,2,0:T(8,128)(2,1)}, bf16[2,1024,704]{1,2,0:T(8,128)(2,1)}, u32[]{:S(2)}, u32[]{:S(2)}) collective-permute-start(bf16[2,1024,704]{1,2,0:T(8,128)(2,1)} %maximum_bitcast_fusion), channel_id=1, source_target_pairs={{0,1},{1,0},{2,3},{3,2},{4,5},{5,4},{6,7},{7,6},{8,9},{9,8},{10,11... | collective-permute-start | bytes 8650760 | tf_op jit(solution)/shard_map/ppermute | solution.py:182
  574.3 72.1 %collective-permute-start.103 = (bf16[704,512]{1,0:T(8,128)(2,1)}, bf16[704,512]{1,0:T(8,128)(2,1)}, u32[]{:S(2)}, u32[]{:S(2)}) collective-permute-start(bf16[704,512]{1,0:T(8,128)(2,1)} %pad_maximum_fusion.7), channel_id=1, source_target_pairs={{0,4},{4,0},{1,5},{5,1},{2,6},{6,2},{3,7},{7,3},{8,12},{12,8},{9,1... | collective-permute-start | bytes 2162696 | tf_op jit(solution)/shard_map/ppermute | solution.py:177
  621.9 28.3 %collective-permute-start.63 = (bf16[1,2,256,1024]{3,2,1,0:T(8,128)(2,1)}, bf16[1,2,256,1024]{3,2,1,0:T(8,128)(2,1)}, u32[]{:S(2)}, u32[]{:S(2)}) collective-permute-start(bf16[1,2,256,1024]{3,2,1,0:T(8,128)(2,1)} %dynamic-slice_bitcast_fusion), channel_id=1, source_target_pairs={{0,2},{1,3},{2,0},{3,1},{4,6},{5,7},{6,4},{7,5},{8,10},{9,11},{10,... | collective-permute-start | bytes 3145736 | tf_op jit(solution)/shard_map/ppermute | solution.py:179
  646.4 60.4 %collective-permute-start.51 = (bf16[1,512,2048]{2,1,0:T(8,128)(2,1)}, bf16[1,512,2048]{2,1,0:T(8,128)(2,1)S(1)}, u32[]{:S(2)}, u32[]{:S(2)}) collective-permute-start(bf16[1,512,2048]{2,1,0:T(8,128)(2,1)} %bitcast.495), channel_id=1, source_target_pairs={{0,1},{1,0},{2,3},{3,2},{4,5},{5,4},{6,7},{7,6},{8,9},{9,8},{10,11... | collective-permute-start | bytes 6291464 | tf_op jit(solution)/shard_map/ppermute | solution.py:182
  650.2 25.6 %collective-permute-start.61 = (bf16[1,2,256,1024]{3,2,1,0:T(8,128)(2,1)S(1)}, bf16[1,2,256,1024]{3,2,1,0:T(8,128)(2,1)S(1)}, u32[]{:S(2)}, u32[]{:S(2)}) collective-permute-start(bf16[1,2,256,1024]{3,2,1,0:T(8,128)(2,1)S(1)} %copy-done.29), channel_id=1, source_target_pairs={{0,4},{4,0},{1,5},{5,1},{2,6},{6,2},{3,7},{7,3},{8,12},{12,8},{9,1... | collective-permute-start | bytes 3145736 | tf_op jit(solution)/shard_map/ppermute | solution.py:177
  652.5 32.3 %collective-permute-start.68 = (bf16[3,1024,256]{2,1,0:T(8,128)(2,1)S(1)}, bf16[3,1024,256]{2,1,0:T(8,128)(2,1)S(1)}, u32[]{:S(2)}, u32[]{:S(2)}) collective-permute-start(bf16[3,1024,256]{2,1,0:T(8,128)(2,1)S(1)} %copy-done.28), channel_id=1, source_target_pairs={{0,1},{1,0},{2,3},{3,2},{4,5},{5,4},{6,7},{7,6},{8,9},{9,8},{10,11... | collective-permute-start | bytes 4718600 | tf_op jit(solution)/shard_map/ppermute | solution.py:182
  653.1 182.0 %collective-permute-start.78 = (bf16[1024,2048]{1,0:T(8,128)(2,1)S(1)}, bf16[1024,2048]{1,0:T(8,128)(2,1)S(1)}, u32[]{:S(2)}, u32[]{:S(2)}) collective-permute-start(bf16[1024,2048]{1,0:T(8,128)(2,1)S(1)} %copy-done.21), channel_id=1, source_target_pairs={{0,1},{1,0},{2,3},{3,2},{4,5},{5,4},{6,7},{7,6},{8,9},{9,8},{10,11... | collective-permute-start | bytes 12582920 | tf_op jit(solution)/shard_map/ppermute | solution.py:182
  675.8 26.9 %collective-permute-start.64 = (bf16[1,256,1024]{2,1,0:T(8,128)(2,1)S(1)}, bf16[1,256,1024]{2,1,0:T(8,128)(2,1)S(1)}, u32[]{:S(2)}, u32[]{:S(2)}) collective-permute-start(bf16[1,256,1024]{2,1,0:T(8,128)(2,1)S(1)} %dynamic-slice_bitcast_fusion.8), channel_id=1, source_target_pairs={{0,4},{4,0},{1,5},{5,1},{2,6},{6,2},{3,7},{7,3},{8,12},{12,8},{9,1... | collective-permute-start | bytes 1572872 | tf_op jit(solution)/shard_map/ppermute | solution.py:177
  684.8 26.9 %collective-permute-start.89 = (bf16[2,256,704]{1,2,0:T(8,128)(2,1)S(1)}, bf16[2,256,704]{1,2,0:T(8,128)(2,1)S(1)}, u32[]{:S(2)}, u32[]{:S(2)}) collective-permute-start(bf16[2,256,704]{1,2,0:T(8,128)(2,1)S(1)} %get-tuple-element.52), channel_id=1, source_target_pairs={{0,24},{8,0},{16,8},{24,16},{1,25},{9,1},{17,9},{25,17},{2,26},{10... | collective-permute-start | bytes 2162696 | tf_op jit(solution)/shard_map/ppermute | solution.py:174
  702.7 45.4 %collective-permute-start.91 = (bf16[2,256,704]{1,2,0:T(8,128)(2,1)S(1)}, bf16[2,256,704]{1,2,0:T(8,128)(2,1)S(1)}, u32[]{:S(2)}, u32[]{:S(2)}) collective-permute-start(bf16[2,256,704]{1,2,0:T(8,128)(2,1)S(1)} %get-tuple-element.53), channel_id=1, source_target_pairs={{0,8},{8,16},{16,24},{24,0},{1,9},{9,17},{17,25},{25,1},{2,10},{10... | collective-permute-start | bytes 2162696 | tf_op jit(solution)/shard_map/ppermute | solution.py:174
  703.5 48.7 %collective-permute-start.88 = (bf16[2,256,704]{1,2,0:T(8,128)(2,1)S(1)}, bf16[2,256,704]{1,2,0:T(8,128)(2,1)S(1)}, u32[]{:S(2)}, u32[]{:S(2)}) collective-permute-start(bf16[2,256,704]{1,2,0:T(8,128)(2,1)S(1)} %get-tuple-element.51), channel_id=1, source_target_pairs={{0,8},{8,16},{16,24},{24,0},{1,9},{9,17},{17,25},{25,1},{2,10},{10... | collective-permute-start | bytes 2162696 | tf_op jit(solution)/shard_map/ppermute | solution.py:174
  706.8 40.7 %collective-permute-start.70 = (bf16[3,256,256]{2,1,0:T(8,128)(2,1)S(1)}, bf16[3,256,256]{2,1,0:T(8,128)(2,1)S(1)}, u32[]{:S(2)}, u32[]{:S(2)}) collective-permute-start(bf16[3,256,256]{2,1,0:T(8,128)(2,1)S(1)} %get-tuple-element.71), channel_id=1, source_target_pairs={{0,24},{8,0},{16,8},{24,16},{1,25},{9,1},{17,9},{25,17},{2,26},{10... | collective-permute-start | bytes 1179656 | tf_op jit(solution)/shard_map/ppermute | solution.py:174
  711.8 42.9 %collective-permute-start.69 = (bf16[3,256,256]{2,1,0:T(8,128)(2,1)S(1)}, bf16[3,256,256]{2,1,0:T(8,128)(2,1)S(1)}, u32[]{:S(2)}, u32[]{:S(2)}) collective-permute-start(bf16[3,256,256]{2,1,0:T(8,128)(2,1)S(1)} %get-tuple-element.68), channel_id=1, source_target_pairs={{0,8},{8,16},{16,24},{24,0},{1,9},{9,17},{17,25},{25,1},{2,10},{10... | collective-permute-start | bytes 1179656 | tf_op jit(solution)/shard_map/ppermute | solution.py:174
  752.2 33.3 %collective-permute-start.93 = (bf16[2,256,704]{1,2,0:T(8,128)(2,1)S(1)}, bf16[2,256,704]{1,2,0:T(8,128)(2,1)S(1)}, u32[]{:S(2)}, u32[]{:S(2)}) collective-permute-start(bf16[2,256,704]{1,2,0:T(8,128)(2,1)S(1)} %get-tuple-element.54), channel_id=1, source_target_pairs={{0,24},{8,0},{16,8},{24,16},{1,25},{9,1},{17,9},{25,17},{2,26},{10... | collective-permute-start | bytes 2162696 | tf_op jit(solution)/shard_map/ppermute | solution.py:174
  754.6 47.6 %collective-permute-start.90 = (bf16[2,256,704]{1,2,0:T(8,128)(2,1)S(1)}, bf16[2,256,704]{1,2,0:T(8,128)(2,1)S(1)}, u32[]{:S(2)}, u32[]{:S(2)}) collective-permute-start(bf16[2,256,704]{1,2,0:T(8,128)(2,1)S(1)} %get-tuple-element.55), channel_id=1, source_target_pairs={{0,24},{8,0},{16,8},{24,16},{1,25},{9,1},{17,9},{25,17},{2,26},{10... | collective-permute-start | bytes 2162696 | tf_op jit(solution)/shard_map/ppermute | solution.py:174
  762.9 54.8 %collective-permute-start.92 = (bf16[2,256,704]{1,2,0:T(8,128)(2,1)S(1)}, bf16[2,256,704]{1,2,0:T(8,128)(2,1)S(1)}, u32[]{:S(2)}, u32[]{:S(2)}) collective-permute-start(bf16[2,256,704]{1,2,0:T(8,128)(2,1)S(1)} %get-tuple-element.56), channel_id=1, source_target_pairs={{0,8},{8,16},{16,24},{24,0},{1,9},{9,17},{17,25},{25,1},{2,10},{10... | collective-permute-start | bytes 2162696 | tf_op jit(solution)/shard_map/ppermute | solution.py:174
  770.1 49.7 %collective-permute-start.65 = (bf16[1,256,2048]{2,1,0:T(8,128)(2,1)S(1)}, bf16[1,256,2048]{2,1,0:T(8,128)(2,1)S(1)}, u32[]{:S(2)}, u32[]{:S(2)}) collective-permute-start(bf16[1,256,2048]{2,1,0:T(8,128)(2,1)S(1)} %fusion.47), channel_id=1, source_target_pairs={{0,2},{1,3},{2,0},{3,1},{4,6},{5,7},{6,4},{7,5},{8,10},{9,11},{10,... | collective-permute-start | bytes 3145736 | tf_op jit(solution)/shard_map/ppermute | solution.py:179
  785.6 49.5 %collective-permute-start.77 = (bf16[1024,256]{1,0:T(8,128)(2,1)S(1)}, bf16[1024,256]{1,0:T(8,128)(2,1)S(1)}, u32[]{:S(2)}, u32[]{:S(2)}) collective-permute-start(bf16[1024,256]{1,0:T(8,128)(2,1)S(1)} %copy-done.34), channel_id=1, source_target_pairs={{0,1},{1,0},{2,3},{3,2},{4,5},{5,4},{6,7},{7,6},{8,9},{9,8},{10,11... | collective-permute-start | bytes 1572872 | tf_op jit(solution)/shard_map/ppermute | solution.py:182
  802.2 23.9 %collective-permute-start.74 = (bf16[3,256,256]{2,1,0:T(8,128)(2,1)S(1)}, bf16[3,256,256]{2,1,0:T(8,128)(2,1)S(1)}, u32[]{:S(2)}, u32[]{:S(2)}) collective-permute-start(bf16[3,256,256]{2,1,0:T(8,128)(2,1)S(1)} %get-tuple-element.69), channel_id=1, source_target_pairs={{0,24},{8,0},{16,8},{24,16},{1,25},{9,1},{17,9},{25,17},{2,26},{10... | collective-permute-start | bytes 1179656 | tf_op jit(solution)/shard_map/ppermute | solution.py:174
  819.8 103.6 %collective-permute-start.94 = (bf16[2,512,704]{1,2,0:T(8,128)(2,1)}, bf16[2,512,704]{1,2,0:T(8,128)(2,1)}, u32[]{:S(2)}, u32[]{:S(2)}) collective-permute-start(bf16[2,512,704]{1,2,0:T(8,128)(2,1)} %pad_maximum_fusion.5), channel_id=1, source_target_pairs={{0,4},{4,0},{1,5},{5,1},{2,6},{6,2},{3,7},{7,3},{8,12},{12,8},{9,1... | collective-permute-start | bytes 4325384 | tf_op jit(solution)/shard_map/ppermute | solution.py:177
  826.1 113.2 %collective-permute-start.66 = (bf16[1,512,2048]{2,1,0:T(8,128)(2,1)S(1)}, bf16[1,512,2048]{2,1,0:T(8,128)(2,1)}, u32[]{:S(2)}, u32[]{:S(2)}) collective-permute-start(bf16[1,512,2048]{2,1,0:T(8,128)(2,1)S(1)} %bitcast.493), channel_id=1, source_target_pairs={{0,1},{1,0},{2,3},{3,2},{4,5},{5,4},{6,7},{7,6},{8,9},{9,8},{10,11... | collective-permute-start | bytes 6291464 | tf_op jit(solution)/shard_map/ppermute | solution.py:182
  834.3 72.0 %collective-permute-start.75 = (bf16[3,512,256]{2,1,0:T(8,128)(2,1)}, bf16[3,512,256]{2,1,0:T(8,128)(2,1)}, u32[]{:S(2)}, u32[]{:S(2)}) collective-permute-start(bf16[3,512,256]{2,1,0:T(8,128)(2,1)} %pad_maximum_fusion.6), channel_id=1, source_target_pairs={{0,4},{4,0},{1,5},{5,1},{2,6},{6,2},{3,7},{7,3},{8,12},{12,8},{9,1... | collective-permute-start | bytes 2359304 | tf_op jit(solution)/shard_map/ppermute | solution.py:177
  837.5 67.3 %collective-permute-start.80 = (bf16[256,256]{1,0:T(8,128)(2,1)S(1)}, bf16[256,256]{1,0:T(8,128)(2,1)S(1)}, u32[]{:S(2)}, u32[]{:S(2)}) collective-permute-start(bf16[256,256]{1,0:T(8,128)(2,1)S(1)} %get-tuple-element.84), channel_id=1, source_target_pairs={{0,24},{8,0},{16,8},{24,16},{1,25},{9,1},{17,9},{25,17},{2,26},{10... | collective-permute-start | bytes 393224 | tf_op jit(solution)/shard_map/ppermute | solution.py:174
  (86 other events, 1573.3 us)

commit v2 on v1

v2 whole, which is shorter than its diff:
```python
import math

import jax
import jax.numpy as jnp
import numpy as np
from jax import lax
from jax.experimental import pallas as pl
from jax.experimental.pallas import tpu as pltpu
from jax.sharding import PartitionSpec as P

HEAD_DIM = 64
ROT = 16
EPSILON = 1e-05
F32 = jnp.float32
LOW = jnp.bfloat16


def rotary_tables(length, width):
    column = np.arange(width) % HEAD_DIM
    half = ROT // 2
    frequency = np.power(10000.0, -2.0 * (column % half) / ROT).astype(np.float32)
    angles = np.arange(length, dtype=np.float32)[:, None] * frequency[None, :]
    inside = column < ROT
    lower = column < half
    sine = np.sin(angles)
    cosine = np.where(inside, np.cos(angles), 1.0)
    minus = np.where(lower, -sine, 0.0)
    plus = np.where(inside & ~lower, sine, 0.0)
    return jnp.asarray(np.stack([cosine, minus, plus]).astype(np.float32))

def light(flops, bytes_accessed, transcendentals):
    return pl.CostEstimate(flops=flops // 100, bytes_accessed=bytes_accessed // 100, transcendentals=0)


def dot_nt(a,b): return lax.dot_general(a,b,(((1,),(1,)),((),())),preferred_element_type=F32)
def dot_nn(a,b): return lax.dot_general(a,b,(((1,),(0,)),((),())),preferred_element_type=F32)
def dot_tn(a,b): return lax.dot_general(a,b,(((0,),(0,)),((),())),preferred_element_type=F32)

def head_masks(width):
    lane=lax.broadcasted_iota(jnp.int32,(1,width),1)
    return [ (lane//HEAD_DIM)==h for h in range(width//HEAD_DIM)]

def fwd_kernel(block, mixed_ref, bias_ref, table_ref, q_ref, k_ref, v_ref, att_ref, lse_ref):
    length, width = q_ref.shape
    half=ROT//2
    def rotated(c):
        v=mixed_ref[c]+bias_ref[c]
        return v*table_ref[0]+pltpu.roll(v,width-half,1)*table_ref[1]+pltpu.roll(v,half,1)*table_ref[2]
    q_ref[...]=(rotated(0)*(1.0/math.sqrt(HEAD_DIM))).astype(LOW)
    k_ref[...]=rotated(1).astype(LOW)
    v_ref[...]=(mixed_ref[2]+bias_ref[2]).astype(LOW)
    masks=head_masks(width)
    row=lax.broadcasted_iota(jnp.int32,(block,block),0)
    col=lax.broadcasted_iota(jnp.int32,(block,block),1)
    for i in range(length//block):
        rows=pl.ds(i*block,block)
        q=q_ref[rows,:]
        out=jnp.zeros((block,width),F32); lse=jnp.zeros((block,width),F32)
        for mask in masks:
            qh=jnp.where(mask,q,jnp.zeros_like(q))
            diag=jnp.where(row>=col,dot_nt(qh,k_ref[rows,:]),-1e30)
            top=jnp.max(diag,axis=1,keepdims=True)
            if i>0:
                rest=dot_nt(qh,k_ref[pl.ds(0,i*block),:])
                top=jnp.maximum(top,jnp.max(rest,axis=1,keepdims=True))
            diag=jnp.exp(diag-top)
            total=jnp.sum(diag,axis=1,keepdims=True)
            acc=dot_nn(diag.astype(LOW),v_ref[rows,:])
            if i>0:
                rest=jnp.exp(rest-top)
                total=total+jnp.sum(rest,axis=1,keepdims=True)
                acc=acc+dot_nn(rest.astype(LOW),v_ref[pl.ds(0,i*block),:])
            out=jnp.where(mask,acc/total,out)
            lse=jnp.where(mask,top+jnp.log(total),lse)
        att_ref[rows,:]=out.astype(LOW)
        lse_ref[rows,:]=lse

def attend_forward(mixed,bias,tables,seqs,length,block=256):
    pair,_,rows,cols=mixed.shape
    width=min(cols,128); groups=cols//width
    tok=lambda o,s,g:(o,s,g)
    spec=pl.BlockSpec((None,length,width),tok)
    shape=lambda d:jax.ShapeDtypeStruct((pair,rows,cols),d)
    return pl.pallas_call(
        lambda *r: fwd_kernel(block,*r),
        grid=(pair,seqs,groups),
        in_specs=[pl.BlockSpec((None,3,length,width),lambda o,s,g:(o,0,s,g)),
                  pl.BlockSpec((None,3,1,width),lambda o,s,g:(o,0,0,g)),
                  pl.BlockSpec((3,length,width),lambda o,s,g:(0,0,0))],
        out_specs=[spec]*5,
        out_shape=[shape(LOW)]*4+[shape(F32)],
        compiler_params=pltpu.CompilerParams(vmem_limit_bytes=48<<20),
        cost_estimate=light(flops=int(4*pair*rows*length*cols*0.6),bytes_accessed=pair*rows*cols*26,transcendentals=pair*rows*length*cols//128),
        name="attend_forward",
    )(mixed,bias,tables)

def bwd_kernel(block,q_ref,k_ref,v_ref,att_ref,lse_ref,do_ref,table_ref,out_ref,dk_acc,dv_acc,dq_acc):
    length,width=q_ref.shape
    half=ROT//2
    masks=head_masks(width)
    row=lax.broadcasted_iota(jnp.int32,(block,block),0)
    col=lax.broadcasted_iota(jnp.int32,(block,block),1)
    count=length//block
    for i in reversed(range(count)):
        rows=pl.ds(i*block,block)
        q=q_ref[rows,:]; do=do_ref[rows,:]; lse=lse_ref[rows,:]
        prod=do.astype(F32)*att_ref[rows,:].astype(F32)
        n=(i+1)*block
        keys=k_ref[pl.ds(0,n),:]; vals=v_ref[pl.ds(0,n),:]
        dq=jnp.zeros((block,width),F32)
        dk=None
        for h,mask in enumerate(masks):
            qh=jnp.where(mask,q,jnp.zeros_like(q)); dh=jnp.where(mask,do,jnp.zeros_like(do))
            delta=jnp.sum(jnp.where(mask,prod,0.0),axis=1,keepdims=True)
            lse_h=lse[:,h*HEAD_DIM:h*HEAD_DIM+1]
            s=dot_nt(qh,keys)
            p=jnp.exp(s-lse_h)
            if i==0:
                p=jnp.where(row>=col,p,0.0)
            else:
                p=jnp.concatenate([p[:,:n-block],jnp.where(row>=col,p[:,n-block:],0.0)],axis=1)
            dp=dot_nt(dh,vals)
            ds=(p*(dp-delta)).astype(LOW)
            pl_low=p.astype(LOW)
            dq=jnp.where(mask,dot_nn(ds,keys),dq)
            tk=dot_tn(ds,qh); tv=dot_tn(pl_low,dh)
            dk=tk if dk is None else dk+tk
            dv=tv if h==0 else dv+tv
        dq_acc[rows,:]=dq*(1.0/math.sqrt(HEAD_DIM))
        if i==count-1:
            dk_acc[...]=dk; dv_acc[...]=dv
        else:
            dk_acc[pl.ds(0,n),:]+=dk; dv_acc[pl.ds(0,n),:]+=dv
    def back(v):
        return v*table_ref[0]+pltpu.roll(v*table_ref[1],half,1)+pltpu.roll(v*table_ref[2],width-half,1)
    out_ref[0]=back(dq_acc[...]).astype(LOW)
    out_ref[1]=back(dk_acc[...]).astype(LOW)
    out_ref[2]=dv_acc[...].astype(LOW)

def attend_back(q,k,v,att,lse,grad,tables,seqs,length,block=256):
    pair,rows,cols=q.shape
    width=min(cols,128); groups=cols//width
    spec=pl.BlockSpec((None,length,width),lambda o,s,g:(o,s,g))
    return pl.pallas_call(
        lambda *r: bwd_kernel(block,*r),
        grid=(pair,seqs,groups),
        in_specs=[spec]*6+[pl.BlockSpec((3,length,width),lambda o,s,g:(0,0,0))],
        out_specs=pl.BlockSpec((None,3,length,width),lambda o,s,g:(o,0,s,g)),
        out_shape=jax.ShapeDtypeStruct((pair,3,rows,cols),LOW),
        scratch_shapes=[pltpu.VMEM((length,width),F32)]*3,
        compiler_params=pltpu.CompilerParams(vmem_limit_bytes=48<<20),
        cost_estimate=light(flops=int(10*pair*rows*length*cols*0.6),bytes_accessed=pair*rows*cols*20,transcendentals=pair*rows*length*cols//128),
        name="attend_back",
    )(q,k,v,att,lse,grad,tables)


VMEM_BYTES = 56 << 20
FORMS = {"nn": dot_nn, "nt": dot_nt, "tn": dot_tn}
ANYWHERE = pl.BlockSpec(memory_space=pl.ANY)


def tiles(size, most):
    while size > most and size % 2 == 0:
        size //= 2
    return size


def lead_spec(lead, block, where):
    return pl.BlockSpec((None,) * len(lead) + block, lambda *at: lead + where(*at))


def products(kind, terms, row_tile, col_tile, name, count=None, dtype=LOW, behind=()):
    one, _, two, _ = terms[0]
    deep = one.shape[-2] if kind == "tn" else one.shape[-1]
    rows = one.shape[-1] if kind == "tn" else one.shape[-2]
    cols = two.shape[-2] if kind == "nt" else two.shape[-1]
    tm, tn = tiles(rows, row_tile), tiles(cols, col_tile)
    one_block = ((deep, tm), lambda c, i, j: (0, i)) if kind == "tn" else ((tm, deep), lambda c, i, j: (i, 0))
    two_block = ((tn, deep), lambda c, i, j: (j, 0)) if kind == "nt" else ((deep, tn), lambda c, i, j: (0, j))
    number = len(terms)

    def kernel(*refs):
        total = sum(FORMS[kind](a[...], b[...]) for a, b in zip(refs[:number], refs[number : 2 * number]))
        refs[-1][...] = total.astype(dtype)

    if count is None:
        ones = [lead_spec(t[1], *one_block) for t in terms]
        out_spec = pl.BlockSpec((tm, tn), lambda c, i, j: (i, j))
        out_shape = (rows, cols)
    else:
        ones = [pl.BlockSpec((None,) + one_block[0], lambda c, i, j: (c,) + one_block[1](c, i, j)) for t in terms]
        out_spec = pl.BlockSpec((None, tm, tn), lambda c, i, j: (c, i, j))
        out_shape = (count, rows, cols)
    many = count or 1
    return pl.pallas_call(
        kernel,
        grid=(many, rows // tm, cols // tn),
        in_specs=ones + [lead_spec(t[3], *two_block) for t in terms] + [ANYWHERE] * len(behind),
        out_specs=out_spec,
        out_shape=jax.ShapeDtypeStruct(out_shape, dtype),
        compiler_params=pltpu.CompilerParams(vmem_limit_bytes=VMEM_BYTES),
        cost_estimate=light(
            flops=2 * rows * deep * cols * number * many,
            bytes_accessed=2 * (many * number * (rows * deep + deep * cols) + many * rows * cols),
            transcendentals=0,
        ),
        name=name,
    )(*[t[0] for t in terms], *[t[2] for t in terms], *behind)


def products_apart(place, kind, terms, col_tile, name, behind=()):
    one, _, two, _ = terms[0]
    deep = one.shape[-2] if kind == "tn" else one.shape[-1]
    rows = one.shape[-1] if kind == "tn" else one.shape[-2]
    cols = two.shape[-2] if kind == "nt" else two.shape[-1]
    tn = tiles(cols // 2, col_tile)
    half = cols // 2 // tn
    piece = rows // 4
    one_block = ((deep, rows), lambda j, at: (0, 0)) if kind == "tn" else ((rows, deep), lambda j, at: (0, 0))
    two_block = ((tn, deep), lambda j, at: (j, 0)) if kind == "nt" else ((deep, tn), lambda j, at: (0, j))
    number = len(terms)

    def kernel(at_ref, *refs):
        total = sum(FORMS[kind](a[...], b[...]) for a, b in zip(refs[:number], refs[number : 2 * number]))
        keep_first, send_first, keep_second, send_second, held = refs[-5:]
        held[...] = total.astype(LOW).reshape(held.shape)
        x, y = at_ref[0], at_ref[1]

        @pl.when(pl.program_id(0) < half)
        def _():
            for other in range(2):
                across = y if other == 0 else 1 - y
                keep_first[other] = held[2 * x + across]
                send_first[other] = held[2 * (1 - x) + across]

        @pl.when(pl.program_id(0) >= half)
        def _():
            for other in range(2):
                along = x if other == 0 else 1 - x
                keep_second[other] = held[2 * along + y]
                send_second[other] = held[2 * along + 1 - y]

    first = pl.BlockSpec((2, piece, tn), lambda j, at: (0, 0, jnp.minimum(j, half - 1)))
    second = pl.BlockSpec((2, piece, tn), lambda j, at: (0, 0, jnp.maximum(j - half, 0)))
    return pl.pallas_call(
        kernel,
        grid_spec=pltpu.PrefetchScalarGridSpec(
            num_scalar_prefetch=1,
            grid=(2 * half,),
            in_specs=[lead_spec(t[1], *one_block) for t in terms]
            + [lead_spec(t[3], *two_block) for t in terms]
            + [ANYWHERE] * len(behind),
            out_specs=[first, first, second, second],
            scratch_shapes=[pltpu.VMEM((4, piece, tn), LOW)],
        ),
        out_shape=[jax.ShapeDtypeStruct((2, piece, cols // 2), LOW)] * 4,
        compiler_params=pltpu.CompilerParams(vmem_limit_bytes=VMEM_BYTES),
        cost_estimate=light(
            flops=2 * rows * deep * cols * number,
            bytes_accessed=2 * (number * (rows * deep + deep * cols) + rows * cols),
            transcendentals=0,
        ),
        name=name,
    )(jnp.stack([place.x, place.y]).astype(jnp.int32), *[t[0] for t in terms], *[t[2] for t in terms], *behind)


def gate_kernel(weight_ref, rows_ref, turned_ref, slope_ref, hidden_ref):
    rows = rows_ref[...]
    gate = dot_nt(weight_ref[0], rows)
    up = dot_nt(weight_ref[1], rows)
    sig = 1.0 / (1.0 + jnp.exp(-gate))
    act = gate * sig
    hidden = (act * up).astype(LOW)
    turned_ref[...] = hidden
    hidden_ref[...] = hidden.T
    slope_ref[0] = (up * sig * (1.0 + gate * (1.0 - sig))).astype(LOW)
    slope_ref[1] = act.astype(LOW)


def gate_up(values, weight):
    rows, feat = values.shape
    units = weight.shape[1]
    tm = tiles(rows, 512)
    return pl.pallas_call(
        gate_kernel,
        grid=(rows // tm,),
        in_specs=[
            pl.BlockSpec((2, units, feat), lambda i: (0, 0, 0)),
            pl.BlockSpec((tm, feat), lambda i: (i, 0)),
        ],
        out_specs=[
            pl.BlockSpec((units, tm), lambda i: (0, i)),
            pl.BlockSpec((2, units, tm), lambda i: (0, 0, i)),
            pl.BlockSpec((tm, units), lambda i: (i, 0)),
        ],
        out_shape=[
            jax.ShapeDtypeStruct((units, rows), LOW),
            jax.ShapeDtypeStruct((2, units, rows), LOW),
            jax.ShapeDtypeStruct((rows, units), LOW),
        ],
        compiler_params=pltpu.CompilerParams(vmem_limit_bytes=VMEM_BYTES),
        cost_estimate=light(
            flops=4 * rows * feat * units,
            bytes_accessed=2 * (rows * feat + 2 * feat * units + 4 * rows * units),
            transcendentals=rows * units,
        ),
        name="gate_up",
    )(weight, values)


def hidden_back_kernel(weight_ref, grad_ref, slope_ref, *refs):
    turned_ref, out_ref = refs[-2:]
    grad = dot_nt(weight_ref[...], grad_ref[...])
    for c in range(2):
        part = (grad * slope_ref[c].astype(F32)).astype(LOW)
        turned_ref[c] = part
        out_ref[c] = part.T


def hidden_back(grad, weight, slope, behind=()):
    rows, feat = grad.shape
    units = weight.shape[0]
    tm = tiles(rows, 512)
    return pl.pallas_call(
        hidden_back_kernel,
        grid=(rows // tm,),
        in_specs=[
            pl.BlockSpec((units, feat), lambda i: (0, 0)),
            pl.BlockSpec((tm, feat), lambda i: (i, 0)),
            pl.BlockSpec((2, units, tm), lambda i: (0, 0, i)),
        ]
        + [ANYWHERE] * len(behind),
        out_specs=[
            pl.BlockSpec((2, units, tm), lambda i: (0, 0, i)),
            pl.BlockSpec((2, tm, units), lambda i: (0, i, 0)),
        ],
        out_shape=[
            jax.ShapeDtypeStruct((2, units, rows), LOW),
            jax.ShapeDtypeStruct((2, rows, units), LOW),
        ],
        compiler_params=pltpu.CompilerParams(vmem_limit_bytes=VMEM_BYTES),
        cost_estimate=light(
            flops=2 * rows * feat * units,
            bytes_accessed=2 * (rows * feat + feat * units + 6 * rows * units),
            transcendentals=0,
        ),
        name="hidden_back",
    )(weight, grad, slope, *behind)


def pieces_of(places, rows, feat, dtype, body, name, operands, behind=()):
    def kernel(at_ref, *refs):
        for step in range(len(places)):
            pl.when(pl.program_id(0) == step)(lambda step=step: body(step, refs, refs[-1]))

    specs = [pl.BlockSpec(v.shape, lambda i, at, n=v.ndim: (0,) * n) for v in operands]
    return pl.pallas_call(
        kernel,
        grid_spec=pltpu.PrefetchScalarGridSpec(
            num_scalar_prefetch=1,
            grid=(len(places),),
            in_specs=specs + [ANYWHERE] * len(behind),
            out_specs=pl.BlockSpec((None, rows, feat), lambda i, at: (at[i], 0, 0)),
        ),
        out_shape=jax.ShapeDtypeStruct((len(places), rows, feat), dtype),
        compiler_params=pltpu.CompilerParams(vmem_limit_bytes=VMEM_BYTES),
        cost_estimate=light(flops=0, bytes_accessed=4 * len(places) * rows * feat, transcendentals=0),
        name=name,
    )(jnp.stack(places).astype(jnp.int32), *operands, *behind)


def lay_rows(one, two, own, over_one, over_two, far, dtype, behind=()):
    rows, feat = own.shape

    def body(step, refs, out_ref):
        start = 0
        for ref in refs[step : step + 1] if step < 3 else refs[3 : 3 + len(far)]:
            out_ref[:, start : start + ref.shape[1]] = ref[...].astype(dtype)
            start += ref.shape[1]

    places = [2 * one + two, 2 * (1 - one) + two, 2 * one + 1 - two, 2 * (1 - one) + 1 - two]
    return pieces_of(places, rows, feat, dtype, body, "lay_rows", [own, over_one, over_two] + list(far), behind)


def norm_first(places, pieces, gain, shift, behind=()):
    rows, feat = pieces[0].shape

    def body(step, refs, out_ref):
        values = refs[step][...].astype(F32)
        out_ref[...] = (centre(values)[0] * refs[4][...] + refs[5][...]).astype(LOW)

    return pieces_of(places, rows, feat, LOW, body, "norm_first", pieces + [gain, shift], behind).reshape(-1, feat)


def lay_pieces(places, pieces, behind=()):
    rows, feat = pieces[0].shape

    def body(step, refs, out_ref):
        out_ref[...] = refs[step][...]

    return pieces_of(places, rows, feat, LOW, body, "lay_pieces", pieces, behind).reshape(-1, feat)


def join(keep_first, came_first, keep_second, came_second, behind=()):
    _, rows, half = keep_first.shape

    def kernel(one, two, three, four, *refs):
        first_stays, first_goes, second_stays, second_goes = refs[-4:]
        first_stays[...] = one[0].astype(F32) + two[0].astype(F32)
        first_goes[...] = (one[1].astype(F32) + two[1].astype(F32)).astype(LOW)
        second_stays[...] = three[0].astype(F32) + four[0].astype(F32)
        second_goes[...] = (three[1].astype(F32) + four[1].astype(F32)).astype(LOW)

    tm = tiles(rows, 128)
    pair = pl.BlockSpec((2, tm, half), lambda i: (0, i, 0))
    flat = pl.BlockSpec((tm, half), lambda i: (i, 0))
    shape = lambda dtype: jax.ShapeDtypeStruct((rows, half), dtype)
    return pl.pallas_call(
        kernel,
        grid=(rows // tm,),
        in_specs=[pair] * 4 + [ANYWHERE] * len(behind),
        out_specs=[flat] * 4,
        out_shape=[shape(F32), shape(LOW)] * 2,
        cost_estimate=light(flops=4 * rows * half, bytes_accessed=28 * rows * half, transcendentals=0),
        compiler_params=pltpu.CompilerParams(vmem_limit_bytes=VMEM_BYTES),
        name="join",
    )(keep_first, came_first, keep_second, came_second, *behind)


def on_rows(kernel, shares, values, tables, outs, sums, name, behind=()):
    rows, half = shares[0].shape
    feat = 2 * half
    tm = tiles(rows, 128)
    count, tabled = len(values), len(tables)

    def body(*refs):
        total = jnp.concatenate(
            [refs[0][...] + refs[1][...].astype(F32), refs[2][...] + refs[3][...].astype(F32)], axis=1
        )
        rest = refs[4 + count + tabled + len(behind) :]
        kernel(total, refs[4 : 4 + count], refs[4 + count : 4 + count + tabled], rest[: len(outs)], rest[len(outs) :])

    block = lambda cols: pl.BlockSpec((tm, cols), lambda i: (i, 0))
    return pl.pallas_call(
        body,
        grid=(rows // tm,),
        in_specs=[block(half)] * 4
        + [block(feat)] * count
        + [pl.BlockSpec((1, feat), lambda i: (0, 0))] * tabled
        + [ANYWHERE] * len(behind),
        out_specs=[block(feat)] * len(outs) + [pl.BlockSpec((2, feat), lambda i: (0, 0))] * sums,
        out_shape=[jax.ShapeDtypeStruct((rows, feat), dtype) for dtype in outs]
        + [jax.ShapeDtypeStruct((2, feat), F32)] * sums,
        cost_estimate=light(flops=20 * rows * feat, bytes_accessed=20 * rows * feat, transcendentals=0),
        compiler_params=pltpu.CompilerParams(vmem_limit_bytes=VMEM_BYTES),
        name=name,
    )(*shares, *values, *tables, *behind)


def centre(values):
    centred = values - jnp.mean(values, axis=1, keepdims=True)
    inv_std = lax.rsqrt(jnp.mean(centred * centred, axis=1, keepdims=True) + EPSILON)
    return centred * inv_std, inv_std


def add_norm(shares, values, gain, shift, behind=()):
    def kernel(total, value_refs, table_refs, out_refs, _):
        middle = value_refs[0][...].astype(F32) + total
        out_refs[0][...] = middle
        out_refs[1][...] = (centre(middle)[0] * table_refs[0][...] + table_refs[1][...]).astype(LOW)

    return on_rows(kernel, shares, [values], [gain, shift], [F32, LOW], 0, "add_norm", behind)


def add_low(shares, values, behind=()):
    def kernel(total, value_refs, _, out_refs, __):
        out_refs[0][...] = (value_refs[0][...].astype(F32) + total).astype(LOW)

    return on_rows(kernel, shares, [values], [], [LOW], 0, "add_low", behind)[0]


def norm_back(shares, values, gain, grad, outs, behind=()):
    def kernel(total, value_refs, table_refs, out_refs, sum_refs):
        scaled, inv_std = centre(value_refs[0][...].astype(F32))
        part = total * table_refs[0][...]
        first = jnp.mean(part, axis=1, keepdims=True)
        second = jnp.mean(part * scaled, axis=1, keepdims=True)
        result = value_refs[1][...].astype(F32) + inv_std * (part - first - scaled * second)
        for ref in out_refs:
            ref[...] = result.astype(ref.dtype)
        sums = sum_refs[0]

        @pl.when(pl.program_id(0) == 0)
        def _():
            sums[...] = jnp.zeros_like(sums)

        sums[0:1, :] += jnp.sum(total * scaled, axis=0, keepdims=True)
        sums[1:2, :] += jnp.sum(total, axis=0, keepdims=True)

    return on_rows(kernel, shares, [values, grad], [gain], outs, 1, "norm_back", behind)


def qkv_back(mine, theirs, my_grad, their_grad, behind=()):
    rows, feat = mine.shape
    count, _, cols = my_grad.shape
    tm = tiles(feat, 512)

    def kernel(mine_ref, theirs_ref, my_ref, their_ref, *refs):
        one, two = mine_ref[...].T, theirs_ref[...].T
        for c in range(count):
            refs[-1][c] = (dot_nn(one, my_ref[c]) + dot_nn(two, their_ref[c])).astype(LOW)

    tall = pl.BlockSpec((rows, tm), lambda i: (0, i))
    whole = pl.BlockSpec((count, rows, cols), lambda i: (0, 0, 0))
    return pl.pallas_call(
        kernel,
        grid=(feat // tm,),
        in_specs=[tall, tall, whole, whole] + [ANYWHERE] * len(behind),
        out_specs=pl.BlockSpec((count, tm, cols), lambda i: (0, i, 0)),
        out_shape=jax.ShapeDtypeStruct((count, feat, cols), LOW),
        cost_estimate=light(
            flops=4 * count * rows * feat * cols,
            bytes_accessed=4 * rows * feat + 4 * count * rows * cols + 2 * count * feat * cols,
            transcendentals=0,
        ),
        compiler_params=pltpu.CompilerParams(vmem_limit_bytes=VMEM_BYTES),
        name="grad_qkv",
    )(mine, theirs, my_grad, their_grad, *behind)


class Place:
    def __init__(self):
        self.fsdp = lax.axis_size("fsdp")
        self.context = lax.axis_size("context")
        self.tensor = lax.axis_size("tensor")
        self.pairs = self.tensor // 2
        self.z = lax.axis_index("fsdp")
        self.x = lax.axis_index("context")
        self.t = lax.axis_index("tensor")
        self.y = self.t // 2
        self.core = self.t % 2

    def square(self, seqs):
        return self.context == 2 and self.pairs == 2 and seqs == 1

    def size(self, which):
        return self.context if which == "x" else self.pairs

    def at(self, which):
        return self.x if which == "x" else self.y

    def shift(self, value, which, step):
        if which == "z":
            n = self.fsdp
            return lax.ppermute(value, "fsdp", [(i, (i + step) % n) for i in range(n)])
        if which == "x":
            n = self.context
            return lax.ppermute(value, "context", [(i, (i + step) % n) for i in range(n)])
        n = self.tensor
        return lax.ppermute(value, "tensor", [(i, (i + 2 * step) % n) for i in range(n)])

    def swap(self, value):
        return lax.ppermute(value, "tensor", [(i, i ^ 1) for i in range(self.tensor)])


def pick(value, index, axis):
    return lax.dynamic_index_in_dim(value, index, axis, keepdims=False)


def scatter_stage(place, value, axis, which):
    n, at = place.size(which), place.at(which)
    total = pick(value, at, axis).astype(F32)
    for step in range(1, n):
        sent = pick(value, (at + step) % n, axis)
        total = total + place.shift(sent, which, step).astype(F32)
    return total


def gather_stage(place, value, axis, which):
    n, at = place.size(which), place.at(which)
    if n == 1:
        return value
    if n == 2:
        return ordered(at, value, place.shift(value, which, 1), axis)
    parts = [value] + [place.shift(value, which, step) for step in range(1, n)]
    order = (at - jnp.arange(n)) % n
    shape = list(value.shape)
    shape[axis] = n * shape[axis]
    return jnp.take(jnp.stack(parts, axis), order, axis=axis).reshape(shape)


def ordered(at, mine, other, axis):
    first = jnp.where(at == 0, mine, other)
    second = jnp.where(at == 0, other, mine)
    return jnp.concatenate([first, second], axis=axis)


def after(value, *others):
    return lax.optimization_barrier((value,) + others)[0]


class RowSum:
    def __init__(self, place, kind, terms, seqs, name, behind=()):
        self.place = place
        self.square = place.square(seqs)
        if self.square:
            self.keep_first, self.sent, self.keep_second, self.second = products_apart(
                place, kind, terms, 512, name, behind
            )
            return
        value = self.sent = products(kind, terms, 1024, 512, name, behind=behind)
        feat = value.shape[1]
        value = value.reshape(seqs, place.context, place.pairs, -1, feat)
        first, second = value[..., : feat // 2], value[..., feat // 2 :]
        first = scatter_stage(place, first, 1, "x").astype(LOW)
        second = scatter_stage(place, second, 2, "y").astype(LOW)
        first = scatter_stage(place, first, 1, "y").reshape(-1, feat // 2)
        second = scatter_stage(place, second, 1, "x").reshape(-1, feat // 2)
        nothing = jnp.zeros(first.shape, LOW)
        self.shares = [first, nothing, second, nothing]

    def start(self, *others):
        if self.square:
            first, second = after((self.sent, self.second), *others) if others else (self.sent, self.second)
            self.came_first = self.place.shift(first, "x", 1)
            self.came_second = self.place.shift(second, "y", 1)
        return self

    def follow(self, behind=()):
        if not self.square:
            return self.shares[0]
        first, first_goes, second, second_goes = join(
            self.keep_first, self.came_first, self.keep_second, self.came_second, behind
        )
        self.shares = [first, self.place.shift(first_goes, "y", 1), second, self.place.shift(second_goes, "x", 1)]
        return first


def spread_rows(place, value, seqs, behind=()):
    feat = value.shape[-1]
    half = feat // 2
    if place.square(seqs):
        over_x = place.shift(value, "x", 1)
        over_y = place.shift(value, "y", 1)
        far_first = place.shift(over_y[:, :half], "x", 1)
        far_second = place.shift(over_x[:, half:], "y", 1)
        whole = lay_rows(place.x, place.y, value, over_x, over_y, [far_first, far_second], LOW, behind)
        return whole.reshape(-1, feat)
    value = value.reshape(seqs, -1, feat)
    rows = value.shape[1]
    first, second = value[..., :half], value[..., half:]
    first = gather_stage(place, first, 1, "y")
    second = gather_stage(place, second, 1, "x")
    first = gather_stage(place, first, 1, "x")
    second = second.reshape(seqs, place.context, rows, half)
    second = gather_stage(place, second, 2, "y").reshape(first.shape)
    return jnp.concatenate([first, second], axis=-1).reshape(-1, feat)


def whole_rows(place, value, seqs, dtype, behind=()):
    feat = value.shape[-1]
    if place.square(seqs):
        over_y, over_core = place.shift(value, "y", 1), place.swap(value)
        whole = lay_rows(place.core, place.y, value, over_core, over_y, [place.swap(over_y)], dtype, behind)
        return whole.reshape(2, -1, feat)
    value = gather_stage(place, value.reshape(seqs, -1, feat), 1, "y")
    return ordered(place.core, value, place.swap(value), 0).astype(dtype)


def other_rows(place, value):
    rows = value.shape[0] // 2
    straight = place.shift(lax.dynamic_slice_in_dim(value, place.y * rows, rows, 0), "x", 1)
    return [value[:rows], value[rows:], straight, place.shift(straight, "y", 1)]


def other_places(place):
    x, y = place.x, place.y
    return [2 * x, 2 * x + 1, 2 * (1 - x) + y, 2 * (1 - x) + 1 - y]


def empty_kernel(out_ref):
    pass


def empty(shape, dtype):
    return pl.pallas_call(
        empty_kernel,
        out_specs=pl.BlockSpec(memory_space=pl.ANY),
        out_shape=jax.ShapeDtypeStruct(shape, dtype),
        name="empty",
    )()


def gather_pack(place, shard, before, behind, ready):
    n, z = place.fsdp, place.z
    blocks, size, cols = shard.shape
    half = blocks // 2
    low = place.shift(before[:half, :size], "z", 1)
    high = place.shift(behind[half:, :size], "z", -1)
    low = after(low, ready)
    whole = empty((blocks, n * size, cols), shard.dtype)
    for part, block, start in (
        (shard, 0, z),
        (before[:, :size], 0, (z + 3) % n),
        (behind[:, :size], 0, (z + 1) % n),
        (low, 0, (z + 2) % n),
        (high, half, (z + 2) % n),
    ):
        whole = lax.dynamic_update_slice(whole, part, (block, start * size, 0))
    return whole, (low, high)


def reduce_shards(place, grad, axis, half_axis, begin, ready):
    n = place.fsdp
    size = grad.shape[axis] // n
    half = (size if axis == half_axis else grad.shape[half_axis]) // 2

    def part(ahead, side):
        shard = lax.dynamic_slice_in_dim(grad, (place.z + ahead) % n * size, size, axis)
        return lax.slice_in_dim(shard, side * half, (side + 1) * half, axis=half_axis).astype(F32)

    def pair(one, two):
        return after(jnp.stack([one, two]).astype(LOW), begin)

    left = place.shift(pair(part(2, 1), part(1, 0)), "z", 1)
    right = place.shift(pair(part(2, 0), part(3, 1)), "z", -1)
    left, right = after((left, right), ready)
    left_high = place.shift((part(1, 1) + left[0].astype(F32)).astype(LOW), "z", 1)
    right_low = place.shift((part(3, 0) + right[0].astype(F32)).astype(LOW), "z", -1)
    low = part(0, 0) + left[1].astype(F32) + right_low.astype(F32)
    high = part(0, 1) + right[1].astype(F32) + left_high.astype(F32)
    return jnp.concatenate([low.astype(LOW), high.astype(LOW)], axis=half_axis)


def total_over(place, value, which):
    n = {"z": place.fsdp, "x": place.context, "y": place.pairs, "core": 2}[which]
    if n == 1:
        return value
    if which == "core":
        return value + place.swap(value)
    if n == 2:
        return value + place.shift(value, which, 1)
    at = {"z": place.z, "x": place.x, "y": place.y}[which]
    parts = jnp.zeros((n,) + value.shape, value.dtype)
    parts = lax.dynamic_update_index_in_dim(parts, value, at, 0)
    for step in range(1, n):
        sent = place.shift(value, which, step)
        parts = lax.dynamic_update_index_in_dim(parts, sent, (at - step) % n, 0)
    return jnp.sum(parts, axis=0)


def small_totals(place, sums, bias, bias_other):
    n, z = place.fsdp, place.z
    feat = sums.shape[1]
    pad = [(0, 1), (0, 0)]
    sent = place.swap(jnp.concatenate([sums, jnp.pad(bias_other, pad)], axis=1))
    sums, bias = sums + sent[:, :feat], jnp.pad(bias, pad) + sent[:, feat:]
    if place.context == 2:
        sent = place.shift(jnp.concatenate([sums, bias], axis=1), "x", 1)
        sums = sums + sent[:, :feat]
        bias = ordered(place.x, bias, sent[:, feat:], 1)
    else:
        sums = total_over(place, sums, "x")
        bias = gather_stage(place, bias, 1, "x")
    size = feat // n
    parts = jnp.zeros((n,) + (4, size + bias.shape[1]), F32)
    for step in range(n):
        part = lax.dynamic_slice_in_dim(sums, (z + step) % n * size, size, 1)
        part = jnp.concatenate([part, bias], axis=1)
        part = place.shift(part, "z", step) if step else part
        parts = lax.dynamic_update_index_in_dim(parts, part, (z - step) % n, 0)
    total = jnp.sum(parts, axis=0)
    return total[:, :size], total[:3, size:]


def local(
    hidden_in,
    norm_gains,
    norm_biases,
    qkv_weight,
    qkv_bias,
    out_weight,
    gate_up_weight,
    down_weight,
    cotangent,
):
    place = Place()
    all_seqs, part_rows, feat = hidden_in.shape
    seqs = all_seqs // 2
    length = part_rows * place.context
    own_rows = part_rows // place.pairs
    head_cols = qkv_bias.shape[1] // place.context
    hidden_cols = down_weight.shape[0] // place.context

    def columns(value, count, axis):
        return lax.dynamic_slice_in_dim(value, place.x * count, count, axis)

    def own_sequences(value):
        return lax.dynamic_slice_in_dim(value, place.core * seqs, seqs, 0)

    def own_piece(value):
        return lax.dynamic_slice_in_dim(value, place.y * own_rows, own_rows, 1)

    pack = jnp.concatenate(
        [columns(qkv_weight, head_cols, 2), columns(out_weight, head_cols, 0).T[None]]
    )
    norm_part = jnp.concatenate([norm_gains, norm_biases]).reshape(-1, head_cols)
    norm_rows = norm_part.shape[0]
    pad = -norm_rows % 16
    part_feat = pack.shape[1]
    norm_block = jnp.pad(norm_part, [(0, pad), (0, 0)])[None]
    extra = jnp.pad(norm_block, [(0, 3), (0, 0), (0, 0)])
    pack = jnp.concatenate([pack, extra], axis=1)
    pack_before, pack_behind = place.shift(pack, "z", 1), place.shift(pack, "z", -1)
    norm_far = place.shift(norm_block, "z", 2)
    hidden_mine = own_sequences(hidden_in)
    hidden_mine = hidden_mine.reshape(-1, feat)
    norms = jnp.zeros((2, 2, feat), F32)
    for step, piece in (
        (0, norm_block),
        (1, pack_before[:1, part_feat:]),
        (2, norm_far),
        (3, pack_behind[:1, part_feat:]),
    ):
        piece = piece[0, :norm_rows].reshape(2, 2, part_feat).astype(F32)
        norms = lax.dynamic_update_slice(norms, piece, (0, 0, (place.z - step) % place.fsdp * part_feat))
    gains, shifts = norms[0][:, None, :], norms[1][:, None, :]
    bias = columns(qkv_bias, head_cols, 1)
    bias_other = place.swap(bias).astype(F32)[None, :, None, :]
    bias = bias.astype(F32)[None, :, None, :]

    gate_up_part = columns(gate_up_weight, hidden_cols, 2).transpose(0, 2, 1)
    down_part = columns(down_weight, hidden_cols, 0)
    top_mine = own_sequences(cotangent)
    if place.square(seqs):
        pieces = other_rows(place, hidden_mine)
        top_pieces = other_rows(place, top_mine.reshape(-1, feat))
        normed = norm_first(other_places(place), pieces, gains[0], shifts[0], behind=[top_pieces[3]])
        grad_top = lay_pieces(other_places(place), top_pieces)
    else:
        whole = gather_stage(place, hidden_mine.reshape(seqs, -1, feat), 1, "x").reshape(-1, feat)
        normed = (centre(whole.astype(F32))[0] * gains[0] + shifts[0]).astype(LOW)
        grad_top = gather_stage(place, top_mine, 1, "x").reshape(seqs * length, feat)
    w_attn, far = gather_pack(place, pack[:, :part_feat], pack_before, pack_behind, normed)
    gate_up_part, down_part = after((gate_up_part, down_part), *far)
    w_gate_up = lax.all_gather(gate_up_part, "fsdp", axis=2, tiled=True)
    w_down = lax.all_gather(down_part, "fsdp", axis=1, tiled=True)
    tables = rotary_tables(length, min(head_cols, 128))
    w_attn_other = place.swap(w_attn)

    def attend(weight, bias):
        mixed = jnp.einsum("rd,cde->cre", normed, weight[:3], preferred_element_type=F32)
        return attend_forward(mixed[None], bias, tables, seqs, length)

    kept = attend(w_attn, bias)
    kept_other = attend(w_attn_other, bias_other)
    attended, attended_other = kept[3][0], kept_other[3][0]
    theirs_top, theirs_one, theirs_attended = place.swap(grad_top), place.swap(normed), place.swap(attended_other)
    attn_sum = RowSum(
        place,
        "nt",
        [(attended, (), w_attn, (3,)), (attended_other, (), w_attn_other, (3,))],
        seqs,
        "out",
        behind=[theirs_top, theirs_one],
    ).start()
    attn_sum.follow()
    inputs = own_piece(hidden_mine.reshape(seqs, -1, feat)).reshape(-1, feat)
    middle, normed_two = add_norm(attn_sum.shares, inputs, gains[1], shifts[1])
    normed_two = spread_rows(place, normed_two, seqs)

    w_gate_up_other = place.swap(after(w_gate_up, middle))
    turned_other, slope_other, hidden_part = gate_up(normed_two, w_gate_up_other)
    theirs_turned, w_down_other = place.swap(turned_other), place.swap(after(w_down, turned_other))
    turned, slope, hidden = gate_up(normed_two, w_gate_up)
    grad_down = products(
        "nn",
        [(turned, (), grad_top, ()), (theirs_turned, (), theirs_top, ())],
        hidden_cols,
        512,
        "grad_down",
    )
    down_sum = lax.psum_scatter(grad_down, "fsdp", scatter_dimension=1, tiled=True)
    grad_gu_turned_other, grad_gu_other = hidden_back(grad_top, w_down_other, slope_other, [grad_down])
    theirs_gu, theirs_two = place.swap(grad_gu_turned_other), place.swap(normed_two)
    grad_gu_turned, grad_gu = hidden_back(grad_top, w_down, slope, [grad_gu_other])
    two_sum = RowSum(
        place,
        "nn",
        [(grad_gu, (c,), w_gate_up, (c,)) for c in range(2)]
        + [(grad_gu_other, (c,), w_gate_up_other, (c,)) for c in range(2)],
        seqs,
        "grad_two",
        behind=[theirs_two, theirs_attended, theirs_gu],
    ).start()
    grad_gate_up = products(
        "nn",
        [(grad_gu_turned, (), normed_two, ()), (theirs_gu, (), theirs_two, ())],
        hidden_cols,
        512,
        "grad_gate_up",
        count=2,
        behind=[two_sum.sent],
    )
    two_next = two_sum.follow([grad_gate_up, down_sum])
    gate_up_sum = lax.psum_scatter(after(grad_gate_up, two_next), "fsdp", scatter_dimension=2, tiled=True)
    down_sums = RowSum(
        place,
        "nn",
        [(hidden, (), w_down, ()), (hidden_part, (), w_down_other, ())],
        seqs,
        "down",
        behind=[two_next],
    )
    top_rows = own_piece(top_mine).reshape(-1, feat)
    grad_middle, mid_low, sums_two = norm_back(
        two_sum.shares, middle, gains[1], top_rows, [F32, LOW], behind=[down_sums.sent]
    )
    grad_mid_low = spread_rows(place, mid_low, seqs)
    down_sum = gather_stage(place, after(down_sum, grad_mid_low), 0, "x")
    down_sums.start(grad_mid_low)

    def attend_grad(kept, weight, behind):
        grad_att = products("nn", [(grad_mid_low, (), weight, (3,))], 1024, head_cols, "grad_att", behind=behind)
        return attend_back(*kept, grad_att[None], tables, seqs, length)[0]

    theirs_mid = place.swap(grad_mid_low)
    grad_mixed_other = attend_grad(kept_other, w_attn_other, [])
    theirs_mixed = place.swap(grad_mixed_other)
    grad_mixed = attend_grad(kept, w_attn, [grad_mixed_other, theirs_mid])
    down_next = down_sums.follow([grad_mixed])
    gate_up_mine = gate_up_sum
    gate_up_sum = gather_stage(place, after(gate_up_sum, grad_mixed), 1, "x")
    final_out = add_low(down_sums.shares, middle, behind=[grad_mixed])
    grad_qkv = qkv_back(normed, theirs_one, grad_mixed, theirs_mixed, behind=[down_next, gate_up_mine])
    one_sum = RowSum(
        place,
        "nt",
        [(grad_mixed, (c,), w_attn, (c,)) for c in range(3)]
        + [(grad_mixed_other, (c,), w_attn_other, (c,)) for c in range(3)],
        seqs,
        "grad_one",
        behind=[grad_qkv],
    ).start()
    grad_out = products(
        "tn",
        [(grad_mid_low, (), attended, ()), (theirs_mid, (), theirs_attended, ())],
        512,
        head_cols,
        "grad_out",
        behind=[one_sum.sent],
    )
    one_next = one_sum.follow([grad_out])
    qkv_sum = reduce_shards(place, grad_qkv, 1, 1, grad_mixed, one_next)
    input_low, sums_one = norm_back(one_sum.shares, inputs, gains[0], grad_middle, [LOW], behind=[one_next])
    out_sum = reduce_shards(place, grad_out, 0, 0, one_next, input_low)
    sums = total_over(place, jnp.concatenate([sums_one, sums_two]), "y")
    input_grad = whole_rows(place, after(input_low, sums), seqs, F32)
    layer_out = whole_rows(place, after(final_out, input_low, sums), seqs, LOW)
    sums, grad_bias = small_totals(
        place,
        sums,
        jnp.sum(grad_mixed.astype(F32), axis=1),
        jnp.sum(grad_mixed_other.astype(F32), axis=1),
    )

    return (
        layer_out,
        input_grad,
        sums[0::2],
        sums[1::2],
        gather_stage(place, qkv_sum, 2, "x").astype(F32),
        grad_bias,
        gather_stage(place, out_sum, 1, "x").T.astype(F32),
        gate_up_sum.transpose(0, 2, 1).astype(F32),
        down_sum.astype(F32),
    )


def solution(mesh):
    placed = (
        P("fsdp", "context", None),
        P(None, "fsdp"),
        P(None, "fsdp"),
        P(None, "fsdp", "tensor"),
        P(None, "tensor"),
        P("tensor", "fsdp"),
        P(None, "fsdp", "tensor"),
        P("tensor", "fsdp"),
        P("fsdp", "context", None),
    )
    return jax.shard_map(
        local,
        mesh=mesh,
        in_specs=placed,
        out_specs=(
            P("fsdp", "context", None),
            P("fsdp", "context", None),
            P(None, "fsdp"),
            P(None, "fsdp"),
            P(None, "fsdp", "tensor"),
            P(None, "tensor"),
            P("tensor", "fsdp"),
            P(None, "fsdp", "tensor"),
            P("tensor", "fsdp"),
        ),
        check_vma=False,
    )
```

time: 956 us -> 726 us (0.76)
  Pallas kernels: 39.4 us -> 257 us
  matrix products: 146 us -> 14.9 us
  waiting for transfers between devices: 383 us -> 258 us
  blocking collectives: 98.5 us -> 0 us
  other arithmetic: 85.2 us -> 30.5 us
  local copies, waits for them, and re-layouts: 106 us -> 67.5 us
  between operations: 2.29 us -> 15.1 us
  starting transfers between devices: 88.1 us -> 76.3 us
    ppermute x40 -> x16, waiting for transfers between devices: 277 us -> 18.7 us  [shift(): return lax.ppermute(value, 'fsdp', [(i, (i + step) % n) for i in range(n)])]
    pallas_call x0 -> x29, Pallas kernels: none -> 215 us  [the longest x4 52.1 us: products_apart(): pl.pallas_call(kernel, grid_spec=pltpu.PrefetchScalarGridSpec(num_scalar_...]
    dot_general x22 -> x2, matrix products: 146 us -> 14.9 us  [attend(): jnp.einsum('rd,cde->cre', normed, weight[:3], preferred_element_type=F32)]
    psum x2 -> x0, blocking collectives: 86.6 us -> none  [the longest x1 63.9 us: local(): lax.psum(jnp.stack([sums_one, sums_two], axis=1), ('fsdp', 'context', 'te...]
    ppermute x18 -> x19, waiting for transfers between devices: 45.1 us -> 124 us  [shift(): lax.ppermute(value, 'context', [(i, (i + step) % n) for i in range(n)])]
    ppermute x14 -> x17, waiting for transfers between devices: 59.7 us -> 102 us  [shift(): lax.ppermute(value, 'tensor', [(i, (i + 2 * step) % n) for i in range(n)])]
    dynamic_update_slice x40 -> x11, local copies, waits for them, and re-layouts: 44.6 us -> 9.13 us  [the longest x4 7.28 us: gather_pack(): whole = lax.dynamic_update_slice(whole, part, (block, start * size, 0))]
    convert_element_type x23 -> x14, other arithmetic: 45.2 us -> 16.4 us  [the longest x4 4.74 us: reduce_shards(): return jnp.concatenate([low.astype(LOW), high.astype(LOW)], axis=half_axis)]
  transfers between devices with their start and end apart: 104 -> 73, of which waited for: 38 -> 29; matrix products, arithmetic and copies ran while one was open for 35% -> 11% of each run, Pallas kernels for 4% -> 31%
where the time goes in v2:
time: 726 us; the launch traced here: 719 us
  waiting for transfers between devices  258 us (36%)
  Pallas kernels  257 us (35%)
  starting transfers between devices  76.3 us (11%)
  local copies, waits for them, and re-layouts  67.5 us (9%)
  other arithmetic  30.5 us (4%)
  between operations  15.1 us (2%)
  matrix products  14.9 us (2%)
    ppermute x19, waiting for transfers between devices, shift(): lax.ppermute(value, 'context', [(i, (i + step) % n) for i in range(n)])  124 us
    ppermute x17, waiting for transfers between devices, shift(): lax.ppermute(value, 'tensor', [(i, (i + 2 * step) % n) for i in range(n)])  102 us
    pallas_call x4, Pallas kernels, products_apart(): pl.pallas_call(kernel, grid_spec=pltpu.PrefetchScalarGridSpec(num_scalar_...  52.1 us
    pallas_call x5, Pallas kernels, products(): pl.pallas_call(kernel, grid=(many, rows // tm, cols // tn), in_specs=ones...  44.5 us
    unnamed x154, local copies, waits for them, and re-layouts  37 us
    pallas_call x6, Pallas kernels, pieces_of(): pl.pallas_call(kernel, grid_spec=pltpu.PrefetchScalarGridSpec(num_scalar_...  35.6 us
    ppermute x16, starting transfers between devices, shift(): return lax.ppermute(value, 'fsdp', [(i, (i + step) % n) for i in range(n)])  33.2 us
    pallas_call x2, Pallas kernels, gate_up(): pl.pallas_call(gate_kernel, grid=(rows // tm,), in_specs=[pl.BlockSpec((2...  24 us
  transfers between devices with their start and end apart: 73, of which 29 were waited for; matrix products, arithmetic and copies ran while one was open for 11% of the time, Pallas kernels for 31%

profile of v2, /device:TPU:0, one launch (start us, length us, event | category | flops | bytes accessed | tf_op | source)
XLA Modules:
  0.0 719.2 jit_solution(4920655626879646384)
XLA Ops:
  12.4 3.0 collective-permute-start
  15.4 3.8 dynamic-slice_bitcast_fusion.5
  23.0 2.6 collective-permute-start.4
  31.6 2.6 copy.32
  34.2 7.2 %collective-permute-done.4 = bf16[1,16,256]{2,1,0:T(8,128)(2,1)S(1)} collective-permute-done((bf16[1,16,256]{2,1,0:T(8,128)(2,1)S(1)}, bf16[1,16,256]{2,1,0:T(8,128)(2,1)S(1)}, u32[]{:S(2)}, u32[]{:S(2)}) %collective-permute-start.4) | collective-permute-done | bytes 8224 | tf_op jit(solution)/shard_map/ppermute | solution.py:555
  41.4 4.2 collective-permute-done.2.refs_2_
  47.1 19.5 %collective-permute-done.6.refs_2_ = bf16[256,2048]{1,0:T(8,128)(2,1)} collective-permute-done((bf16[256,2048]{1,0:T(8,128)(2,1)}, bf16[256,2048]{1,0:T(8,128)(2,1)}, u32[]{:S(2)}, u32[]{:S(2)}) %collective-permute-start.6) | collective-permute-done | bytes 1048608 | tf_op jit(solution)/shard_map/ppermute | solution.py:558
  77.0 13.5 %collective-permute-done.7.refs_6_.refs_3_ = bf16[256,2048]{1,0:T(8,128)(2,1)S(1)} collective-permute-done((bf16[256,2048]{1,0:T(8,128)(2,1)}, bf16[256,2048]{1,0:T(8,128)(2,1)S(1)}, u32[]{:S(2)}, u32[]{:S(2)}) %collective-permute-start.7) | collective-permute-done | bytes 1048608 | tf_op jit(solution)/shard_map/ppermute | solution.py:560
  91.5 7.1 norm_first.1
  108.3 5.8 lay_pieces.1
  115.8 5.7 collective-permute-done.10
  121.5 7.5 %fusion.5.r_0_ = f32[1,3,1024,256]{3,2,1,0:T(8,128)} fusion(bf16[1024,2048,1]{1,0,2:T(8,128)(2,1)} %bitcast.151, bf16[4,2048,256]{2,1,0:T(8,128)(2,1)S(1)} %copy-done.29), kind=kOutput, calls=%fused_computation.9 | convolution fusion | flops 3221225472 | bytes 10485760 | tf_op jit(solution)/shard_map/rd,cde->cre/dot_general | solution.py:852
  129.0 9.3 %attend_forward.2 = (bf16[1,1024,256]{2,1,0:T(8,128)(2,1)S(1)}, bf16[1,1024,256]{2,1,0:T(8,128)(2,1)S(1)}, bf16[1,1024,256]{2,1,0:T(8,128)(2,1)S(1)}, bf16[1,102...) custom-call(f32[1,3,1024,256]{3,2,1,0:T(8,128)} %fusion.5.r_0_, f32[1,3,1,256]{3,2,1,0:T(1,128)S(1)} %copy.23.r_1_, ...), custom_call_target="tpu_custom_call" | custom-call | flops 6442450 | bytes 68157 | tf_op jit(solution)/shard_map/attend_forward/pallas_call | solution.py:84
  141.5 7.4 %fusion.8.r_0_ = f32[1,3,1024,256]{3,2,1,0:T(8,128)} fusion(bf16[1024,2048,1]{1,0,2:T(8,128)(2,1)S(1)} %bitcast.153, bf16[4,2048,256]{2,1,0:T(8,128)(2,1)} %collective-permute-done.9.refs_3_.refs_1_.refs_9_.refs_10_.refs_11_), kind=kOutput, calls=%fused_computation.10 | convolution fusion | flops 3221225472 | bytes 10485760 | tf_op jit(solution)/shard_map/rd,cde->cre/dot_general | solution.py:852
  148.9 9.6 %attend_forward.3 = (bf16[1,1024,256]{2,1,0:T(8,128)(2,1)S(1)}, bf16[1,1024,256]{2,1,0:T(8,128)(2,1)S(1)}, bf16[1,1024,256]{2,1,0:T(8,128)(2,1)S(1)}, bf16[1,102...) custom-call(f32[1,3,1024,256]{3,2,1,0:T(8,128)} %fusion.8.r_0_, f32[1,3,1,256]{3,2,1,0:T(1,128)S(1)} %reshape.93.r_1_, ...), custom_call_target="tpu_custom_call" | custom-call | flops 6442450 | bytes 68157 | tf_op jit(solution)/shard_map/attend_forward/pallas_call | solution.py:84
  162.7 7.4 %out.1 = (bf16[2,256,1024]{2,1,0:T(8,128)(2,1)}, bf16[2,256,1024]{2,1,0:T(8,128)(2,1)}, bf16[2,256,1024]{2,1,0:T(8,128)(2,1)}, bf16[2,256,1024]{2,1,0:T(8,128)(2,1)}) custom-call(s32[2]{0:T(128)} %pad_add_fusion.1.at_ref, bf16[1024,256]{1,0:T(8,128)(2,1)} %bitcast.132, bf16[1024,256]{1,0:T(8,128)(2,1)} %bitcast.134, ...), custom_call_target="tpu_custom_call" | custom-call | flops 21474836 | bytes 73400 | tf_op jit(solution)/shard_map/out/pallas_call | solution.py:245
  173.2 22.4 %collective-permute-done.13.two = bf16[2,256,1024]{2,1,0:T(8,128)(2,1)S(1)} collective-permute-done((bf16[2,256,1024]{2,1,0:T(8,128)(2,1)}, bf16[2,256,1024]{2,1,0:T(8,128)(2,1)S(1)}, u32[]{:S(2)}, u32[]{:S(2)}) %collective-permute-start.13) | collective-permute-done | bytes 1048608 | tf_op jit(solution)/shard_map/ppermute | solution.py:558
  197.9 3.5 join.4
  203.5 11.0 %collective-permute-done.15.refs_1_ = bf16[256,1024]{1,0:T(8,128)(2,1)S(1)} collective-permute-done((bf16[256,1024]{1,0:T(8,128)(2,1)}, bf16[256,1024]{1,0:T(8,128)(2,1)S(1)}, u32[]{:S(2)}, u32[]{:S(2)}) %collective-permute-start.15) | collective-permute-done | bytes 524320 | tf_op jit(solution)/shard_map/ppermute | solution.py:560
  216.6 3.5 add_norm.1
  221.7 24.3 %collective-permute-done.18.refs_2_ = bf16[256,2048]{1,0:T(8,128)(2,1)S(1)} collective-permute-done((bf16[256,2048]{1,0:T(8,128)(2,1)}, bf16[256,2048]{1,0:T(8,128)(2,1)S(1)}, u32[]{:S(2)}, u32[]{:S(2)}) %collective-permute-start.18) | collective-permute-done | bytes 1048608 | tf_op jit(solution)/shard_map/ppermute | solution.py:560
  250.0 10.8 %collective-permute-done.19.refs_3_ = bf16[256,1024]{1,0:T(8,128)(2,1)S(1)} collective-permute-done((bf16[256,1024]{1,0:T(8,128)(2,1)}, bf16[256,1024]{1,0:T(8,128)(2,1)S(1)}, u32[]{:S(2)}, u32[]{:S(2)}) %collective-permute-start.19) | collective-permute-done | bytes 524320 | tf_op jit(solution)/shard_map/ppermute | solution.py:558
  263.3 5.3 lay_rows.4
  268.6 12.1 %gate_up.3 = (bf16[704,1024]{1,0:T(8,128)(2,1)}, bf16[2,704,1024]{2,1,0:T(8,128)(2,1)}, bf16[1024,704]{1,0:T(8,128)(2,1)}) custom-call(bf16[2,704,2048]{2,1,0:T(8,128)(2,1)} %collective-permute-done.21.weight_ref.refs_6_.refs_7_, bf16[1024,2048]{1,0:T(8,128)(2,1)} %bitcast.142), custom_call_target="tpu_custom_call" | custom-call | flops 59055800 | bytes 157286 | tf_op jit(solution)/shard_map/gate_up/pallas_call | solution.py:284
  280.6 8.7 %all-gather.5.cloned.1.call-done.weight_ref.refs_2_ = bf16[704,2048]{1,0:T(8,128)(2,1)} async-done(((bf16[704,512]{1,0:T(8,128)(2,1)}), bf16[704,2048]{1,0:T(8,128)(2,1)}) %all-gather.5.cloned.1.call-update) | async-done | bytes 2883600 | tf_op jit(solution)/shard_map/all_gather | solution.py:847
  289.3 11.9 %gate_up.2 = (bf16[704,1024]{1,0:T(8,128)(2,1)}, bf16[2,704,1024]{2,1,0:T(8,128)(2,1)}, bf16[1024,704]{1,0:T(8,128)(2,1)}) custom-call(bf16[2,704,2048]{2,1,0:T(8,128)(2,1)} %all-gather.3.cloned.1.call-done.weight_ref.refs_4_.refs_5_, bf16[1024,2048]{1,0:T(8,128)(2,1)} %bitcast.143), custom_call_target="tpu_custom_call" | custom-call | flops 59055800 | bytes 157286 | tf_op jit(solution)/shard_map/gate_up/pallas_call | solution.py:284
  301.2 10.3 %grad_down.1.refs_0_ = bf16[704,2048]{1,0:T(8,128)(2,1)} custom-call(bf16[704,1024]{1,0:T(8,128)(2,1)} %get-tuple-element.110.refs_0_, bf16[704,1024]{1,0:T(8,128)(2,1)} %collective-permute-done.23.refs_1_, bf16[1024,2048]{1,0:T(8,128)(2,1)} %bitcast.139, bf16[1024,2048]{1,0:T(8,128)(2,1)} %collective-permute-done.11.refs_4_.refs_3_), custom_call_target="tpu_custom_call" | custom-call | flops 59055800 | bytes 141557 | tf_op jit(solution)/shard_map/grad_down/pallas_call | solution.py:195
  313.7 8.7 %hidden_back.2 = (bf16[2,704,1024]{2,1,0:T(8,128)(2,1)}, bf16[2,1024,704]{2,1,0:T(8,128)(2,1)}) custom-call(bf16[704,2048]{1,0:T(8,128)(2,1)} %copy-done.32, bf16[1024,2048]{1,0:T(8,128)(2,1)} %bitcast.140, bf16[2,704,1024]{2,1,0:T(8,128)(2,1)} %get-tuple-element.109.slope_ref, bf16[704,2048]{1,0:T(8,128)(2,1)} %grad_down.1.refs_0_), custom_call_target="tpu_custom_call" | custom-call | flops 29527900 | bytes 157286 | tf_op jit(solution)/shard_map/hidden_back/pallas_call | solution.py:324
  322.9 8.6 %hidden_back.3 = (bf16[2,704,1024]{2,1,0:T(8,128)(2,1)}, bf16[2,1024,704]{2,1,0:T(8,128)(2,1)}) custom-call(bf16[704,2048]{1,0:T(8,128)(2,1)} %all-gather.5.cloned.1.call-done.weight_ref.refs_2_, bf16[1024,2048]{1,0:T(8,128)(2,1)} %bitcast.141, bf16[2,704,1024]{2,1,0:T(8,128)(2,1)} %get-tuple-element.108.slope_ref, ...), custom_call_target="tpu_custom_call" | custom-call | flops 29527900 | bytes 157286 | tf_op jit(solution)/shard_map/hidden_back/pallas_call | solution.py:324
  333.6 20.1 %grad_two.1 = (bf16[2,256,1024]{2,1,0:T(8,128)(2,1)}, bf16[2,256,1024]{2,1,0:T(8,128)(2,1)}, bf16[2,256,1024]{2,1,0:T(8,128)(2,1)}, bf16[2,256,1024]{2,1,0:T(8,128)(2,1)}) custom-call(s32[2]{0:T(128)} %pad_add_fusion.1.at_ref, bf16[2,1024,704]{2,1,0:T(8,128)(2,1)} %get-tuple-element.112.refs_0_.refs_1_, ...), custom_call_target="tpu_custom_call" | custom-call | flops 118111600 | bytes 214958 | tf_op jit(solution)/shard_map/grad_two/pallas_call | solution.py:245
  356.7 18.4 %grad_gate_up.1.refs_0_ = bf16[2,704,2048]{2,1,0:T(8,128)(2,1)} custom-call(bf16[2,704,1024]{2,1,0:T(8,128)(2,1)} %get-tuple-element.118.refs_0_, bf16[2,704,1024]{2,1,0:T(8,128)(2,1)} %collective-permute-done.26.refs_10_.refs_1_, bf16[1024,2048]{1,0:T(8,128)(2,1)} %bitcast.145, bf16[1024,2048]{1,0:T(8,128)(2,1)} %copy-done.30, ...), custom_call_target="tpu_custom_call" | custom-call | flops 118111600 | bytes 283115 | tf_op jit(solution)/shard_map/grad_gate_up/pallas_call | solution.py:195
  375.1 4.0 collective-permute-done.27.two
  381.3 3.5 join.5
  387.9 12.0 %down.1 = (bf16[2,256,1024]{2,1,0:T(8,128)(2,1)}, bf16[2,256,1024]{2,1,0:T(8,128)(2,1)}, bf16[2,256,1024]{2,1,0:T(8,128)(2,1)}, bf16[2,256,1024]{2,1,0:T(8,128)(2,1)}) custom-call(s32[2]{0:T(128)} %pad_add_fusion.1.at_ref, bf16[1024,704]{1,0:T(8,128)(2,1)} %get-tuple-element.101.refs_0_, bf16[1024,704]{1,0:T(8,128)(2,1)} %get-tuple-element.104.refs_1_, ...), custom_call_target="tpu_custom_call" | custom-call | flops 59055800 | bytes 128450 | tf_op jit(solution)/shard_map/down/pallas_call | solution.py:245
  401.0 4.8 norm_back.2
  407.9 22.0 %collective-permute-done.32.refs_2_ = bf16[256,2048]{1,0:T(8,128)(2,1)S(1)} collective-permute-done((bf16[256,2048]{1,0:T(8,128)(2,1)}, bf16[256,2048]{1,0:T(8,128)(2,1)S(1)}, u32[]{:S(2)}, u32[]{:S(2)}) %collective-permute-start.32) | collective-permute-done | bytes 1048608 | tf_op jit(solution)/shard_map/ppermute | solution.py:560
  432.5 9.2 %collective-permute-done.33.refs_3_ = bf16[256,1024]{1,0:T(8,128)(2,1)S(1)} collective-permute-done((bf16[256,1024]{1,0:T(8,128)(2,1)S(1)}, bf16[256,1024]{1,0:T(8,128)(2,1)S(1)}, u32[]{:S(2)}, u32[]{:S(2)}) %collective-permute-start.33) | collective-permute-done | bytes 524320 | tf_op jit(solution)/shard_map/ppermute | solution.py:558
  443.4 5.3 lay_rows.5
  448.8 4.7 grad_att.2
  454.6 11.4 %attend_back.2 = bf16[1,3,1024,256]{3,2,1,0:T(8,128)(2,1)S(1)} custom-call(bf16[1,1024,256]{2,1,0:T(8,128)(2,1)S(1)} %copy-done.24, bf16[1,1024,256]{2,1,0:T(8,128)(2,1)S(1)} %copy-done.26, bf16[1,1024,256]{2,1,0:T(8,128)(2,1)S(1)} %copy-done.28, bf16[1,1024,256]{2,1,0:T(8,128)(2,1)S(1)} %copy-done.10, f32[1,1024,256]{2,1,0:T(8,128)S(1)} %copy-done.16, ...), custom_call_target="tpu_custom_call" | custom-call | flops 16106127 | bytes 52428 | tf_op jit(solution)/shard_map/attend_back/pallas_call | solution.py:144
  468.7 4.5 grad_att.3
  474.3 11.2 %attend_back.3 = bf16[1,3,1024,256]{3,2,1,0:T(8,128)(2,1)S(1)} custom-call(bf16[1,1024,256]{2,1,0:T(8,128)(2,1)S(1)} %copy-done.18, bf16[1,1024,256]{2,1,0:T(8,128)(2,1)S(1)} %copy-done.20, bf16[1,1024,256]{2,1,0:T(8,128)(2,1)S(1)} %copy-done.22, bf16[1,1024,256]{2,1,0:T(8,128)(2,1)S(1)} %copy-done.8, f32[1,1024,256]{2,1,0:T(8,128)S(1)} %copy-done.14, ...), custom_call_target="tpu_custom_call" | custom-call | flops 16106127 | bytes 52428 | tf_op jit(solution)/shard_map/attend_back/pallas_call | solution.py:144
  486.6 5.1 collective-permute-done.35.two
  493.8 3.4 join.6
  497.2 11.1 %grad_qkv.1.refs_12_ = bf16[3,2048,256]{2,1,0:T(8,128)(2,1)} custom-call(bf16[1024,2048]{1,0:T(8,128)(2,1)} %bitcast.152, bf16[1024,2048]{1,0:T(8,128)(2,1)} %collective-permute-done.12.refs_5_.theirs_ref, bf16[3,1024,256]{2,1,0:T(8,128)(2,1)} %bitcast.122, bf16[3,1024,256]{2,1,0:T(8,128)(2,1)} %collective-permute-done.40.their_ref, ...), custom_call_target="tpu_custom_call" | custom-call | flops 64424508 | bytes 146800 | tf_op jit(solution)/shard_map/grad_qkv/pallas_call | solution.py:515
  508.4 12.5 %grad_one.1 = (bf16[2,256,1024]{2,1,0:T(8,128)(2,1)}, bf16[2,256,1024]{2,1,0:T(8,128)(2,1)}, bf16[2,256,1024]{2,1,0:T(8,128)(2,1)}, bf16[2,256,1024]{2,1,0:T(8,128)(2,1)}) custom-call(s32[2]{0:T(128)} %pad_add_fusion.1.at_ref, bf16[3,1024,256]{2,1,0:T(8,128)(2,1)} %bitcast.123, bf16[3,1024,256]{2,1,0:T(8,128)(2,1)} %bitcast.124, ...), custom_call_target="tpu_custom_call" | custom-call | flops 64424508 | bytes 136314 | tf_op jit(solution)/shard_map/grad_one/pallas_call | solution.py:245
  527.3 2.7 collective-permute-start.57
  532.5 28.3 %collective-permute-done.68 = bf16[704,512]{1,0:T(8,128)(2,1)} collective-permute-done((bf16[704,512]{1,0:T(8,128)(2,1)S(1)}, bf16[704,512]{1,0:T(8,128)(2,1)}, u32[]{:S(2)}, u32[]{:S(2)}) %collective-permute-start.68) | collective-permute-done | bytes 720928 | tf_op jit(solution)/shard_map/ppermute | solution.py:558
  567.1 6.7 grad_out.1.refs_0_
  573.8 3.6 join.7
  581.3 5.1 collective-permute-start.59
  586.6 3.5 add_low.1.refs_0_
  591.1 4.7 collective-permute-done.59
  596.5 4.3 collective-permute-start.63
  602.4 14.7 %collective-permute-done.44.refs_3_ = bf16[256,1024]{1,0:T(8,128)(2,1)S(1)} collective-permute-done((bf16[256,1024]{1,0:T(8,128)(2,1)}, bf16[256,1024]{1,0:T(8,128)(2,1)S(1)}, u32[]{:S(2)}, u32[]{:S(2)}) %collective-permute-start.44) | collective-permute-done | bytes 524320 | tf_op jit(solution)/shard_map/ppermute | solution.py:558
  617.8 4.5 norm_back.3
  627.2 3.4 convert_bitcast_fusion
  630.6 6.3 copy.27
  639.2 5.0 collective-permute-start.64
  654.1 4.6 collective-permute-done.65
  664.9 4.3 collective-permute-done.66
  670.3 21.4 %collective-permute-done.50.refs_2_ = bf16[256,2048]{1,0:T(8,128)(2,1)} collective-permute-done((bf16[256,2048]{1,0:T(8,128)(2,1)}, bf16[256,2048]{1,0:T(8,128)(2,1)}, u32[]{:S(2)}, u32[]{:S(2)}) %collective-permute-start.50) | collective-permute-done | bytes 1048608 | tf_op jit(solution)/shard_map/ppermute | solution.py:560
  700.1 5.3 lay_rows.6
  705.5 6.6 lay_rows.7
  (359 shorter events, 148.5 us)
Async XLA Ops:
  7.2 212.9 %all-gather.3.cloned.1.call-start = ((), (), s32[]{:S(2)}) async-start(), calls=%async_computation.2 | async-start | bytes 7208960 | tf_op jit(solution)/shard_map/all_gather | solution.py:846
  12.4 55.7 %collective-permute-start = (bf16[4,528,256]{2,1,0:T(8,128)(2,1)}, bf16[4,528,256]{2,1,0:T(8,128)(2,1)}, u32[]{:S(2)}, u32[]{:S(2)}) collective-permute-start(bf16[4,528,256]{2,1,0:T(8,128)(2,1)} %fusion.11), channel_id=1, source_target_pairs={{0,8},{8,16},{16,24},{24,0},{1,9},{9,17},{17,25},{25,1},{2,10},{10... | collective-permute-start | bytes 3244040 | tf_op jit(solution)/shard_map/ppermute | solution.py:555
  19.2 26.4 %collective-permute-start.2 = (bf16[256,2048]{1,0:T(8,128)(2,1)}, bf16[256,2048]{1,0:T(8,128)(2,1)}, u32[]{:S(2)}, u32[]{:S(2)}) collective-permute-start(bf16[256,2048]{1,0:T(8,128)(2,1)} %get-tuple-element.181.refs_4_), channel_id=1, source_target_pairs={{0,4},{4,0},{1,5},{5,1},{2,6},{6,2},{3,7},{7,3},{8,12},{12,8},{9,1... | collective-permute-start | bytes 3145736 | tf_op jit(solution)/shard_map/ppermute | solution.py:558
  22.5 44.2 %collective-permute-start.6 = (bf16[256,2048]{1,0:T(8,128)(2,1)}, bf16[256,2048]{1,0:T(8,128)(2,1)}, u32[]{:S(2)}, u32[]{:S(2)}) collective-permute-start(bf16[256,2048]{1,0:T(8,128)(2,1)} %get-tuple-element.180.refs_5_), channel_id=1, source_target_pairs={{0,4},{4,0},{1,5},{5,1},{2,6},{6,2},{3,7},{7,3},{8,12},{12,8},{9,1... | collective-permute-start | bytes 3145736 | tf_op jit(solution)/shard_map/ppermute | solution.py:558
  23.0 18.4 %collective-permute-start.4 = (bf16[1,16,256]{2,1,0:T(8,128)(2,1)S(1)}, bf16[1,16,256]{2,1,0:T(8,128)(2,1)S(1)}, u32[]{:S(2)}, u32[]{:S(2)}) collective-permute-start(bf16[1,16,256]{2,1,0:T(8,128)(2,1)S(1)} %pad_bitcast_fusion), channel_id=1, source_target_pairs={{0,16},{8,24},{16,0},{24,8},{1,17},{9,25},{17,1},{25,9},{2,18},{10... | collective-permute-start | bytes 24584 | tf_op jit(solution)/shard_map/ppermute | solution.py:555
  25.6 46.7 %collective-permute-start.5 = (bf16[4,528,256]{2,1,0:T(8,128)(2,1)}, bf16[4,528,256]{2,1,0:T(8,128)(2,1)}, u32[]{:S(2)}, u32[]{:S(2)}) collective-permute-start(bf16[4,528,256]{2,1,0:T(8,128)(2,1)} %fusion.11), channel_id=1, source_target_pairs={{0,24},{8,0},{16,8},{24,16},{1,25},{9,1},{17,9},{25,17},{2,26},{10... | collective-permute-start | bytes 3244040 | tf_op jit(solution)/shard_map/ppermute | solution.py:555
  45.6 31.4 %collective-permute-start.3 = (bf16[256,2048]{1,0:T(8,128)(2,1)}, bf16[256,2048]{1,0:T(8,128)(2,1)S(1)}, u32[]{:S(2)}, u32[]{:S(2)}) collective-permute-start(bf16[256,2048]{1,0:T(8,128)(2,1)} %collective-permute-done.2.refs_2_), channel_id=1, source_target_pairs={{0,2},{1,3},{2,0},{3,1},{4,6},{5,7},{6,4},{7,5},{8,10},{9,11},{10,... | collective-permute-start | bytes 3145736 | tf_op jit(solution)/shard_map/ppermute | solution.py:560
  66.6 23.9 %collective-permute-start.7 = (bf16[256,2048]{1,0:T(8,128)(2,1)}, bf16[256,2048]{1,0:T(8,128)(2,1)S(1)}, u32[]{:S(2)}, u32[]{:S(2)}) collective-permute-start(bf16[256,2048]{1,0:T(8,128)(2,1)} %collective-permute-done.6.refs_2_), channel_id=1, source_target_pairs={{0,2},{1,3},{2,0},{3,1},{4,6},{5,7},{6,4},{7,5},{8,10},{9,11},{10,... | collective-permute-start | bytes 3145736 | tf_op jit(solution)/shard_map/ppermute | solution.py:560
  70.0 28.6 %collective-permute-start.1 = (bf16[2,512,256]{2,1,0:T(8,128)(2,1)}, bf16[2,512,256]{2,1,0:T(8,128)(2,1)}, u32[]{:S(2)}, u32[]{:S(2)}) collective-permute-start(bf16[2,512,256]{2,1,0:T(8,128)(2,1)} %slice.248), channel_id=1, source_target_pairs={{0,8},{8,16},{16,24},{24,0},{1,9},{9,17},{17,25},{25,1},{2,10},{10... | collective-permute-start | bytes 1572872 | tf_op jit(solution)/shard_map/ppermute | solution.py:555
  74.1 24.6 %collective-permute-start.8 = (bf16[2,512,256]{2,1,0:T(8,128)(2,1)S(1)}, bf16[2,512,256]{2,1,0:T(8,128)(2,1)S(1)}, u32[]{:S(2)}, u32[]{:S(2)}) collective-permute-start(bf16[2,512,256]{2,1,0:T(8,128)(2,1)S(1)} %slice.255), channel_id=1, source_target_pairs={{0,24},{8,0},{16,8},{24,16},{1,25},{9,1},{17,9},{25,17},{2,26},{10... | collective-permute-start | bytes 1572872 | tf_op jit(solution)/shard_map/ppermute | solution.py:555
  99.5 189.8 %all-gather.5.cloned.1.call-start = ((), (), s32[]{:S(2)}) async-start(), calls=%async_computation.3 | async-start | bytes 3604480 | tf_op jit(solution)/shard_map/all_gather | solution.py:847
  108.3 33.2 %collective-permute-start.9 = (bf16[4,2048,256]{2,1,0:T(8,128)(2,1)}, bf16[4,2048,256]{2,1,0:T(8,128)(2,1)}, u32[]{:S(2)}, u32[]{:S(2)}) collective-permute-start(bf16[4,2048,256]{2,1,0:T(8,128)(2,1)} %constant_dynamic-update-slice_fusion.refs_2_.refs_1_.refs_6_.refs_7_.refs_8_), channel_id=1, source_target_pairs={{0,1},{1,0},{2,3},{3,2},{4,5},{5,4},{6,7},{7,6},{8,9},{9,8},{10,11... | collective-permute-start | bytes 12582920 | tf_op jit(solution)/shard_map/ppermute | solution.py:563
  114.2 48.6 %collective-permute-start.11 = (bf16[1024,2048]{1,0:T(8,128)(2,1)}, bf16[1024,2048]{1,0:T(8,128)(2,1)}, u32[]{:S(2)}, u32[]{:S(2)}) collective-permute-start(bf16[1024,2048]{1,0:T(8,128)(2,1)} %bitcast.138), channel_id=1, source_target_pairs={{0,1},{1,0},{2,3},{3,2},{4,5},{5,4},{6,7},{7,6},{8,9},{9,8},{10,11... | collective-permute-start | bytes 12582920 | tf_op jit(solution)/shard_map/ppermute | solution.py:563
  114.7 48.1 %collective-permute-start.12 = (bf16[1024,2048]{1,0:T(8,128)(2,1)}, bf16[1024,2048]{1,0:T(8,128)(2,1)}, u32[]{:S(2)}, u32[]{:S(2)}) collective-permute-start(bf16[1024,2048]{1,0:T(8,128)(2,1)} %bitcast.150), channel_id=1, source_target_pairs={{0,1},{1,0},{2,3},{3,2},{4,5},{5,4},{6,7},{7,6},{8,9},{9,8},{10,11... | collective-permute-start | bytes 12582920 | tf_op jit(solution)/shard_map/ppermute | solution.py:563
  170.1 25.5 %collective-permute-start.13 = (bf16[2,256,1024]{2,1,0:T(8,128)(2,1)}, bf16[2,256,1024]{2,1,0:T(8,128)(2,1)S(1)}, u32[]{:S(2)}, u32[]{:S(2)}) collective-permute-start(bf16[2,256,1024]{2,1,0:T(8,128)(2,1)} %get-tuple-element.93), channel_id=1, source_target_pairs={{0,4},{4,0},{1,5},{5,1},{2,6},{6,2},{3,7},{7,3},{8,12},{12,8},{9,1... | collective-permute-start | bytes 3145736 | tf_op jit(solution)/shard_map/ppermute | solution.py:558
  171.7 25.2 %collective-permute-start.14 = (bf16[2,256,1024]{2,1,0:T(8,128)(2,1)}, bf16[2,256,1024]{2,1,0:T(8,128)(2,1)S(1)}, u32[]{:S(2)}, u32[]{:S(2)}) collective-permute-start(bf16[2,256,1024]{2,1,0:T(8,128)(2,1)} %get-tuple-element.95), channel_id=1, source_target_pairs={{0,2},{1,3},{2,0},{3,1},{4,6},{5,7},{6,4},{7,5},{8,10},{9,11},{10,... | collective-permute-start | bytes 3145736 | tf_op jit(solution)/shard_map/ppermute | solution.py:560
  201.4 13.2 %collective-permute-start.15 = (bf16[256,1024]{1,0:T(8,128)(2,1)}, bf16[256,1024]{1,0:T(8,128)(2,1)S(1)}, u32[]{:S(2)}, u32[]{:S(2)}) collective-permute-start(bf16[256,1024]{1,0:T(8,128)(2,1)} %get-tuple-element.97), channel_id=1, source_target_pairs={{0,2},{1,3},{2,0},{3,1},{4,6},{5,7},{6,4},{7,5},{8,10},{9,11},{10,... | collective-permute-start | bytes 1572872 | tf_op jit(solution)/shard_map/ppermute | solution.py:560
  202.9 12.9 %collective-permute-start.16 = (bf16[256,1024]{1,0:T(8,128)(2,1)}, bf16[256,1024]{1,0:T(8,128)(2,1)S(1)}, u32[]{:S(2)}, u32[]{:S(2)}) collective-permute-start(bf16[256,1024]{1,0:T(8,128)(2,1)} %get-tuple-element.99), channel_id=1, source_target_pairs={{0,4},{4,0},{1,5},{5,1},{2,6},{6,2},{3,7},{7,3},{8,12},{12,8},{9,1... | collective-permute-start | bytes 1572872 | tf_op jit(solution)/shard_map/ppermute | solution.py:558
  220.1 48.5 %collective-permute-start.21 = (bf16[2,704,2048]{2,1,0:T(8,128)(2,1)}, bf16[2,704,2048]{2,1,0:T(8,128)(2,1)}, u32[]{:S(2)}, u32[]{:S(2)}) collective-permute-start(bf16[2,704,2048]{2,1,0:T(8,128)(2,1)} %all-gather.3.cloned.1.call-done.weight_ref.refs_4_.refs_5_), channel_id=1, source_target_pairs={{0,1},{1,0},{2,3},{3,2},{4,5},{5,4},{6,7},{7,6},{8,9},{9,8},{10,11... | collective-permute-start | bytes 17301512 | tf_op jit(solution)/shard_map/ppermute | solution.py:563
  220.2 160.1 %reduce-scatter.3.cloned.1.call-start = ((), (), s32[]{:S(2)}) async-start(), calls=%async_computation.4 | async-start | bytes 3604480 | tf_op jit(solution)/shard_map/reduce_scatter | solution.py:883
  220.2 25.8 %collective-permute-start.18 = (bf16[256,2048]{1,0:T(8,128)(2,1)}, bf16[256,2048]{1,0:T(8,128)(2,1)S(1)}, u32[]{:S(2)}, u32[]{:S(2)}) collective-permute-start(bf16[256,2048]{1,0:T(8,128)(2,1)} %get-tuple-element.100.refs_0_), channel_id=1, source_target_pairs={{0,2},{1,3},{2,0},{3,1},{4,6},{5,7},{6,4},{7,5},{8,10},{9,11},{10,... | collective-permute-start | bytes 3145736 | tf_op jit(solution)/shard_map/ppermute | solution.py:560
  220.8 27.1 %collective-permute-start.17 = (bf16[256,2048]{1,0:T(8,128)(2,1)}, bf16[256,2048]{1,0:T(8,128)(2,1)S(1)}, u32[]{:S(2)}, u32[]{:S(2)}) collective-permute-start(bf16[256,2048]{1,0:T(8,128)(2,1)} %get-tuple-element.100.refs_0_), channel_id=1, source_target_pairs={{0,4},{4,0},{1,5},{5,1},{2,6},{6,2},{3,7},{7,3},{8,12},{12,8},{9,1... | collective-permute-start | bytes 3145736 | tf_op jit(solution)/shard_map/ppermute | solution.py:558
  246.9 13.9 %collective-permute-start.19 = (bf16[256,1024]{1,0:T(8,128)(2,1)}, bf16[256,1024]{1,0:T(8,128)(2,1)S(1)}, u32[]{:S(2)}, u32[]{:S(2)}) collective-permute-start(bf16[256,1024]{1,0:T(8,128)(2,1)} %slice.262), channel_id=1, source_target_pairs={{0,4},{4,0},{1,5},{5,1},{2,6},{6,2},{3,7},{7,3},{8,12},{12,8},{9,1... | collective-permute-start | bytes 1572872 | tf_op jit(solution)/shard_map/ppermute | solution.py:558
  248.8 13.6 %collective-permute-start.20 = (bf16[256,1024]{1,0:T(8,128)(2,1)}, bf16[256,1024]{1,0:T(8,128)(2,1)S(1)}, u32[]{:S(2)}, u32[]{:S(2)}) collective-permute-start(bf16[256,1024]{1,0:T(8,128)(2,1)} %slice.263), channel_id=1, source_target_pairs={{0,2},{1,3},{2,0},{3,1},{4,6},{5,7},{6,4},{7,5},{8,10},{9,11},{10,... | collective-permute-start | bytes 1572872 | tf_op jit(solution)/shard_map/ppermute | solution.py:560
  280.6 20.6 %collective-permute-start.23 = (bf16[704,1024]{1,0:T(8,128)(2,1)}, bf16[704,1024]{1,0:T(8,128)(2,1)}, u32[]{:S(2)}, u32[]{:S(2)}) collective-permute-start(bf16[704,1024]{1,0:T(8,128)(2,1)} %get-tuple-element.106), channel_id=1, source_target_pairs={{0,1},{1,0},{2,3},{3,2},{4,5},{5,4},{6,7},{7,6},{8,9},{9,8},{10,11... | collective-permute-start | bytes 4325384 | tf_op jit(solution)/shard_map/ppermute | solution.py:563
  289.3 22.8 %collective-permute-start.22 = (bf16[704,2048]{1,0:T(8,128)(2,1)}, bf16[704,2048]{1,0:T(8,128)(2,1)S(1)}, u32[]{:S(2)}, u32[]{:S(2)}) collective-permute-start(bf16[704,2048]{1,0:T(8,128)(2,1)} %all-gather.5.cloned.1.call-done.weight_ref.refs_2_), channel_id=1, source_target_pairs={{0,1},{1,0},{2,3},{3,2},{4,5},{5,4},{6,7},{7,6},{8,9},{9,8},{10,11... | collective-permute-start | bytes 8650760 | tf_op jit(solution)/shard_map/ppermute | solution.py:563
  311.5 185.7 %reduce-scatter.5.cloned.1.call-start = ((), (), s32[]{:S(2)}) async-start(), calls=%async_computation.5 | async-start | bytes 7208960 | tf_op jit(solution)/shard_map/reduce_scatter | solution.py:906
  311.6 19.9 %collective-permute-start.24 = (bf16[1024,2048]{1,0:T(8,128)(2,1)}, bf16[1024,2048]{1,0:T(8,128)(2,1)S(1)}, u32[]{:S(2)}, u32[]{:S(2)}) collective-permute-start(bf16[1024,2048]{1,0:T(8,128)(2,1)} %bitcast.144), channel_id=1, source_target_pairs={{0,1},{1,0},{2,3},{3,2},{4,5},{5,4},{6,7},{7,6},{8,9},{9,8},{10,11... | collective-permute-start | bytes 12582920 | tf_op jit(solution)/shard_map/ppermute | solution.py:563
  353.8 25.3 %collective-permute-start.27 = (bf16[2,256,1024]{2,1,0:T(8,128)(2,1)}, bf16[2,256,1024]{2,1,0:T(8,128)(2,1)S(1)}, u32[]{:S(2)}, u32[]{:S(2)}) collective-permute-start(bf16[2,256,1024]{2,1,0:T(8,128)(2,1)} %get-tuple-element.115.refs_4_), channel_id=1, source_target_pairs={{0,4},{4,0},{1,5},{5,1},{2,6},{6,2},{3,7},{7,3},{8,12},{12,8},{9,1... | collective-permute-start | bytes 3145736 | tf_op jit(solution)/shard_map/ppermute | solution.py:558
  355.2 25.1 %collective-permute-start.28 = (bf16[2,256,1024]{2,1,0:T(8,128)(2,1)}, bf16[2,256,1024]{2,1,0:T(8,128)(2,1)S(1)}, u32[]{:S(2)}, u32[]{:S(2)}) collective-permute-start(bf16[2,256,1024]{2,1,0:T(8,128)(2,1)} %get-tuple-element.117), channel_id=1, source_target_pairs={{0,2},{1,3},{2,0},{3,1},{4,6},{5,7},{6,4},{7,5},{8,10},{9,11},{10,... | collective-permute-start | bytes 3145736 | tf_op jit(solution)/shard_map/ppermute | solution.py:560
  385.8 14.1 %collective-permute-start.29 = (bf16[256,1024]{1,0:T(8,128)(2,1)S(1)}, bf16[256,1024]{1,0:T(8,128)(2,1)S(1)}, u32[]{:S(2)}, u32[]{:S(2)}) collective-permute-start(bf16[256,1024]{1,0:T(8,128)(2,1)S(1)} %copy-done.74), channel_id=1, source_target_pairs={{0,2},{1,3},{2,0},{3,1},{4,6},{5,7},{6,4},{7,5},{8,10},{9,11},{10,... | collective-permute-start | bytes 1572872 | tf_op jit(solution)/shard_map/ppermute | solution.py:560
  387.3 12.7 %collective-permute-start.30 = (bf16[256,1024]{1,0:T(8,128)(2,1)S(1)}, bf16[256,1024]{1,0:T(8,128)(2,1)S(1)}, u32[]{:S(2)}, u32[]{:S(2)}) collective-permute-start(bf16[256,1024]{1,0:T(8,128)(2,1)S(1)} %copy-done.73), channel_id=1, source_target_pairs={{0,4},{4,0},{1,5},{5,1},{2,6},{6,2},{3,7},{7,3},{8,12},{12,8},{9,1... | collective-permute-start | bytes 1572872 | tf_op jit(solution)/shard_map/ppermute | solution.py:558
  405.8 24.1 %collective-permute-start.32 = (bf16[256,2048]{1,0:T(8,128)(2,1)}, bf16[256,2048]{1,0:T(8,128)(2,1)S(1)}, u32[]{:S(2)}, u32[]{:S(2)}) collective-permute-start(bf16[256,2048]{1,0:T(8,128)(2,1)} %get-tuple-element.126.refs_0_), channel_id=1, source_target_pairs={{0,2},{1,3},{2,0},{3,1},{4,6},{5,7},{6,4},{7,5},{8,10},{9,11},{10,... | collective-permute-start | bytes 3145736 | tf_op jit(solution)/shard_map/ppermute | solution.py:560
  406.5 24.5 %collective-permute-start.31 = (bf16[256,2048]{1,0:T(8,128)(2,1)}, bf16[256,2048]{1,0:T(8,128)(2,1)S(1)}, u32[]{:S(2)}, u32[]{:S(2)}) collective-permute-start(bf16[256,2048]{1,0:T(8,128)(2,1)} %get-tuple-element.126.refs_0_), channel_id=1, source_target_pairs={{0,4},{4,0},{1,5},{5,1},{2,6},{6,2},{3,7},{7,3},{8,12},{12,8},{9,1... | collective-permute-start | bytes 3145736 | tf_op jit(solution)/shard_map/ppermute | solution.py:558
  429.9 11.8 %collective-permute-start.33 = (bf16[256,1024]{1,0:T(8,128)(2,1)S(1)}, bf16[256,1024]{1,0:T(8,128)(2,1)S(1)}, u32[]{:S(2)}, u32[]{:S(2)}) collective-permute-start(bf16[256,1024]{1,0:T(8,128)(2,1)S(1)} %slice.264), channel_id=1, source_target_pairs={{0,4},{4,0},{1,5},{5,1},{2,6},{6,2},{3,7},{7,3},{8,12},{12,8},{9,1... | collective-permute-start | bytes 1572872 | tf_op jit(solution)/shard_map/ppermute | solution.py:558
  431.0 11.1 %collective-permute-start.34 = (bf16[256,1024]{1,0:T(8,128)(2,1)S(1)}, bf16[256,1024]{1,0:T(8,128)(2,1)S(1)}, u32[]{:S(2)}, u32[]{:S(2)}) collective-permute-start(bf16[256,1024]{1,0:T(8,128)(2,1)S(1)} %slice.265), channel_id=1, source_target_pairs={{0,2},{1,3},{2,0},{3,1},{4,6},{5,7},{6,4},{7,5},{8,10},{9,11},{10,... | collective-permute-start | bytes 1572872 | tf_op jit(solution)/shard_map/ppermute | solution.py:560
  448.7 19.9 %collective-permute-start.37 = (bf16[1024,2048]{1,0:T(8,128)(2,1)}, bf16[1024,2048]{1,0:T(8,128)(2,1)}, u32[]{:S(2)}, u32[]{:S(2)}) collective-permute-start(bf16[1024,2048]{1,0:T(8,128)(2,1)} %bitcast.146), channel_id=1, source_target_pairs={{0,1},{1,0},{2,3},{3,2},{4,5},{5,4},{6,7},{7,6},{8,9},{9,8},{10,11... | collective-permute-start | bytes 12582920 | tf_op jit(solution)/shard_map/ppermute | solution.py:563
  466.0 31.2 %collective-permute-start.40 = (bf16[3,1024,256]{2,1,0:T(8,128)(2,1)S(1)}, bf16[3,1024,256]{2,1,0:T(8,128)(2,1)}, u32[]{:S(2)}, u32[]{:S(2)}) collective-permute-start(bf16[3,1024,256]{2,1,0:T(8,128)(2,1)S(1)} %bitcast.127), channel_id=1, source_target_pairs={{0,1},{1,0},{2,3},{3,2},{4,5},{5,4},{6,7},{7,6},{8,9},{9,8},{10,11... | collective-permute-start | bytes 4718600 | tf_op jit(solution)/shard_map/ppermute | solution.py:563
  466.4 25.3 %collective-permute-start.35 = (bf16[2,256,1024]{2,1,0:T(8,128)(2,1)S(1)}, bf16[2,256,1024]{2,1,0:T(8,128)(2,1)S(1)}, u32[]{:S(2)}, u32[]{:S(2)}) collective-permute-start(bf16[2,256,1024]{2,1,0:T(8,128)(2,1)S(1)} %copy-done.47), channel_id=1, source_target_pairs={{0,4},{4,0},{1,5},{5,1},{2,6},{6,2},{3,7},{7,3},{8,12},{12,8},{9,1... | collective-permute-start | bytes 3145736 | tf_op jit(solution)/shard_map/ppermute | solution.py:558
  467.6 25.2 %collective-permute-start.36 = (bf16[2,256,1024]{2,1,0:T(8,128)(2,1)}, bf16[2,256,1024]{2,1,0:T(8,128)(2,1)S(1)}, u32[]{:S(2)}, u32[]{:S(2)}) collective-permute-start(bf16[2,256,1024]{2,1,0:T(8,128)(2,1)} %get-tuple-element.129), channel_id=1, source_target_pairs={{0,2},{1,3},{2,0},{3,1},{4,6},{5,7},{6,4},{7,5},{8,10},{9,11},{10,... | collective-permute-start | bytes 3145736 | tf_op jit(solution)/shard_map/ppermute | solution.py:560
  520.9 42.2 %collective-permute-start.41 = (bf16[2,256,1024]{2,1,0:T(8,128)(2,1)}, bf16[2,256,1024]{2,1,0:T(8,128)(2,1)}, u32[]{:S(2)}, u32[]{:S(2)}) collective-permute-start(bf16[2,256,1024]{2,1,0:T(8,128)(2,1)} %get-tuple-element.144.refs_4_), channel_id=1, source_target_pairs={{0,4},{4,0},{1,5},{5,1},{2,6},{6,2},{3,7},{7,3},{8,12},{12,8},{9,1... | collective-permute-start | bytes 3145736 | tf_op jit(solution)/shard_map/ppermute | solution.py:558
  521.9 42.4 %collective-permute-start.42 = (bf16[2,256,1024]{2,1,0:T(8,128)(2,1)}, bf16[2,256,1024]{2,1,0:T(8,128)(2,1)}, u32[]{:S(2)}, u32[]{:S(2)}) collective-permute-start(bf16[2,256,1024]{2,1,0:T(8,128)(2,1)} %get-tuple-element.146), channel_id=1, source_target_pairs={{0,2},{1,3},{2,0},{3,1},{4,6},{5,7},{6,4},{7,5},{8,10},{9,11},{10,... | collective-permute-start | bytes 3145736 | tf_op jit(solution)/shard_map/ppermute | solution.py:560
  523.1 37.8 %collective-permute-start.68 = (bf16[704,512]{1,0:T(8,128)(2,1)S(1)}, bf16[704,512]{1,0:T(8,128)(2,1)}, u32[]{:S(2)}, u32[]{:S(2)}) collective-permute-start(bf16[704,512]{1,0:T(8,128)(2,1)S(1)} %copy-done.39), channel_id=1, source_target_pairs={{0,4},{4,0},{1,5},{5,1},{2,6},{6,2},{3,7},{7,3},{8,12},{12,8},{9,1... | collective-permute-start | bytes 2162696 | tf_op jit(solution)/shard_map/ppermute | solution.py:558
  527.3 50.1 %collective-permute-start.57 = (bf16[2,3,256,256]{3,2,1,0:T(8,128)(2,1)}, bf16[2,3,256,256]{3,2,1,0:T(8,128)(2,1)S(1)}, u32[]{:S(2)}, u32[]{:S(2)}) collective-permute-start(bf16[2,3,256,256]{3,2,1,0:T(8,128)(2,1)} %get-tuple-element.157), channel_id=1, source_target_pairs={{0,8},{8,16},{16,24},{24,0},{1,9},{9,17},{17,25},{25,1},{2,10},{10... | collective-permute-start | bytes 2359304 | tf_op jit(solution)/shard_map/ppermute | solution.py:555
  530.1 48.5 %collective-permute-start.58 = (bf16[2,3,256,256]{3,2,1,0:T(8,128)(2,1)S(1)}, bf16[2,3,256,256]{3,2,1,0:T(8,128)(2,1)S(1)}, u32[]{:S(2)}, u32[]{:S(2)}) collective-permute-start(bf16[2,3,256,256]{3,2,1,0:T(8,128)(2,1)S(1)} %get-tuple-element.158), channel_id=1, source_target_pairs={{0,24},{8,0},{16,8},{24,16},{1,25},{9,1},{17,9},{25,17},{2,26},{10... | collective-permute-start | bytes 2359304 | tf_op jit(solution)/shard_map/ppermute | solution.py:555
  562.1 19.2 %collective-permute-start.38 = (bf16[256,1024]{1,0:T(8,128)(2,1)}, bf16[256,1024]{1,0:T(8,128)(2,1)S(1)}, u32[]{:S(2)}, u32[]{:S(2)}) collective-permute-start(bf16[256,1024]{1,0:T(8,128)(2,1)} %get-tuple-element.139), channel_id=1, source_target_pairs={{0,2},{1,3},{2,0},{3,1},{4,6},{5,7},{6,4},{7,5},{8,10},{9,11},{10,... | collective-permute-start | bytes 1572872 | tf_op jit(solution)/shard_map/ppermute | solution.py:560
  563.1 23.5 %collective-permute-start.39 = (bf16[256,1024]{1,0:T(8,128)(2,1)}, bf16[256,1024]{1,0:T(8,128)(2,1)}, u32[]{:S(2)}, u32[]{:S(2)}) collective-permute-start(bf16[256,1024]{1,0:T(8,128)(2,1)} %get-tuple-element.141), channel_id=1, source_target_pairs={{0,4},{4,0},{1,5},{5,1},{2,6},{6,2},{3,7},{7,3},{8,12},{12,8},{9,1... | collective-permute-start | bytes 1572872 | tf_op jit(solution)/shard_map/ppermute | solution.py:558
  564.3 60.1 %collective-permute-start.67 = (bf16[2,704,512]{2,1,0:T(8,128)(2,1)S(1)}, bf16[2,704,512]{2,1,0:T(8,128)(2,1)S(1)}, u32[]{:S(2)}, u32[]{:S(2)}) collective-permute-start(bf16[2,704,512]{2,1,0:T(8,128)(2,1)S(1)} %copy-done.36), channel_id=1, source_target_pairs={{0,4},{4,0},{1,5},{5,1},{2,6},{6,2},{3,7},{7,3},{8,12},{12,8},{9,1... | collective-permute-start | bytes 4325384 | tf_op jit(solution)/shard_map/ppermute | solution.py:558
  577.4 24.9 %collective-permute-start.43 = (bf16[256,1024]{1,0:T(8,128)(2,1)}, bf16[256,1024]{1,0:T(8,128)(2,1)S(1)}, u32[]{:S(2)}, u32[]{:S(2)}) collective-permute-start(bf16[256,1024]{1,0:T(8,128)(2,1)} %get-tuple-element.148), channel_id=1, source_target_pairs={{0,2},{1,3},{2,0},{3,1},{4,6},{5,7},{6,4},{7,5},{8,10},{9,11},{10,... | collective-permute-start | bytes 1572872 | tf_op jit(solution)/shard_map/ppermute | solution.py:560
  578.5 38.5 %collective-permute-start.44 = (bf16[256,1024]{1,0:T(8,128)(2,1)}, bf16[256,1024]{1,0:T(8,128)(2,1)S(1)}, u32[]{:S(2)}, u32[]{:S(2)}) collective-permute-start(bf16[256,1024]{1,0:T(8,128)(2,1)} %get-tuple-element.150), channel_id=1, source_target_pairs={{0,4},{4,0},{1,5},{5,1},{2,6},{6,2},{3,7},{7,3},{8,12},{12,8},{9,1... | collective-permute-start | bytes 1572872 | tf_op jit(solution)/shard_map/ppermute | solution.py:558
  581.3 14.5 %collective-permute-start.59 = (bf16[3,256,256]{2,1,0:T(8,128)(2,1)}, bf16[3,256,256]{2,1,0:T(8,128)(2,1)S(1)}, u32[]{:S(2)}, u32[]{:S(2)}) collective-permute-start(bf16[3,256,256]{2,1,0:T(8,128)(2,1)} %fusion.15), channel_id=1, source_target_pairs={{0,24},{8,0},{16,8},{24,16},{1,25},{9,1},{17,9},{25,17},{2,26},{10... | collective-permute-start | bytes 1179656 | tf_op jit(solution)/shard_map/ppermute | solution.py:555
  591.1 45.8 %collective-permute-start.62 = (bf16[2,256,256]{2,1,0:T(8,128)(2,1)}, bf16[2,256,256]{2,1,0:T(8,128)(2,1)}, u32[]{:S(2)}, u32[]{:S(2)}) collective-permute-start(bf16[2,256,256]{2,1,0:T(8,128)(2,1)} %get-tuple-element.161), channel_id=1, source_target_pairs={{0,8},{8,16},{16,24},{24,0},{1,9},{9,17},{17,25},{25,1},{2,10},{10... | collective-permute-start | bytes 786440 | tf_op jit(solution)/shard_map/ppermute | solution.py:555
  596.5 40.4 %collective-permute-start.63 = (bf16[2,256,256]{2,1,0:T(8,128)(2,1)}, bf16[2,256,256]{2,1,0:T(8,128)(2,1)}, u32[]{:S(2)}, u32[]{:S(2)}) collective-permute-start(bf16[2,256,256]{2,1,0:T(8,128)(2,1)} %get-tuple-element.162), channel_id=1, source_target_pairs={{0,24},{8,0},{16,8},{24,16},{1,25},{9,1},{17,9},{25,17},{2,26},{10... | collective-permute-start | bytes 786440 | tf_op jit(solution)/shard_map/ppermute | solution.py:555
  602.3 57.7 %collective-permute-start.60 = (bf16[3,256,256]{2,1,0:T(8,128)(2,1)S(1)}, bf16[3,256,256]{2,1,0:T(8,128)(2,1)}, u32[]{:S(2)}, u32[]{:S(2)}) collective-permute-start(bf16[3,256,256]{2,1,0:T(8,128)(2,1)S(1)} %get-tuple-element.185), channel_id=1, source_target_pairs={{0,8},{8,16},{16,24},{24,0},{1,9},{9,17},{17,25},{25,1},{2,10},{10... | collective-permute-start | bytes 1179656 | tf_op jit(solution)/shard_map/ppermute | solution.py:555
  627.1 9.8 %collective-permute-start.52 = (f32[4,2304]{1,0:T(4,128)S(1)}, f32[4,2304]{1,0:T(4,128)S(1)}, u32[]{:S(2)}, u32[]{:S(2)}) collective-permute-start(f32[4,2304]{1,0:T(4,128)S(1)} %select_maximum_fusion), channel_id=1, source_target_pairs={{0,1},{1,0},{2,3},{3,2},{4,5},{5,4},{6,7},{7,6},{8,9},{9,8},{10,11... | collective-permute-start | bytes 110600 | tf_op jit(solution)/shard_map/ppermute | solution.py:563
  637.0 9.3 %collective-permute-start.53 = (f32[4,2304]{1,0:T(4,128)S(1)}, f32[4,2304]{1,0:T(4,128)S(1)}, u32[]{:S(2)}, u32[]{:S(2)}) collective-permute-start(f32[4,2304]{1,0:T(4,128)S(1)} %pad_maximum_fusion.6), channel_id=1, source_target_pairs={{0,4},{4,0},{1,5},{5,1},{2,6},{6,2},{3,7},{7,3},{8,12},{12,8},{9,1... | collective-permute-start | bytes 110600 | tf_op jit(solution)/shard_map/ppermute | solution.py:558
  644.2 26.1 %collective-permute-start.47 = (bf16[256,2048]{1,0:T(8,128)(2,1)S(1)}, bf16[256,2048]{1,0:T(8,128)(2,1)}, u32[]{:S(2)}, u32[]{:S(2)}) collective-permute-start(bf16[256,2048]{1,0:T(8,128)(2,1)S(1)} %copy-done.37), channel_id=1, source_target_pairs={{0,2},{1,3},{2,0},{3,1},{4,6},{5,7},{6,4},{7,5},{8,10},{9,11},{10,... | collective-permute-start | bytes 3145736 | tf_op jit(solution)/shard_map/ppermute | solution.py:560
  645.2 46.6 %collective-permute-start.50 = (bf16[256,2048]{1,0:T(8,128)(2,1)}, bf16[256,2048]{1,0:T(8,128)(2,1)}, u32[]{:S(2)}, u32[]{:S(2)}) collective-permute-start(bf16[256,2048]{1,0:T(8,128)(2,1)} %get-tuple-element.156.refs_0_), channel_id=1, source_target_pairs={{0,2},{1,3},{2,0},{3,1},{4,6},{5,7},{6,4},{7,5},{8,10},{9,11},{10,... | collective-permute-start | bytes 3145736 | tf_op jit(solution)/shard_map/ppermute | solution.py:560
  647.6 15.6 %collective-permute-start.55 = (f32[4,1024]{1,0:T(4,128)S(1)}, f32[4,1024]{1,0:T(4,128)S(1)}, u32[]{:S(2)}, u32[]{:S(2)}) collective-permute-start(f32[4,1024]{1,0:T(4,128)S(1)} %get-tuple-element.216), channel_id=1, source_target_pairs={{0,16},{8,24},{16,0},{24,8},{1,17},{9,25},{17,1},{25,9},{2,18},{10... | collective-permute-start | bytes 49160 | tf_op jit(solution)/shard_map/ppermute | solution.py:555
  663.2 33.4 %collective-permute-start.61 = (bf16[3,512,256]{2,1,0:T(8,128)(2,1)}, bf16[3,512,256]{2,1,0:T(8,128)(2,1)}, u32[]{:S(2)}, u32[]{:S(2)}) collective-permute-start(bf16[3,512,256]{2,1,0:T(8,128)(2,1)} %pad_maximum_fusion.2), channel_id=1, source_target_pairs={{0,4},{4,0},{1,5},{5,1},{2,6},{6,2},{3,7},{7,3},{8,12},{12,8},{9,1... | collective-permute-start | bytes 2359304 | tf_op jit(solution)/shard_map/ppermute | solution.py:558
  664.9 35.2 %collective-permute-start.46 = (bf16[256,2048]{1,0:T(8,128)(2,1)S(1)}, bf16[256,2048]{1,0:T(8,128)(2,1)}, u32[]{:S(2)}, u32[]{:S(2)}) collective-permute-start(bf16[256,2048]{1,0:T(8,128)(2,1)S(1)} %copy-done.37), channel_id=1, source_target_pairs={{0,1},{1,0},{2,3},{3,2},{4,5},{5,4},{6,7},{7,6},{8,9},{9,8},{10,11... | collective-permute-start | bytes 3145736 | tf_op jit(solution)/shard_map/ppermute | solution.py:563
  669.2 36.3 %collective-permute-start.49 = (bf16[256,2048]{1,0:T(8,128)(2,1)}, bf16[256,2048]{1,0:T(8,128)(2,1)}, u32[]{:S(2)}, u32[]{:S(2)}) collective-permute-start(bf16[256,2048]{1,0:T(8,128)(2,1)} %get-tuple-element.156.refs_0_), channel_id=1, source_target_pairs={{0,1},{1,0},{2,3},{3,2},{4,5},{5,4},{6,7},{7,6},{8,9},{9,8},{10,11... | collective-permute-start | bytes 3145736 | tf_op jit(solution)/shard_map/ppermute | solution.py:563
  670.3 29.8 %collective-permute-start.48 = (bf16[256,2048]{1,0:T(8,128)(2,1)}, bf16[256,2048]{1,0:T(8,128)(2,1)}, u32[]{:S(2)}, u32[]{:S(2)}) collective-permute-start(bf16[256,2048]{1,0:T(8,128)(2,1)} %collective-permute-done.47.refs_2_), channel_id=1, source_target_pairs={{0,1},{1,0},{2,3},{3,2},{4,5},{5,4},{6,7},{7,6},{8,9},{9,8},{10,11... | collective-permute-start | bytes 3145736 | tf_op jit(solution)/shard_map/ppermute | solution.py:563
  691.8 13.7 %collective-permute-start.51 = (bf16[256,2048]{1,0:T(8,128)(2,1)}, bf16[256,2048]{1,0:T(8,128)(2,1)}, u32[]{:S(2)}, u32[]{:S(2)}) collective-permute-start(bf16[256,2048]{1,0:T(8,128)(2,1)} %collective-permute-done.50.refs_2_), channel_id=1, source_target_pairs={{0,1},{1,0},{2,3},{3,2},{4,5},{5,4},{6,7},{7,6},{8,9},{9,8},{10,11... | collective-permute-start | bytes 3145736 | tf_op jit(solution)/shard_map/ppermute | solution.py:563
  (84 other events, 489.0 us)
Sparse Core Ops, SparseCore 0:
  99.6 117.9 all-gather.2
  220.3 68.9 all-gather.4
  311.6 57.7 reduce-scatter.2
  384.9 103.3 reduce-scatter.4

commit v3 on v2

--- a/solution.py
+++ b/solution.py
@@ -40,7 +40,8 @@
     lane=lax.broadcasted_iota(jnp.int32,(1,width),1)
     return [ (lane//HEAD_DIM)==h for h in range(width//HEAD_DIM)]
 
-def fwd_kernel(block, mixed_ref, bias_ref, table_ref, q_ref, k_ref, v_ref, att_ref, lse_ref):
+def fwd_kernel(block, mixed_ref, bias_ref, table_ref, *refs):
+    q_ref, k_ref, v_ref, att_ref, lse_ref = refs[-5:]
     length, width = q_ref.shape
     half=ROT//2
     def rotated(c):
@@ -75,7 +76,7 @@
         att_ref[rows,:]=out.astype(LOW)
         lse_ref[rows,:]=lse
 
-def attend_forward(mixed,bias,tables,seqs,length,block=256):
+def attend_forward(mixed,bias,tables,seqs,length,behind=(),block=256):
     pair,_,rows,cols=mixed.shape
     width=min(cols,128); groups=cols//width
     tok=lambda o,s,g:(o,s,g)
@@ -86,13 +87,13 @@
         grid=(pair,seqs,groups),
         in_specs=[pl.BlockSpec((None,3,length,width),lambda o,s,g:(o,0,s,g)),
                   pl.BlockSpec((None,3,1,width),lambda o,s,g:(o,0,0,g)),
-                  pl.BlockSpec((3,length,width),lambda o,s,g:(0,0,0))],
+                  pl.BlockSpec((3,length,width),lambda o,s,g:(0,0,0))]+[pl.BlockSpec(memory_space=pl.ANY)]*len(behind),
         out_specs=[spec]*5,
         out_shape=[shape(LOW)]*4+[shape(F32)],
         compiler_params=pltpu.CompilerParams(vmem_limit_bytes=48<<20),
         cost_estimate=light(flops=int(4*pair*rows*length*cols*0.6),bytes_accessed=pair*rows*cols*26,transcendentals=pair*rows*length*cols//128),
         name="attend_forward",
-    )(mixed,bias,tables)
+    )(mixed,bias,tables,*behind)
 
 def bwd_kernel(block,q_ref,k_ref,v_ref,att_ref,lse_ref,do_ref,table_ref,out_ref,dk_acc,dv_acc,dq_acc):
     length,width=q_ref.shape
@@ -589,6 +590,20 @@
     return jnp.take(jnp.stack(parts, axis), order, axis=axis).reshape(shape)
 
 
+class Gathered:
+    def __init__(self, place, value, axis):
+        self.place, self.value, self.axis = place, value, axis
+        if place.context == 2:
+            self.raw = place.shift(value, "x", 1)
+        else:
+            self.raw = gather_stage(place, value, axis, "x")
+
+    def whole(self):
+        if self.place.context != 2:
+            return self.raw
+        return ordered(self.place.x, self.value, self.raw, self.axis)
+
+
 def ordered(at, mine, other, axis):
     first = jnp.where(at == 0, mine, other)
     second = jnp.where(at == 0, other, mine)
@@ -662,9 +677,9 @@
     if place.square(seqs):
         over_y, over_core = place.shift(value, "y", 1), place.swap(value)
         whole = lay_rows(place.core, place.y, value, over_core, over_y, [place.swap(over_y)], dtype, behind)
-        return whole.reshape(2, -1, feat)
+        return whole.reshape(2, -1, feat), over_y
     value = gather_stage(place, value.reshape(seqs, -1, feat), 1, "y")
-    return ordered(place.core, value, place.swap(value), 0).astype(dtype)
+    return ordered(place.core, value, place.swap(value), 0).astype(dtype), value
 
 
 def other_rows(place, value):
@@ -678,58 +693,66 @@
     return [2 * x, 2 * x + 1, 2 * (1 - x) + y, 2 * (1 - x) + 1 - y]
 
 
-def empty_kernel(out_ref):
+def empty_kernel(*refs):
     pass
 
 
-def empty(shape, dtype):
+def empty(shape, dtype, behind=()):
     return pl.pallas_call(
         empty_kernel,
-        out_specs=pl.BlockSpec(memory_space=pl.ANY),
+        in_specs=[ANYWHERE] * len(behind),
+        out_specs=ANYWHERE,
         out_shape=jax.ShapeDtypeStruct(shape, dtype),
         name="empty",
-    )()
-
-
-def gather_pack(place, shard, before, behind, ready):
+    )(*behind)
+
+
+def lay_shards(place, shard, before, behind, low, high, ready):
     n, z = place.fsdp, place.z
     blocks, size, cols = shard.shape
-    half = blocks // 2
-    low = place.shift(before[:half, :size], "z", 1)
-    high = place.shift(behind[half:, :size], "z", -1)
-    low = after(low, ready)
-    whole = empty((blocks, n * size, cols), shard.dtype)
+    whole = empty((blocks, n * size, cols), shard.dtype, ready)
     for part, block, start in (
         (shard, 0, z),
         (before[:, :size], 0, (z + 3) % n),
         (behind[:, :size], 0, (z + 1) % n),
-        (low, 0, (z + 2) % n),
-        (high, half, (z + 2) % n),
+        (low[:, :size], 0, (z + 2) % n),
+        (high, blocks // 2, (z + 2) % n),
     ):
         whole = lax.dynamic_update_slice(whole, part, (block, start * size, 0))
-    return whole, (low, high)
-
-
-def reduce_shards(place, grad, axis, half_axis, begin, ready):
-    n = place.fsdp
-    size = grad.shape[axis] // n
-    half = (size if axis == half_axis else grad.shape[half_axis]) // 2
-
-    def part(ahead, side):
-        shard = lax.dynamic_slice_in_dim(grad, (place.z + ahead) % n * size, size, axis)
-        return lax.slice_in_dim(shard, side * half, (side + 1) * half, axis=half_axis).astype(F32)
-
-    def pair(one, two):
-        return after(jnp.stack([one, two]).astype(LOW), begin)
-
-    left = place.shift(pair(part(2, 1), part(1, 0)), "z", 1)
-    right = place.shift(pair(part(2, 0), part(3, 1)), "z", -1)
-    left, right = after((left, right), ready)
-    left_high = place.shift((part(1, 1) + left[0].astype(F32)).astype(LOW), "z", 1)
-    right_low = place.shift((part(3, 0) + right[0].astype(F32)).astype(LOW), "z", -1)
-    low = part(0, 0) + left[1].astype(F32) + right_low.astype(F32)
-    high = part(0, 1) + right[1].astype(F32) + left_high.astype(F32)
-    return jnp.concatenate([low.astype(LOW), high.astype(LOW)], axis=half_axis)
+    return whole
+
+
+class Shards:
+    def __init__(self, place, grad, axis, half_axis, begin):
+        self.place, self.grad, self.axis, self.half_axis = place, grad, axis, half_axis
+        self.size = grad.shape[axis] // place.fsdp
+        self.half = (self.size if axis == half_axis else grad.shape[half_axis]) // 2
+
+        def pair(one, two):
+            return after(jnp.stack([one, two]).astype(LOW), begin)
+
+        self.left = place.shift(pair(self.part(2, 1), self.part(1, 0)), "z", 1)
+        self.right = place.shift(pair(self.part(2, 0), self.part(3, 1)), "z", -1)
+
+    def part(self, ahead, side):
+        place, half = self.place, self.half
+        start = (place.z + ahead) % place.fsdp * self.size
+        shard = lax.dynamic_slice_in_dim(self.grad, start, self.size, self.axis)
+        return lax.slice_in_dim(shard, side * half, (side + 1) * half, axis=self.half_axis).astype(F32)
+
+    def follow(self, *ready):
+        place = self.place
+        self.left, self.right = after((self.left, self.right), *ready)
+        high = (self.part(1, 1) + self.left[0].astype(F32)).astype(LOW)
+        low = (self.part(3, 0) + self.right[0].astype(F32)).astype(LOW)
+        self.high, self.low = place.shift(high, "z", 1), place.shift(low, "z", -1)
+        return low
+
+    def total(self, *ready):
+        high, low = after((self.high, self.low), *ready) if ready else (self.high, self.low)
+        low = self.part(0, 0) + self.left[1].astype(F32) + low.astype(F32)
+        high = self.part(0, 1) + self.right[1].astype(F32) + high.astype(F32)
+        return jnp.concatenate([low.astype(LOW), high.astype(LOW)], axis=self.half_axis)
 
 
 def total_over(place, value, which):
@@ -755,22 +778,24 @@
     pad = [(0, 1), (0, 0)]
     sent = place.swap(jnp.concatenate([sums, jnp.pad(bias_other, pad)], axis=1))
     sums, bias = sums + sent[:, :feat], jnp.pad(bias, pad) + sent[:, feat:]
-    if place.context == 2:
-        sent = place.shift(jnp.concatenate([sums, bias], axis=1), "x", 1)
-        sums = sums + sent[:, :feat]
-        bias = ordered(place.x, bias, sent[:, feat:], 1)
-    else:
-        sums = total_over(place, sums, "x")
-        bias = gather_stage(place, bias, 1, "x")
     size = feat // n
-    parts = jnp.zeros((n,) + (4, size + bias.shape[1]), F32)
+    came = []
     for step in range(n):
         part = lax.dynamic_slice_in_dim(sums, (z + step) % n * size, size, 1)
         part = jnp.concatenate([part, bias], axis=1)
-        part = place.shift(part, "z", step) if step else part
-        parts = lax.dynamic_update_index_in_dim(parts, part, (z - step) % n, 0)
-    total = jnp.sum(parts, axis=0)
-    return total[:, :size], total[:3, size:]
+        came.append(place.shift(part, "z", step) if step else part)
+    came = lax.optimization_barrier(tuple(came))
+    parts = jnp.zeros((n,) + came[0].shape, F32)
+    for step in range(n):
+        parts = lax.dynamic_update_index_in_dim(parts, came[step], (z - step) % n, 0)
+    return jnp.sum(parts, axis=0)
+
+
+def last_totals(place, totals, size):
+    if place.context == 2:
+        sent = place.shift(totals, "x", 1)
+        return totals[:, :size] + sent[:, :size], ordered(place.x, totals[:3, size:], sent[:3, size:], 1)
+    return total_over(place, totals[:, :size], "x"), gather_stage(place, totals[:3, size:], 1, "x")
 
 
 def local(
@@ -812,62 +837,70 @@
     extra = jnp.pad(norm_block, [(0, 3), (0, 0), (0, 0)])
     pack = jnp.concatenate([pack, extra], axis=1)
     pack_before, pack_behind = place.shift(pack, "z", 1), place.shift(pack, "z", -1)
-    norm_far = place.shift(norm_block, "z", 2)
-    hidden_mine = own_sequences(hidden_in)
-    hidden_mine = hidden_mine.reshape(-1, feat)
+    bias = columns(qkv_bias, head_cols, 1)
+    bias_swapped = place.swap(bias)
+    bias_other = bias_swapped.astype(F32)[None, :, None, :]
+    bias = bias.astype(F32)[None, :, None, :]
+    hidden_mine = own_sequences(hidden_in).reshape(-1, feat)
+    top_mine = own_sequences(cotangent)
+    if place.square(seqs):
+        pieces = other_rows(place, hidden_mine)
+        top_pieces = other_rows(place, top_mine.reshape(-1, feat))
+        pack_before, pack_behind = after((pack_before, pack_behind), pieces[2], bias_swapped)
+    else:
+        whole = gather_stage(place, hidden_mine.reshape(seqs, -1, feat), 1, "x").reshape(-1, feat)
+        pieces = top_pieces = [whole] * 4
+    half = pack.shape[0] // 2
+    pack_low = place.shift(pack_before[:half], "z", 1)
+    pack_high = place.shift(pack_behind[half:, :part_feat], "z", -1)
     norms = jnp.zeros((2, 2, feat), F32)
     for step, piece in (
         (0, norm_block),
         (1, pack_before[:1, part_feat:]),
-        (2, norm_far),
+        (2, pack_low[:1, part_feat:]),
         (3, pack_behind[:1, part_feat:]),
     ):
         piece = piece[0, :norm_rows].reshape(2, 2, part_feat).astype(F32)
         norms = lax.dynamic_update_slice(norms, piece, (0, 0, (place.z - step) % place.fsdp * part_feat))
     gains, shifts = norms[0][:, None, :], norms[1][:, None, :]
-    bias = columns(qkv_bias, head_cols, 1)
-    bias_other = place.swap(bias).astype(F32)[None, :, None, :]
-    bias = bias.astype(F32)[None, :, None, :]
-
     gate_up_part = columns(gate_up_weight, hidden_cols, 2).transpose(0, 2, 1)
     down_part = columns(down_weight, hidden_cols, 0)
-    top_mine = own_sequences(cotangent)
     if place.square(seqs):
-        pieces = other_rows(place, hidden_mine)
-        top_pieces = other_rows(place, top_mine.reshape(-1, feat))
-        normed = norm_first(other_places(place), pieces, gains[0], shifts[0], behind=[top_pieces[3]])
-        grad_top = lay_pieces(other_places(place), top_pieces)
+        normed = norm_first(other_places(place), pieces, gains[0], shifts[0])
+        top_last = top_pieces[3]
     else:
-        whole = gather_stage(place, hidden_mine.reshape(seqs, -1, feat), 1, "x").reshape(-1, feat)
         normed = (centre(whole.astype(F32))[0] * gains[0] + shifts[0]).astype(LOW)
-        grad_top = gather_stage(place, top_mine, 1, "x").reshape(seqs * length, feat)
-    w_attn, far = gather_pack(place, pack[:, :part_feat], pack_before, pack_behind, normed)
-    gate_up_part, down_part = after((gate_up_part, down_part), *far)
+        grad_top = top_last = gather_stage(place, top_mine, 1, "x").reshape(seqs * length, feat)
+    w_attn = lay_shards(place, pack[:, :part_feat], pack_before, pack_behind, pack_low, after(pack_high, normed), [pieces[3], gate_up_part, down_part])
+    gate_up_part, down_part = after((gate_up_part, down_part), pack_low, pack_high, top_pieces[2])
     w_gate_up = lax.all_gather(gate_up_part, "fsdp", axis=2, tiled=True)
     w_down = lax.all_gather(down_part, "fsdp", axis=1, tiled=True)
     tables = rotary_tables(length, min(head_cols, 128))
     w_attn_other = place.swap(w_attn)
 
-    def attend(weight, bias):
+    def attend(weight, bias, behind):
         mixed = jnp.einsum("rd,cde->cre", normed, weight[:3], preferred_element_type=F32)
-        return attend_forward(mixed[None], bias, tables, seqs, length)
-
-    kept = attend(w_attn, bias)
-    kept_other = attend(w_attn_other, bias_other)
+        return attend_forward(mixed[None], bias, tables, seqs, length, behind)
+
+    kept = attend(w_attn, bias, [])
+    kept_other = attend(w_attn_other, bias_other, [kept[3], top_last])
     attended, attended_other = kept[3][0], kept_other[3][0]
-    theirs_top, theirs_one, theirs_attended = place.swap(grad_top), place.swap(normed), place.swap(attended_other)
     attn_sum = RowSum(
         place,
         "nt",
         [(attended, (), w_attn, (3,)), (attended_other, (), w_attn_other, (3,))],
         seqs,
         "out",
-        behind=[theirs_top, theirs_one],
     ).start()
-    attn_sum.follow()
+    if place.square(seqs):
+        grad_top = lay_pieces(other_places(place), top_pieces, [attn_sum.sent])
+    theirs_top, theirs_one, theirs_attended = place.swap(grad_top), place.swap(normed), place.swap(attended_other)
+    attn_sum.follow([grad_top])
     inputs = own_piece(hidden_mine.reshape(seqs, -1, feat)).reshape(-1, feat)
-    middle, normed_two = add_norm(attn_sum.shares, inputs, gains[1], shifts[1])
-    normed_two = spread_rows(place, normed_two, seqs)
+    middle, normed_two = add_norm(
+        attn_sum.shares, inputs, gains[1], shifts[1], behind=[theirs_attended]
+    )
+    normed_two = spread_rows(place, normed_two, seqs, [theirs_top, theirs_one])
 
     w_gate_up_other = place.swap(after(w_gate_up, middle))
     turned_other, slope_other, hidden_part = gate_up(normed_two, w_gate_up_other)
@@ -891,7 +924,7 @@
         + [(grad_gu_other, (c,), w_gate_up_other, (c,)) for c in range(2)],
         seqs,
         "grad_two",
-        behind=[theirs_two, theirs_attended, theirs_gu],
+        behind=[theirs_two, theirs_gu],
     ).start()
     grad_gate_up = products(
         "nn",
@@ -917,7 +950,7 @@
         two_sum.shares, middle, gains[1], top_rows, [F32, LOW], behind=[down_sums.sent]
     )
     grad_mid_low = spread_rows(place, mid_low, seqs)
-    down_sum = gather_stage(place, after(down_sum, grad_mid_low), 0, "x")
+    down_whole = lax.all_gather(after(down_sum, grad_mid_low), "context", axis=0, tiled=True)
     down_sums.start(grad_mid_low)
 
     def attend_grad(kept, weight, behind):
@@ -927,12 +960,18 @@
     theirs_mid = place.swap(grad_mid_low)
     grad_mixed_other = attend_grad(kept_other, w_attn_other, [])
     theirs_mixed = place.swap(grad_mixed_other)
-    grad_mixed = attend_grad(kept, w_attn, [grad_mixed_other, theirs_mid])
-    down_next = down_sums.follow([grad_mixed])
-    gate_up_mine = gate_up_sum
-    gate_up_sum = gather_stage(place, after(gate_up_sum, grad_mixed), 1, "x")
+    grad_out = products(
+        "tn",
+        [(grad_mid_low, (), attended, ()), (theirs_mid, (), theirs_attended, ())],
+        512,
+        head_cols,
+        "grad_out",
+        behind=[grad_mixed_other],
+    )
+    down_next = down_sums.follow([grad_out])
+    grad_mixed = attend_grad(kept, w_attn, [down_next])
     final_out = add_low(down_sums.shares, middle, behind=[grad_mixed])
-    grad_qkv = qkv_back(normed, theirs_one, grad_mixed, theirs_mixed, behind=[down_next, gate_up_mine])
+    out_sum = lax.psum_scatter(grad_out, "fsdp", scatter_dimension=0, tiled=True)
     one_sum = RowSum(
         place,
         "nt",
@@ -940,40 +979,47 @@
         + [(grad_mixed_other, (c,), w_attn_other, (c,)) for c in range(3)],
         seqs,
         "grad_one",
-        behind=[grad_qkv],
+        behind=[final_out],
     ).start()
-    grad_out = products(
-        "tn",
-        [(grad_mid_low, (), attended, ()), (theirs_mid, (), theirs_attended, ())],
-        512,
-        head_cols,
-        "grad_out",
-        behind=[one_sum.sent],
-    )
-    one_next = one_sum.follow([grad_out])
-    qkv_sum = reduce_shards(place, grad_qkv, 1, 1, grad_mixed, one_next)
-    input_low, sums_one = norm_back(one_sum.shares, inputs, gains[0], grad_middle, [LOW], behind=[one_next])
-    out_sum = reduce_shards(place, grad_out, 0, 0, one_next, input_low)
+    grad_qkv = qkv_back(
+        normed, theirs_one, grad_mixed, theirs_mixed, behind=[one_sum.sent, gate_up_sum]
+    )
+    qkv_shards = Shards(place, grad_qkv, 1, 1, grad_mixed)
+    one_next = one_sum.follow([grad_qkv])
+    qkv_next = qkv_shards.follow(one_next)
+    input_low, sums_one = norm_back(
+        one_sum.shares,
+        inputs,
+        gains[0],
+        grad_middle,
+        [LOW],
+        behind=[one_next, qkv_next],
+    )
+    gate_up_whole = lax.all_gather(gate_up_sum, "context", axis=1, tiled=True)
     sums = total_over(place, jnp.concatenate([sums_one, sums_two]), "y")
-    input_grad = whole_rows(place, after(input_low, sums), seqs, F32)
-    layer_out = whole_rows(place, after(final_out, input_low, sums), seqs, LOW)
-    sums, grad_bias = small_totals(
+    input_grad, over_y = whole_rows(place, after(input_low, sums), seqs, F32)
+    totals = small_totals(
         place,
-        sums,
+        after(sums, qkv_shards.low, qkv_shards.high),
         jnp.sum(grad_mixed.astype(F32), axis=1),
         jnp.sum(grad_mixed_other.astype(F32), axis=1),
     )
+    qkv_sum = qkv_shards.total()
+    qkv_gathered = Gathered(place, qkv_sum, 2)
+    out_gathered = Gathered(place, after(out_sum, qkv_sum), 1)
+    layer_out, _ = whole_rows(place, after(final_out, over_y), seqs, LOW)
+    sums, grad_bias = last_totals(place, after(totals, qkv_sum), norm_gains.shape[1])
 
     return (
         layer_out,
         input_grad,
         sums[0::2],
         sums[1::2],
-        gather_stage(place, qkv_sum, 2, "x").astype(F32),
+        qkv_gathered.whole().astype(F32),
         grad_bias,
-        gather_stage(place, out_sum, 1, "x").T.astype(F32),
-        gate_up_sum.transpose(0, 2, 1).astype(F32),
-        down_sum.astype(F32),
+        out_gathered.whole().T.astype(F32),
+        gate_up_whole.transpose(0, 2, 1).astype(F32),
+        down_whole.astype(F32),
     )
 
 

time: 726 us -> 668 us (0.920)
  waiting for transfers between devices: 258 us -> 230 us
  starting transfers between devices: 76.3 us -> 61.5 us
  local copies, waits for them, and re-layouts: 67.5 us -> 57.1 us
    ppermute x16 -> x11, waiting for transfers between devices: 18.7 us -> 69 us  [shift(): return lax.ppermute(value, 'fsdp', [(i, (i + step) % n) for i in range(n)])]
    ppermute x19 -> x17, waiting for transfers between devices: 124 us -> 87.6 us  [shift(): lax.ppermute(value, 'context', [(i, (i + step) % n) for i in range(n)])]
    ppermute x17, waiting for transfers between devices: 102 us -> 73.6 us  [shift(): lax.ppermute(value, 'tensor', [(i, (i + 2 * step) % n) for i in range(n)])]
    ppermute x16 -> x11, starting transfers between devices: 33.2 us -> 20.9 us  [shift(): return lax.ppermute(value, 'fsdp', [(i, (i + step) % n) for i in range(n)])]
    all_gather x1, waiting for transfers between devices: 8.65 us -> 0.01 us  [local(): w_down = lax.all_gather(down_part, 'fsdp', axis=1, tiled=True)]
    unnamed x154 -> x124, local copies, waits for them, and re-layouts: 37 us -> 30.4 us
    ppermute x19 -> x17, starting transfers between devices: 20.2 us -> 17.6 us  [shift(): lax.ppermute(value, 'context', [(i, (i + step) % n) for i in range(n)])]
    convert_element_type x10 -> x7, other arithmetic: 15.1 us -> 14.6 us  [the longest x1 5.17 us: local(): gate_up_whole.transpose(0, 2, 1).astype(F32)]
  transfers between devices with their start and end apart: 73 -> 69, of which waited for: 29 -> 28; matrix products, arithmetic and copies ran while one was open for 11% -> 11% of each run, Pallas kernels for 31% -> 38%
where the time goes in v3:
time: 668 us; the launch traced here: 663 us
  Pallas kernels  258 us (39%)
  waiting for transfers between devices  230 us (34%)
  starting transfers between devices  61.5 us (9%)
  local copies, waits for them, and re-layouts  57.1 us (9%)
  other arithmetic  28.4 us (4%)
  between operations  15.5 us (2%)
  matrix products  12.2 us (2%)
    ppermute x17, waiting for transfers between devices, shift(): lax.ppermute(value, 'context', [(i, (i + step) % n) for i in range(n)])  87.6 us
    ppermute x17, waiting for transfers between devices, shift(): lax.ppermute(value, 'tensor', [(i, (i + 2 * step) % n) for i in range(n)])  73.6 us
    ppermute x11, waiting for transfers between devices, shift(): return lax.ppermute(value, 'fsdp', [(i, (i + step) % n) for i in range(n)])  69 us
    pallas_call x4, Pallas kernels, products_apart(): pl.pallas_call(kernel, grid_spec=pltpu.PrefetchScalarGridSpec(num_scalar_...  52.5 us
    pallas_call x5, Pallas kernels, products(): pl.pallas_call(kernel, grid=(many, rows // tm, cols // tn), in_specs=ones...  44.3 us
    pallas_call x6, Pallas kernels, pieces_of(): pl.pallas_call(kernel, grid_spec=pltpu.PrefetchScalarGridSpec(num_scalar_...  36.1 us
    unnamed x124, local copies, waits for them, and re-layouts  30.4 us
    pallas_call x2, Pallas kernels, gate_up(): pl.pallas_call(gate_kernel, grid=(rows // tm,), in_specs=[pl.BlockSpec((2...  24 us
  transfers between devices with their start and end apart: 69, of which 28 were waited for; matrix products, arithmetic and copies ran while one was open for 11% of the time, Pallas kernels for 38%

profile of v3, /device:TPU:0, one launch (start us, length us, event | category | flops | bytes accessed | tf_op | source)
XLA Modules:
  0.0 662.8 jit_solution(16537845560504148206)
XLA Ops:
  12.4 3.0 collective-permute-start
  17.5 3.8 dynamic-slice_bitcast_fusion.2
  27.2 2.6 copy.32
  29.9 17.8 %collective-permute-done.2.refs_2_ = bf16[256,2048]{1,0:T(8,128)(2,1)} collective-permute-done((bf16[256,2048]{1,0:T(8,128)(2,1)}, bf16[256,2048]{1,0:T(8,128)(2,1)}, u32[]{:S(2)}, u32[]{:S(2)}) %collective-permute-start.2) | collective-permute-done | bytes 1048608 | tf_op jit(solution)/shard_map/ppermute | solution.py:559
  47.7 16.5 %collective-permute-done.1 = bf16[4,528,256]{2,1,0:T(8,128)(2,1)} collective-permute-done((bf16[4,528,256]{2,1,0:T(8,128)(2,1)}, bf16[4,528,256]{2,1,0:T(8,128)(2,1)}, u32[]{:S(2)}, u32[]{:S(2)}) %collective-permute-start.1) | collective-permute-done | bytes 1081376 | tf_op jit(solution)/shard_map/ppermute | solution.py:556
  67.6 2.8 collective-permute-start.5
  75.3 16.7 %collective-permute-done.5 = bf16[2,512,256]{2,1,0:T(8,128)(2,1)S(1)} collective-permute-done((bf16[2,512,256]{2,1,0:T(8,128)(2,1)S(1)}, bf16[2,512,256]{2,1,0:T(8,128)(2,1)S(1)}, u32[]{:S(2)}, u32[]{:S(2)}) %collective-permute-start.5) | collective-permute-done | bytes 524320 | tf_op jit(solution)/shard_map/ppermute | solution.py:556
  93.7 3.5 collective-permute-done.7.refs_0_.refs_3_
  98.2 7.6 %norm_first.1 = bf16[4,256,2048]{2,1,0:T(8,128)(2,1)} custom-call(s32[4]{0:T(128)} %add_add_fusion.1.at_ref, bf16[256,2048]{1,0:T(8,128)(2,1)} %get-tuple-element.190.refs_0_, bf16[256,2048]{1,0:T(8,128)(2,1)} %get-tuple-element.189.refs_1_, bf16[256,2048]{1,0:T(8,128)(2,1)} %collective-permute-done.2.refs_2_, bf16[256,2048]{1,0:T(8,128)(2,1)} %copy-done.34, ...), custom_call_target="tpu_custom_call" | custom-call | bytes 83886 | tf_op jit(solution)/shard_map/norm_first/pallas_call | solution.py:358
  107.9 2.4 slice_dynamic-update-slice_fusion.1
  110.4 2.3 slice_dynamic-update-slice_fusion
  117.5 7.1 %fusion.5.r_0_ = f32[1,3,1024,256]{3,2,1,0:T(8,128)} fusion(bf16[1024,2048,1]{1,0,2:T(8,128)(2,1)S(1)} %bitcast.130, bf16[4,2048,256]{2,1,0:T(8,128)(2,1)} %constant_dynamic-update-slice_fusion.refs_2_.refs_1_.refs_6_.refs_7_.refs_8_), kind=kOutput, calls=%fused_computation.9 | convolution fusion | flops 3221225472 | bytes 10485760 | tf_op jit(solution)/shard_map/rd,cde->cre/dot_general | solution.py:882
  124.6 9.4 %attend_forward.2 = (bf16[1,1024,256]{2,1,0:T(8,128)(2,1)S(1)}, bf16[1,1024,256]{2,1,0:T(8,128)(2,1)S(1)}, bf16[1,1024,256]{2,1,0:T(8,128)(2,1)S(1)}, bf16[1,102...) custom-call(f32[1,3,1024,256]{3,2,1,0:T(8,128)} %fusion.5.r_0_, f32[1,3,1,256]{3,2,1,0:T(1,128)S(1)} %copy.23.r_1_, ...), custom_call_target="tpu_custom_call" | custom-call | flops 6442450 | bytes 68157 | tf_op jit(solution)/shard_map/attend_forward/pallas_call | solution.py:85
  134.0 5.1 fusion.8.r_0_
  139.1 2.6 collective-permute-done.9.r_4_.refs_3_
  141.7 10.0 %attend_forward.3 = (bf16[1,1024,256]{2,1,0:T(8,128)(2,1)S(1)}, bf16[1,1024,256]{2,1,0:T(8,128)(2,1)S(1)}, bf16[1,1024,256]{2,1,0:T(8,128)(2,1)S(1)}, bf16[1,102...) custom-call(f32[1,3,1024,256]{3,2,1,0:T(8,128)} %fusion.8.r_0_, f32[1,3,1,256]{3,2,1,0:T(1,128)S(1)} %reshape.85.r_1_, ...), custom_call_target="tpu_custom_call" | custom-call | flops 6442450 | bytes 68157 | tf_op jit(solution)/shard_map/attend_forward/pallas_call | solution.py:85
  154.1 7.5 %out.1 = (bf16[2,256,1024]{2,1,0:T(8,128)(2,1)}, bf16[2,256,1024]{2,1,0:T(8,128)(2,1)}, bf16[2,256,1024]{2,1,0:T(8,128)(2,1)}, bf16[2,256,1024]{2,1,0:T(8,128)(2,1)}) custom-call(s32[2]{0:T(128)} %pad_add_fusion.1.at_ref, bf16[1024,256]{1,0:T(8,128)(2,1)} %bitcast.109, bf16[1024,256]{1,0:T(8,128)(2,1)} %bitcast.111, ...), custom_call_target="tpu_custom_call" | custom-call | flops 21474836 | bytes 73400 | tf_op jit(solution)/shard_map/out/pallas_call | solution.py:246
  164.7 5.3 lay_pieces.1
  170.0 16.8 %collective-permute-done.10.two = bf16[2,256,1024]{2,1,0:T(8,128)(2,1)S(1)} collective-permute-done((bf16[2,256,1024]{2,1,0:T(8,128)(2,1)}, bf16[2,256,1024]{2,1,0:T(8,128)(2,1)S(1)}, u32[]{:S(2)}, u32[]{:S(2)}) %collective-permute-start.10) | collective-permute-done | bytes 1048608 | tf_op jit(solution)/shard_map/ppermute | solution.py:559
  189.0 3.5 join.4
  194.6 10.6 %collective-permute-done.12.refs_1_ = bf16[256,1024]{1,0:T(8,128)(2,1)S(1)} collective-permute-done((bf16[256,1024]{1,0:T(8,128)(2,1)}, bf16[256,1024]{1,0:T(8,128)(2,1)S(1)}, u32[]{:S(2)}, u32[]{:S(2)}) %collective-permute-start.12) | collective-permute-done | bytes 524320 | tf_op jit(solution)/shard_map/ppermute | solution.py:561
  207.3 3.5 add_norm.1
  213.0 24.3 %collective-permute-done.16.refs_2_ = bf16[256,2048]{1,0:T(8,128)(2,1)S(1)} collective-permute-done((bf16[256,2048]{1,0:T(8,128)(2,1)}, bf16[256,2048]{1,0:T(8,128)(2,1)S(1)}, u32[]{:S(2)}, u32[]{:S(2)}) %collective-permute-start.16) | collective-permute-done | bytes 1048608 | tf_op jit(solution)/shard_map/ppermute | solution.py:561
  242.1 9.9 %collective-permute-done.17.refs_3_ = bf16[256,1024]{1,0:T(8,128)(2,1)S(1)} collective-permute-done((bf16[256,1024]{1,0:T(8,128)(2,1)}, bf16[256,1024]{1,0:T(8,128)(2,1)S(1)}, u32[]{:S(2)}, u32[]{:S(2)}) %collective-permute-start.17) | collective-permute-done | bytes 524320 | tf_op jit(solution)/shard_map/ppermute | solution.py:559
  252.0 2.6 collective-permute-done.18.refs_4_
  254.6 5.9 lay_rows.4
  260.6 12.0 %gate_up.3 = (bf16[704,1024]{1,0:T(8,128)(2,1)}, bf16[2,704,1024]{2,1,0:T(8,128)(2,1)}, bf16[1024,704]{1,0:T(8,128)(2,1)}) custom-call(bf16[2,704,2048]{2,1,0:T(8,128)(2,1)} %collective-permute-done.21.weight_ref.refs_6_.refs_7_, bf16[1024,2048]{1,0:T(8,128)(2,1)} %bitcast.120), custom_call_target="tpu_custom_call" | custom-call | flops 59055800 | bytes 157286 | tf_op jit(solution)/shard_map/gate_up/pallas_call | solution.py:285
  273.1 12.0 %gate_up.2 = (bf16[704,1024]{1,0:T(8,128)(2,1)}, bf16[2,704,1024]{2,1,0:T(8,128)(2,1)}, bf16[1024,704]{1,0:T(8,128)(2,1)}) custom-call(bf16[2,704,2048]{2,1,0:T(8,128)(2,1)} %all-gather.5.cloned.1.call-done.weight_ref.refs_4_.refs_5_, bf16[1024,2048]{1,0:T(8,128)(2,1)} %bitcast.121), custom_call_target="tpu_custom_call" | custom-call | flops 59055800 | bytes 157286 | tf_op jit(solution)/shard_map/gate_up/pallas_call | solution.py:285
  286.2 10.2 %grad_down.1.refs_0_ = bf16[704,2048]{1,0:T(8,128)(2,1)} custom-call(bf16[704,1024]{1,0:T(8,128)(2,1)} %get-tuple-element.116.refs_0_, bf16[704,1024]{1,0:T(8,128)(2,1)} %copy-done.45, bf16[1024,2048]{1,0:T(8,128)(2,1)} %bitcast.117, bf16[1024,2048]{1,0:T(8,128)(2,1)} %collective-permute-done.19.refs_5_.refs_3_), custom_call_target="tpu_custom_call" | custom-call | flops 59055800 | bytes 141557 | tf_op jit(solution)/shard_map/grad_down/pallas_call | solution.py:196
  296.6 8.9 %hidden_back.2 = (bf16[2,704,1024]{2,1,0:T(8,128)(2,1)}, bf16[2,1024,704]{2,1,0:T(8,128)(2,1)}) custom-call(bf16[704,2048]{1,0:T(8,128)(2,1)} %collective-permute-done.22.weight_ref.refs_3_, bf16[1024,2048]{1,0:T(8,128)(2,1)} %bitcast.118, bf16[2,704,1024]{2,1,0:T(8,128)(2,1)} %get-tuple-element.115.slope_ref, bf16[704,2048]{1,0:T(8,128)(2,1)} %grad_down.1.refs_0_), custom_call_target="tpu_custom_call" | custom-call | flops 29527900 | bytes 157286 | tf_op jit(solution)/shard_map/hidden_back/pallas_call | solution.py:325
  306.1 8.6 %hidden_back.3 = (bf16[2,704,1024]{2,1,0:T(8,128)(2,1)}, bf16[2,1024,704]{2,1,0:T(8,128)(2,1)}) custom-call(bf16[704,2048]{1,0:T(8,128)(2,1)} %all-gather.7.cloned.1.call-done.weight_ref.refs_2_, bf16[1024,2048]{1,0:T(8,128)(2,1)} %bitcast.119, bf16[2,704,1024]{2,1,0:T(8,128)(2,1)} %get-tuple-element.114.slope_ref, ...), custom_call_target="tpu_custom_call" | custom-call | flops 29527900 | bytes 157286 | tf_op jit(solution)/shard_map/hidden_back/pallas_call | solution.py:325
  316.8 20.2 %grad_two.1 = (bf16[2,256,1024]{2,1,0:T(8,128)(2,1)}, bf16[2,256,1024]{2,1,0:T(8,128)(2,1)}, bf16[2,256,1024]{2,1,0:T(8,128)(2,1)}, bf16[2,256,1024]{2,1,0:T(8,128)(2,1)}) custom-call(s32[2]{0:T(128)} %pad_add_fusion.1.at_ref, bf16[2,1024,704]{2,1,0:T(8,128)(2,1)} %get-tuple-element.118.refs_0_.refs_1_, ...), custom_call_target="tpu_custom_call" | custom-call | flops 118111600 | bytes 214958 | tf_op jit(solution)/shard_map/grad_two/pallas_call | solution.py:246
  338.2 18.1 %grad_gate_up.1.refs_0_ = bf16[2,704,2048]{2,1,0:T(8,128)(2,1)} custom-call(bf16[2,704,1024]{2,1,0:T(8,128)(2,1)} %get-tuple-element.124.refs_0_, bf16[2,704,1024]{2,1,0:T(8,128)(2,1)} %collective-permute-done.25.refs_9_.refs_1_, bf16[1024,2048]{1,0:T(8,128)(2,1)} %bitcast.123, bf16[1024,2048]{1,0:T(8,128)(2,1)} %copy-done.31, ...), custom_call_target="tpu_custom_call" | custom-call | flops 118111600 | bytes 283115 | tf_op jit(solution)/shard_map/grad_gate_up/pallas_call | solution.py:196
  356.2 6.1 collective-permute-done.26.two
  363.3 3.5 join.5
  369.1 12.4 %down.1 = (bf16[2,256,1024]{2,1,0:T(8,128)(2,1)}, bf16[2,256,1024]{2,1,0:T(8,128)(2,1)}, bf16[2,256,1024]{2,1,0:T(8,128)(2,1)}, bf16[2,256,1024]{2,1,0:T(8,128)(2,1)}) custom-call(s32[2]{0:T(128)} %pad_add_fusion.1.at_ref, bf16[1024,704]{1,0:T(8,128)(2,1)} %get-tuple-element.107.refs_0_, bf16[1024,704]{1,0:T(8,128)(2,1)} %get-tuple-element.110.refs_1_, ...), custom_call_target="tpu_custom_call" | custom-call | flops 59055800 | bytes 128450 | tf_op jit(solution)/shard_map/down/pallas_call | solution.py:246
  382.5 4.8 norm_back.2
  390.4 21.6 %collective-permute-done.31.refs_2_ = bf16[256,2048]{1,0:T(8,128)(2,1)S(1)} collective-permute-done((bf16[256,2048]{1,0:T(8,128)(2,1)}, bf16[256,2048]{1,0:T(8,128)(2,1)S(1)}, u32[]{:S(2)}, u32[]{:S(2)}) %collective-permute-start.31) | collective-permute-done | bytes 1048608 | tf_op jit(solution)/shard_map/ppermute | solution.py:561
  414.4 10.2 %collective-permute-done.32.refs_3_ = bf16[256,1024]{1,0:T(8,128)(2,1)S(1)} collective-permute-done((bf16[256,1024]{1,0:T(8,128)(2,1)S(1)}, bf16[256,1024]{1,0:T(8,128)(2,1)S(1)}, u32[]{:S(2)}, u32[]{:S(2)}) %collective-permute-start.32) | collective-permute-done | bytes 524320 | tf_op jit(solution)/shard_map/ppermute | solution.py:559
  426.2 5.3 lay_rows.5
  434.0 4.5 grad_att.2
  439.5 11.4 %attend_back.2 = bf16[1,3,1024,256]{3,2,1,0:T(8,128)(2,1)S(1)} custom-call(bf16[1,1024,256]{2,1,0:T(8,128)(2,1)S(1)} %copy-done.23, bf16[1,1024,256]{2,1,0:T(8,128)(2,1)S(1)} %copy-done.25, bf16[1,1024,256]{2,1,0:T(8,128)(2,1)S(1)} %copy-done.27, bf16[1,1024,256]{2,1,0:T(8,128)(2,1)S(1)} %copy-done.11, f32[1,1024,256]{2,1,0:T(8,128)S(1)} %get-tuple-element.139.r_4_, ...), custom_call_target="tpu_custom_call" | custom-call | flops 16106127 | bytes 52428 | tf_op jit(solution)/shard_map/attend_back/pallas_call | solution.py:145
  452.1 6.7 %grad_out.1.refs_0_ = bf16[2048,256]{1,0:T(8,128)(2,1)} custom-call(bf16[1024,2048]{1,0:T(8,128)(2,1)} %bitcast.126, bf16[1024,2048]{1,0:T(8,128)(2,1)} %collective-permute-done.36.refs_1_, bf16[1024,256]{1,0:T(8,128)(2,1)} %bitcast.110, bf16[1024,256]{1,0:T(8,128)(2,1)} %copy-done.42, bf16[3,1024,256]{2,1,0:T(8,128)(2,1)} %bitcast.105), custom_call_target="tpu_custom_call" | custom-call | flops 21474836 | bytes 104857 | tf_op jit(solution)/shard_map/grad_out/pallas_call | solution.py:196
  458.7 3.5 join.6
  464.2 4.8 grad_att.3
  470.1 11.4 %attend_back.3 = bf16[1,3,1024,256]{3,2,1,0:T(8,128)(2,1)S(1)} custom-call(bf16[1,1024,256]{2,1,0:T(8,128)(2,1)S(1)} %copy-done.17, bf16[1,1024,256]{2,1,0:T(8,128)(2,1)S(1)} %copy-done.19, bf16[1,1024,256]{2,1,0:T(8,128)(2,1)S(1)} %copy-done.21, bf16[1,1024,256]{2,1,0:T(8,128)(2,1)S(1)} %copy-done.8, f32[1,1024,256]{2,1,0:T(8,128)S(1)} %copy-done.15, ...), custom_call_target="tpu_custom_call" | custom-call | flops 16106127 | bytes 52428 | tf_op jit(solution)/shard_map/attend_back/pallas_call | solution.py:145
  482.8 3.4 add_low.1.refs_12_.refs_0_
  486.2 12.3 %grad_one.1 = (bf16[2,256,1024]{2,1,0:T(8,128)(2,1)}, bf16[2,256,1024]{2,1,0:T(8,128)(2,1)}, bf16[2,256,1024]{2,1,0:T(8,128)(2,1)}, bf16[2,256,1024]{2,1,0:T(8,128)(2,1)}) custom-call(s32[2]{0:T(128)} %pad_add_fusion.1.at_ref, bf16[3,1024,256]{2,1,0:T(8,128)(2,1)} %bitcast.100, bf16[3,1024,256]{2,1,0:T(8,128)(2,1)} %bitcast.101, ...), custom_call_target="tpu_custom_call" | custom-call | flops 64424508 | bytes 136314 | tf_op jit(solution)/shard_map/grad_one/pallas_call | solution.py:246
  501.9 10.9 %grad_qkv.1.refs_0_ = bf16[3,2048,256]{2,1,0:T(8,128)(2,1)} custom-call(bf16[1024,2048]{1,0:T(8,128)(2,1)} %bitcast.129, bf16[1024,2048]{1,0:T(8,128)(2,1)} %collective-permute-done.20.refs_6_.theirs_ref, bf16[3,1024,256]{2,1,0:T(8,128)(2,1)} %bitcast.103, bf16[3,1024,256]{2,1,0:T(8,128)(2,1)} %copy-done.44, ...), custom_call_target="tpu_custom_call" | custom-call | flops 64424508 | bytes 146800 | tf_op jit(solution)/shard_map/grad_qkv/pallas_call | solution.py:516
  516.2 3.8 collective-permute-start.45
  520.0 3.3 collective-permute-done.39.two
  524.0 3.6 join.7
  530.1 10.0 %collective-permute-done.44 = bf16[2,3,256,256]{3,2,1,0:T(8,128)(2,1)} collective-permute-done((bf16[2,3,256,256]{3,2,1,0:T(8,128)(2,1)}, bf16[2,3,256,256]{3,2,1,0:T(8,128)(2,1)}, u32[]{:S(2)}, u32[]{:S(2)}) %collective-permute-start.44) | collective-permute-done | bytes 786464 | tf_op jit(solution)/shard_map/ppermute | solution.py:556
  540.0 14.3 %collective-permute-done.45 = bf16[2,3,256,256]{3,2,1,0:T(8,128)(2,1)} collective-permute-done((bf16[2,3,256,256]{3,2,1,0:T(8,128)(2,1)}, bf16[2,3,256,256]{3,2,1,0:T(8,128)(2,1)}, u32[]{:S(2)}, u32[]{:S(2)}) %collective-permute-start.45) | collective-permute-done | bytes 786464 | tf_op jit(solution)/shard_map/ppermute | solution.py:556
  555.5 2.4 collective-permute-start.53
  558.2 4.5 norm_back.3
  571.9 7.9 %collective-permute-done.54 = bf16[3,256,256]{2,1,0:T(8,128)(2,1)S(1)} collective-permute-done((bf16[3,256,256]{2,1,0:T(8,128)(2,1)S(1)}, bf16[3,256,256]{2,1,0:T(8,128)(2,1)S(1)}, u32[]{:S(2)}, u32[]{:S(2)}) %collective-permute-start.54) | collective-permute-done | bytes 393248 | tf_op jit(solution)/shard_map/ppermute | solution.py:556
  589.4 5.1 collective-permute-done.47.refs_2_
  596.6 3.3 convert_element_type.150
  603.9 21.7 %collective-permute-done.61 = bf16[512,256]{1,0:T(8,128)(2,1)S(1)} collective-permute-done((bf16[512,256]{1,0:T(8,128)(2,1)}, bf16[512,256]{1,0:T(8,128)(2,1)S(1)}, u32[]{:S(2)}, u32[]{:S(2)}) %collective-permute-start.61) | collective-permute-done | bytes 262176 | tf_op jit(solution)/shard_map/ppermute | solution.py:559
  632.0 5.2 convert_bitcast_fusion
  637.2 6.2 copy.27
  643.4 6.6 %lay_rows.7 = f32[4,256,2048]{2,1,0:T(8,128)} custom-call(s32[4]{0:T(128)} %pad_add_fusion.at_ref, bf16[256,2048]{1,0:T(8,128)(2,1)} %get-tuple-element.164.refs_0_, bf16[256,2048]{1,0:T(8,128)(2,1)} %collective-permute-done.51.refs_1_, bf16[256,2048]{1,0:T(8,128)(2,1)} %collective-permute-done.47.refs_2_, bf16[256,2048]{1,0:T(8,128)(2,1)} %collective-permute-done.52.refs_3_), custom_call_target="tpu_custom_call" | custom-call | bytes 83886 | tf_op jit(solution)/shard_map/lay_rows/pallas_call | solution.py:358
  650.1 5.3 lay_rows.6
  (314 shorter events, 118.0 us)
Async XLA Ops:
  7.2 203.6 %all-gather.5.cloned.1.call-start = ((), (), s32[]{:S(2)}) async-start(), calls=%async_computation.3 | async-start | bytes 7208960 | tf_op jit(solution)/shard_map/all_gather | solution.py:876
  12.4 35.3 %collective-permute-start = (bf16[4,528,256]{2,1,0:T(8,128)(2,1)}, bf16[4,528,256]{2,1,0:T(8,128)(2,1)}, u32[]{:S(2)}, u32[]{:S(2)}) collective-permute-start(bf16[4,528,256]{2,1,0:T(8,128)(2,1)} %fusion.11), channel_id=1, source_target_pairs={{0,8},{8,16},{16,24},{24,0},{1,9},{9,17},{17,25},{25,1},{2,10},{10... | collective-permute-start | bytes 3244040 | tf_op jit(solution)/shard_map/ppermute | solution.py:556
  15.4 48.8 %collective-permute-start.1 = (bf16[4,528,256]{2,1,0:T(8,128)(2,1)}, bf16[4,528,256]{2,1,0:T(8,128)(2,1)}, u32[]{:S(2)}, u32[]{:S(2)}) collective-permute-start(bf16[4,528,256]{2,1,0:T(8,128)(2,1)} %fusion.11), channel_id=1, source_target_pairs={{0,24},{8,0},{16,8},{24,16},{1,25},{9,1},{17,9},{25,17},{2,26},{10... | collective-permute-start | bytes 3244040 | tf_op jit(solution)/shard_map/ppermute | solution.py:556
  21.3 26.4 %collective-permute-start.2 = (bf16[256,2048]{1,0:T(8,128)(2,1)}, bf16[256,2048]{1,0:T(8,128)(2,1)}, u32[]{:S(2)}, u32[]{:S(2)}) collective-permute-start(bf16[256,2048]{1,0:T(8,128)(2,1)} %get-tuple-element.191.refs_4_), channel_id=1, source_target_pairs={{0,4},{4,0},{1,5},{5,1},{2,6},{6,2},{3,7},{7,3},{8,12},{12,8},{9,1... | collective-permute-start | bytes 3145736 | tf_op jit(solution)/shard_map/ppermute | solution.py:559
  24.9 50.4 %collective-permute-start.6 = (bf16[256,2048]{1,0:T(8,128)(2,1)}, bf16[256,2048]{1,0:T(8,128)(2,1)}, u32[]{:S(2)}, u32[]{:S(2)}) collective-permute-start(bf16[256,2048]{1,0:T(8,128)(2,1)} %get-tuple-element.188.refs_5_), channel_id=1, source_target_pairs={{0,4},{4,0},{1,5},{5,1},{2,6},{6,2},{3,7},{7,3},{8,12},{12,8},{9,1... | collective-permute-start | bytes 3145736 | tf_op jit(solution)/shard_map/ppermute | solution.py:559
  65.3 26.7 %collective-permute-start.4 = (bf16[2,528,256]{2,1,0:T(8,128)(2,1)S(1)}, bf16[2,528,256]{2,1,0:T(8,128)(2,1)}, u32[]{:S(2)}, u32[]{:S(2)}) collective-permute-start(bf16[2,528,256]{2,1,0:T(8,128)(2,1)S(1)} %slice.159), channel_id=1, source_target_pairs={{0,8},{8,16},{16,24},{24,0},{1,9},{9,17},{17,25},{25,1},{2,10},{10... | collective-permute-start | bytes 1622024 | tf_op jit(solution)/shard_map/ppermute | solution.py:556
  67.6 24.4 %collective-permute-start.5 = (bf16[2,512,256]{2,1,0:T(8,128)(2,1)S(1)}, bf16[2,512,256]{2,1,0:T(8,128)(2,1)S(1)}, u32[]{:S(2)}, u32[]{:S(2)}) collective-permute-start(bf16[2,512,256]{2,1,0:T(8,128)(2,1)S(1)} %slice.160), channel_id=1, source_target_pairs={{0,24},{8,0},{16,8},{24,16},{1,25},{9,1},{17,9},{25,17},{2,26},{10... | collective-permute-start | bytes 1572872 | tf_op jit(solution)/shard_map/ppermute | solution.py:556
  73.1 24.1 %collective-permute-start.7 = (bf16[256,2048]{1,0:T(8,128)(2,1)}, bf16[256,2048]{1,0:T(8,128)(2,1)S(1)}, u32[]{:S(2)}, u32[]{:S(2)}) collective-permute-start(bf16[256,2048]{1,0:T(8,128)(2,1)} %collective-permute-done.2.refs_2_), channel_id=1, source_target_pairs={{0,2},{1,3},{2,0},{3,1},{4,6},{5,7},{6,4},{7,5},{8,10},{9,11},{10,... | collective-permute-start | bytes 3145736 | tf_op jit(solution)/shard_map/ppermute | solution.py:561
  92.0 180.6 %all-gather.7.cloned.1.call-start = ((), (), s32[]{:S(2)}) async-start(), calls=%async_computation.4 | async-start | bytes 3604480 | tf_op jit(solution)/shard_map/all_gather | solution.py:877
  115.3 18.7 %collective-permute-start.8 = (bf16[4,2048,256]{2,1,0:T(8,128)(2,1)}, bf16[4,2048,256]{2,1,0:T(8,128)(2,1)S(1)}, u32[]{:S(2)}, u32[]{:S(2)}) collective-permute-start(bf16[4,2048,256]{2,1,0:T(8,128)(2,1)} %constant_dynamic-update-slice_fusion.refs_2_.refs_1_.refs_6_.refs_7_.refs_8_), channel_id=1, source_target_pairs={{0,1},{1,0},{2,3},{3,2},{4,5},{5,4},{6,7},{7,6},{8,9},{9,8},{10,11... | collective-permute-start | bytes 12582920 | tf_op jit(solution)/shard_map/ppermute | solution.py:564
  115.9 25.8 %collective-permute-start.9 = (bf16[256,2048]{1,0:T(8,128)(2,1)}, bf16[256,2048]{1,0:T(8,128)(2,1)S(1)}, u32[]{:S(2)}, u32[]{:S(2)}) collective-permute-start(bf16[256,2048]{1,0:T(8,128)(2,1)} %collective-permute-done.6.refs_2_), channel_id=1, source_target_pairs={{0,2},{1,3},{2,0},{3,1},{4,6},{5,7},{6,4},{7,5},{8,10},{9,11},{10,... | collective-permute-start | bytes 3145736 | tf_op jit(solution)/shard_map/ppermute | solution.py:561
  161.6 25.2 %collective-permute-start.10 = (bf16[2,256,1024]{2,1,0:T(8,128)(2,1)}, bf16[2,256,1024]{2,1,0:T(8,128)(2,1)S(1)}, u32[]{:S(2)}, u32[]{:S(2)}) collective-permute-start(bf16[2,256,1024]{2,1,0:T(8,128)(2,1)} %get-tuple-element.99.refs_4_), channel_id=1, source_target_pairs={{0,4},{4,0},{1,5},{5,1},{2,6},{6,2},{3,7},{7,3},{8,12},{12,8},{9,1... | collective-permute-start | bytes 3145736 | tf_op jit(solution)/shard_map/ppermute | solution.py:559
  163.2 24.8 %collective-permute-start.11 = (bf16[2,256,1024]{2,1,0:T(8,128)(2,1)}, bf16[2,256,1024]{2,1,0:T(8,128)(2,1)S(1)}, u32[]{:S(2)}, u32[]{:S(2)}) collective-permute-start(bf16[2,256,1024]{2,1,0:T(8,128)(2,1)} %get-tuple-element.101), channel_id=1, source_target_pairs={{0,2},{1,3},{2,0},{3,1},{4,6},{5,7},{6,4},{7,5},{8,10},{9,11},{10,... | collective-permute-start | bytes 3145736 | tf_op jit(solution)/shard_map/ppermute | solution.py:561
  164.7 29.9 %collective-permute-start.14 = (bf16[1024,256]{1,0:T(8,128)(2,1)S(1)}, bf16[1024,256]{1,0:T(8,128)(2,1)S(1)}, u32[]{:S(2)}, u32[]{:S(2)}) collective-permute-start(bf16[1024,256]{1,0:T(8,128)(2,1)S(1)} %bitcast.112), channel_id=1, source_target_pairs={{0,1},{1,0},{2,3},{3,2},{4,5},{5,4},{6,7},{7,6},{8,9},{9,8},{10,11... | collective-permute-start | bytes 1572872 | tf_op jit(solution)/shard_map/ppermute | solution.py:564
  192.5 12.8 %collective-permute-start.12 = (bf16[256,1024]{1,0:T(8,128)(2,1)}, bf16[256,1024]{1,0:T(8,128)(2,1)S(1)}, u32[]{:S(2)}, u32[]{:S(2)}) collective-permute-start(bf16[256,1024]{1,0:T(8,128)(2,1)} %get-tuple-element.103), channel_id=1, source_target_pairs={{0,2},{1,3},{2,0},{3,1},{4,6},{5,7},{6,4},{7,5},{8,10},{9,11},{10,... | collective-permute-start | bytes 1572872 | tf_op jit(solution)/shard_map/ppermute | solution.py:561
  194.0 12.5 %collective-permute-start.13 = (bf16[256,1024]{1,0:T(8,128)(2,1)}, bf16[256,1024]{1,0:T(8,128)(2,1)S(1)}, u32[]{:S(2)}, u32[]{:S(2)}) collective-permute-start(bf16[256,1024]{1,0:T(8,128)(2,1)} %get-tuple-element.105), channel_id=1, source_target_pairs={{0,4},{4,0},{1,5},{5,1},{2,6},{6,2},{3,7},{7,3},{8,12},{12,8},{9,1... | collective-permute-start | bytes 1572872 | tf_op jit(solution)/shard_map/ppermute | solution.py:559
  210.8 49.8 %collective-permute-start.21 = (bf16[2,704,2048]{2,1,0:T(8,128)(2,1)}, bf16[2,704,2048]{2,1,0:T(8,128)(2,1)}, u32[]{:S(2)}, u32[]{:S(2)}) collective-permute-start(bf16[2,704,2048]{2,1,0:T(8,128)(2,1)} %all-gather.5.cloned.1.call-done.weight_ref.refs_4_.refs_5_), channel_id=1, source_target_pairs={{0,1},{1,0},{2,3},{3,2},{4,5},{5,4},{6,7},{7,6},{8,9},{9,8},{10,11... | collective-permute-start | bytes 17301512 | tf_op jit(solution)/shard_map/ppermute | solution.py:564
  210.9 31.2 %collective-permute-start.20 = (bf16[1024,2048]{1,0:T(8,128)(2,1)}, bf16[1024,2048]{1,0:T(8,128)(2,1)}, u32[]{:S(2)}, u32[]{:S(2)}) collective-permute-start(bf16[1024,2048]{1,0:T(8,128)(2,1)} %bitcast.128), channel_id=1, source_target_pairs={{0,1},{1,0},{2,3},{3,2},{4,5},{5,4},{6,7},{7,6},{8,9},{9,8},{10,11... | collective-permute-start | bytes 12582920 | tf_op jit(solution)/shard_map/ppermute | solution.py:564
  211.4 43.3 %collective-permute-start.19 = (bf16[1024,2048]{1,0:T(8,128)(2,1)}, bf16[1024,2048]{1,0:T(8,128)(2,1)}, u32[]{:S(2)}, u32[]{:S(2)}) collective-permute-start(bf16[1024,2048]{1,0:T(8,128)(2,1)} %bitcast.116), channel_id=1, source_target_pairs={{0,1},{1,0},{2,3},{3,2},{4,5},{5,4},{6,7},{7,6},{8,9},{9,8},{10,11... | collective-permute-start | bytes 12582920 | tf_op jit(solution)/shard_map/ppermute | solution.py:564
  211.5 151.5 %reduce-scatter.4.cloned.1.call-start = ((), (), s32[]{:S(2)}) async-start(), calls=%async_computation.5 | async-start | bytes 3604480 | tf_op jit(solution)/shard_map/reduce_scatter | solution.py:916
  211.5 25.8 %collective-permute-start.16 = (bf16[256,2048]{1,0:T(8,128)(2,1)}, bf16[256,2048]{1,0:T(8,128)(2,1)S(1)}, u32[]{:S(2)}, u32[]{:S(2)}) collective-permute-start(bf16[256,2048]{1,0:T(8,128)(2,1)} %get-tuple-element.106.refs_0_), channel_id=1, source_target_pairs={{0,2},{1,3},{2,0},{3,1},{4,6},{5,7},{6,4},{7,5},{8,10},{9,11},{10,... | collective-permute-start | bytes 3145736 | tf_op jit(solution)/shard_map/ppermute | solution.py:561
  212.1 27.1 %collective-permute-start.15 = (bf16[256,2048]{1,0:T(8,128)(2,1)}, bf16[256,2048]{1,0:T(8,128)(2,1)S(1)}, u32[]{:S(2)}, u32[]{:S(2)}) collective-permute-start(bf16[256,2048]{1,0:T(8,128)(2,1)} %get-tuple-element.106.refs_0_), channel_id=1, source_target_pairs={{0,4},{4,0},{1,5},{5,1},{2,6},{6,2},{3,7},{7,3},{8,12},{12,8},{9,1... | collective-permute-start | bytes 3145736 | tf_op jit(solution)/shard_map/ppermute | solution.py:559
  238.2 13.8 %collective-permute-start.17 = (bf16[256,1024]{1,0:T(8,128)(2,1)}, bf16[256,1024]{1,0:T(8,128)(2,1)S(1)}, u32[]{:S(2)}, u32[]{:S(2)}) collective-permute-start(bf16[256,1024]{1,0:T(8,128)(2,1)} %slice.215), channel_id=1, source_target_pairs={{0,4},{4,0},{1,5},{5,1},{2,6},{6,2},{3,7},{7,3},{8,12},{12,8},{9,1... | collective-permute-start | bytes 1572872 | tf_op jit(solution)/shard_map/ppermute | solution.py:559
  241.0 13.6 %collective-permute-start.18 = (bf16[256,1024]{1,0:T(8,128)(2,1)}, bf16[256,1024]{1,0:T(8,128)(2,1)}, u32[]{:S(2)}, u32[]{:S(2)}) collective-permute-start(bf16[256,1024]{1,0:T(8,128)(2,1)} %slice.216), channel_id=1, source_target_pairs={{0,2},{1,3},{2,0},{3,1},{4,6},{5,7},{6,4},{7,5},{8,10},{9,11},{10,... | collective-permute-start | bytes 1572872 | tf_op jit(solution)/shard_map/ppermute | solution.py:561
  272.6 12.5 %collective-permute-start.23 = (bf16[704,1024]{1,0:T(8,128)(2,1)}, bf16[704,1024]{1,0:T(8,128)(2,1)S(1)}, u32[]{:S(2)}, u32[]{:S(2)}) collective-permute-start(bf16[704,1024]{1,0:T(8,128)(2,1)} %get-tuple-element.112), channel_id=1, source_target_pairs={{0,1},{1,0},{2,3},{3,2},{4,5},{5,4},{6,7},{7,6},{8,9},{9,8},{10,11... | collective-permute-start | bytes 4325384 | tf_op jit(solution)/shard_map/ppermute | solution.py:564
  272.6 24.0 %collective-permute-start.22 = (bf16[704,2048]{1,0:T(8,128)(2,1)}, bf16[704,2048]{1,0:T(8,128)(2,1)}, u32[]{:S(2)}, u32[]{:S(2)}) collective-permute-start(bf16[704,2048]{1,0:T(8,128)(2,1)} %all-gather.7.cloned.1.call-done.weight_ref.refs_2_), channel_id=1, source_target_pairs={{0,1},{1,0},{2,3},{3,2},{4,5},{5,4},{6,7},{7,6},{8,9},{9,8},{10,11... | collective-permute-start | bytes 8650760 | tf_op jit(solution)/shard_map/ppermute | solution.py:564
  296.5 204.3 %reduce-scatter.6.cloned.1.call-start = ((), (), s32[]{:S(2)}) async-start(), calls=%async_computation.6 | async-start | bytes 7208960 | tf_op jit(solution)/shard_map/reduce_scatter | solution.py:939
  296.5 18.2 %collective-permute-start.24 = (bf16[1024,2048]{1,0:T(8,128)(2,1)}, bf16[1024,2048]{1,0:T(8,128)(2,1)S(1)}, u32[]{:S(2)}, u32[]{:S(2)}) collective-permute-start(bf16[1024,2048]{1,0:T(8,128)(2,1)} %bitcast.122), channel_id=1, source_target_pairs={{0,1},{1,0},{2,3},{3,2},{4,5},{5,4},{6,7},{7,6},{8,9},{9,8},{10,11... | collective-permute-start | bytes 12582920 | tf_op jit(solution)/shard_map/ppermute | solution.py:564
  305.5 9.2 %collective-permute-start.25 = (bf16[2,704,1024]{2,1,0:T(8,128)(2,1)}, bf16[2,704,1024]{2,1,0:T(8,128)(2,1)}, u32[]{:S(2)}, u32[]{:S(2)}) collective-permute-start(bf16[2,704,1024]{2,1,0:T(8,128)(2,1)} %get-tuple-element.119), channel_id=1, source_target_pairs={{0,1},{1,0},{2,3},{3,2},{4,5},{5,4},{6,7},{7,6},{8,9},{9,8},{10,11... | collective-permute-start | bytes 8650760 | tf_op jit(solution)/shard_map/ppermute | solution.py:564
  337.0 25.3 %collective-permute-start.26 = (bf16[2,256,1024]{2,1,0:T(8,128)(2,1)}, bf16[2,256,1024]{2,1,0:T(8,128)(2,1)S(1)}, u32[]{:S(2)}, u32[]{:S(2)}) collective-permute-start(bf16[2,256,1024]{2,1,0:T(8,128)(2,1)} %get-tuple-element.121.refs_4_), channel_id=1, source_target_pairs={{0,4},{4,0},{1,5},{5,1},{2,6},{6,2},{3,7},{7,3},{8,12},{12,8},{9,1... | collective-permute-start | bytes 3145736 | tf_op jit(solution)/shard_map/ppermute | solution.py:559
  337.8 25.2 %collective-permute-start.27 = (bf16[2,256,1024]{2,1,0:T(8,128)(2,1)}, bf16[2,256,1024]{2,1,0:T(8,128)(2,1)}, u32[]{:S(2)}, u32[]{:S(2)}) collective-permute-start(bf16[2,256,1024]{2,1,0:T(8,128)(2,1)} %get-tuple-element.123), channel_id=1, source_target_pairs={{0,2},{1,3},{2,0},{3,1},{4,6},{5,7},{6,4},{7,5},{8,10},{9,11},{10,... | collective-permute-start | bytes 3145736 | tf_op jit(solution)/shard_map/ppermute | solution.py:561
  366.8 229.9 %all-gather.11.cloned.1.call-start = ((), (), s32[]{:S(2)}) async-start(), calls=%async_computation.9 | async-start | bytes 2162688 | tf_op jit(solution)/shard_map/all_gather | solution.py:953
  367.8 13.7 %collective-permute-start.28 = (bf16[256,1024]{1,0:T(8,128)(2,1)S(1)}, bf16[256,1024]{1,0:T(8,128)(2,1)S(1)}, u32[]{:S(2)}, u32[]{:S(2)}) collective-permute-start(bf16[256,1024]{1,0:T(8,128)(2,1)S(1)} %copy-done.59), channel_id=1, source_target_pairs={{0,2},{1,3},{2,0},{3,1},{4,6},{5,7},{6,4},{7,5},{8,10},{9,11},{10,... | collective-permute-start | bytes 1572872 | tf_op jit(solution)/shard_map/ppermute | solution.py:561
  368.0 13.4 %collective-permute-start.29 = (bf16[256,1024]{1,0:T(8,128)(2,1)S(1)}, bf16[256,1024]{1,0:T(8,128)(2,1)S(1)}, u32[]{:S(2)}, u32[]{:S(2)}) collective-permute-start(bf16[256,1024]{1,0:T(8,128)(2,1)S(1)} %copy-done.58), channel_id=1, source_target_pairs={{0,4},{4,0},{1,5},{5,1},{2,6},{6,2},{3,7},{7,3},{8,12},{12,8},{9,1... | collective-permute-start | bytes 1572872 | tf_op jit(solution)/shard_map/ppermute | solution.py:559
  387.3 24.7 %collective-permute-start.31 = (bf16[256,2048]{1,0:T(8,128)(2,1)}, bf16[256,2048]{1,0:T(8,128)(2,1)S(1)}, u32[]{:S(2)}, u32[]{:S(2)}) collective-permute-start(bf16[256,2048]{1,0:T(8,128)(2,1)} %get-tuple-element.132.refs_0_), channel_id=1, source_target_pairs={{0,2},{1,3},{2,0},{3,1},{4,6},{5,7},{6,4},{7,5},{8,10},{9,11},{10,... | collective-permute-start | bytes 3145736 | tf_op jit(solution)/shard_map/ppermute | solution.py:561
  389.1 24.1 %collective-permute-start.30 = (bf16[256,2048]{1,0:T(8,128)(2,1)}, bf16[256,2048]{1,0:T(8,128)(2,1)S(1)}, u32[]{:S(2)}, u32[]{:S(2)}) collective-permute-start(bf16[256,2048]{1,0:T(8,128)(2,1)} %get-tuple-element.132.refs_0_), channel_id=1, source_target_pairs={{0,4},{4,0},{1,5},{5,1},{2,6},{6,2},{3,7},{7,3},{8,12},{12,8},{9,1... | collective-permute-start | bytes 3145736 | tf_op jit(solution)/shard_map/ppermute | solution.py:559
  412.1 12.5 %collective-permute-start.32 = (bf16[256,1024]{1,0:T(8,128)(2,1)S(1)}, bf16[256,1024]{1,0:T(8,128)(2,1)S(1)}, u32[]{:S(2)}, u32[]{:S(2)}) collective-permute-start(bf16[256,1024]{1,0:T(8,128)(2,1)S(1)} %slice.217), channel_id=1, source_target_pairs={{0,4},{4,0},{1,5},{5,1},{2,6},{6,2},{3,7},{7,3},{8,12},{12,8},{9,1... | collective-permute-start | bytes 1572872 | tf_op jit(solution)/shard_map/ppermute | solution.py:559
  413.3 12.0 %collective-permute-start.33 = (bf16[256,1024]{1,0:T(8,128)(2,1)S(1)}, bf16[256,1024]{1,0:T(8,128)(2,1)S(1)}, u32[]{:S(2)}, u32[]{:S(2)}) collective-permute-start(bf16[256,1024]{1,0:T(8,128)(2,1)S(1)} %slice.218), channel_id=1, source_target_pairs={{0,2},{1,3},{2,0},{3,1},{4,6},{5,7},{6,4},{7,5},{8,10},{9,11},{10,... | collective-permute-start | bytes 1572872 | tf_op jit(solution)/shard_map/ppermute | solution.py:561
  431.5 19.5 %collective-permute-start.36 = (bf16[1024,2048]{1,0:T(8,128)(2,1)}, bf16[1024,2048]{1,0:T(8,128)(2,1)}, u32[]{:S(2)}, u32[]{:S(2)}) collective-permute-start(bf16[1024,2048]{1,0:T(8,128)(2,1)} %bitcast.124), channel_id=1, source_target_pairs={{0,1},{1,0},{2,3},{3,2},{4,5},{5,4},{6,7},{7,6},{8,9},{9,8},{10,11... | collective-permute-start | bytes 12582920 | tf_op jit(solution)/shard_map/ppermute | solution.py:564
  431.5 169.8 %reduce-scatter.8.cloned.1.call-start = ((), (), s32[]{:S(2)}) async-start(), calls=%async_computation.7 | async-start | bytes 1310720 | tf_op jit(solution)/shard_map/reduce_scatter | solution.py:974
  431.6 27.1 %collective-permute-start.34 = (bf16[2,256,1024]{2,1,0:T(8,128)(2,1)}, bf16[2,256,1024]{2,1,0:T(8,128)(2,1)}, u32[]{:S(2)}, u32[]{:S(2)}) collective-permute-start(bf16[2,256,1024]{2,1,0:T(8,128)(2,1)} %get-tuple-element.133.refs_7_), channel_id=1, source_target_pairs={{0,4},{4,0},{1,5},{5,1},{2,6},{6,2},{3,7},{7,3},{8,12},{12,8},{9,1... | collective-permute-start | bytes 3145736 | tf_op jit(solution)/shard_map/ppermute | solution.py:559
  432.7 26.0 %collective-permute-start.35 = (bf16[2,256,1024]{2,1,0:T(8,128)(2,1)}, bf16[2,256,1024]{2,1,0:T(8,128)(2,1)}, u32[]{:S(2)}, u32[]{:S(2)}) collective-permute-start(bf16[2,256,1024]{2,1,0:T(8,128)(2,1)} %get-tuple-element.135), channel_id=1, source_target_pairs={{0,2},{1,3},{2,0},{3,1},{4,6},{5,7},{6,4},{7,5},{8,10},{9,11},{10,... | collective-permute-start | bytes 3145736 | tf_op jit(solution)/shard_map/ppermute | solution.py:561
  451.0 49.8 %collective-permute-start.41 = (bf16[3,1024,256]{2,1,0:T(8,128)(2,1)S(1)}, bf16[3,1024,256]{2,1,0:T(8,128)(2,1)S(1)}, u32[]{:S(2)}, u32[]{:S(2)}) collective-permute-start(bf16[3,1024,256]{2,1,0:T(8,128)(2,1)S(1)} %bitcast.104), channel_id=1, source_target_pairs={{0,1},{1,0},{2,3},{3,2},{4,5},{5,4},{6,7},{7,6},{8,9},{9,8},{10,11... | collective-permute-start | bytes 4718600 | tf_op jit(solution)/shard_map/ppermute | solution.py:564
  462.2 20.5 %collective-permute-start.37 = (bf16[256,1024]{1,0:T(8,128)(2,1)}, bf16[256,1024]{1,0:T(8,128)(2,1)}, u32[]{:S(2)}, u32[]{:S(2)}) collective-permute-start(bf16[256,1024]{1,0:T(8,128)(2,1)} %get-tuple-element.141), channel_id=1, source_target_pairs={{0,2},{1,3},{2,0},{3,1},{4,6},{5,7},{6,4},{7,5},{8,10},{9,11},{10,... | collective-permute-start | bytes 1572872 | tf_op jit(solution)/shard_map/ppermute | solution.py:561
  463.0 19.7 %collective-permute-start.38 = (bf16[256,1024]{1,0:T(8,128)(2,1)}, bf16[256,1024]{1,0:T(8,128)(2,1)}, u32[]{:S(2)}, u32[]{:S(2)}) collective-permute-start(bf16[256,1024]{1,0:T(8,128)(2,1)} %get-tuple-element.143), channel_id=1, source_target_pairs={{0,4},{4,0},{1,5},{5,1},{2,6},{6,2},{3,7},{7,3},{8,12},{12,8},{9,1... | collective-permute-start | bytes 1572872 | tf_op jit(solution)/shard_map/ppermute | solution.py:559
  464.1 167.9 %all-gather.9.cloned.1.call-start = ((), (), s32[]{:S(2)}) async-start(), calls=%async_computation.8 | async-start | bytes 4325376 | tf_op jit(solution)/shard_map/all_gather | solution.py:998
  498.5 24.8 %collective-permute-start.39 = (bf16[2,256,1024]{2,1,0:T(8,128)(2,1)}, bf16[2,256,1024]{2,1,0:T(8,128)(2,1)}, u32[]{:S(2)}, u32[]{:S(2)}) collective-permute-start(bf16[2,256,1024]{2,1,0:T(8,128)(2,1)} %get-tuple-element.149.refs_0_), channel_id=1, source_target_pairs={{0,4},{4,0},{1,5},{5,1},{2,6},{6,2},{3,7},{7,3},{8,12},{12,8},{9,1... | collective-permute-start | bytes 3145736 | tf_op jit(solution)/shard_map/ppermute | solution.py:559
  499.6 24.4 %collective-permute-start.40 = (bf16[2,256,1024]{2,1,0:T(8,128)(2,1)}, bf16[2,256,1024]{2,1,0:T(8,128)(2,1)}, u32[]{:S(2)}, u32[]{:S(2)}) collective-permute-start(bf16[2,256,1024]{2,1,0:T(8,128)(2,1)} %get-tuple-element.151), channel_id=1, source_target_pairs={{0,2},{1,3},{2,0},{3,1},{4,6},{5,7},{6,4},{7,5},{8,10},{9,11},{10,... | collective-permute-start | bytes 3145736 | tf_op jit(solution)/shard_map/ppermute | solution.py:561
  515.2 24.8 %collective-permute-start.44 = (bf16[2,3,256,256]{3,2,1,0:T(8,128)(2,1)}, bf16[2,3,256,256]{3,2,1,0:T(8,128)(2,1)}, u32[]{:S(2)}, u32[]{:S(2)}) collective-permute-start(bf16[2,3,256,256]{3,2,1,0:T(8,128)(2,1)} %pad_maximum_fusion), channel_id=1, source_target_pairs={{0,8},{8,16},{16,24},{24,0},{1,9},{9,17},{17,25},{25,1},{2,10},{10... | collective-permute-start | bytes 2359304 | tf_op jit(solution)/shard_map/ppermute | solution.py:556
  516.2 38.2 %collective-permute-start.45 = (bf16[2,3,256,256]{3,2,1,0:T(8,128)(2,1)}, bf16[2,3,256,256]{3,2,1,0:T(8,128)(2,1)}, u32[]{:S(2)}, u32[]{:S(2)}) collective-permute-start(bf16[2,3,256,256]{3,2,1,0:T(8,128)(2,1)} %pad_maximum_fusion.1), channel_id=1, source_target_pairs={{0,24},{8,0},{16,8},{24,16},{1,25},{9,1},{17,9},{25,17},{2,26},{10... | collective-permute-start | bytes 2359304 | tf_op jit(solution)/shard_map/ppermute | solution.py:556
  527.6 30.6 %collective-permute-start.42 = (bf16[256,1024]{1,0:T(8,128)(2,1)}, bf16[256,1024]{1,0:T(8,128)(2,1)}, u32[]{:S(2)}, u32[]{:S(2)}) collective-permute-start(bf16[256,1024]{1,0:T(8,128)(2,1)} %get-tuple-element.154), channel_id=1, source_target_pairs={{0,2},{1,3},{2,0},{3,1},{4,6},{5,7},{6,4},{7,5},{8,10},{9,11},{10,... | collective-permute-start | bytes 1572872 | tf_op jit(solution)/shard_map/ppermute | solution.py:561
  528.8 29.4 %collective-permute-start.43 = (bf16[256,1024]{1,0:T(8,128)(2,1)}, bf16[256,1024]{1,0:T(8,128)(2,1)}, u32[]{:S(2)}, u32[]{:S(2)}) collective-permute-start(bf16[256,1024]{1,0:T(8,128)(2,1)} %get-tuple-element.156), channel_id=1, source_target_pairs={{0,4},{4,0},{1,5},{5,1},{2,6},{6,2},{3,7},{7,3},{8,12},{12,8},{9,1... | collective-permute-start | bytes 1572872 | tf_op jit(solution)/shard_map/ppermute | solution.py:559
  555.5 11.0 %collective-permute-start.53 = (bf16[3,256,256]{2,1,0:T(8,128)(2,1)S(1)}, bf16[3,256,256]{2,1,0:T(8,128)(2,1)}, u32[]{:S(2)}, u32[]{:S(2)}) collective-permute-start(bf16[3,256,256]{2,1,0:T(8,128)(2,1)S(1)} %fusion.17.refs_8_), channel_id=1, source_target_pairs={{0,24},{8,0},{16,8},{24,16},{1,25},{9,1},{17,9},{25,17},{2,26},{10... | collective-permute-start | bytes 1179656 | tf_op jit(solution)/shard_map/ppermute | solution.py:556
  563.5 6.0 collective-permute-start.46
  568.0 11.8 %collective-permute-start.54 = (bf16[3,256,256]{2,1,0:T(8,128)(2,1)S(1)}, bf16[3,256,256]{2,1,0:T(8,128)(2,1)S(1)}, u32[]{:S(2)}, u32[]{:S(2)}) collective-permute-start(bf16[3,256,256]{2,1,0:T(8,128)(2,1)S(1)} %get-tuple-element.193), channel_id=1, source_target_pairs={{0,8},{8,16},{16,24},{24,0},{1,9},{9,17},{17,25},{25,1},{2,10},{10... | collective-permute-start | bytes 1179656 | tf_op jit(solution)/shard_map/ppermute | solution.py:556
  570.3 24.2 %collective-permute-start.47 = (bf16[256,2048]{1,0:T(8,128)(2,1)}, bf16[256,2048]{1,0:T(8,128)(2,1)}, u32[]{:S(2)}, u32[]{:S(2)}) collective-permute-start(bf16[256,2048]{1,0:T(8,128)(2,1)} %get-tuple-element.164.refs_0_), channel_id=1, source_target_pairs={{0,2},{1,3},{2,0},{3,1},{4,6},{5,7},{6,4},{7,5},{8,10},{9,11},{10,... | collective-permute-start | bytes 3145736 | tf_op jit(solution)/shard_map/ppermute | solution.py:561
  587.7 14.4 %collective-permute-start.59 = (f32[4,768]{1,0:T(4,128)S(1)}, f32[4,768]{1,0:T(4,128)S(1)}, u32[]{:S(2)}, u32[]{:S(2)}) collective-permute-start(f32[4,768]{1,0:T(4,128)S(1)} %reduce_sum.29), channel_id=1, source_target_pairs={{0,4},{4,0},{1,5},{5,1},{2,6},{6,2},{3,7},{7,3},{8,12},{12,8},{9,1... | collective-permute-start | bytes 36872 | tf_op jit(solution)/shard_map/ppermute | solution.py:559
  594.4 34.1 %collective-permute-start.49 = (bf16[256,2048]{1,0:T(8,128)(2,1)}, bf16[256,2048]{1,0:T(8,128)(2,1)}, u32[]{:S(2)}, u32[]{:S(2)}) collective-permute-start(bf16[256,2048]{1,0:T(8,128)(2,1)} %add_low.1.refs_12_.refs_0_), channel_id=1, source_target_pairs={{0,2},{1,3},{2,0},{3,1},{4,6},{5,7},{6,4},{7,5},{8,10},{9,11},{10,... | collective-permute-start | bytes 3145736 | tf_op jit(solution)/shard_map/ppermute | solution.py:561
  600.0 43.4 %collective-permute-start.51 = (bf16[256,2048]{1,0:T(8,128)(2,1)}, bf16[256,2048]{1,0:T(8,128)(2,1)}, u32[]{:S(2)}, u32[]{:S(2)}) collective-permute-start(bf16[256,2048]{1,0:T(8,128)(2,1)} %get-tuple-element.164.refs_0_), channel_id=1, source_target_pairs={{0,1},{1,0},{2,3},{3,2},{4,5},{5,4},{6,7},{7,6},{8,9},{9,8},{10,11... | collective-permute-start | bytes 3145736 | tf_op jit(solution)/shard_map/ppermute | solution.py:564
  600.0 28.5 %collective-permute-start.60 = (bf16[3,512,256]{2,1,0:T(8,128)(2,1)S(1)}, bf16[3,512,256]{2,1,0:T(8,128)(2,1)}, u32[]{:S(2)}, u32[]{:S(2)}) collective-permute-start(bf16[3,512,256]{2,1,0:T(8,128)(2,1)S(1)} %pad_maximum_fusion.2), channel_id=1, source_target_pairs={{0,4},{4,0},{1,5},{5,1},{2,6},{6,2},{3,7},{7,3},{8,12},{12,8},{9,1... | collective-permute-start | bytes 2359304 | tf_op jit(solution)/shard_map/ppermute | solution.py:559
  601.4 24.2 %collective-permute-start.61 = (bf16[512,256]{1,0:T(8,128)(2,1)}, bf16[512,256]{1,0:T(8,128)(2,1)S(1)}, u32[]{:S(2)}, u32[]{:S(2)}) collective-permute-start(bf16[512,256]{1,0:T(8,128)(2,1)} %reduce-scatter.8.cloned.1.call-done), channel_id=1, source_target_pairs={{0,4},{4,0},{1,5},{5,1},{2,6},{6,2},{3,7},{7,3},{8,12},{12,8},{9,1... | collective-permute-start | bytes 786440 | tf_op jit(solution)/shard_map/ppermute | solution.py:559
  628.0 22.1 %collective-permute-start.48 = (bf16[256,2048]{1,0:T(8,128)(2,1)}, bf16[256,2048]{1,0:T(8,128)(2,1)}, u32[]{:S(2)}, u32[]{:S(2)}) collective-permute-start(bf16[256,2048]{1,0:T(8,128)(2,1)} %add_low.1.refs_12_.refs_0_), channel_id=1, source_target_pairs={{0,1},{1,0},{2,3},{3,2},{4,5},{5,4},{6,7},{7,6},{8,9},{9,8},{10,11... | collective-permute-start | bytes 3145736 | tf_op jit(solution)/shard_map/ppermute | solution.py:564
  628.0 15.4 %collective-permute-start.52 = (bf16[256,2048]{1,0:T(8,128)(2,1)}, bf16[256,2048]{1,0:T(8,128)(2,1)}, u32[]{:S(2)}, u32[]{:S(2)}) collective-permute-start(bf16[256,2048]{1,0:T(8,128)(2,1)} %collective-permute-done.47.refs_2_), channel_id=1, source_target_pairs={{0,1},{1,0},{2,3},{3,2},{4,5},{5,4},{6,7},{7,6},{8,9},{9,8},{10,11... | collective-permute-start | bytes 3145736 | tf_op jit(solution)/shard_map/ppermute | solution.py:564
  628.5 21.6 %collective-permute-start.50 = (bf16[256,2048]{1,0:T(8,128)(2,1)}, bf16[256,2048]{1,0:T(8,128)(2,1)}, u32[]{:S(2)}, u32[]{:S(2)}) collective-permute-start(bf16[256,2048]{1,0:T(8,128)(2,1)} %collective-permute-done.49.refs_2_), channel_id=1, source_target_pairs={{0,1},{1,0},{2,3},{3,2},{4,5},{5,4},{6,7},{7,6},{8,9},{9,8},{10,11... | collective-permute-start | bytes 3145736 | tf_op jit(solution)/shard_map/ppermute | solution.py:564
  (65 other events, 374.0 us)
Sparse Core Ops, SparseCore 0:
  92.2 106.0 all-gather.4
  211.6 55.9 all-gather.6
  296.6 53.0 reduce-scatter.3
  366.9 98.9 reduce-scatter.5
  467.3 26.2 all-gather.10
  495.7 29.4 reduce-scatter.7
  558.3 41.2 all-gather.8

commit v4 on v3

--- a/solution.py
+++ b/solution.py
@@ -672,14 +672,22 @@
     return jnp.concatenate([first, second], axis=-1).reshape(-1, feat)
 
 
-def whole_rows(place, value, seqs, dtype, behind=()):
-    feat = value.shape[-1]
-    if place.square(seqs):
-        over_y, over_core = place.shift(value, "y", 1), place.swap(value)
-        whole = lay_rows(place.core, place.y, value, over_core, over_y, [place.swap(over_y)], dtype, behind)
-        return whole.reshape(2, -1, feat), over_y
-    value = gather_stage(place, value.reshape(seqs, -1, feat), 1, "y")
-    return ordered(place.core, value, place.swap(value), 0).astype(dtype), value
+class WholeRows:
+    def __init__(self, place, value, seqs):
+        self.place, self.value, self.seqs = place, value, seqs
+        if place.square(seqs):
+            self.over_y, self.over_core = place.shift(value, "y", 1), place.swap(value)
+        else:
+            self.over_y = gather_stage(place, value.reshape(seqs, -1, value.shape[-1]), 1, "y")
+            self.over_core = place.swap(self.over_y)
+
+    def whole(self, dtype, ready=(), behind=()):
+        place, value = self.place, self.value
+        if not place.square(self.seqs):
+            return ordered(place.core, self.over_y, self.over_core, 0).astype(dtype)
+        far = [place.swap(after(self.over_y, *ready) if ready else self.over_y)]
+        whole = lay_rows(place.core, place.y, value, self.over_core, self.over_y, far, dtype, behind)
+        return whole.reshape(2, -1, value.shape[-1])
 
 
 def other_rows(place, value):
@@ -950,7 +958,7 @@
         two_sum.shares, middle, gains[1], top_rows, [F32, LOW], behind=[down_sums.sent]
     )
     grad_mid_low = spread_rows(place, mid_low, seqs)
-    down_whole = lax.all_gather(after(down_sum, grad_mid_low), "context", axis=0, tiled=True)
+    down_gathered = Gathered(place, after(down_sum, grad_mid_low), 0)
     down_sums.start(grad_mid_low)
 
     def attend_grad(kept, weight, behind):
@@ -979,7 +987,7 @@
         + [(grad_mixed_other, (c,), w_attn_other, (c,)) for c in range(3)],
         seqs,
         "grad_one",
-        behind=[final_out],
+        behind=[final_out, down_gathered.raw],
     ).start()
     grad_qkv = qkv_back(
         normed, theirs_one, grad_mixed, theirs_mixed, behind=[one_sum.sent, gate_up_sum]
@@ -987,28 +995,27 @@
     qkv_shards = Shards(place, grad_qkv, 1, 1, grad_mixed)
     one_next = one_sum.follow([grad_qkv])
     qkv_next = qkv_shards.follow(one_next)
+    layer_rows = WholeRows(place, after(final_out, one_sum.shares[1], one_sum.shares[3]), seqs)
     input_low, sums_one = norm_back(
-        one_sum.shares,
-        inputs,
-        gains[0],
-        grad_middle,
-        [LOW],
-        behind=[one_next, qkv_next],
-    )
-    gate_up_whole = lax.all_gather(gate_up_sum, "context", axis=1, tiled=True)
-    sums = total_over(place, jnp.concatenate([sums_one, sums_two]), "y")
-    input_grad, over_y = whole_rows(place, after(input_low, sums), seqs, F32)
+        one_sum.shares, inputs, gains[0], grad_middle, [LOW], behind=[one_next, qkv_next]
+    )
+    gate_up_out = lax.all_gather(gate_up_sum, "context", axis=1, tiled=True)
+    gate_up_out = gate_up_out.transpose(0, 2, 1).astype(F32)
+    sums = after(jnp.concatenate([sums_one, sums_two]), layer_rows.over_y)
+    sums = total_over(place, sums, "y")
+    input_rows = WholeRows(place, after(input_low, sums), seqs)
     totals = small_totals(
         place,
-        after(sums, qkv_shards.low, qkv_shards.high),
+        after(sums, qkv_shards.low, qkv_shards.high, gate_up_out),
         jnp.sum(grad_mixed.astype(F32), axis=1),
         jnp.sum(grad_mixed_other.astype(F32), axis=1),
     )
     qkv_sum = qkv_shards.total()
     qkv_gathered = Gathered(place, qkv_sum, 2)
     out_gathered = Gathered(place, after(out_sum, qkv_sum), 1)
-    layer_out, _ = whole_rows(place, after(final_out, over_y), seqs, LOW)
     sums, grad_bias = last_totals(place, after(totals, qkv_sum), norm_gains.shape[1])
+    layer_out = layer_rows.whole(LOW)
+    input_grad = input_rows.whole(F32, [qkv_gathered.raw])
 
     return (
         layer_out,
@@ -1018,8 +1025,8 @@
         qkv_gathered.whole().astype(F32),
         grad_bias,
         out_gathered.whole().T.astype(F32),
-        gate_up_whole.transpose(0, 2, 1).astype(F32),
-        down_whole.astype(F32),
+        gate_up_out,
+        down_gathered.whole().astype(F32),
     )
 
 

time: 668 us -> 648 us (0.970)
  waiting for transfers between devices: 230 us -> 216 us
    ppermute x11, waiting for transfers between devices: 69 us -> 60.7 us  [shift(): return lax.ppermute(value, 'fsdp', [(i, (i + step) % n) for i in range(n)])]
    ppermute x17 -> x18, waiting for transfers between devices: 87.6 us -> 82 us  [shift(): lax.ppermute(value, 'context', [(i, (i + step) % n) for i in range(n)])]
    ppermute x17 -> x18, starting transfers between devices: 17.6 us -> 18.2 us  [shift(): lax.ppermute(value, 'context', [(i, (i + step) % n) for i in range(n)])]
    unnamed x124 -> x128, local copies, waits for them, and re-layouts: 30.4 us -> 30.2 us
  transfers between devices with their start and end apart: 69 -> 69, of which waited for: 28 -> 30; matrix products, arithmetic and copies ran while one was open for 11% -> 11% of each run, Pallas kernels for 38% -> 39%
where the time goes in v4:
time: 648 us; the launch traced here: 643 us
  Pallas kernels  258 us (40%)
  waiting for transfers between devices  216 us (33%)
  local copies, waits for them, and re-layouts  56.9 us (9%)
  starting transfers between devices  56.6 us (9%)
  other arithmetic  27.3 us (4%)
  between operations  15.5 us (2%)
  matrix products  12.2 us (2%)
    ppermute x18, waiting for transfers between devices, shift(): lax.ppermute(value, 'context', [(i, (i + step) % n) for i in range(n)])  82 us
    ppermute x17, waiting for transfers between devices, shift(): lax.ppermute(value, 'tensor', [(i, (i + 2 * step) % n) for i in range(n)])  73.5 us
    ppermute x11, waiting for transfers between devices, shift(): return lax.ppermute(value, 'fsdp', [(i, (i + step) % n) for i in range(n)])  60.7 us
    pallas_call x4, Pallas kernels, products_apart(): pl.pallas_call(kernel, grid_spec=pltpu.PrefetchScalarGridSpec(num_scalar_...  52.6 us
    pallas_call x5, Pallas kernels, products(): pl.pallas_call(kernel, grid=(many, rows // tm, cols // tn), in_specs=ones...  44.2 us
    pallas_call x6, Pallas kernels, pieces_of(): pl.pallas_call(kernel, grid_spec=pltpu.PrefetchScalarGridSpec(num_scalar_...  36.2 us
    unnamed x128, local copies, waits for them, and re-layouts  30.2 us
    pallas_call x2, Pallas kernels, gate_up(): pl.pallas_call(gate_kernel, grid=(rows // tm,), in_specs=[pl.BlockSpec((2...  23.9 us
  transfers between devices with their start and end apart: 69, of which 30 were waited for; matrix products, arithmetic and copies ran while one was open for 11% of the time, Pallas kernels for 39%

profile of v4, /device:TPU:0, one launch (start us, length us, event | category | flops | bytes accessed | tf_op | source)
XLA Modules:
  0.0 643.2 jit_solution(11387842594704849247)
XLA Ops:
  12.4 3.0 collective-permute-start
  17.5 3.8 dynamic-slice_bitcast_fusion.2
  27.2 2.6 copy.32
  29.9 17.8 %collective-permute-done.2.refs_2_ = bf16[256,2048]{1,0:T(8,128)(2,1)} collective-permute-done((bf16[256,2048]{1,0:T(8,128)(2,1)}, bf16[256,2048]{1,0:T(8,128)(2,1)}, u32[]{:S(2)}, u32[]{:S(2)}) %collective-permute-start.2) | collective-permute-done | bytes 1048608 | tf_op jit(solution)/shard_map/ppermute | solution.py:559
  47.7 16.5 %collective-permute-done.1 = bf16[4,528,256]{2,1,0:T(8,128)(2,1)} collective-permute-done((bf16[4,528,256]{2,1,0:T(8,128)(2,1)}, bf16[4,528,256]{2,1,0:T(8,128)(2,1)}, u32[]{:S(2)}, u32[]{:S(2)}) %collective-permute-start.1) | collective-permute-done | bytes 1081376 | tf_op jit(solution)/shard_map/ppermute | solution.py:556
  67.6 2.8 collective-permute-start.5
  75.3 16.7 %collective-permute-done.5 = bf16[2,512,256]{2,1,0:T(8,128)(2,1)S(1)} collective-permute-done((bf16[2,512,256]{2,1,0:T(8,128)(2,1)S(1)}, bf16[2,512,256]{2,1,0:T(8,128)(2,1)S(1)}, u32[]{:S(2)}, u32[]{:S(2)}) %collective-permute-start.5) | collective-permute-done | bytes 524320 | tf_op jit(solution)/shard_map/ppermute | solution.py:556
  93.7 3.5 collective-permute-done.7.refs_0_.refs_3_
  98.1 7.6 %norm_first.1 = bf16[4,256,2048]{2,1,0:T(8,128)(2,1)} custom-call(s32[4]{0:T(128)} %add_add_fusion.1.at_ref, bf16[256,2048]{1,0:T(8,128)(2,1)} %get-tuple-element.194.refs_0_, bf16[256,2048]{1,0:T(8,128)(2,1)} %get-tuple-element.193.refs_1_, bf16[256,2048]{1,0:T(8,128)(2,1)} %collective-permute-done.2.refs_2_, bf16[256,2048]{1,0:T(8,128)(2,1)} %copy-done.34, ...), custom_call_target="tpu_custom_call" | custom-call | bytes 83886 | tf_op jit(solution)/shard_map/norm_first/pallas_call | solution.py:358
  107.9 2.4 slice_dynamic-update-slice_fusion.1
  110.3 2.3 slice_dynamic-update-slice_fusion
  117.5 7.1 %fusion.5.r_0_ = f32[1,3,1024,256]{3,2,1,0:T(8,128)} fusion(bf16[1024,2048,1]{1,0,2:T(8,128)(2,1)S(1)} %bitcast.130, bf16[4,2048,256]{2,1,0:T(8,128)(2,1)} %constant_dynamic-update-slice_fusion.refs_2_.refs_1_.refs_6_.refs_7_.refs_8_), kind=kOutput, calls=%fused_computation.9 | convolution fusion | flops 3221225472 | bytes 10485760 | tf_op jit(solution)/shard_map/rd,cde->cre/dot_general | solution.py:890
  124.6 9.4 %attend_forward.2 = (bf16[1,1024,256]{2,1,0:T(8,128)(2,1)S(1)}, bf16[1,1024,256]{2,1,0:T(8,128)(2,1)S(1)}, bf16[1,1024,256]{2,1,0:T(8,128)(2,1)S(1)}, bf16[1,102...) custom-call(f32[1,3,1024,256]{3,2,1,0:T(8,128)} %fusion.5.r_0_, f32[1,3,1,256]{3,2,1,0:T(1,128)S(1)} %copy.23.r_1_, ...), custom_call_target="tpu_custom_call" | custom-call | flops 6442450 | bytes 68157 | tf_op jit(solution)/shard_map/attend_forward/pallas_call | solution.py:85
  134.0 5.1 fusion.8.r_0_
  139.1 2.6 collective-permute-done.9.r_4_.refs_3_
  141.7 10.0 %attend_forward.3 = (bf16[1,1024,256]{2,1,0:T(8,128)(2,1)S(1)}, bf16[1,1024,256]{2,1,0:T(8,128)(2,1)S(1)}, bf16[1,1024,256]{2,1,0:T(8,128)(2,1)S(1)}, bf16[1,102...) custom-call(f32[1,3,1024,256]{3,2,1,0:T(8,128)} %fusion.8.r_0_, f32[1,3,1,256]{3,2,1,0:T(1,128)S(1)} %reshape.85.r_1_, ...), custom_call_target="tpu_custom_call" | custom-call | flops 6442450 | bytes 68157 | tf_op jit(solution)/shard_map/attend_forward/pallas_call | solution.py:85
  154.1 7.5 %out.1 = (bf16[2,256,1024]{2,1,0:T(8,128)(2,1)}, bf16[2,256,1024]{2,1,0:T(8,128)(2,1)}, bf16[2,256,1024]{2,1,0:T(8,128)(2,1)}, bf16[2,256,1024]{2,1,0:T(8,128)(2,1)}) custom-call(s32[2]{0:T(128)} %pad_add_fusion.1.at_ref, bf16[1024,256]{1,0:T(8,128)(2,1)} %bitcast.109, bf16[1024,256]{1,0:T(8,128)(2,1)} %bitcast.111, ...), custom_call_target="tpu_custom_call" | custom-call | flops 21474836 | bytes 73400 | tf_op jit(solution)/shard_map/out/pallas_call | solution.py:246
  164.8 5.3 lay_pieces.1
  170.1 16.8 %collective-permute-done.10.two = bf16[2,256,1024]{2,1,0:T(8,128)(2,1)S(1)} collective-permute-done((bf16[2,256,1024]{2,1,0:T(8,128)(2,1)}, bf16[2,256,1024]{2,1,0:T(8,128)(2,1)S(1)}, u32[]{:S(2)}, u32[]{:S(2)}) %collective-permute-start.10) | collective-permute-done | bytes 1048608 | tf_op jit(solution)/shard_map/ppermute | solution.py:559
  189.0 3.5 join.4
  194.7 10.6 %collective-permute-done.12.refs_1_ = bf16[256,1024]{1,0:T(8,128)(2,1)S(1)} collective-permute-done((bf16[256,1024]{1,0:T(8,128)(2,1)}, bf16[256,1024]{1,0:T(8,128)(2,1)S(1)}, u32[]{:S(2)}, u32[]{:S(2)}) %collective-permute-start.12) | collective-permute-done | bytes 524320 | tf_op jit(solution)/shard_map/ppermute | solution.py:561
  207.4 3.5 add_norm.1
  213.1 24.3 %collective-permute-done.16.refs_2_ = bf16[256,2048]{1,0:T(8,128)(2,1)S(1)} collective-permute-done((bf16[256,2048]{1,0:T(8,128)(2,1)}, bf16[256,2048]{1,0:T(8,128)(2,1)S(1)}, u32[]{:S(2)}, u32[]{:S(2)}) %collective-permute-start.16) | collective-permute-done | bytes 1048608 | tf_op jit(solution)/shard_map/ppermute | solution.py:561
  242.2 9.9 %collective-permute-done.17.refs_3_ = bf16[256,1024]{1,0:T(8,128)(2,1)S(1)} collective-permute-done((bf16[256,1024]{1,0:T(8,128)(2,1)}, bf16[256,1024]{1,0:T(8,128)(2,1)S(1)}, u32[]{:S(2)}, u32[]{:S(2)}) %collective-permute-start.17) | collective-permute-done | bytes 524320 | tf_op jit(solution)/shard_map/ppermute | solution.py:559
  252.1 2.6 collective-permute-done.18.refs_4_
  254.7 5.9 lay_rows.4
  260.7 12.0 %gate_up.3 = (bf16[704,1024]{1,0:T(8,128)(2,1)}, bf16[2,704,1024]{2,1,0:T(8,128)(2,1)}, bf16[1024,704]{1,0:T(8,128)(2,1)}) custom-call(bf16[2,704,2048]{2,1,0:T(8,128)(2,1)} %collective-permute-done.21.weight_ref.refs_6_.refs_7_, bf16[1024,2048]{1,0:T(8,128)(2,1)} %bitcast.120), custom_call_target="tpu_custom_call" | custom-call | flops 59055800 | bytes 157286 | tf_op jit(solution)/shard_map/gate_up/pallas_call | solution.py:285
  273.2 11.9 %gate_up.2 = (bf16[704,1024]{1,0:T(8,128)(2,1)}, bf16[2,704,1024]{2,1,0:T(8,128)(2,1)}, bf16[1024,704]{1,0:T(8,128)(2,1)}) custom-call(bf16[2,704,2048]{2,1,0:T(8,128)(2,1)} %all-gather.4.cloned.1.call-done.weight_ref.refs_4_.refs_5_, bf16[1024,2048]{1,0:T(8,128)(2,1)} %bitcast.121), custom_call_target="tpu_custom_call" | custom-call | flops 59055800 | bytes 157286 | tf_op jit(solution)/shard_map/gate_up/pallas_call | solution.py:285
  286.3 10.3 %grad_down.1.refs_0_ = bf16[704,2048]{1,0:T(8,128)(2,1)} custom-call(bf16[704,1024]{1,0:T(8,128)(2,1)} %get-tuple-element.118.refs_0_, bf16[704,1024]{1,0:T(8,128)(2,1)} %copy-done.44, bf16[1024,2048]{1,0:T(8,128)(2,1)} %bitcast.117, bf16[1024,2048]{1,0:T(8,128)(2,1)} %collective-permute-done.19.refs_5_.refs_3_), custom_call_target="tpu_custom_call" | custom-call | flops 59055800 | bytes 141557 | tf_op jit(solution)/shard_map/grad_down/pallas_call | solution.py:196
  296.7 8.9 %hidden_back.2 = (bf16[2,704,1024]{2,1,0:T(8,128)(2,1)}, bf16[2,1024,704]{2,1,0:T(8,128)(2,1)}) custom-call(bf16[704,2048]{1,0:T(8,128)(2,1)} %collective-permute-done.22.weight_ref.refs_3_, bf16[1024,2048]{1,0:T(8,128)(2,1)} %bitcast.118, bf16[2,704,1024]{2,1,0:T(8,128)(2,1)} %get-tuple-element.117.slope_ref, bf16[704,2048]{1,0:T(8,128)(2,1)} %grad_down.1.refs_0_), custom_call_target="tpu_custom_call" | custom-call | flops 29527900 | bytes 157286 | tf_op jit(solution)/shard_map/hidden_back/pallas_call | solution.py:325
  306.2 8.6 %hidden_back.3 = (bf16[2,704,1024]{2,1,0:T(8,128)(2,1)}, bf16[2,1024,704]{2,1,0:T(8,128)(2,1)}) custom-call(bf16[704,2048]{1,0:T(8,128)(2,1)} %all-gather.6.cloned.1.call-done.weight_ref.refs_2_, bf16[1024,2048]{1,0:T(8,128)(2,1)} %bitcast.119, bf16[2,704,1024]{2,1,0:T(8,128)(2,1)} %get-tuple-element.116.slope_ref, ...), custom_call_target="tpu_custom_call" | custom-call | flops 29527900 | bytes 157286 | tf_op jit(solution)/shard_map/hidden_back/pallas_call | solution.py:325
  317.0 20.2 %grad_two.1 = (bf16[2,256,1024]{2,1,0:T(8,128)(2,1)}, bf16[2,256,1024]{2,1,0:T(8,128)(2,1)}, bf16[2,256,1024]{2,1,0:T(8,128)(2,1)}, bf16[2,256,1024]{2,1,0:T(8,128)(2,1)}) custom-call(s32[2]{0:T(128)} %pad_add_fusion.1.at_ref, bf16[2,1024,704]{2,1,0:T(8,128)(2,1)} %get-tuple-element.120.refs_0_.refs_1_, ...), custom_call_target="tpu_custom_call" | custom-call | flops 118111600 | bytes 214958 | tf_op jit(solution)/shard_map/grad_two/pallas_call | solution.py:246
  338.3 18.1 %grad_gate_up.1.refs_0_ = bf16[2,704,2048]{2,1,0:T(8,128)(2,1)} custom-call(bf16[2,704,1024]{2,1,0:T(8,128)(2,1)} %get-tuple-element.126.refs_0_, bf16[2,704,1024]{2,1,0:T(8,128)(2,1)} %collective-permute-done.25.refs_9_.refs_1_, bf16[1024,2048]{1,0:T(8,128)(2,1)} %bitcast.123, bf16[1024,2048]{1,0:T(8,128)(2,1)} %copy-done.30, ...), custom_call_target="tpu_custom_call" | custom-call | flops 118111600 | bytes 283115 | tf_op jit(solution)/shard_map/grad_gate_up/pallas_call | solution.py:196
  356.4 6.1 collective-permute-done.26.two
  363.4 3.5 join.5
  369.2 12.5 %down.1 = (bf16[2,256,1024]{2,1,0:T(8,128)(2,1)}, bf16[2,256,1024]{2,1,0:T(8,128)(2,1)}, bf16[2,256,1024]{2,1,0:T(8,128)(2,1)}, bf16[2,256,1024]{2,1,0:T(8,128)(2,1)}) custom-call(s32[2]{0:T(128)} %pad_add_fusion.1.at_ref, bf16[1024,704]{1,0:T(8,128)(2,1)} %get-tuple-element.109.refs_0_, bf16[1024,704]{1,0:T(8,128)(2,1)} %get-tuple-element.112.refs_1_, ...), custom_call_target="tpu_custom_call" | custom-call | flops 59055800 | bytes 128450 | tf_op jit(solution)/shard_map/down/pallas_call | solution.py:246
  382.7 4.8 norm_back.2
  390.6 21.8 %collective-permute-done.31.refs_2_ = bf16[256,2048]{1,0:T(8,128)(2,1)S(1)} collective-permute-done((bf16[256,2048]{1,0:T(8,128)(2,1)}, bf16[256,2048]{1,0:T(8,128)(2,1)S(1)}, u32[]{:S(2)}, u32[]{:S(2)}) %collective-permute-start.31) | collective-permute-done | bytes 1048608 | tf_op jit(solution)/shard_map/ppermute | solution.py:561
  414.9 10.1 %collective-permute-done.32.refs_3_ = bf16[256,1024]{1,0:T(8,128)(2,1)S(1)} collective-permute-done((bf16[256,1024]{1,0:T(8,128)(2,1)S(1)}, bf16[256,1024]{1,0:T(8,128)(2,1)S(1)}, u32[]{:S(2)}, u32[]{:S(2)}) %collective-permute-start.32) | collective-permute-done | bytes 524320 | tf_op jit(solution)/shard_map/ppermute | solution.py:559
  426.7 5.3 lay_rows.5
  434.6 4.5 grad_att.2
  440.1 11.2 %attend_back.2 = bf16[1,3,1024,256]{3,2,1,0:T(8,128)(2,1)S(1)} custom-call(bf16[1,1024,256]{2,1,0:T(8,128)(2,1)S(1)} %copy-done.23, bf16[1,1024,256]{2,1,0:T(8,128)(2,1)S(1)} %copy-done.25, bf16[1,1024,256]{2,1,0:T(8,128)(2,1)S(1)} %copy-done.27, bf16[1,1024,256]{2,1,0:T(8,128)(2,1)S(1)} %copy-done.11, f32[1,1024,256]{2,1,0:T(8,128)S(1)} %get-tuple-element.141.r_4_, ...), custom_call_target="tpu_custom_call" | custom-call | flops 16106127 | bytes 52428 | tf_op jit(solution)/shard_map/attend_back/pallas_call | solution.py:145
  452.5 6.7 %grad_out.1.refs_0_ = bf16[2048,256]{1,0:T(8,128)(2,1)} custom-call(bf16[1024,2048]{1,0:T(8,128)(2,1)} %bitcast.126, bf16[1024,2048]{1,0:T(8,128)(2,1)} %collective-permute-done.36.refs_1_, bf16[1024,256]{1,0:T(8,128)(2,1)} %bitcast.110, bf16[1024,256]{1,0:T(8,128)(2,1)} %copy-done.42, bf16[3,1024,256]{2,1,0:T(8,128)(2,1)} %bitcast.105), custom_call_target="tpu_custom_call" | custom-call | flops 21474836 | bytes 104857 | tf_op jit(solution)/shard_map/grad_out/pallas_call | solution.py:196
  460.3 3.8 join.6
  465.7 4.7 grad_att.3
  471.4 11.2 %attend_back.3 = bf16[1,3,1024,256]{3,2,1,0:T(8,128)(2,1)S(1)} custom-call(bf16[1,1024,256]{2,1,0:T(8,128)(2,1)S(1)} %copy-done.17, bf16[1,1024,256]{2,1,0:T(8,128)(2,1)S(1)} %copy-done.19, bf16[1,1024,256]{2,1,0:T(8,128)(2,1)S(1)} %copy-done.21, bf16[1,1024,256]{2,1,0:T(8,128)(2,1)S(1)} %copy-done.8, f32[1,1024,256]{2,1,0:T(8,128)S(1)} %copy-done.15, ...), custom_call_target="tpu_custom_call" | custom-call | flops 16106127 | bytes 52428 | tf_op jit(solution)/shard_map/attend_back/pallas_call | solution.py:145
  483.8 4.7 collective-permute-done.38.refs_3_
  488.6 3.5 add_low.1.refs_12_.refs_0_
  492.9 12.4 %grad_one.1 = (bf16[2,256,1024]{2,1,0:T(8,128)(2,1)}, bf16[2,256,1024]{2,1,0:T(8,128)(2,1)}, bf16[2,256,1024]{2,1,0:T(8,128)(2,1)}, bf16[2,256,1024]{2,1,0:T(8,128)(2,1)}) custom-call(s32[2]{0:T(128)} %pad_add_fusion.1.at_ref, bf16[3,1024,256]{2,1,0:T(8,128)(2,1)} %bitcast.100, bf16[3,1024,256]{2,1,0:T(8,128)(2,1)} %bitcast.101, ...), custom_call_target="tpu_custom_call" | custom-call | flops 64424508 | bytes 136314 | tf_op jit(solution)/shard_map/grad_one/pallas_call | solution.py:246
  507.0 10.9 %grad_qkv.1.refs_0_ = bf16[3,2048,256]{2,1,0:T(8,128)(2,1)} custom-call(bf16[1024,2048]{1,0:T(8,128)(2,1)} %bitcast.129, bf16[1024,2048]{1,0:T(8,128)(2,1)} %collective-permute-done.20.refs_6_.theirs_ref, bf16[3,1024,256]{2,1,0:T(8,128)(2,1)} %bitcast.103, bf16[3,1024,256]{2,1,0:T(8,128)(2,1)} %collective-permute-done.42.their_ref, ...), custom_call_target="tpu_custom_call" | custom-call | flops 64424508 | bytes 146800 | tf_op jit(solution)/shard_map/grad_qkv/pallas_call | solution.py:516
  520.5 3.8 collective-permute-start.49
  524.3 5.4 collective-permute-done.40.two
  530.6 4.0 join.7
  536.3 5.6 collective-permute-done.48
  541.9 13.6 %collective-permute-done.49 = bf16[2,3,256,256]{3,2,1,0:T(8,128)(2,1)} collective-permute-done((bf16[2,3,256,256]{3,2,1,0:T(8,128)(2,1)}, bf16[2,3,256,256]{3,2,1,0:T(8,128)(2,1)}, u32[]{:S(2)}, u32[]{:S(2)}) %collective-permute-start.49) | collective-permute-done | bytes 786464 | tf_op jit(solution)/shard_map/ppermute | solution.py:556
  562.0 5.2 collective-permute-done.53
  572.4 4.8 norm_back.3
  577.3 2.9 collective-permute-done.54
  590.3 5.2 convert_bitcast_fusion
  598.8 7.1 %collective-permute-done.55 = bf16[3,512,256]{2,1,0:T(8,128)(2,1)} collective-permute-done((bf16[3,512,256]{2,1,0:T(8,128)(2,1)}, bf16[3,512,256]{2,1,0:T(8,128)(2,1)}, u32[]{:S(2)}, u32[]{:S(2)}) %collective-permute-start.55) | collective-permute-done | bytes 786464 | tf_op jit(solution)/shard_map/ppermute | solution.py:559
  608.4 3.5 collective-permute-done.52.refs_2_
  615.8 5.3 lay_rows.6
  621.1 6.2 copy.27
  629.2 6.6 %lay_rows.7 = f32[4,256,2048]{2,1,0:T(8,128)} custom-call(s32[4]{0:T(128)} %pad_add_fusion.at_ref, bf16[256,2048]{1,0:T(8,128)(2,1)} %get-tuple-element.169.refs_0_, bf16[256,2048]{1,0:T(8,128)(2,1)} %collective-permute-done.51.refs_1_, bf16[256,2048]{1,0:T(8,128)(2,1)} %collective-permute-done.52.refs_2_, bf16[256,2048]{1,0:T(8,128)(2,1)} %collective-permute-done.56.refs_3_), custom_call_target="tpu_custom_call" | custom-call | bytes 83886 | tf_op jit(solution)/shard_map/lay_rows/pallas_call | solution.py:358
  (318 shorter events, 117.7 us)
Async XLA Ops:
  7.2 203.7 %all-gather.4.cloned.1.call-start = ((), (), s32[]{:S(2)}) async-start(), calls=%async_computation.3 | async-start | bytes 7208960 | tf_op jit(solution)/shard_map/all_gather | solution.py:884
  12.4 35.3 %collective-permute-start = (bf16[4,528,256]{2,1,0:T(8,128)(2,1)}, bf16[4,528,256]{2,1,0:T(8,128)(2,1)}, u32[]{:S(2)}, u32[]{:S(2)}) collective-permute-start(bf16[4,528,256]{2,1,0:T(8,128)(2,1)} %fusion.11), channel_id=1, source_target_pairs={{0,8},{8,16},{16,24},{24,0},{1,9},{9,17},{17,25},{25,1},{2,10},{10... | collective-permute-start | bytes 3244040 | tf_op jit(solution)/shard_map/ppermute | solution.py:556
  15.4 48.8 %collective-permute-start.1 = (bf16[4,528,256]{2,1,0:T(8,128)(2,1)}, bf16[4,528,256]{2,1,0:T(8,128)(2,1)}, u32[]{:S(2)}, u32[]{:S(2)}) collective-permute-start(bf16[4,528,256]{2,1,0:T(8,128)(2,1)} %fusion.11), channel_id=1, source_target_pairs={{0,24},{8,0},{16,8},{24,16},{1,25},{9,1},{17,9},{25,17},{2,26},{10... | collective-permute-start | bytes 3244040 | tf_op jit(solution)/shard_map/ppermute | solution.py:556
  21.3 26.4 %collective-permute-start.2 = (bf16[256,2048]{1,0:T(8,128)(2,1)}, bf16[256,2048]{1,0:T(8,128)(2,1)}, u32[]{:S(2)}, u32[]{:S(2)}) collective-permute-start(bf16[256,2048]{1,0:T(8,128)(2,1)} %get-tuple-element.195.refs_4_), channel_id=1, source_target_pairs={{0,4},{4,0},{1,5},{5,1},{2,6},{6,2},{3,7},{7,3},{8,12},{12,8},{9,1... | collective-permute-start | bytes 3145736 | tf_op jit(solution)/shard_map/ppermute | solution.py:559
  24.9 50.4 %collective-permute-start.6 = (bf16[256,2048]{1,0:T(8,128)(2,1)}, bf16[256,2048]{1,0:T(8,128)(2,1)}, u32[]{:S(2)}, u32[]{:S(2)}) collective-permute-start(bf16[256,2048]{1,0:T(8,128)(2,1)} %get-tuple-element.192.refs_5_), channel_id=1, source_target_pairs={{0,4},{4,0},{1,5},{5,1},{2,6},{6,2},{3,7},{7,3},{8,12},{12,8},{9,1... | collective-permute-start | bytes 3145736 | tf_op jit(solution)/shard_map/ppermute | solution.py:559
  65.3 26.7 %collective-permute-start.4 = (bf16[2,528,256]{2,1,0:T(8,128)(2,1)S(1)}, bf16[2,528,256]{2,1,0:T(8,128)(2,1)}, u32[]{:S(2)}, u32[]{:S(2)}) collective-permute-start(bf16[2,528,256]{2,1,0:T(8,128)(2,1)S(1)} %slice.159), channel_id=1, source_target_pairs={{0,8},{8,16},{16,24},{24,0},{1,9},{9,17},{17,25},{25,1},{2,10},{10... | collective-permute-start | bytes 1622024 | tf_op jit(solution)/shard_map/ppermute | solution.py:556
  67.6 24.4 %collective-permute-start.5 = (bf16[2,512,256]{2,1,0:T(8,128)(2,1)S(1)}, bf16[2,512,256]{2,1,0:T(8,128)(2,1)S(1)}, u32[]{:S(2)}, u32[]{:S(2)}) collective-permute-start(bf16[2,512,256]{2,1,0:T(8,128)(2,1)S(1)} %slice.160), channel_id=1, source_target_pairs={{0,24},{8,0},{16,8},{24,16},{1,25},{9,1},{17,9},{25,17},{2,26},{10... | collective-permute-start | bytes 1572872 | tf_op jit(solution)/shard_map/ppermute | solution.py:556
  73.1 24.1 %collective-permute-start.7 = (bf16[256,2048]{1,0:T(8,128)(2,1)}, bf16[256,2048]{1,0:T(8,128)(2,1)S(1)}, u32[]{:S(2)}, u32[]{:S(2)}) collective-permute-start(bf16[256,2048]{1,0:T(8,128)(2,1)} %collective-permute-done.2.refs_2_), channel_id=1, source_target_pairs={{0,2},{1,3},{2,0},{3,1},{4,6},{5,7},{6,4},{7,5},{8,10},{9,11},{10,... | collective-permute-start | bytes 3145736 | tf_op jit(solution)/shard_map/ppermute | solution.py:561
  92.1 180.6 %all-gather.6.cloned.1.call-start = ((), (), s32[]{:S(2)}) async-start(), calls=%async_computation.4 | async-start | bytes 3604480 | tf_op jit(solution)/shard_map/all_gather | solution.py:885
  115.3 18.7 %collective-permute-start.8 = (bf16[4,2048,256]{2,1,0:T(8,128)(2,1)}, bf16[4,2048,256]{2,1,0:T(8,128)(2,1)S(1)}, u32[]{:S(2)}, u32[]{:S(2)}) collective-permute-start(bf16[4,2048,256]{2,1,0:T(8,128)(2,1)} %constant_dynamic-update-slice_fusion.refs_2_.refs_1_.refs_6_.refs_7_.refs_8_), channel_id=1, source_target_pairs={{0,1},{1,0},{2,3},{3,2},{4,5},{5,4},{6,7},{7,6},{8,9},{9,8},{10,11... | collective-permute-start | bytes 12582920 | tf_op jit(solution)/shard_map/ppermute | solution.py:564
  115.9 25.8 %collective-permute-start.9 = (bf16[256,2048]{1,0:T(8,128)(2,1)}, bf16[256,2048]{1,0:T(8,128)(2,1)S(1)}, u32[]{:S(2)}, u32[]{:S(2)}) collective-permute-start(bf16[256,2048]{1,0:T(8,128)(2,1)} %collective-permute-done.6.refs_2_), channel_id=1, source_target_pairs={{0,2},{1,3},{2,0},{3,1},{4,6},{5,7},{6,4},{7,5},{8,10},{9,11},{10,... | collective-permute-start | bytes 3145736 | tf_op jit(solution)/shard_map/ppermute | solution.py:561
  161.7 25.2 %collective-permute-start.10 = (bf16[2,256,1024]{2,1,0:T(8,128)(2,1)}, bf16[2,256,1024]{2,1,0:T(8,128)(2,1)S(1)}, u32[]{:S(2)}, u32[]{:S(2)}) collective-permute-start(bf16[2,256,1024]{2,1,0:T(8,128)(2,1)} %get-tuple-element.101.refs_4_), channel_id=1, source_target_pairs={{0,4},{4,0},{1,5},{5,1},{2,6},{6,2},{3,7},{7,3},{8,12},{12,8},{9,1... | collective-permute-start | bytes 3145736 | tf_op jit(solution)/shard_map/ppermute | solution.py:559
  163.3 24.8 %collective-permute-start.11 = (bf16[2,256,1024]{2,1,0:T(8,128)(2,1)}, bf16[2,256,1024]{2,1,0:T(8,128)(2,1)S(1)}, u32[]{:S(2)}, u32[]{:S(2)}) collective-permute-start(bf16[2,256,1024]{2,1,0:T(8,128)(2,1)} %get-tuple-element.103), channel_id=1, source_target_pairs={{0,2},{1,3},{2,0},{3,1},{4,6},{5,7},{6,4},{7,5},{8,10},{9,11},{10,... | collective-permute-start | bytes 3145736 | tf_op jit(solution)/shard_map/ppermute | solution.py:561
  164.8 30.0 %collective-permute-start.14 = (bf16[1024,256]{1,0:T(8,128)(2,1)S(1)}, bf16[1024,256]{1,0:T(8,128)(2,1)S(1)}, u32[]{:S(2)}, u32[]{:S(2)}) collective-permute-start(bf16[1024,256]{1,0:T(8,128)(2,1)S(1)} %bitcast.112), channel_id=1, source_target_pairs={{0,1},{1,0},{2,3},{3,2},{4,5},{5,4},{6,7},{7,6},{8,9},{9,8},{10,11... | collective-permute-start | bytes 1572872 | tf_op jit(solution)/shard_map/ppermute | solution.py:564
  192.6 12.8 %collective-permute-start.12 = (bf16[256,1024]{1,0:T(8,128)(2,1)}, bf16[256,1024]{1,0:T(8,128)(2,1)S(1)}, u32[]{:S(2)}, u32[]{:S(2)}) collective-permute-start(bf16[256,1024]{1,0:T(8,128)(2,1)} %get-tuple-element.105), channel_id=1, source_target_pairs={{0,2},{1,3},{2,0},{3,1},{4,6},{5,7},{6,4},{7,5},{8,10},{9,11},{10,... | collective-permute-start | bytes 1572872 | tf_op jit(solution)/shard_map/ppermute | solution.py:561
  194.1 12.5 %collective-permute-start.13 = (bf16[256,1024]{1,0:T(8,128)(2,1)}, bf16[256,1024]{1,0:T(8,128)(2,1)S(1)}, u32[]{:S(2)}, u32[]{:S(2)}) collective-permute-start(bf16[256,1024]{1,0:T(8,128)(2,1)} %get-tuple-element.107), channel_id=1, source_target_pairs={{0,4},{4,0},{1,5},{5,1},{2,6},{6,2},{3,7},{7,3},{8,12},{12,8},{9,1... | collective-permute-start | bytes 1572872 | tf_op jit(solution)/shard_map/ppermute | solution.py:559
  210.9 49.8 %collective-permute-start.21 = (bf16[2,704,2048]{2,1,0:T(8,128)(2,1)}, bf16[2,704,2048]{2,1,0:T(8,128)(2,1)}, u32[]{:S(2)}, u32[]{:S(2)}) collective-permute-start(bf16[2,704,2048]{2,1,0:T(8,128)(2,1)} %all-gather.4.cloned.1.call-done.weight_ref.refs_4_.refs_5_), channel_id=1, source_target_pairs={{0,1},{1,0},{2,3},{3,2},{4,5},{5,4},{6,7},{7,6},{8,9},{9,8},{10,11... | collective-permute-start | bytes 17301512 | tf_op jit(solution)/shard_map/ppermute | solution.py:564
  211.0 31.3 %collective-permute-start.20 = (bf16[1024,2048]{1,0:T(8,128)(2,1)}, bf16[1024,2048]{1,0:T(8,128)(2,1)}, u32[]{:S(2)}, u32[]{:S(2)}) collective-permute-start(bf16[1024,2048]{1,0:T(8,128)(2,1)} %bitcast.128), channel_id=1, source_target_pairs={{0,1},{1,0},{2,3},{3,2},{4,5},{5,4},{6,7},{7,6},{8,9},{9,8},{10,11... | collective-permute-start | bytes 12582920 | tf_op jit(solution)/shard_map/ppermute | solution.py:564
  211.5 43.2 %collective-permute-start.19 = (bf16[1024,2048]{1,0:T(8,128)(2,1)}, bf16[1024,2048]{1,0:T(8,128)(2,1)}, u32[]{:S(2)}, u32[]{:S(2)}) collective-permute-start(bf16[1024,2048]{1,0:T(8,128)(2,1)} %bitcast.116), channel_id=1, source_target_pairs={{0,1},{1,0},{2,3},{3,2},{4,5},{5,4},{6,7},{7,6},{8,9},{9,8},{10,11... | collective-permute-start | bytes 12582920 | tf_op jit(solution)/shard_map/ppermute | solution.py:564
  211.6 151.5 %reduce-scatter.4.cloned.1.call-start = ((), (), s32[]{:S(2)}) async-start(), calls=%async_computation.5 | async-start | bytes 3604480 | tf_op jit(solution)/shard_map/reduce_scatter | solution.py:924
  211.6 25.8 %collective-permute-start.16 = (bf16[256,2048]{1,0:T(8,128)(2,1)}, bf16[256,2048]{1,0:T(8,128)(2,1)S(1)}, u32[]{:S(2)}, u32[]{:S(2)}) collective-permute-start(bf16[256,2048]{1,0:T(8,128)(2,1)} %get-tuple-element.108.refs_0_), channel_id=1, source_target_pairs={{0,2},{1,3},{2,0},{3,1},{4,6},{5,7},{6,4},{7,5},{8,10},{9,11},{10,... | collective-permute-start | bytes 3145736 | tf_op jit(solution)/shard_map/ppermute | solution.py:561
  212.2 27.1 %collective-permute-start.15 = (bf16[256,2048]{1,0:T(8,128)(2,1)}, bf16[256,2048]{1,0:T(8,128)(2,1)S(1)}, u32[]{:S(2)}, u32[]{:S(2)}) collective-permute-start(bf16[256,2048]{1,0:T(8,128)(2,1)} %get-tuple-element.108.refs_0_), channel_id=1, source_target_pairs={{0,4},{4,0},{1,5},{5,1},{2,6},{6,2},{3,7},{7,3},{8,12},{12,8},{9,1... | collective-permute-start | bytes 3145736 | tf_op jit(solution)/shard_map/ppermute | solution.py:559
  238.3 13.8 %collective-permute-start.17 = (bf16[256,1024]{1,0:T(8,128)(2,1)}, bf16[256,1024]{1,0:T(8,128)(2,1)S(1)}, u32[]{:S(2)}, u32[]{:S(2)}) collective-permute-start(bf16[256,1024]{1,0:T(8,128)(2,1)} %slice.215), channel_id=1, source_target_pairs={{0,4},{4,0},{1,5},{5,1},{2,6},{6,2},{3,7},{7,3},{8,12},{12,8},{9,1... | collective-permute-start | bytes 1572872 | tf_op jit(solution)/shard_map/ppermute | solution.py:559
  241.1 13.6 %collective-permute-start.18 = (bf16[256,1024]{1,0:T(8,128)(2,1)}, bf16[256,1024]{1,0:T(8,128)(2,1)}, u32[]{:S(2)}, u32[]{:S(2)}) collective-permute-start(bf16[256,1024]{1,0:T(8,128)(2,1)} %slice.216), channel_id=1, source_target_pairs={{0,2},{1,3},{2,0},{3,1},{4,6},{5,7},{6,4},{7,5},{8,10},{9,11},{10,... | collective-permute-start | bytes 1572872 | tf_op jit(solution)/shard_map/ppermute | solution.py:561
  272.7 12.5 %collective-permute-start.23 = (bf16[704,1024]{1,0:T(8,128)(2,1)}, bf16[704,1024]{1,0:T(8,128)(2,1)S(1)}, u32[]{:S(2)}, u32[]{:S(2)}) collective-permute-start(bf16[704,1024]{1,0:T(8,128)(2,1)} %get-tuple-element.114), channel_id=1, source_target_pairs={{0,1},{1,0},{2,3},{3,2},{4,5},{5,4},{6,7},{7,6},{8,9},{9,8},{10,11... | collective-permute-start | bytes 4325384 | tf_op jit(solution)/shard_map/ppermute | solution.py:564
  272.7 24.1 %collective-permute-start.22 = (bf16[704,2048]{1,0:T(8,128)(2,1)}, bf16[704,2048]{1,0:T(8,128)(2,1)}, u32[]{:S(2)}, u32[]{:S(2)}) collective-permute-start(bf16[704,2048]{1,0:T(8,128)(2,1)} %all-gather.6.cloned.1.call-done.weight_ref.refs_2_), channel_id=1, source_target_pairs={{0,1},{1,0},{2,3},{3,2},{4,5},{5,4},{6,7},{7,6},{8,9},{9,8},{10,11... | collective-permute-start | bytes 8650760 | tf_op jit(solution)/shard_map/ppermute | solution.py:564
  296.6 210.5 %reduce-scatter.6.cloned.1.call-start = ((), (), s32[]{:S(2)}) async-start(), calls=%async_computation.6 | async-start | bytes 7208960 | tf_op jit(solution)/shard_map/reduce_scatter | solution.py:947
  296.6 18.2 %collective-permute-start.24 = (bf16[1024,2048]{1,0:T(8,128)(2,1)}, bf16[1024,2048]{1,0:T(8,128)(2,1)S(1)}, u32[]{:S(2)}, u32[]{:S(2)}) collective-permute-start(bf16[1024,2048]{1,0:T(8,128)(2,1)} %bitcast.122), channel_id=1, source_target_pairs={{0,1},{1,0},{2,3},{3,2},{4,5},{5,4},{6,7},{7,6},{8,9},{9,8},{10,11... | collective-permute-start | bytes 12582920 | tf_op jit(solution)/shard_map/ppermute | solution.py:564
  305.7 9.2 %collective-permute-start.25 = (bf16[2,704,1024]{2,1,0:T(8,128)(2,1)}, bf16[2,704,1024]{2,1,0:T(8,128)(2,1)}, u32[]{:S(2)}, u32[]{:S(2)}) collective-permute-start(bf16[2,704,1024]{2,1,0:T(8,128)(2,1)} %get-tuple-element.121), channel_id=1, source_target_pairs={{0,1},{1,0},{2,3},{3,2},{4,5},{5,4},{6,7},{7,6},{8,9},{9,8},{10,11... | collective-permute-start | bytes 8650760 | tf_op jit(solution)/shard_map/ppermute | solution.py:564
  337.2 25.3 %collective-permute-start.26 = (bf16[2,256,1024]{2,1,0:T(8,128)(2,1)}, bf16[2,256,1024]{2,1,0:T(8,128)(2,1)S(1)}, u32[]{:S(2)}, u32[]{:S(2)}) collective-permute-start(bf16[2,256,1024]{2,1,0:T(8,128)(2,1)} %get-tuple-element.123.refs_4_), channel_id=1, source_target_pairs={{0,4},{4,0},{1,5},{5,1},{2,6},{6,2},{3,7},{7,3},{8,12},{12,8},{9,1... | collective-permute-start | bytes 3145736 | tf_op jit(solution)/shard_map/ppermute | solution.py:559
  337.9 25.2 %collective-permute-start.27 = (bf16[2,256,1024]{2,1,0:T(8,128)(2,1)}, bf16[2,256,1024]{2,1,0:T(8,128)(2,1)}, u32[]{:S(2)}, u32[]{:S(2)}) collective-permute-start(bf16[2,256,1024]{2,1,0:T(8,128)(2,1)} %get-tuple-element.125), channel_id=1, source_target_pairs={{0,2},{1,3},{2,0},{3,1},{4,6},{5,7},{6,4},{7,5},{8,10},{9,11},{10,... | collective-permute-start | bytes 3145736 | tf_op jit(solution)/shard_map/ppermute | solution.py:561
  366.9 215.4 %reduce-scatter.8.cloned.1.call-start = ((), (), s32[]{:S(2)}) async-start(), calls=%async_computation.8 | async-start | bytes 1310720 | tf_op jit(solution)/shard_map/reduce_scatter | solution.py:982
  367.9 13.8 %collective-permute-start.28 = (bf16[256,1024]{1,0:T(8,128)(2,1)S(1)}, bf16[256,1024]{1,0:T(8,128)(2,1)S(1)}, u32[]{:S(2)}, u32[]{:S(2)}) collective-permute-start(bf16[256,1024]{1,0:T(8,128)(2,1)S(1)} %copy-done.61), channel_id=1, source_target_pairs={{0,2},{1,3},{2,0},{3,1},{4,6},{5,7},{6,4},{7,5},{8,10},{9,11},{10,... | collective-permute-start | bytes 1572872 | tf_op jit(solution)/shard_map/ppermute | solution.py:561
  368.1 13.6 %collective-permute-start.29 = (bf16[256,1024]{1,0:T(8,128)(2,1)S(1)}, bf16[256,1024]{1,0:T(8,128)(2,1)S(1)}, u32[]{:S(2)}, u32[]{:S(2)}) collective-permute-start(bf16[256,1024]{1,0:T(8,128)(2,1)S(1)} %copy-done.60), channel_id=1, source_target_pairs={{0,4},{4,0},{1,5},{5,1},{2,6},{6,2},{3,7},{7,3},{8,12},{12,8},{9,1... | collective-permute-start | bytes 1572872 | tf_op jit(solution)/shard_map/ppermute | solution.py:559
  387.5 24.9 %collective-permute-start.31 = (bf16[256,2048]{1,0:T(8,128)(2,1)}, bf16[256,2048]{1,0:T(8,128)(2,1)S(1)}, u32[]{:S(2)}, u32[]{:S(2)}) collective-permute-start(bf16[256,2048]{1,0:T(8,128)(2,1)} %get-tuple-element.134.refs_0_), channel_id=1, source_target_pairs={{0,2},{1,3},{2,0},{3,1},{4,6},{5,7},{6,4},{7,5},{8,10},{9,11},{10,... | collective-permute-start | bytes 3145736 | tf_op jit(solution)/shard_map/ppermute | solution.py:561
  389.3 24.4 %collective-permute-start.30 = (bf16[256,2048]{1,0:T(8,128)(2,1)}, bf16[256,2048]{1,0:T(8,128)(2,1)S(1)}, u32[]{:S(2)}, u32[]{:S(2)}) collective-permute-start(bf16[256,2048]{1,0:T(8,128)(2,1)} %get-tuple-element.134.refs_0_), channel_id=1, source_target_pairs={{0,4},{4,0},{1,5},{5,1},{2,6},{6,2},{3,7},{7,3},{8,12},{12,8},{9,1... | collective-permute-start | bytes 3145736 | tf_op jit(solution)/shard_map/ppermute | solution.py:559
  412.4 12.6 %collective-permute-start.32 = (bf16[256,1024]{1,0:T(8,128)(2,1)S(1)}, bf16[256,1024]{1,0:T(8,128)(2,1)S(1)}, u32[]{:S(2)}, u32[]{:S(2)}) collective-permute-start(bf16[256,1024]{1,0:T(8,128)(2,1)S(1)} %slice.217), channel_id=1, source_target_pairs={{0,4},{4,0},{1,5},{5,1},{2,6},{6,2},{3,7},{7,3},{8,12},{12,8},{9,1... | collective-permute-start | bytes 1572872 | tf_op jit(solution)/shard_map/ppermute | solution.py:559
  413.7 12.2 %collective-permute-start.33 = (bf16[256,1024]{1,0:T(8,128)(2,1)S(1)}, bf16[256,1024]{1,0:T(8,128)(2,1)S(1)}, u32[]{:S(2)}, u32[]{:S(2)}) collective-permute-start(bf16[256,1024]{1,0:T(8,128)(2,1)S(1)} %slice.218), channel_id=1, source_target_pairs={{0,2},{1,3},{2,0},{3,1},{4,6},{5,7},{6,4},{7,5},{8,10},{9,11},{10,... | collective-permute-start | bytes 1572872 | tf_op jit(solution)/shard_map/ppermute | solution.py:561
  432.1 19.4 %collective-permute-start.36 = (bf16[1024,2048]{1,0:T(8,128)(2,1)}, bf16[1024,2048]{1,0:T(8,128)(2,1)}, u32[]{:S(2)}, u32[]{:S(2)}) collective-permute-start(bf16[1024,2048]{1,0:T(8,128)(2,1)} %bitcast.124), channel_id=1, source_target_pairs={{0,1},{1,0},{2,3},{3,2},{4,5},{5,4},{6,7},{7,6},{8,9},{9,8},{10,11... | collective-permute-start | bytes 12582920 | tf_op jit(solution)/shard_map/ppermute | solution.py:564
  432.1 28.2 %collective-permute-start.34 = (bf16[2,256,1024]{2,1,0:T(8,128)(2,1)}, bf16[2,256,1024]{2,1,0:T(8,128)(2,1)}, u32[]{:S(2)}, u32[]{:S(2)}) collective-permute-start(bf16[2,256,1024]{2,1,0:T(8,128)(2,1)} %get-tuple-element.135.refs_7_), channel_id=1, source_target_pairs={{0,4},{4,0},{1,5},{5,1},{2,6},{6,2},{3,7},{7,3},{8,12},{12,8},{9,1... | collective-permute-start | bytes 3145736 | tf_op jit(solution)/shard_map/ppermute | solution.py:559
  433.1 27.1 %collective-permute-start.35 = (bf16[2,256,1024]{2,1,0:T(8,128)(2,1)}, bf16[2,256,1024]{2,1,0:T(8,128)(2,1)}, u32[]{:S(2)}, u32[]{:S(2)}) collective-permute-start(bf16[2,256,1024]{2,1,0:T(8,128)(2,1)} %get-tuple-element.137), channel_id=1, source_target_pairs={{0,2},{1,3},{2,0},{3,1},{4,6},{5,7},{6,4},{7,5},{8,10},{9,11},{10,... | collective-permute-start | bytes 3145736 | tf_op jit(solution)/shard_map/ppermute | solution.py:561
  451.4 55.7 %collective-permute-start.42 = (bf16[3,1024,256]{2,1,0:T(8,128)(2,1)S(1)}, bf16[3,1024,256]{2,1,0:T(8,128)(2,1)}, u32[]{:S(2)}, u32[]{:S(2)}) collective-permute-start(bf16[3,1024,256]{2,1,0:T(8,128)(2,1)S(1)} %bitcast.104), channel_id=1, source_target_pairs={{0,1},{1,0},{2,3},{3,2},{4,5},{5,4},{6,7},{7,6},{8,9},{9,8},{10,11... | collective-permute-start | bytes 4718600 | tf_op jit(solution)/shard_map/ppermute | solution.py:564
  459.2 131.1 %all-gather.8.cloned.1.call-start = ((), (), s32[]{:S(2)}) async-start(), calls=%async_computation.7 | async-start | bytes 4325376 | tf_op jit(solution)/shard_map/all_gather | solution.py:1002
  459.2 32.8 %collective-permute-start.39 = (bf16[704,512]{1,0:T(8,128)(2,1)S(1)}, bf16[704,512]{1,0:T(8,128)(2,1)S(1)}, u32[]{:S(2)}, u32[]{:S(2)}) collective-permute-start(bf16[704,512]{1,0:T(8,128)(2,1)S(1)} %copy-done.35), channel_id=1, source_target_pairs={{0,4},{4,0},{1,5},{5,1},{2,6},{6,2},{3,7},{7,3},{8,12},{12,8},{9,1... | collective-permute-start | bytes 2162696 | tf_op jit(solution)/shard_map/ppermute | solution.py:559
  464.0 19.8 %collective-permute-start.37 = (bf16[256,1024]{1,0:T(8,128)(2,1)}, bf16[256,1024]{1,0:T(8,128)(2,1)S(1)}, u32[]{:S(2)}, u32[]{:S(2)}) collective-permute-start(bf16[256,1024]{1,0:T(8,128)(2,1)} %get-tuple-element.143), channel_id=1, source_target_pairs={{0,2},{1,3},{2,0},{3,1},{4,6},{5,7},{6,4},{7,5},{8,10},{9,11},{10,... | collective-permute-start | bytes 1572872 | tf_op jit(solution)/shard_map/ppermute | solution.py:561
  464.7 23.9 %collective-permute-start.38 = (bf16[256,1024]{1,0:T(8,128)(2,1)}, bf16[256,1024]{1,0:T(8,128)(2,1)}, u32[]{:S(2)}, u32[]{:S(2)}) collective-permute-start(bf16[256,1024]{1,0:T(8,128)(2,1)} %get-tuple-element.145), channel_id=1, source_target_pairs={{0,4},{4,0},{1,5},{5,1},{2,6},{6,2},{3,7},{7,3},{8,12},{12,8},{9,1... | collective-permute-start | bytes 1572872 | tf_op jit(solution)/shard_map/ppermute | solution.py:559
  505.3 24.4 %collective-permute-start.40 = (bf16[2,256,1024]{2,1,0:T(8,128)(2,1)}, bf16[2,256,1024]{2,1,0:T(8,128)(2,1)S(1)}, u32[]{:S(2)}, u32[]{:S(2)}) collective-permute-start(bf16[2,256,1024]{2,1,0:T(8,128)(2,1)} %get-tuple-element.152.refs_0_), channel_id=1, source_target_pairs={{0,4},{4,0},{1,5},{5,1},{2,6},{6,2},{3,7},{7,3},{8,12},{12,8},{9,1... | collective-permute-start | bytes 3145736 | tf_op jit(solution)/shard_map/ppermute | solution.py:559
  506.3 24.1 %collective-permute-start.41 = (bf16[2,256,1024]{2,1,0:T(8,128)(2,1)}, bf16[2,256,1024]{2,1,0:T(8,128)(2,1)}, u32[]{:S(2)}, u32[]{:S(2)}) collective-permute-start(bf16[2,256,1024]{2,1,0:T(8,128)(2,1)} %get-tuple-element.154), channel_id=1, source_target_pairs={{0,2},{1,3},{2,0},{3,1},{4,6},{5,7},{6,4},{7,5},{8,10},{9,11},{10,... | collective-permute-start | bytes 3145736 | tf_op jit(solution)/shard_map/ppermute | solution.py:561
  519.5 22.4 %collective-permute-start.48 = (bf16[2,3,256,256]{3,2,1,0:T(8,128)(2,1)S(1)}, bf16[2,3,256,256]{3,2,1,0:T(8,128)(2,1)}, u32[]{:S(2)}, u32[]{:S(2)}) collective-permute-start(bf16[2,3,256,256]{3,2,1,0:T(8,128)(2,1)S(1)} %pad_maximum_fusion), channel_id=1, source_target_pairs={{0,8},{8,16},{16,24},{24,0},{1,9},{9,17},{17,25},{25,1},{2,10},{10... | collective-permute-start | bytes 2359304 | tf_op jit(solution)/shard_map/ppermute | solution.py:556
  520.5 35.1 %collective-permute-start.49 = (bf16[2,3,256,256]{3,2,1,0:T(8,128)(2,1)}, bf16[2,3,256,256]{3,2,1,0:T(8,128)(2,1)}, u32[]{:S(2)}, u32[]{:S(2)}) collective-permute-start(bf16[2,3,256,256]{3,2,1,0:T(8,128)(2,1)} %pad_maximum_fusion.1), channel_id=1, source_target_pairs={{0,24},{8,0},{16,8},{24,16},{1,25},{9,1},{17,9},{25,17},{2,26},{10... | collective-permute-start | bytes 2359304 | tf_op jit(solution)/shard_map/ppermute | solution.py:556
  534.6 24.0 %collective-permute-start.43 = (bf16[256,1024]{1,0:T(8,128)(2,1)}, bf16[256,1024]{1,0:T(8,128)(2,1)}, u32[]{:S(2)}, u32[]{:S(2)}) collective-permute-start(bf16[256,1024]{1,0:T(8,128)(2,1)} %get-tuple-element.156), channel_id=1, source_target_pairs={{0,2},{1,3},{2,0},{3,1},{4,6},{5,7},{6,4},{7,5},{8,10},{9,11},{10,... | collective-permute-start | bytes 1572872 | tf_op jit(solution)/shard_map/ppermute | solution.py:561
  535.1 25.4 %collective-permute-start.44 = (bf16[256,1024]{1,0:T(8,128)(2,1)}, bf16[256,1024]{1,0:T(8,128)(2,1)}, u32[]{:S(2)}, u32[]{:S(2)}) collective-permute-start(bf16[256,1024]{1,0:T(8,128)(2,1)} %get-tuple-element.157), channel_id=1, source_target_pairs={{0,4},{4,0},{1,5},{5,1},{2,6},{6,2},{3,7},{7,3},{8,12},{12,8},{9,1... | collective-permute-start | bytes 1572872 | tf_op jit(solution)/shard_map/ppermute | solution.py:559
  556.8 10.4 %collective-permute-start.53 = (bf16[3,256,256]{2,1,0:T(8,128)(2,1)S(1)}, bf16[3,256,256]{2,1,0:T(8,128)(2,1)}, u32[]{:S(2)}, u32[]{:S(2)}) collective-permute-start(bf16[3,256,256]{2,1,0:T(8,128)(2,1)S(1)} %fusion.17.refs_8_), channel_id=1, source_target_pairs={{0,24},{8,0},{16,8},{24,16},{1,25},{9,1},{17,9},{25,17},{2,26},{10... | collective-permute-start | bytes 1179656 | tf_op jit(solution)/shard_map/ppermute | solution.py:556
  560.5 22.8 %collective-permute-start.46 = (bf16[256,2048]{1,0:T(8,128)(2,1)S(1)}, bf16[256,2048]{1,0:T(8,128)(2,1)}, u32[]{:S(2)}, u32[]{:S(2)}) collective-permute-start(bf16[256,2048]{1,0:T(8,128)(2,1)S(1)} %copy-done.31), channel_id=1, source_target_pairs={{0,2},{1,3},{2,0},{3,1},{4,6},{5,7},{6,4},{7,5},{8,10},{9,11},{10,... | collective-permute-start | bytes 3145736 | tf_op jit(solution)/shard_map/ppermute | solution.py:561
  568.9 11.2 %collective-permute-start.54 = (bf16[3,256,256]{2,1,0:T(8,128)(2,1)S(1)}, bf16[3,256,256]{2,1,0:T(8,128)(2,1)S(1)}, u32[]{:S(2)}, u32[]{:S(2)}) collective-permute-start(bf16[3,256,256]{2,1,0:T(8,128)(2,1)S(1)} %get-tuple-element.197), channel_id=1, source_target_pairs={{0,8},{8,16},{16,24},{24,0},{1,9},{9,17},{17,25},{25,1},{2,10},{10... | collective-permute-start | bytes 1179656 | tf_op jit(solution)/shard_map/ppermute | solution.py:556
  582.3 6.9 %collective-permute-start.62 = (bf16[512,256]{1,0:T(8,128)(2,1)}, bf16[512,256]{1,0:T(8,128)(2,1)S(1)}, u32[]{:S(2)}, u32[]{:S(2)}) collective-permute-start(bf16[512,256]{1,0:T(8,128)(2,1)} %reduce-scatter.8.cloned.1.call-done), channel_id=1, source_target_pairs={{0,4},{4,0},{1,5},{5,1},{2,6},{6,2},{3,7},{7,3},{8,12},{12,8},{9,1... | collective-permute-start | bytes 786440 | tf_op jit(solution)/shard_map/ppermute | solution.py:559
  585.1 30.7 %collective-permute-start.45 = (bf16[256,2048]{1,0:T(8,128)(2,1)S(1)}, bf16[256,2048]{1,0:T(8,128)(2,1)}, u32[]{:S(2)}, u32[]{:S(2)}) collective-permute-start(bf16[256,2048]{1,0:T(8,128)(2,1)S(1)} %copy-done.31), channel_id=1, source_target_pairs={{0,1},{1,0},{2,3},{3,2},{4,5},{5,4},{6,7},{7,6},{8,9},{9,8},{10,11... | collective-permute-start | bytes 3145736 | tf_op jit(solution)/shard_map/ppermute | solution.py:564
  585.2 20.7 %collective-permute-start.55 = (bf16[3,512,256]{2,1,0:T(8,128)(2,1)}, bf16[3,512,256]{2,1,0:T(8,128)(2,1)}, u32[]{:S(2)}, u32[]{:S(2)}) collective-permute-start(bf16[3,512,256]{2,1,0:T(8,128)(2,1)} %pad_maximum_fusion.2), channel_id=1, source_target_pairs={{0,4},{4,0},{1,5},{5,1},{2,6},{6,2},{3,7},{7,3},{8,12},{12,8},{9,1... | collective-permute-start | bytes 2359304 | tf_op jit(solution)/shard_map/ppermute | solution.py:559
  587.3 24.5 %collective-permute-start.52 = (bf16[256,2048]{1,0:T(8,128)(2,1)}, bf16[256,2048]{1,0:T(8,128)(2,1)}, u32[]{:S(2)}, u32[]{:S(2)}) collective-permute-start(bf16[256,2048]{1,0:T(8,128)(2,1)} %get-tuple-element.169.refs_0_), channel_id=1, source_target_pairs={{0,2},{1,3},{2,0},{3,1},{4,6},{5,7},{6,4},{7,5},{8,10},{9,11},{10,... | collective-permute-start | bytes 3145736 | tf_op jit(solution)/shard_map/ppermute | solution.py:561
  597.1 14.7 %collective-permute-start.58 = (f32[4,768]{1,0:T(4,128)S(1)}, f32[4,768]{1,0:T(4,128)S(1)}, u32[]{:S(2)}, u32[]{:S(2)}) collective-permute-start(f32[4,768]{1,0:T(4,128)S(1)} %get-tuple-element.219), channel_id=1, source_target_pairs={{0,8},{8,16},{16,24},{24,0},{1,9},{9,17},{17,25},{25,1},{2,10},{10... | collective-permute-start | bytes 36872 | tf_op jit(solution)/shard_map/ppermute | solution.py:556
  597.1 15.2 %collective-permute-start.59 = (f32[4,768]{1,0:T(4,128)S(1)}, f32[4,768]{1,0:T(4,128)S(1)}, u32[]{:S(2)}, u32[]{:S(2)}) collective-permute-start(f32[4,768]{1,0:T(4,128)S(1)} %get-tuple-element.220), channel_id=1, source_target_pairs={{0,16},{8,24},{16,0},{24,8},{1,17},{9,25},{17,1},{25,9},{2,18},{10... | collective-permute-start | bytes 36872 | tf_op jit(solution)/shard_map/ppermute | solution.py:556
  611.8 17.3 %collective-permute-start.51 = (bf16[256,2048]{1,0:T(8,128)(2,1)}, bf16[256,2048]{1,0:T(8,128)(2,1)}, u32[]{:S(2)}, u32[]{:S(2)}) collective-permute-start(bf16[256,2048]{1,0:T(8,128)(2,1)} %get-tuple-element.169.refs_0_), channel_id=1, source_target_pairs={{0,1},{1,0},{2,3},{3,2},{4,5},{5,4},{6,7},{7,6},{8,9},{9,8},{10,11... | collective-permute-start | bytes 3145736 | tf_op jit(solution)/shard_map/ppermute | solution.py:564
  612.3 16.8 %collective-permute-start.56 = (bf16[256,2048]{1,0:T(8,128)(2,1)}, bf16[256,2048]{1,0:T(8,128)(2,1)}, u32[]{:S(2)}, u32[]{:S(2)}) collective-permute-start(bf16[256,2048]{1,0:T(8,128)(2,1)} %collective-permute-done.52.refs_2_), channel_id=1, source_target_pairs={{0,1},{1,0},{2,3},{3,2},{4,5},{5,4},{6,7},{7,6},{8,9},{9,8},{10,11... | collective-permute-start | bytes 3145736 | tf_op jit(solution)/shard_map/ppermute | solution.py:564
  612.5 14.8 %collective-permute-start.61 = (f32[4,768]{1,0:T(4,128)S(1)}, f32[4,768]{1,0:T(4,128)S(1)}, u32[]{:S(2)}, u32[]{:S(2)}) collective-permute-start(f32[4,768]{1,0:T(4,128)S(1)} %reduce_sum.29), channel_id=1, source_target_pairs={{0,4},{4,0},{1,5},{5,1},{2,6},{6,2},{3,7},{7,3},{8,12},{12,8},{9,1... | collective-permute-start | bytes 36872 | tf_op jit(solution)/shard_map/ppermute | solution.py:559
  (67 other events, 365.8 us)
Sparse Core Ops, SparseCore 0:
  92.2 106.0 all-gather.3
  211.7 55.9 all-gather.5
  296.7 53.0 reduce-scatter.3
  367.0 98.9 reduce-scatter.5
  468.1 27.6 reduce-scatter.7
  524.4 50.7 all-gather.7

commit v5 on v4

--- a/solution.py
+++ b/solution.py
@@ -527,6 +527,25 @@
         compiler_params=pltpu.CompilerParams(vmem_limit_bytes=VMEM_BYTES),
         name="grad_qkv",
     )(mine, theirs, my_grad, their_grad, *behind)
+
+
+def turn(value, behind=()):
+    count, rows, cols = value.shape
+    tn = tiles(cols, 128)
+
+    def kernel(value_ref, *refs):
+        refs[-1][...] = value_ref[...].astype(F32).T
+
+    return pl.pallas_call(
+        kernel,
+        grid=(count, cols // tn),
+        in_specs=[pl.BlockSpec((None, rows, tn), lambda c, j: (c, 0, j))] + [ANYWHERE] * len(behind),
+        out_specs=pl.BlockSpec((None, tn, rows), lambda c, j: (c, j, 0)),
+        out_shape=jax.ShapeDtypeStruct((count, cols, rows), F32),
+        cost_estimate=light(flops=count * rows * cols, bytes_accessed=6 * count * rows * cols, transcendentals=0),
+        compiler_params=pltpu.CompilerParams(vmem_limit_bytes=VMEM_BYTES),
+        name="turn",
+    )(value, *behind)
 
 
 class Place:
@@ -1000,13 +1019,14 @@
         one_sum.shares, inputs, gains[0], grad_middle, [LOW], behind=[one_next, qkv_next]
     )
     gate_up_out = lax.all_gather(gate_up_sum, "context", axis=1, tiled=True)
-    gate_up_out = gate_up_out.transpose(0, 2, 1).astype(F32)
+    gate_up_out = turn(gate_up_out)
     sums = after(jnp.concatenate([sums_one, sums_two]), layer_rows.over_y)
     sums = total_over(place, sums, "y")
     input_rows = WholeRows(place, after(input_low, sums), seqs)
+    layer_out = layer_rows.whole(LOW)
     totals = small_totals(
         place,
-        after(sums, qkv_shards.low, qkv_shards.high, gate_up_out),
+        after(sums, qkv_shards.low, qkv_shards.high, gate_up_out, input_rows.over_y, layer_out),
         jnp.sum(grad_mixed.astype(F32), axis=1),
         jnp.sum(grad_mixed_other.astype(F32), axis=1),
     )
@@ -1014,7 +1034,6 @@
     qkv_gathered = Gathered(place, qkv_sum, 2)
     out_gathered = Gathered(place, after(out_sum, qkv_sum), 1)
     sums, grad_bias = last_totals(place, after(totals, qkv_sum), norm_gains.shape[1])
-    layer_out = layer_rows.whole(LOW)
     input_grad = input_rows.whole(F32, [qkv_gathered.raw])
 
     return (

time: 648 us -> 636 us (0.981)
  waiting for transfers between devices: 216 us -> 207 us
  Pallas kernels: 258 us -> 265 us
    ppermute x11, waiting for transfers between devices: 60.7 us -> 45.2 us  [shift(): return lax.ppermute(value, 'fsdp', [(i, (i + step) % n) for i in range(n)])]
    ppermute x17, waiting for transfers between devices: 73.5 us -> 80.5 us  [shift(): lax.ppermute(value, 'tensor', [(i, (i + 2 * step) % n) for i in range(n)])]
    pallas_call x0 -> x1, Pallas kernels: none -> 6.96 us  [turn(): pl.pallas_call(kernel, grid=(count, cols // tn), in_specs=[pl.BlockSpec((...]
    unnamed x128 -> x133, local copies, waits for them, and re-layouts: 30.2 us -> 24.9 us
  transfers between devices with their start and end apart: 69 -> 69, of which waited for: 30 -> 31; matrix products, arithmetic and copies ran while one was open for 11% -> 10% of each run, Pallas kernels for 39% -> 40%
where the time goes in v5:
time: 636 us; the launch traced here: 632 us
  Pallas kernels  265 us (42%)
  waiting for transfers between devices  207 us (33%)
  starting transfers between devices  57.8 us (9%)
  local copies, waits for them, and re-layouts  51.6 us (8%)
  other arithmetic  23.1 us (4%)
  between operations  15.5 us (2%)
  matrix products  12.2 us (2%)
    ppermute x18, waiting for transfers between devices, shift(): lax.ppermute(value, 'context', [(i, (i + step) % n) for i in range(n)])  80.9 us
    ppermute x17, waiting for transfers between devices, shift(): lax.ppermute(value, 'tensor', [(i, (i + 2 * step) % n) for i in range(n)])  80.5 us
    pallas_call x4, Pallas kernels, products_apart(): pl.pallas_call(kernel, grid_spec=pltpu.PrefetchScalarGridSpec(num_scalar_...  52.6 us
    ppermute x11, waiting for transfers between devices, shift(): return lax.ppermute(value, 'fsdp', [(i, (i + step) % n) for i in range(n)])  45.2 us
    pallas_call x5, Pallas kernels, products(): pl.pallas_call(kernel, grid=(many, rows // tm, cols // tn), in_specs=ones...  44.2 us
    pallas_call x6, Pallas kernels, pieces_of(): pl.pallas_call(kernel, grid_spec=pltpu.PrefetchScalarGridSpec(num_scalar_...  36.1 us
    unnamed x133, local copies, waits for them, and re-layouts  24.9 us
    pallas_call x2, Pallas kernels, gate_up(): pl.pallas_call(gate_kernel, grid=(rows // tm,), in_specs=[pl.BlockSpec((2...  23.9 us
  transfers between devices with their start and end apart: 69, of which 31 were waited for; matrix products, arithmetic and copies ran while one was open for 10% of the time, Pallas kernels for 40%

profile of v5, /device:TPU:0, one launch (start us, length us, event | category | flops | bytes accessed | tf_op | source)
XLA Modules:
  0.0 631.6 jit_solution(12738399224941332514)
XLA Ops:
  12.4 3.0 collective-permute-start
  17.5 3.8 dynamic-slice_bitcast_fusion.2
  27.2 2.6 copy.31
  29.9 17.8 %collective-permute-done.2.refs_2_ = bf16[256,2048]{1,0:T(8,128)(2,1)} collective-permute-done((bf16[256,2048]{1,0:T(8,128)(2,1)}, bf16[256,2048]{1,0:T(8,128)(2,1)}, u32[]{:S(2)}, u32[]{:S(2)}) %collective-permute-start.2) | collective-permute-done | bytes 1048608 | tf_op jit(solution)/shard_map/ppermute | solution.py:578
  47.7 16.5 %collective-permute-done.1 = bf16[4,528,256]{2,1,0:T(8,128)(2,1)} collective-permute-done((bf16[4,528,256]{2,1,0:T(8,128)(2,1)}, bf16[4,528,256]{2,1,0:T(8,128)(2,1)}, u32[]{:S(2)}, u32[]{:S(2)}) %collective-permute-start.1) | collective-permute-done | bytes 1081376 | tf_op jit(solution)/shard_map/ppermute | solution.py:575
  67.6 2.8 collective-permute-start.5
  75.3 16.7 %collective-permute-done.5 = bf16[2,512,256]{2,1,0:T(8,128)(2,1)S(1)} collective-permute-done((bf16[2,512,256]{2,1,0:T(8,128)(2,1)S(1)}, bf16[2,512,256]{2,1,0:T(8,128)(2,1)S(1)}, u32[]{:S(2)}, u32[]{:S(2)}) %collective-permute-start.5) | collective-permute-done | bytes 524320 | tf_op jit(solution)/shard_map/ppermute | solution.py:575
  93.7 3.5 collective-permute-done.7.refs_0_.refs_3_
  98.2 7.6 %norm_first.1 = bf16[4,256,2048]{2,1,0:T(8,128)(2,1)} custom-call(s32[4]{0:T(128)} %add_add_fusion.1.at_ref, bf16[256,2048]{1,0:T(8,128)(2,1)} %get-tuple-element.194.refs_0_, bf16[256,2048]{1,0:T(8,128)(2,1)} %get-tuple-element.193.refs_1_, bf16[256,2048]{1,0:T(8,128)(2,1)} %collective-permute-done.2.refs_2_, bf16[256,2048]{1,0:T(8,128)(2,1)} %copy-done.34, ...), custom_call_target="tpu_custom_call" | custom-call | bytes 83886 | tf_op jit(solution)/shard_map/norm_first/pallas_call | solution.py:358
  108.0 2.4 slice_dynamic-update-slice_fusion.1
  117.6 7.1 %fusion.5.r_0_ = f32[1,3,1024,256]{3,2,1,0:T(8,128)} fusion(bf16[1024,2048,1]{1,0,2:T(8,128)(2,1)S(1)} %bitcast.128, bf16[4,2048,256]{2,1,0:T(8,128)(2,1)} %constant_dynamic-update-slice_fusion.refs_2_.refs_1_.refs_6_.refs_7_.refs_8_), kind=kOutput, calls=%fused_computation.8 | convolution fusion | flops 3221225472 | bytes 10485760 | tf_op jit(solution)/shard_map/rd,cde->cre/dot_general | solution.py:909
  124.7 9.4 %attend_forward.2 = (bf16[1,1024,256]{2,1,0:T(8,128)(2,1)S(1)}, bf16[1,1024,256]{2,1,0:T(8,128)(2,1)S(1)}, bf16[1,1024,256]{2,1,0:T(8,128)(2,1)S(1)}, bf16[1,102...) custom-call(f32[1,3,1024,256]{3,2,1,0:T(8,128)} %fusion.5.r_0_, f32[1,3,1,256]{3,2,1,0:T(1,128)S(1)} %copy.23.r_1_, ...), custom_call_target="tpu_custom_call" | custom-call | flops 6442450 | bytes 68157 | tf_op jit(solution)/shard_map/attend_forward/pallas_call | solution.py:85
  134.1 5.1 fusion.8.r_0_
  139.2 2.6 collective-permute-done.9.r_4_.refs_3_
  141.8 10.0 %attend_forward.3 = (bf16[1,1024,256]{2,1,0:T(8,128)(2,1)S(1)}, bf16[1,1024,256]{2,1,0:T(8,128)(2,1)S(1)}, bf16[1,1024,256]{2,1,0:T(8,128)(2,1)S(1)}, bf16[1,102...) custom-call(f32[1,3,1024,256]{3,2,1,0:T(8,128)} %fusion.8.r_0_, f32[1,3,1,256]{3,2,1,0:T(1,128)S(1)} %reshape.85.r_1_, ...), custom_call_target="tpu_custom_call" | custom-call | flops 6442450 | bytes 68157 | tf_op jit(solution)/shard_map/attend_forward/pallas_call | solution.py:85
  154.2 7.5 %out.1 = (bf16[2,256,1024]{2,1,0:T(8,128)(2,1)}, bf16[2,256,1024]{2,1,0:T(8,128)(2,1)}, bf16[2,256,1024]{2,1,0:T(8,128)(2,1)}, bf16[2,256,1024]{2,1,0:T(8,128)(2,1)}) custom-call(s32[2]{0:T(128)} %pad_add_fusion.1.at_ref, bf16[1024,256]{1,0:T(8,128)(2,1)} %bitcast.107, bf16[1024,256]{1,0:T(8,128)(2,1)} %bitcast.109, ...), custom_call_target="tpu_custom_call" | custom-call | flops 21474836 | bytes 73400 | tf_op jit(solution)/shard_map/out/pallas_call | solution.py:246
  164.8 5.3 lay_pieces.1
  170.1 16.8 %collective-permute-done.10.two = bf16[2,256,1024]{2,1,0:T(8,128)(2,1)S(1)} collective-permute-done((bf16[2,256,1024]{2,1,0:T(8,128)(2,1)}, bf16[2,256,1024]{2,1,0:T(8,128)(2,1)S(1)}, u32[]{:S(2)}, u32[]{:S(2)}) %collective-permute-start.10) | collective-permute-done | bytes 1048608 | tf_op jit(solution)/shard_map/ppermute | solution.py:578
  189.0 3.5 join.4
  194.7 10.6 %collective-permute-done.12.refs_1_ = bf16[256,1024]{1,0:T(8,128)(2,1)S(1)} collective-permute-done((bf16[256,1024]{1,0:T(8,128)(2,1)}, bf16[256,1024]{1,0:T(8,128)(2,1)S(1)}, u32[]{:S(2)}, u32[]{:S(2)}) %collective-permute-start.12) | collective-permute-done | bytes 524320 | tf_op jit(solution)/shard_map/ppermute | solution.py:580
  207.4 3.5 add_norm.1
  213.1 24.3 %collective-permute-done.16.refs_2_ = bf16[256,2048]{1,0:T(8,128)(2,1)S(1)} collective-permute-done((bf16[256,2048]{1,0:T(8,128)(2,1)}, bf16[256,2048]{1,0:T(8,128)(2,1)S(1)}, u32[]{:S(2)}, u32[]{:S(2)}) %collective-permute-start.16) | collective-permute-done | bytes 1048608 | tf_op jit(solution)/shard_map/ppermute | solution.py:580
  242.2 9.9 %collective-permute-done.17.refs_3_ = bf16[256,1024]{1,0:T(8,128)(2,1)S(1)} collective-permute-done((bf16[256,1024]{1,0:T(8,128)(2,1)}, bf16[256,1024]{1,0:T(8,128)(2,1)S(1)}, u32[]{:S(2)}, u32[]{:S(2)}) %collective-permute-start.17) | collective-permute-done | bytes 524320 | tf_op jit(solution)/shard_map/ppermute | solution.py:578
  252.1 2.6 collective-permute-done.18.refs_4_
  254.7 5.9 lay_rows.4
  260.7 12.0 %gate_up.3 = (bf16[704,1024]{1,0:T(8,128)(2,1)}, bf16[2,704,1024]{2,1,0:T(8,128)(2,1)}, bf16[1024,704]{1,0:T(8,128)(2,1)}) custom-call(bf16[2,704,2048]{2,1,0:T(8,128)(2,1)} %collective-permute-done.21.weight_ref.refs_6_.refs_7_, bf16[1024,2048]{1,0:T(8,128)(2,1)} %bitcast.118), custom_call_target="tpu_custom_call" | custom-call | flops 59055800 | bytes 157286 | tf_op jit(solution)/shard_map/gate_up/pallas_call | solution.py:285
  273.2 11.9 %gate_up.2 = (bf16[704,1024]{1,0:T(8,128)(2,1)}, bf16[2,704,1024]{2,1,0:T(8,128)(2,1)}, bf16[1024,704]{1,0:T(8,128)(2,1)}) custom-call(bf16[2,704,2048]{2,1,0:T(8,128)(2,1)} %all-gather.4.cloned.1.call-done.weight_ref.refs_4_.refs_5_, bf16[1024,2048]{1,0:T(8,128)(2,1)} %bitcast.119), custom_call_target="tpu_custom_call" | custom-call | flops 59055800 | bytes 157286 | tf_op jit(solution)/shard_map/gate_up/pallas_call | solution.py:285
  286.3 10.2 %grad_down.1.refs_0_ = bf16[704,2048]{1,0:T(8,128)(2,1)} custom-call(bf16[704,1024]{1,0:T(8,128)(2,1)} %get-tuple-element.118.refs_0_, bf16[704,1024]{1,0:T(8,128)(2,1)} %copy-done.46, bf16[1024,2048]{1,0:T(8,128)(2,1)} %bitcast.115, bf16[1024,2048]{1,0:T(8,128)(2,1)} %collective-permute-done.19.refs_5_.refs_3_), custom_call_target="tpu_custom_call" | custom-call | flops 59055800 | bytes 141557 | tf_op jit(solution)/shard_map/grad_down/pallas_call | solution.py:196
  296.7 8.9 %hidden_back.2 = (bf16[2,704,1024]{2,1,0:T(8,128)(2,1)}, bf16[2,1024,704]{2,1,0:T(8,128)(2,1)}) custom-call(bf16[704,2048]{1,0:T(8,128)(2,1)} %collective-permute-done.22.weight_ref.refs_3_, bf16[1024,2048]{1,0:T(8,128)(2,1)} %bitcast.116, bf16[2,704,1024]{2,1,0:T(8,128)(2,1)} %get-tuple-element.117.slope_ref, bf16[704,2048]{1,0:T(8,128)(2,1)} %grad_down.1.refs_0_), custom_call_target="tpu_custom_call" | custom-call | flops 29527900 | bytes 157286 | tf_op jit(solution)/shard_map/hidden_back/pallas_call | solution.py:325
  306.2 8.6 %hidden_back.3 = (bf16[2,704,1024]{2,1,0:T(8,128)(2,1)}, bf16[2,1024,704]{2,1,0:T(8,128)(2,1)}) custom-call(bf16[704,2048]{1,0:T(8,128)(2,1)} %all-gather.6.cloned.1.call-done.weight_ref.refs_2_, bf16[1024,2048]{1,0:T(8,128)(2,1)} %bitcast.117, bf16[2,704,1024]{2,1,0:T(8,128)(2,1)} %get-tuple-element.116.slope_ref, ...), custom_call_target="tpu_custom_call" | custom-call | flops 29527900 | bytes 157286 | tf_op jit(solution)/shard_map/hidden_back/pallas_call | solution.py:325
  316.9 20.2 %grad_two.1 = (bf16[2,256,1024]{2,1,0:T(8,128)(2,1)}, bf16[2,256,1024]{2,1,0:T(8,128)(2,1)}, bf16[2,256,1024]{2,1,0:T(8,128)(2,1)}, bf16[2,256,1024]{2,1,0:T(8,128)(2,1)}) custom-call(s32[2]{0:T(128)} %pad_add_fusion.1.at_ref, bf16[2,1024,704]{2,1,0:T(8,128)(2,1)} %get-tuple-element.120.refs_0_.refs_1_, ...), custom_call_target="tpu_custom_call" | custom-call | flops 118111600 | bytes 214958 | tf_op jit(solution)/shard_map/grad_two/pallas_call | solution.py:246
  338.2 18.1 %grad_gate_up.1.refs_0_ = bf16[2,704,2048]{2,1,0:T(8,128)(2,1)} custom-call(bf16[2,704,1024]{2,1,0:T(8,128)(2,1)} %get-tuple-element.126.refs_0_, bf16[2,704,1024]{2,1,0:T(8,128)(2,1)} %collective-permute-done.25.refs_9_.refs_1_, bf16[1024,2048]{1,0:T(8,128)(2,1)} %bitcast.121, bf16[1024,2048]{1,0:T(8,128)(2,1)} %copy-done.30, ...), custom_call_target="tpu_custom_call" | custom-call | flops 118111600 | bytes 283115 | tf_op jit(solution)/shard_map/grad_gate_up/pallas_call | solution.py:196
  356.2 6.1 collective-permute-done.26.two
  363.3 3.5 join.5
  369.0 12.5 %down.1 = (bf16[2,256,1024]{2,1,0:T(8,128)(2,1)}, bf16[2,256,1024]{2,1,0:T(8,128)(2,1)}, bf16[2,256,1024]{2,1,0:T(8,128)(2,1)}, bf16[2,256,1024]{2,1,0:T(8,128)(2,1)}) custom-call(s32[2]{0:T(128)} %pad_add_fusion.1.at_ref, bf16[1024,704]{1,0:T(8,128)(2,1)} %get-tuple-element.109.refs_0_, bf16[1024,704]{1,0:T(8,128)(2,1)} %get-tuple-element.112.refs_1_, ...), custom_call_target="tpu_custom_call" | custom-call | flops 59055800 | bytes 128450 | tf_op jit(solution)/shard_map/down/pallas_call | solution.py:246
  382.6 4.8 norm_back.2
  390.5 21.7 %collective-permute-done.31.refs_2_ = bf16[256,2048]{1,0:T(8,128)(2,1)S(1)} collective-permute-done((bf16[256,2048]{1,0:T(8,128)(2,1)}, bf16[256,2048]{1,0:T(8,128)(2,1)S(1)}, u32[]{:S(2)}, u32[]{:S(2)}) %collective-permute-start.31) | collective-permute-done | bytes 1048608 | tf_op jit(solution)/shard_map/ppermute | solution.py:580
  414.8 10.0 %collective-permute-done.32.refs_3_ = bf16[256,1024]{1,0:T(8,128)(2,1)S(1)} collective-permute-done((bf16[256,1024]{1,0:T(8,128)(2,1)S(1)}, bf16[256,1024]{1,0:T(8,128)(2,1)S(1)}, u32[]{:S(2)}, u32[]{:S(2)}) %collective-permute-start.32) | collective-permute-done | bytes 524320 | tf_op jit(solution)/shard_map/ppermute | solution.py:578
  426.5 5.3 lay_rows.5
  434.4 4.5 grad_att.2
  440.0 11.2 %attend_back.2 = bf16[1,3,1024,256]{3,2,1,0:T(8,128)(2,1)S(1)} custom-call(bf16[1,1024,256]{2,1,0:T(8,128)(2,1)S(1)} %copy-done.23, bf16[1,1024,256]{2,1,0:T(8,128)(2,1)S(1)} %copy-done.25, bf16[1,1024,256]{2,1,0:T(8,128)(2,1)S(1)} %copy-done.27, bf16[1,1024,256]{2,1,0:T(8,128)(2,1)S(1)} %copy-done.11, f32[1,1024,256]{2,1,0:T(8,128)S(1)} %get-tuple-element.141.r_4_, ...), custom_call_target="tpu_custom_call" | custom-call | flops 16106127 | bytes 52428 | tf_op jit(solution)/shard_map/attend_back/pallas_call | solution.py:145
  452.3 6.7 %grad_out.1.refs_0_ = bf16[2048,256]{1,0:T(8,128)(2,1)} custom-call(bf16[1024,2048]{1,0:T(8,128)(2,1)} %bitcast.124, bf16[1024,2048]{1,0:T(8,128)(2,1)} %collective-permute-done.36.refs_1_, bf16[1024,256]{1,0:T(8,128)(2,1)} %bitcast.108, bf16[1024,256]{1,0:T(8,128)(2,1)} %copy-done.44, bf16[3,1024,256]{2,1,0:T(8,128)(2,1)} %bitcast.103), custom_call_target="tpu_custom_call" | custom-call | flops 21474836 | bytes 104857 | tf_op jit(solution)/shard_map/grad_out/pallas_call | solution.py:196
  460.1 3.7 join.6
  465.5 4.7 grad_att.3
  471.3 11.2 %attend_back.3 = bf16[1,3,1024,256]{3,2,1,0:T(8,128)(2,1)S(1)} custom-call(bf16[1,1024,256]{2,1,0:T(8,128)(2,1)S(1)} %copy-done.17, bf16[1,1024,256]{2,1,0:T(8,128)(2,1)S(1)} %copy-done.19, bf16[1,1024,256]{2,1,0:T(8,128)(2,1)S(1)} %copy-done.21, bf16[1,1024,256]{2,1,0:T(8,128)(2,1)S(1)} %copy-done.8, f32[1,1024,256]{2,1,0:T(8,128)S(1)} %copy-done.15, ...), custom_call_target="tpu_custom_call" | custom-call | flops 16106127 | bytes 52428 | tf_op jit(solution)/shard_map/attend_back/pallas_call | solution.py:145
  483.7 4.6 collective-permute-done.38.refs_3_
  489.1 3.4 add_low.1.refs_12_.refs_0_
  493.5 12.4 %grad_one.1 = (bf16[2,256,1024]{2,1,0:T(8,128)(2,1)}, bf16[2,256,1024]{2,1,0:T(8,128)(2,1)}, bf16[2,256,1024]{2,1,0:T(8,128)(2,1)}, bf16[2,256,1024]{2,1,0:T(8,128)(2,1)}) custom-call(s32[2]{0:T(128)} %pad_add_fusion.1.at_ref, bf16[3,1024,256]{2,1,0:T(8,128)(2,1)} %bitcast.98, bf16[3,1024,256]{2,1,0:T(8,128)(2,1)} %bitcast.99, ...), custom_call_target="tpu_custom_call" | custom-call | flops 64424508 | bytes 136314 | tf_op jit(solution)/shard_map/grad_one/pallas_call | solution.py:246
  507.6 10.9 %grad_qkv.1.refs_0_ = bf16[3,2048,256]{2,1,0:T(8,128)(2,1)} custom-call(bf16[1024,2048]{1,0:T(8,128)(2,1)} %bitcast.127, bf16[1024,2048]{1,0:T(8,128)(2,1)} %collective-permute-done.20.refs_6_.theirs_ref, bf16[3,1024,256]{2,1,0:T(8,128)(2,1)} %bitcast.101, bf16[3,1024,256]{2,1,0:T(8,128)(2,1)} %collective-permute-done.42.their_ref, ...), custom_call_target="tpu_custom_call" | custom-call | flops 64424508 | bytes 146800 | tf_op jit(solution)/shard_map/grad_qkv/pallas_call | solution.py:516
  521.1 3.8 collective-permute-start.49
  524.9 5.5 collective-permute-done.40.two
  531.3 3.5 join.7
  536.6 10.8 %collective-permute-done.43.refs_1_ = bf16[256,1024]{1,0:T(8,128)(2,1)} collective-permute-done((bf16[256,1024]{1,0:T(8,128)(2,1)}, bf16[256,1024]{1,0:T(8,128)(2,1)}, u32[]{:S(2)}, u32[]{:S(2)}) %collective-permute-start.43) | collective-permute-done | bytes 524320 | tf_op jit(solution)/shard_map/ppermute | solution.py:580
  547.4 5.1 collective-permute-done.44.refs_3_
  553.7 2.5 collective-permute-done.49
  559.4 4.8 norm_back.3
  564.2 3.6 collective-permute-done.53
  575.6 5.1 collective-permute-done.54
  584.0 3.4 maximum_convert_fusion.1
  588.7 2.7 collective-permute-done.62
  591.4 5.3 lay_rows.6
  596.7 7.0 %turn.1 = f32[2,512,1408]{2,1,0:T(8,128)} custom-call(bf16[2,1408,512]{2,1,0:T(8,128)(2,1)} %all-gather.8.cloned.1.call-done.value_ref), custom_call_target="tpu_custom_call" | custom-call | flops 14417 | bytes 86507 | tf_op jit(solution)/shard_map/turn/pallas_call | solution.py:539
  606.0 3.7 collective-permute-start.60
  617.6 6.6 %lay_rows.7 = f32[4,256,2048]{2,1,0:T(8,128)} custom-call(s32[4]{0:T(128)} %pad_add_fusion.at_ref, bf16[256,2048]{1,0:T(8,128)(2,1)} %get-tuple-element.169.refs_0_, bf16[256,2048]{1,0:T(8,128)(2,1)} %collective-permute-done.51.refs_1_, bf16[256,2048]{1,0:T(8,128)(2,1)} %collective-permute-done.52.refs_2_, bf16[256,2048]{1,0:T(8,128)(2,1)} %collective-permute-done.56.refs_3_), custom_call_target="tpu_custom_call" | custom-call | bytes 83886 | tf_op jit(solution)/shard_map/lay_rows/pallas_call | solution.py:358
  (323 shorter events, 114.6 us)
Async XLA Ops:
  7.2 203.7 %all-gather.4.cloned.1.call-start = ((), (), s32[]{:S(2)}) async-start(), calls=%async_computation.3 | async-start | bytes 7208960 | tf_op jit(solution)/shard_map/all_gather | solution.py:903
  12.4 35.3 %collective-permute-start = (bf16[4,528,256]{2,1,0:T(8,128)(2,1)}, bf16[4,528,256]{2,1,0:T(8,128)(2,1)}, u32[]{:S(2)}, u32[]{:S(2)}) collective-permute-start(bf16[4,528,256]{2,1,0:T(8,128)(2,1)} %fusion.11), channel_id=1, source_target_pairs={{0,8},{8,16},{16,24},{24,0},{1,9},{9,17},{17,25},{25,1},{2,10},{10... | collective-permute-start | bytes 3244040 | tf_op jit(solution)/shard_map/ppermute | solution.py:575
  15.4 48.8 %collective-permute-start.1 = (bf16[4,528,256]{2,1,0:T(8,128)(2,1)}, bf16[4,528,256]{2,1,0:T(8,128)(2,1)}, u32[]{:S(2)}, u32[]{:S(2)}) collective-permute-start(bf16[4,528,256]{2,1,0:T(8,128)(2,1)} %fusion.11), channel_id=1, source_target_pairs={{0,24},{8,0},{16,8},{24,16},{1,25},{9,1},{17,9},{25,17},{2,26},{10... | collective-permute-start | bytes 3244040 | tf_op jit(solution)/shard_map/ppermute | solution.py:575
  21.3 26.4 %collective-permute-start.2 = (bf16[256,2048]{1,0:T(8,128)(2,1)}, bf16[256,2048]{1,0:T(8,128)(2,1)}, u32[]{:S(2)}, u32[]{:S(2)}) collective-permute-start(bf16[256,2048]{1,0:T(8,128)(2,1)} %get-tuple-element.195.refs_4_), channel_id=1, source_target_pairs={{0,4},{4,0},{1,5},{5,1},{2,6},{6,2},{3,7},{7,3},{8,12},{12,8},{9,1... | collective-permute-start | bytes 3145736 | tf_op jit(solution)/shard_map/ppermute | solution.py:578
  24.9 50.4 %collective-permute-start.6 = (bf16[256,2048]{1,0:T(8,128)(2,1)}, bf16[256,2048]{1,0:T(8,128)(2,1)}, u32[]{:S(2)}, u32[]{:S(2)}) collective-permute-start(bf16[256,2048]{1,0:T(8,128)(2,1)} %get-tuple-element.192.refs_5_), channel_id=1, source_target_pairs={{0,4},{4,0},{1,5},{5,1},{2,6},{6,2},{3,7},{7,3},{8,12},{12,8},{9,1... | collective-permute-start | bytes 3145736 | tf_op jit(solution)/shard_map/ppermute | solution.py:578
  65.3 26.7 %collective-permute-start.4 = (bf16[2,528,256]{2,1,0:T(8,128)(2,1)S(1)}, bf16[2,528,256]{2,1,0:T(8,128)(2,1)}, u32[]{:S(2)}, u32[]{:S(2)}) collective-permute-start(bf16[2,528,256]{2,1,0:T(8,128)(2,1)S(1)} %slice.159), channel_id=1, source_target_pairs={{0,8},{8,16},{16,24},{24,0},{1,9},{9,17},{17,25},{25,1},{2,10},{10... | collective-permute-start | bytes 1622024 | tf_op jit(solution)/shard_map/ppermute | solution.py:575
  67.6 24.4 %collective-permute-start.5 = (bf16[2,512,256]{2,1,0:T(8,128)(2,1)S(1)}, bf16[2,512,256]{2,1,0:T(8,128)(2,1)S(1)}, u32[]{:S(2)}, u32[]{:S(2)}) collective-permute-start(bf16[2,512,256]{2,1,0:T(8,128)(2,1)S(1)} %slice.160), channel_id=1, source_target_pairs={{0,24},{8,0},{16,8},{24,16},{1,25},{9,1},{17,9},{25,17},{2,26},{10... | collective-permute-start | bytes 1572872 | tf_op jit(solution)/shard_map/ppermute | solution.py:575
  73.1 24.1 %collective-permute-start.7 = (bf16[256,2048]{1,0:T(8,128)(2,1)}, bf16[256,2048]{1,0:T(8,128)(2,1)S(1)}, u32[]{:S(2)}, u32[]{:S(2)}) collective-permute-start(bf16[256,2048]{1,0:T(8,128)(2,1)} %collective-permute-done.2.refs_2_), channel_id=1, source_target_pairs={{0,2},{1,3},{2,0},{3,1},{4,6},{5,7},{6,4},{7,5},{8,10},{9,11},{10,... | collective-permute-start | bytes 3145736 | tf_op jit(solution)/shard_map/ppermute | solution.py:580
  92.0 180.6 %all-gather.6.cloned.1.call-start = ((), (), s32[]{:S(2)}) async-start(), calls=%async_computation.4 | async-start | bytes 3604480 | tf_op jit(solution)/shard_map/all_gather | solution.py:904
  115.3 18.7 %collective-permute-start.8 = (bf16[4,2048,256]{2,1,0:T(8,128)(2,1)}, bf16[4,2048,256]{2,1,0:T(8,128)(2,1)S(1)}, u32[]{:S(2)}, u32[]{:S(2)}) collective-permute-start(bf16[4,2048,256]{2,1,0:T(8,128)(2,1)} %constant_dynamic-update-slice_fusion.refs_2_.refs_1_.refs_6_.refs_7_.refs_8_), channel_id=1, source_target_pairs={{0,1},{1,0},{2,3},{3,2},{4,5},{5,4},{6,7},{7,6},{8,9},{9,8},{10,11... | collective-permute-start | bytes 12582920 | tf_op jit(solution)/shard_map/ppermute | solution.py:583
  116.0 25.8 %collective-permute-start.9 = (bf16[256,2048]{1,0:T(8,128)(2,1)}, bf16[256,2048]{1,0:T(8,128)(2,1)S(1)}, u32[]{:S(2)}, u32[]{:S(2)}) collective-permute-start(bf16[256,2048]{1,0:T(8,128)(2,1)} %collective-permute-done.6.refs_2_), channel_id=1, source_target_pairs={{0,2},{1,3},{2,0},{3,1},{4,6},{5,7},{6,4},{7,5},{8,10},{9,11},{10,... | collective-permute-start | bytes 3145736 | tf_op jit(solution)/shard_map/ppermute | solution.py:580
  161.7 25.2 %collective-permute-start.10 = (bf16[2,256,1024]{2,1,0:T(8,128)(2,1)}, bf16[2,256,1024]{2,1,0:T(8,128)(2,1)S(1)}, u32[]{:S(2)}, u32[]{:S(2)}) collective-permute-start(bf16[2,256,1024]{2,1,0:T(8,128)(2,1)} %get-tuple-element.101.refs_4_), channel_id=1, source_target_pairs={{0,4},{4,0},{1,5},{5,1},{2,6},{6,2},{3,7},{7,3},{8,12},{12,8},{9,1... | collective-permute-start | bytes 3145736 | tf_op jit(solution)/shard_map/ppermute | solution.py:578
  163.3 24.8 %collective-permute-start.11 = (bf16[2,256,1024]{2,1,0:T(8,128)(2,1)}, bf16[2,256,1024]{2,1,0:T(8,128)(2,1)S(1)}, u32[]{:S(2)}, u32[]{:S(2)}) collective-permute-start(bf16[2,256,1024]{2,1,0:T(8,128)(2,1)} %get-tuple-element.103), channel_id=1, source_target_pairs={{0,2},{1,3},{2,0},{3,1},{4,6},{5,7},{6,4},{7,5},{8,10},{9,11},{10,... | collective-permute-start | bytes 3145736 | tf_op jit(solution)/shard_map/ppermute | solution.py:580
  164.8 29.9 %collective-permute-start.14 = (bf16[1024,256]{1,0:T(8,128)(2,1)S(1)}, bf16[1024,256]{1,0:T(8,128)(2,1)S(1)}, u32[]{:S(2)}, u32[]{:S(2)}) collective-permute-start(bf16[1024,256]{1,0:T(8,128)(2,1)S(1)} %bitcast.110), channel_id=1, source_target_pairs={{0,1},{1,0},{2,3},{3,2},{4,5},{5,4},{6,7},{7,6},{8,9},{9,8},{10,11... | collective-permute-start | bytes 1572872 | tf_op jit(solution)/shard_map/ppermute | solution.py:583
  192.5 12.8 %collective-permute-start.12 = (bf16[256,1024]{1,0:T(8,128)(2,1)}, bf16[256,1024]{1,0:T(8,128)(2,1)S(1)}, u32[]{:S(2)}, u32[]{:S(2)}) collective-permute-start(bf16[256,1024]{1,0:T(8,128)(2,1)} %get-tuple-element.105), channel_id=1, source_target_pairs={{0,2},{1,3},{2,0},{3,1},{4,6},{5,7},{6,4},{7,5},{8,10},{9,11},{10,... | collective-permute-start | bytes 1572872 | tf_op jit(solution)/shard_map/ppermute | solution.py:580
  194.1 12.5 %collective-permute-start.13 = (bf16[256,1024]{1,0:T(8,128)(2,1)}, bf16[256,1024]{1,0:T(8,128)(2,1)S(1)}, u32[]{:S(2)}, u32[]{:S(2)}) collective-permute-start(bf16[256,1024]{1,0:T(8,128)(2,1)} %get-tuple-element.107), channel_id=1, source_target_pairs={{0,4},{4,0},{1,5},{5,1},{2,6},{6,2},{3,7},{7,3},{8,12},{12,8},{9,1... | collective-permute-start | bytes 1572872 | tf_op jit(solution)/shard_map/ppermute | solution.py:578
  210.9 49.8 %collective-permute-start.21 = (bf16[2,704,2048]{2,1,0:T(8,128)(2,1)}, bf16[2,704,2048]{2,1,0:T(8,128)(2,1)}, u32[]{:S(2)}, u32[]{:S(2)}) collective-permute-start(bf16[2,704,2048]{2,1,0:T(8,128)(2,1)} %all-gather.4.cloned.1.call-done.weight_ref.refs_4_.refs_5_), channel_id=1, source_target_pairs={{0,1},{1,0},{2,3},{3,2},{4,5},{5,4},{6,7},{7,6},{8,9},{9,8},{10,11... | collective-permute-start | bytes 17301512 | tf_op jit(solution)/shard_map/ppermute | solution.py:583
  210.9 31.2 %collective-permute-start.20 = (bf16[1024,2048]{1,0:T(8,128)(2,1)}, bf16[1024,2048]{1,0:T(8,128)(2,1)}, u32[]{:S(2)}, u32[]{:S(2)}) collective-permute-start(bf16[1024,2048]{1,0:T(8,128)(2,1)} %bitcast.126), channel_id=1, source_target_pairs={{0,1},{1,0},{2,3},{3,2},{4,5},{5,4},{6,7},{7,6},{8,9},{9,8},{10,11... | collective-permute-start | bytes 12582920 | tf_op jit(solution)/shard_map/ppermute | solution.py:583
  211.4 43.3 %collective-permute-start.19 = (bf16[1024,2048]{1,0:T(8,128)(2,1)}, bf16[1024,2048]{1,0:T(8,128)(2,1)}, u32[]{:S(2)}, u32[]{:S(2)}) collective-permute-start(bf16[1024,2048]{1,0:T(8,128)(2,1)} %bitcast.114), channel_id=1, source_target_pairs={{0,1},{1,0},{2,3},{3,2},{4,5},{5,4},{6,7},{7,6},{8,9},{9,8},{10,11... | collective-permute-start | bytes 12582920 | tf_op jit(solution)/shard_map/ppermute | solution.py:583
  211.5 151.4 %reduce-scatter.4.cloned.1.call-start = ((), (), s32[]{:S(2)}) async-start(), calls=%async_computation.5 | async-start | bytes 3604480 | tf_op jit(solution)/shard_map/reduce_scatter | solution.py:943
  211.6 25.8 %collective-permute-start.16 = (bf16[256,2048]{1,0:T(8,128)(2,1)}, bf16[256,2048]{1,0:T(8,128)(2,1)S(1)}, u32[]{:S(2)}, u32[]{:S(2)}) collective-permute-start(bf16[256,2048]{1,0:T(8,128)(2,1)} %get-tuple-element.108.refs_0_), channel_id=1, source_target_pairs={{0,2},{1,3},{2,0},{3,1},{4,6},{5,7},{6,4},{7,5},{8,10},{9,11},{10,... | collective-permute-start | bytes 3145736 | tf_op jit(solution)/shard_map/ppermute | solution.py:580
  212.1 27.1 %collective-permute-start.15 = (bf16[256,2048]{1,0:T(8,128)(2,1)}, bf16[256,2048]{1,0:T(8,128)(2,1)S(1)}, u32[]{:S(2)}, u32[]{:S(2)}) collective-permute-start(bf16[256,2048]{1,0:T(8,128)(2,1)} %get-tuple-element.108.refs_0_), channel_id=1, source_target_pairs={{0,4},{4,0},{1,5},{5,1},{2,6},{6,2},{3,7},{7,3},{8,12},{12,8},{9,1... | collective-permute-start | bytes 3145736 | tf_op jit(solution)/shard_map/ppermute | solution.py:578
  238.3 13.8 %collective-permute-start.17 = (bf16[256,1024]{1,0:T(8,128)(2,1)}, bf16[256,1024]{1,0:T(8,128)(2,1)S(1)}, u32[]{:S(2)}, u32[]{:S(2)}) collective-permute-start(bf16[256,1024]{1,0:T(8,128)(2,1)} %slice.215), channel_id=1, source_target_pairs={{0,4},{4,0},{1,5},{5,1},{2,6},{6,2},{3,7},{7,3},{8,12},{12,8},{9,1... | collective-permute-start | bytes 1572872 | tf_op jit(solution)/shard_map/ppermute | solution.py:578
  241.1 13.6 %collective-permute-start.18 = (bf16[256,1024]{1,0:T(8,128)(2,1)}, bf16[256,1024]{1,0:T(8,128)(2,1)}, u32[]{:S(2)}, u32[]{:S(2)}) collective-permute-start(bf16[256,1024]{1,0:T(8,128)(2,1)} %slice.216), channel_id=1, source_target_pairs={{0,2},{1,3},{2,0},{3,1},{4,6},{5,7},{6,4},{7,5},{8,10},{9,11},{10,... | collective-permute-start | bytes 1572872 | tf_op jit(solution)/shard_map/ppermute | solution.py:580
  272.7 12.5 %collective-permute-start.23 = (bf16[704,1024]{1,0:T(8,128)(2,1)}, bf16[704,1024]{1,0:T(8,128)(2,1)S(1)}, u32[]{:S(2)}, u32[]{:S(2)}) collective-permute-start(bf16[704,1024]{1,0:T(8,128)(2,1)} %get-tuple-element.114), channel_id=1, source_target_pairs={{0,1},{1,0},{2,3},{3,2},{4,5},{5,4},{6,7},{7,6},{8,9},{9,8},{10,11... | collective-permute-start | bytes 4325384 | tf_op jit(solution)/shard_map/ppermute | solution.py:583
  272.7 24.0 %collective-permute-start.22 = (bf16[704,2048]{1,0:T(8,128)(2,1)}, bf16[704,2048]{1,0:T(8,128)(2,1)}, u32[]{:S(2)}, u32[]{:S(2)}) collective-permute-start(bf16[704,2048]{1,0:T(8,128)(2,1)} %all-gather.6.cloned.1.call-done.weight_ref.refs_2_), channel_id=1, source_target_pairs={{0,1},{1,0},{2,3},{3,2},{4,5},{5,4},{6,7},{7,6},{8,9},{9,8},{10,11... | collective-permute-start | bytes 8650760 | tf_op jit(solution)/shard_map/ppermute | solution.py:583
  296.5 211.1 %reduce-scatter.6.cloned.1.call-start = ((), (), s32[]{:S(2)}) async-start(), calls=%async_computation.6 | async-start | bytes 7208960 | tf_op jit(solution)/shard_map/reduce_scatter | solution.py:966
  296.6 18.2 %collective-permute-start.24 = (bf16[1024,2048]{1,0:T(8,128)(2,1)}, bf16[1024,2048]{1,0:T(8,128)(2,1)S(1)}, u32[]{:S(2)}, u32[]{:S(2)}) collective-permute-start(bf16[1024,2048]{1,0:T(8,128)(2,1)} %bitcast.120), channel_id=1, source_target_pairs={{0,1},{1,0},{2,3},{3,2},{4,5},{5,4},{6,7},{7,6},{8,9},{9,8},{10,11... | collective-permute-start | bytes 12582920 | tf_op jit(solution)/shard_map/ppermute | solution.py:583
  305.6 9.2 %collective-permute-start.25 = (bf16[2,704,1024]{2,1,0:T(8,128)(2,1)}, bf16[2,704,1024]{2,1,0:T(8,128)(2,1)}, u32[]{:S(2)}, u32[]{:S(2)}) collective-permute-start(bf16[2,704,1024]{2,1,0:T(8,128)(2,1)} %get-tuple-element.121), channel_id=1, source_target_pairs={{0,1},{1,0},{2,3},{3,2},{4,5},{5,4},{6,7},{7,6},{8,9},{9,8},{10,11... | collective-permute-start | bytes 8650760 | tf_op jit(solution)/shard_map/ppermute | solution.py:583
  337.1 25.3 %collective-permute-start.26 = (bf16[2,256,1024]{2,1,0:T(8,128)(2,1)}, bf16[2,256,1024]{2,1,0:T(8,128)(2,1)S(1)}, u32[]{:S(2)}, u32[]{:S(2)}) collective-permute-start(bf16[2,256,1024]{2,1,0:T(8,128)(2,1)} %get-tuple-element.123.refs_4_), channel_id=1, source_target_pairs={{0,4},{4,0},{1,5},{5,1},{2,6},{6,2},{3,7},{7,3},{8,12},{12,8},{9,1... | collective-permute-start | bytes 3145736 | tf_op jit(solution)/shard_map/ppermute | solution.py:578
  337.8 25.2 %collective-permute-start.27 = (bf16[2,256,1024]{2,1,0:T(8,128)(2,1)}, bf16[2,256,1024]{2,1,0:T(8,128)(2,1)}, u32[]{:S(2)}, u32[]{:S(2)}) collective-permute-start(bf16[2,256,1024]{2,1,0:T(8,128)(2,1)} %get-tuple-element.125), channel_id=1, source_target_pairs={{0,2},{1,3},{2,0},{3,1},{4,6},{5,7},{6,4},{7,5},{8,10},{9,11},{10,... | collective-permute-start | bytes 3145736 | tf_op jit(solution)/shard_map/ppermute | solution.py:580
  366.8 216.2 %reduce-scatter.8.cloned.1.call-start = ((), (), s32[]{:S(2)}) async-start(), calls=%async_computation.8 | async-start | bytes 1310720 | tf_op jit(solution)/shard_map/reduce_scatter | solution.py:1001
  367.8 13.8 %collective-permute-start.28 = (bf16[256,1024]{1,0:T(8,128)(2,1)S(1)}, bf16[256,1024]{1,0:T(8,128)(2,1)S(1)}, u32[]{:S(2)}, u32[]{:S(2)}) collective-permute-start(bf16[256,1024]{1,0:T(8,128)(2,1)S(1)} %copy-done.64), channel_id=1, source_target_pairs={{0,2},{1,3},{2,0},{3,1},{4,6},{5,7},{6,4},{7,5},{8,10},{9,11},{10,... | collective-permute-start | bytes 1572872 | tf_op jit(solution)/shard_map/ppermute | solution.py:580
  368.0 13.6 %collective-permute-start.29 = (bf16[256,1024]{1,0:T(8,128)(2,1)S(1)}, bf16[256,1024]{1,0:T(8,128)(2,1)S(1)}, u32[]{:S(2)}, u32[]{:S(2)}) collective-permute-start(bf16[256,1024]{1,0:T(8,128)(2,1)S(1)} %copy-done.63), channel_id=1, source_target_pairs={{0,4},{4,0},{1,5},{5,1},{2,6},{6,2},{3,7},{7,3},{8,12},{12,8},{9,1... | collective-permute-start | bytes 1572872 | tf_op jit(solution)/shard_map/ppermute | solution.py:578
  387.3 24.9 %collective-permute-start.31 = (bf16[256,2048]{1,0:T(8,128)(2,1)}, bf16[256,2048]{1,0:T(8,128)(2,1)S(1)}, u32[]{:S(2)}, u32[]{:S(2)}) collective-permute-start(bf16[256,2048]{1,0:T(8,128)(2,1)} %get-tuple-element.134.refs_0_), channel_id=1, source_target_pairs={{0,2},{1,3},{2,0},{3,1},{4,6},{5,7},{6,4},{7,5},{8,10},{9,11},{10,... | collective-permute-start | bytes 3145736 | tf_op jit(solution)/shard_map/ppermute | solution.py:580
  389.2 24.3 %collective-permute-start.30 = (bf16[256,2048]{1,0:T(8,128)(2,1)}, bf16[256,2048]{1,0:T(8,128)(2,1)S(1)}, u32[]{:S(2)}, u32[]{:S(2)}) collective-permute-start(bf16[256,2048]{1,0:T(8,128)(2,1)} %get-tuple-element.134.refs_0_), channel_id=1, source_target_pairs={{0,4},{4,0},{1,5},{5,1},{2,6},{6,2},{3,7},{7,3},{8,12},{12,8},{9,1... | collective-permute-start | bytes 3145736 | tf_op jit(solution)/shard_map/ppermute | solution.py:578
  412.3 12.6 %collective-permute-start.32 = (bf16[256,1024]{1,0:T(8,128)(2,1)S(1)}, bf16[256,1024]{1,0:T(8,128)(2,1)S(1)}, u32[]{:S(2)}, u32[]{:S(2)}) collective-permute-start(bf16[256,1024]{1,0:T(8,128)(2,1)S(1)} %slice.217), channel_id=1, source_target_pairs={{0,4},{4,0},{1,5},{5,1},{2,6},{6,2},{3,7},{7,3},{8,12},{12,8},{9,1... | collective-permute-start | bytes 1572872 | tf_op jit(solution)/shard_map/ppermute | solution.py:578
  413.6 12.1 %collective-permute-start.33 = (bf16[256,1024]{1,0:T(8,128)(2,1)S(1)}, bf16[256,1024]{1,0:T(8,128)(2,1)S(1)}, u32[]{:S(2)}, u32[]{:S(2)}) collective-permute-start(bf16[256,1024]{1,0:T(8,128)(2,1)S(1)} %slice.218), channel_id=1, source_target_pairs={{0,2},{1,3},{2,0},{3,1},{4,6},{5,7},{6,4},{7,5},{8,10},{9,11},{10,... | collective-permute-start | bytes 1572872 | tf_op jit(solution)/shard_map/ppermute | solution.py:580
  431.9 19.4 %collective-permute-start.36 = (bf16[1024,2048]{1,0:T(8,128)(2,1)}, bf16[1024,2048]{1,0:T(8,128)(2,1)}, u32[]{:S(2)}, u32[]{:S(2)}) collective-permute-start(bf16[1024,2048]{1,0:T(8,128)(2,1)} %bitcast.122), channel_id=1, source_target_pairs={{0,1},{1,0},{2,3},{3,2},{4,5},{5,4},{6,7},{7,6},{8,9},{9,8},{10,11... | collective-permute-start | bytes 12582920 | tf_op jit(solution)/shard_map/ppermute | solution.py:583
  431.9 28.2 %collective-permute-start.34 = (bf16[2,256,1024]{2,1,0:T(8,128)(2,1)}, bf16[2,256,1024]{2,1,0:T(8,128)(2,1)}, u32[]{:S(2)}, u32[]{:S(2)}) collective-permute-start(bf16[2,256,1024]{2,1,0:T(8,128)(2,1)} %get-tuple-element.135.refs_7_), channel_id=1, source_target_pairs={{0,4},{4,0},{1,5},{5,1},{2,6},{6,2},{3,7},{7,3},{8,12},{12,8},{9,1... | collective-permute-start | bytes 3145736 | tf_op jit(solution)/shard_map/ppermute | solution.py:578
  433.0 27.1 %collective-permute-start.35 = (bf16[2,256,1024]{2,1,0:T(8,128)(2,1)}, bf16[2,256,1024]{2,1,0:T(8,128)(2,1)}, u32[]{:S(2)}, u32[]{:S(2)}) collective-permute-start(bf16[2,256,1024]{2,1,0:T(8,128)(2,1)} %get-tuple-element.137), channel_id=1, source_target_pairs={{0,2},{1,3},{2,0},{3,1},{4,6},{5,7},{6,4},{7,5},{8,10},{9,11},{10,... | collective-permute-start | bytes 3145736 | tf_op jit(solution)/shard_map/ppermute | solution.py:580
  451.2 56.4 %collective-permute-start.42 = (bf16[3,1024,256]{2,1,0:T(8,128)(2,1)S(1)}, bf16[3,1024,256]{2,1,0:T(8,128)(2,1)}, u32[]{:S(2)}, u32[]{:S(2)}) collective-permute-start(bf16[3,1024,256]{2,1,0:T(8,128)(2,1)S(1)} %bitcast.102), channel_id=1, source_target_pairs={{0,1},{1,0},{2,3},{3,2},{4,5},{5,4},{6,7},{7,6},{8,9},{9,8},{10,11... | collective-permute-start | bytes 4718600 | tf_op jit(solution)/shard_map/ppermute | solution.py:583
  459.0 137.7 %all-gather.8.cloned.1.call-start = ((), (), s32[]{:S(2)}) async-start(), calls=%async_computation.7 | async-start | bytes 4325376 | tf_op jit(solution)/shard_map/all_gather | solution.py:1021
  459.1 33.5 %collective-permute-start.39 = (bf16[704,512]{1,0:T(8,128)(2,1)S(1)}, bf16[704,512]{1,0:T(8,128)(2,1)S(1)}, u32[]{:S(2)}, u32[]{:S(2)}) collective-permute-start(bf16[704,512]{1,0:T(8,128)(2,1)S(1)} %copy-done.35), channel_id=1, source_target_pairs={{0,4},{4,0},{1,5},{5,1},{2,6},{6,2},{3,7},{7,3},{8,12},{12,8},{9,1... | collective-permute-start | bytes 2162696 | tf_op jit(solution)/shard_map/ppermute | solution.py:578
  463.8 19.9 %collective-permute-start.37 = (bf16[256,1024]{1,0:T(8,128)(2,1)}, bf16[256,1024]{1,0:T(8,128)(2,1)S(1)}, u32[]{:S(2)}, u32[]{:S(2)}) collective-permute-start(bf16[256,1024]{1,0:T(8,128)(2,1)} %get-tuple-element.143), channel_id=1, source_target_pairs={{0,2},{1,3},{2,0},{3,1},{4,6},{5,7},{6,4},{7,5},{8,10},{9,11},{10,... | collective-permute-start | bytes 1572872 | tf_op jit(solution)/shard_map/ppermute | solution.py:580
  464.5 23.8 %collective-permute-start.38 = (bf16[256,1024]{1,0:T(8,128)(2,1)}, bf16[256,1024]{1,0:T(8,128)(2,1)S(1)}, u32[]{:S(2)}, u32[]{:S(2)}) collective-permute-start(bf16[256,1024]{1,0:T(8,128)(2,1)} %get-tuple-element.145), channel_id=1, source_target_pairs={{0,4},{4,0},{1,5},{5,1},{2,6},{6,2},{3,7},{7,3},{8,12},{12,8},{9,1... | collective-permute-start | bytes 1572872 | tf_op jit(solution)/shard_map/ppermute | solution.py:578
  505.9 24.5 %collective-permute-start.40 = (bf16[2,256,1024]{2,1,0:T(8,128)(2,1)}, bf16[2,256,1024]{2,1,0:T(8,128)(2,1)S(1)}, u32[]{:S(2)}, u32[]{:S(2)}) collective-permute-start(bf16[2,256,1024]{2,1,0:T(8,128)(2,1)} %get-tuple-element.152.refs_0_), channel_id=1, source_target_pairs={{0,4},{4,0},{1,5},{5,1},{2,6},{6,2},{3,7},{7,3},{8,12},{12,8},{9,1... | collective-permute-start | bytes 3145736 | tf_op jit(solution)/shard_map/ppermute | solution.py:578
  506.9 24.2 %collective-permute-start.41 = (bf16[2,256,1024]{2,1,0:T(8,128)(2,1)}, bf16[2,256,1024]{2,1,0:T(8,128)(2,1)}, u32[]{:S(2)}, u32[]{:S(2)}) collective-permute-start(bf16[2,256,1024]{2,1,0:T(8,128)(2,1)} %get-tuple-element.154), channel_id=1, source_target_pairs={{0,2},{1,3},{2,0},{3,1},{4,6},{5,7},{6,4},{7,5},{8,10},{9,11},{10,... | collective-permute-start | bytes 3145736 | tf_op jit(solution)/shard_map/ppermute | solution.py:580
  520.0 33.7 %collective-permute-start.48 = (bf16[2,3,256,256]{3,2,1,0:T(8,128)(2,1)S(1)}, bf16[2,3,256,256]{3,2,1,0:T(8,128)(2,1)}, u32[]{:S(2)}, u32[]{:S(2)}) collective-permute-start(bf16[2,3,256,256]{3,2,1,0:T(8,128)(2,1)S(1)} %pad_maximum_fusion), channel_id=1, source_target_pairs={{0,8},{8,16},{16,24},{24,0},{1,9},{9,17},{17,25},{25,1},{2,10},{10... | collective-permute-start | bytes 2359304 | tf_op jit(solution)/shard_map/ppermute | solution.py:575
  521.1 35.2 %collective-permute-start.49 = (bf16[2,3,256,256]{3,2,1,0:T(8,128)(2,1)}, bf16[2,3,256,256]{3,2,1,0:T(8,128)(2,1)}, u32[]{:S(2)}, u32[]{:S(2)}) collective-permute-start(bf16[2,3,256,256]{3,2,1,0:T(8,128)(2,1)} %pad_maximum_fusion.1), channel_id=1, source_target_pairs={{0,24},{8,0},{16,8},{24,16},{1,25},{9,1},{17,9},{25,17},{2,26},{10... | collective-permute-start | bytes 2359304 | tf_op jit(solution)/shard_map/ppermute | solution.py:575
  534.9 12.5 %collective-permute-start.43 = (bf16[256,1024]{1,0:T(8,128)(2,1)}, bf16[256,1024]{1,0:T(8,128)(2,1)}, u32[]{:S(2)}, u32[]{:S(2)}) collective-permute-start(bf16[256,1024]{1,0:T(8,128)(2,1)} %get-tuple-element.156), channel_id=1, source_target_pairs={{0,2},{1,3},{2,0},{3,1},{4,6},{5,7},{6,4},{7,5},{8,10},{9,11},{10,... | collective-permute-start | bytes 1572872 | tf_op jit(solution)/shard_map/ppermute | solution.py:580
  535.6 17.0 %collective-permute-start.44 = (bf16[256,1024]{1,0:T(8,128)(2,1)}, bf16[256,1024]{1,0:T(8,128)(2,1)}, u32[]{:S(2)}, u32[]{:S(2)}) collective-permute-start(bf16[256,1024]{1,0:T(8,128)(2,1)} %get-tuple-element.157), channel_id=1, source_target_pairs={{0,4},{4,0},{1,5},{5,1},{2,6},{6,2},{3,7},{7,3},{8,12},{12,8},{9,1... | collective-permute-start | bytes 1572872 | tf_op jit(solution)/shard_map/ppermute | solution.py:578
  552.5 17.7 %collective-permute-start.46 = (bf16[256,2048]{1,0:T(8,128)(2,1)S(1)}, bf16[256,2048]{1,0:T(8,128)(2,1)}, u32[]{:S(2)}, u32[]{:S(2)}) collective-permute-start(bf16[256,2048]{1,0:T(8,128)(2,1)S(1)} %copy-done.31), channel_id=1, source_target_pairs={{0,2},{1,3},{2,0},{3,1},{4,6},{5,7},{6,4},{7,5},{8,10},{9,11},{10,... | collective-permute-start | bytes 3145736 | tf_op jit(solution)/shard_map/ppermute | solution.py:580
  557.5 10.3 %collective-permute-start.53 = (bf16[3,256,256]{2,1,0:T(8,128)(2,1)S(1)}, bf16[3,256,256]{2,1,0:T(8,128)(2,1)S(1)}, u32[]{:S(2)}, u32[]{:S(2)}) collective-permute-start(bf16[3,256,256]{2,1,0:T(8,128)(2,1)S(1)} %fusion.17.refs_8_), channel_id=1, source_target_pairs={{0,24},{8,0},{16,8},{24,16},{1,25},{9,1},{17,9},{25,17},{2,26},{10... | collective-permute-start | bytes 1179656 | tf_op jit(solution)/shard_map/ppermute | solution.py:575
  569.4 11.3 %collective-permute-start.54 = (bf16[3,256,256]{2,1,0:T(8,128)(2,1)S(1)}, bf16[3,256,256]{2,1,0:T(8,128)(2,1)S(1)}, u32[]{:S(2)}, u32[]{:S(2)}) collective-permute-start(bf16[3,256,256]{2,1,0:T(8,128)(2,1)S(1)} %get-tuple-element.197), channel_id=1, source_target_pairs={{0,8},{8,16},{16,24},{24,0},{1,9},{9,17},{17,25},{25,1},{2,10},{10... | collective-permute-start | bytes 1179656 | tf_op jit(solution)/shard_map/ppermute | solution.py:575
  572.8 18.6 %collective-permute-start.45 = (bf16[256,2048]{1,0:T(8,128)(2,1)S(1)}, bf16[256,2048]{1,0:T(8,128)(2,1)}, u32[]{:S(2)}, u32[]{:S(2)}) collective-permute-start(bf16[256,2048]{1,0:T(8,128)(2,1)S(1)} %copy-done.31), channel_id=1, source_target_pairs={{0,1},{1,0},{2,3},{3,2},{4,5},{5,4},{6,7},{7,6},{8,9},{9,8},{10,11... | collective-permute-start | bytes 3145736 | tf_op jit(solution)/shard_map/ppermute | solution.py:583
  572.8 18.6 %collective-permute-start.47 = (bf16[256,2048]{1,0:T(8,128)(2,1)}, bf16[256,2048]{1,0:T(8,128)(2,1)}, u32[]{:S(2)}, u32[]{:S(2)}) collective-permute-start(bf16[256,2048]{1,0:T(8,128)(2,1)} %collective-permute-done.46.refs_2_), channel_id=1, source_target_pairs={{0,1},{1,0},{2,3},{3,2},{4,5},{5,4},{6,7},{7,6},{8,9},{9,8},{10,11... | collective-permute-start | bytes 3145736 | tf_op jit(solution)/shard_map/ppermute | solution.py:583
  574.2 29.5 %collective-permute-start.52 = (bf16[256,2048]{1,0:T(8,128)(2,1)}, bf16[256,2048]{1,0:T(8,128)(2,1)}, u32[]{:S(2)}, u32[]{:S(2)}) collective-permute-start(bf16[256,2048]{1,0:T(8,128)(2,1)} %get-tuple-element.169.refs_0_), channel_id=1, source_target_pairs={{0,2},{1,3},{2,0},{3,1},{4,6},{5,7},{6,4},{7,5},{8,10},{9,11},{10,... | collective-permute-start | bytes 3145736 | tf_op jit(solution)/shard_map/ppermute | solution.py:580
  583.0 8.4 %collective-permute-start.62 = (bf16[512,256]{1,0:T(8,128)(2,1)}, bf16[512,256]{1,0:T(8,128)(2,1)S(1)}, u32[]{:S(2)}, u32[]{:S(2)}) collective-permute-start(bf16[512,256]{1,0:T(8,128)(2,1)} %reduce-scatter.8.cloned.1.call-done), channel_id=1, source_target_pairs={{0,4},{4,0},{1,5},{5,1},{2,6},{6,2},{3,7},{7,3},{8,12},{12,8},{9,1... | collective-permute-start | bytes 786440 | tf_op jit(solution)/shard_map/ppermute | solution.py:578
  587.6 22.1 %collective-permute-start.55 = (bf16[3,512,256]{2,1,0:T(8,128)(2,1)}, bf16[3,512,256]{2,1,0:T(8,128)(2,1)}, u32[]{:S(2)}, u32[]{:S(2)}) collective-permute-start(bf16[3,512,256]{2,1,0:T(8,128)(2,1)} %pad_maximum_fusion.2), channel_id=1, source_target_pairs={{0,4},{4,0},{1,5},{5,1},{2,6},{6,2},{3,7},{7,3},{8,12},{12,8},{9,1... | collective-permute-start | bytes 2359304 | tf_op jit(solution)/shard_map/ppermute | solution.py:578
  591.4 26.3 %collective-permute-start.51 = (bf16[256,2048]{1,0:T(8,128)(2,1)}, bf16[256,2048]{1,0:T(8,128)(2,1)}, u32[]{:S(2)}, u32[]{:S(2)}) collective-permute-start(bf16[256,2048]{1,0:T(8,128)(2,1)} %get-tuple-element.169.refs_0_), channel_id=1, source_target_pairs={{0,1},{1,0},{2,3},{3,2},{4,5},{5,4},{6,7},{7,6},{8,9},{9,8},{10,11... | collective-permute-start | bytes 3145736 | tf_op jit(solution)/shard_map/ppermute | solution.py:583
  605.8 5.5 collective-permute-start.58
  606.0 5.9 collective-permute-start.60
  611.1 6.5 %collective-permute-start.56 = (bf16[256,2048]{1,0:T(8,128)(2,1)}, bf16[256,2048]{1,0:T(8,128)(2,1)}, u32[]{:S(2)}, u32[]{:S(2)}) collective-permute-start(bf16[256,2048]{1,0:T(8,128)(2,1)} %collective-permute-done.52.refs_2_), channel_id=1, source_target_pairs={{0,1},{1,0},{2,3},{3,2},{4,5},{5,4},{6,7},{7,6},{8,9},{9,8},{10,11... | collective-permute-start | bytes 3145736 | tf_op jit(solution)/shard_map/ppermute | solution.py:583
  (70 other events, 359.7 us)
Sparse Core Ops, SparseCore 0:
  92.2 106.0 all-gather.3
  211.7 55.9 all-gather.5
  296.6 53.0 reduce-scatter.3
  366.9 98.9 reduce-scatter.5
  468.0 27.6 reduce-scatter.7
  536.7 42.0 all-gather.7

commit v6 on v5

--- a/solution.py
+++ b/solution.py
@@ -531,7 +531,7 @@
 
 def turn(value, behind=()):
     count, rows, cols = value.shape
-    tn = tiles(cols, 128)
+    tn = tiles(cols, 256)
 
     def kernel(value_ref, *refs):
         refs[-1][...] = value_ref[...].astype(F32).T

time: 636 us -> 635 us (level)
  no operation moved by 1% of the time
where the time goes in v6:
time: 635 us; the launch traced here: 630 us
  Pallas kernels  263 us (41%)
  waiting for transfers between devices  207 us (33%)
  starting transfers between devices  57.8 us (9%)
  local copies, waits for them, and re-layouts  51.6 us (8%)
  other arithmetic  23.1 us (4%)
  between operations  15.5 us (2%)
  matrix products  12.2 us (2%)
    ppermute x18, waiting for transfers between devices, shift(): lax.ppermute(value, 'context', [(i, (i + step) % n) for i in range(n)])  80.9 us
    ppermute x17, waiting for transfers between devices, shift(): lax.ppermute(value, 'tensor', [(i, (i + 2 * step) % n) for i in range(n)])  80.5 us
    pallas_call x4, Pallas kernels, products_apart(): pl.pallas_call(kernel, grid_spec=pltpu.PrefetchScalarGridSpec(num_scalar_...  52.6 us
    ppermute x11, waiting for transfers between devices, shift(): return lax.ppermute(value, 'fsdp', [(i, (i + step) % n) for i in range(n)])  45.2 us
    pallas_call x5, Pallas kernels, products(): pl.pallas_call(kernel, grid=(many, rows // tm, cols // tn), in_specs=ones...  44.2 us
    pallas_call x6, Pallas kernels, pieces_of(): pl.pallas_call(kernel, grid_spec=pltpu.PrefetchScalarGridSpec(num_scalar_...  36.1 us
    unnamed x133, local copies, waits for them, and re-layouts  24.9 us
    pallas_call x2, Pallas kernels, gate_up(): pl.pallas_call(gate_kernel, grid=(rows // tm,), in_specs=[pl.BlockSpec((2...  23.9 us
  transfers between devices with their start and end apart: 69, of which 31 were waited for; matrix products, arithmetic and copies ran while one was open for 10% of the time, Pallas kernels for 40%

profile of v6, /device:TPU:0, one launch (start us, length us, event | category | flops | bytes accessed | tf_op | source)
XLA Modules:
  0.0 629.8 jit_solution(5603218874369578208)
XLA Ops:
  12.4 3.0 collective-permute-start
  17.5 3.8 dynamic-slice_bitcast_fusion.2
  27.2 2.6 copy.31
  29.9 17.8 %collective-permute-done.2.refs_2_ = bf16[256,2048]{1,0:T(8,128)(2,1)} collective-permute-done((bf16[256,2048]{1,0:T(8,128)(2,1)}, bf16[256,2048]{1,0:T(8,128)(2,1)}, u32[]{:S(2)}, u32[]{:S(2)}) %collective-permute-start.2) | collective-permute-done | bytes 1048608 | tf_op jit(solution)/shard_map/ppermute | solution.py:578
  47.7 16.5 %collective-permute-done.1 = bf16[4,528,256]{2,1,0:T(8,128)(2,1)} collective-permute-done((bf16[4,528,256]{2,1,0:T(8,128)(2,1)}, bf16[4,528,256]{2,1,0:T(8,128)(2,1)}, u32[]{:S(2)}, u32[]{:S(2)}) %collective-permute-start.1) | collective-permute-done | bytes 1081376 | tf_op jit(solution)/shard_map/ppermute | solution.py:575
  67.6 2.8 collective-permute-start.5
  75.3 16.7 %collective-permute-done.5 = bf16[2,512,256]{2,1,0:T(8,128)(2,1)S(1)} collective-permute-done((bf16[2,512,256]{2,1,0:T(8,128)(2,1)S(1)}, bf16[2,512,256]{2,1,0:T(8,128)(2,1)S(1)}, u32[]{:S(2)}, u32[]{:S(2)}) %collective-permute-start.5) | collective-permute-done | bytes 524320 | tf_op jit(solution)/shard_map/ppermute | solution.py:575
  93.7 3.5 collective-permute-done.7.refs_0_.refs_3_
  98.2 7.6 %norm_first.1 = bf16[4,256,2048]{2,1,0:T(8,128)(2,1)} custom-call(s32[4]{0:T(128)} %add_add_fusion.1.at_ref, bf16[256,2048]{1,0:T(8,128)(2,1)} %get-tuple-element.194.refs_0_, bf16[256,2048]{1,0:T(8,128)(2,1)} %get-tuple-element.193.refs_1_, bf16[256,2048]{1,0:T(8,128)(2,1)} %collective-permute-done.2.refs_2_, bf16[256,2048]{1,0:T(8,128)(2,1)} %copy-done.34, ...), custom_call_target="tpu_custom_call" | custom-call | bytes 83886 | tf_op jit(solution)/shard_map/norm_first/pallas_call | solution.py:358
  108.0 2.4 slice_dynamic-update-slice_fusion.1
  117.6 7.1 %fusion.5.r_0_ = f32[1,3,1024,256]{3,2,1,0:T(8,128)} fusion(bf16[1024,2048,1]{1,0,2:T(8,128)(2,1)S(1)} %bitcast.128, bf16[4,2048,256]{2,1,0:T(8,128)(2,1)} %constant_dynamic-update-slice_fusion.refs_2_.refs_1_.refs_6_.refs_7_.refs_8_), kind=kOutput, calls=%fused_computation.8 | convolution fusion | flops 3221225472 | bytes 10485760 | tf_op jit(solution)/shard_map/rd,cde->cre/dot_general | solution.py:909
  124.7 9.4 %attend_forward.2 = (bf16[1,1024,256]{2,1,0:T(8,128)(2,1)S(1)}, bf16[1,1024,256]{2,1,0:T(8,128)(2,1)S(1)}, bf16[1,1024,256]{2,1,0:T(8,128)(2,1)S(1)}, bf16[1,102...) custom-call(f32[1,3,1024,256]{3,2,1,0:T(8,128)} %fusion.5.r_0_, f32[1,3,1,256]{3,2,1,0:T(1,128)S(1)} %copy.23.r_1_, ...), custom_call_target="tpu_custom_call" | custom-call | flops 6442450 | bytes 68157 | tf_op jit(solution)/shard_map/attend_forward/pallas_call | solution.py:85
  134.1 5.1 fusion.8.r_0_
  139.2 2.6 collective-permute-done.9.r_4_.refs_3_
  141.8 10.0 %attend_forward.3 = (bf16[1,1024,256]{2,1,0:T(8,128)(2,1)S(1)}, bf16[1,1024,256]{2,1,0:T(8,128)(2,1)S(1)}, bf16[1,1024,256]{2,1,0:T(8,128)(2,1)S(1)}, bf16[1,102...) custom-call(f32[1,3,1024,256]{3,2,1,0:T(8,128)} %fusion.8.r_0_, f32[1,3,1,256]{3,2,1,0:T(1,128)S(1)} %reshape.85.r_1_, ...), custom_call_target="tpu_custom_call" | custom-call | flops 6442450 | bytes 68157 | tf_op jit(solution)/shard_map/attend_forward/pallas_call | solution.py:85
  154.2 7.5 %out.1 = (bf16[2,256,1024]{2,1,0:T(8,128)(2,1)}, bf16[2,256,1024]{2,1,0:T(8,128)(2,1)}, bf16[2,256,1024]{2,1,0:T(8,128)(2,1)}, bf16[2,256,1024]{2,1,0:T(8,128)(2,1)}) custom-call(s32[2]{0:T(128)} %pad_add_fusion.1.at_ref, bf16[1024,256]{1,0:T(8,128)(2,1)} %bitcast.107, bf16[1024,256]{1,0:T(8,128)(2,1)} %bitcast.109, ...), custom_call_target="tpu_custom_call" | custom-call | flops 21474836 | bytes 73400 | tf_op jit(solution)/shard_map/out/pallas_call | solution.py:246
  164.8 5.3 lay_pieces.1
  170.1 16.8 %collective-permute-done.10.two = bf16[2,256,1024]{2,1,0:T(8,128)(2,1)S(1)} collective-permute-done((bf16[2,256,1024]{2,1,0:T(8,128)(2,1)}, bf16[2,256,1024]{2,1,0:T(8,128)(2,1)S(1)}, u32[]{:S(2)}, u32[]{:S(2)}) %collective-permute-start.10) | collective-permute-done | bytes 1048608 | tf_op jit(solution)/shard_map/ppermute | solution.py:578
  189.0 3.5 join.4
  194.7 10.6 %collective-permute-done.12.refs_1_ = bf16[256,1024]{1,0:T(8,128)(2,1)S(1)} collective-permute-done((bf16[256,1024]{1,0:T(8,128)(2,1)}, bf16[256,1024]{1,0:T(8,128)(2,1)S(1)}, u32[]{:S(2)}, u32[]{:S(2)}) %collective-permute-start.12) | collective-permute-done | bytes 524320 | tf_op jit(solution)/shard_map/ppermute | solution.py:580
  207.4 3.5 add_norm.1
  213.1 24.3 %collective-permute-done.16.refs_2_ = bf16[256,2048]{1,0:T(8,128)(2,1)S(1)} collective-permute-done((bf16[256,2048]{1,0:T(8,128)(2,1)}, bf16[256,2048]{1,0:T(8,128)(2,1)S(1)}, u32[]{:S(2)}, u32[]{:S(2)}) %collective-permute-start.16) | collective-permute-done | bytes 1048608 | tf_op jit(solution)/shard_map/ppermute | solution.py:580
  242.2 9.9 %collective-permute-done.17.refs_3_ = bf16[256,1024]{1,0:T(8,128)(2,1)S(1)} collective-permute-done((bf16[256,1024]{1,0:T(8,128)(2,1)}, bf16[256,1024]{1,0:T(8,128)(2,1)S(1)}, u32[]{:S(2)}, u32[]{:S(2)}) %collective-permute-start.17) | collective-permute-done | bytes 524320 | tf_op jit(solution)/shard_map/ppermute | solution.py:578
  252.1 2.6 collective-permute-done.18.refs_4_
  254.7 5.9 lay_rows.4
  260.7 12.0 %gate_up.3 = (bf16[704,1024]{1,0:T(8,128)(2,1)}, bf16[2,704,1024]{2,1,0:T(8,128)(2,1)}, bf16[1024,704]{1,0:T(8,128)(2,1)}) custom-call(bf16[2,704,2048]{2,1,0:T(8,128)(2,1)} %collective-permute-done.21.weight_ref.refs_6_.refs_7_, bf16[1024,2048]{1,0:T(8,128)(2,1)} %bitcast.118), custom_call_target="tpu_custom_call" | custom-call | flops 59055800 | bytes 157286 | tf_op jit(solution)/shard_map/gate_up/pallas_call | solution.py:285
  273.2 11.9 %gate_up.2 = (bf16[704,1024]{1,0:T(8,128)(2,1)}, bf16[2,704,1024]{2,1,0:T(8,128)(2,1)}, bf16[1024,704]{1,0:T(8,128)(2,1)}) custom-call(bf16[2,704,2048]{2,1,0:T(8,128)(2,1)} %all-gather.4.cloned.1.call-done.weight_ref.refs_4_.refs_5_, bf16[1024,2048]{1,0:T(8,128)(2,1)} %bitcast.119), custom_call_target="tpu_custom_call" | custom-call | flops 59055800 | bytes 157286 | tf_op jit(solution)/shard_map/gate_up/pallas_call | solution.py:285
  286.3 10.2 %grad_down.1.refs_0_ = bf16[704,2048]{1,0:T(8,128)(2,1)} custom-call(bf16[704,1024]{1,0:T(8,128)(2,1)} %get-tuple-element.118.refs_0_, bf16[704,1024]{1,0:T(8,128)(2,1)} %copy-done.46, bf16[1024,2048]{1,0:T(8,128)(2,1)} %bitcast.115, bf16[1024,2048]{1,0:T(8,128)(2,1)} %collective-permute-done.19.refs_5_.refs_3_), custom_call_target="tpu_custom_call" | custom-call | flops 59055800 | bytes 141557 | tf_op jit(solution)/shard_map/grad_down/pallas_call | solution.py:196
  296.7 8.9 %hidden_back.2 = (bf16[2,704,1024]{2,1,0:T(8,128)(2,1)}, bf16[2,1024,704]{2,1,0:T(8,128)(2,1)}) custom-call(bf16[704,2048]{1,0:T(8,128)(2,1)} %collective-permute-done.22.weight_ref.refs_3_, bf16[1024,2048]{1,0:T(8,128)(2,1)} %bitcast.116, bf16[2,704,1024]{2,1,0:T(8,128)(2,1)} %get-tuple-element.117.slope_ref, bf16[704,2048]{1,0:T(8,128)(2,1)} %grad_down.1.refs_0_), custom_call_target="tpu_custom_call" | custom-call | flops 29527900 | bytes 157286 | tf_op jit(solution)/shard_map/hidden_back/pallas_call | solution.py:325
  306.2 8.6 %hidden_back.3 = (bf16[2,704,1024]{2,1,0:T(8,128)(2,1)}, bf16[2,1024,704]{2,1,0:T(8,128)(2,1)}) custom-call(bf16[704,2048]{1,0:T(8,128)(2,1)} %all-gather.6.cloned.1.call-done.weight_ref.refs_2_, bf16[1024,2048]{1,0:T(8,128)(2,1)} %bitcast.117, bf16[2,704,1024]{2,1,0:T(8,128)(2,1)} %get-tuple-element.116.slope_ref, ...), custom_call_target="tpu_custom_call" | custom-call | flops 29527900 | bytes 157286 | tf_op jit(solution)/shard_map/hidden_back/pallas_call | solution.py:325
  316.9 20.2 %grad_two.1 = (bf16[2,256,1024]{2,1,0:T(8,128)(2,1)}, bf16[2,256,1024]{2,1,0:T(8,128)(2,1)}, bf16[2,256,1024]{2,1,0:T(8,128)(2,1)}, bf16[2,256,1024]{2,1,0:T(8,128)(2,1)}) custom-call(s32[2]{0:T(128)} %pad_add_fusion.1.at_ref, bf16[2,1024,704]{2,1,0:T(8,128)(2,1)} %get-tuple-element.120.refs_0_.refs_1_, ...), custom_call_target="tpu_custom_call" | custom-call | flops 118111600 | bytes 214958 | tf_op jit(solution)/shard_map/grad_two/pallas_call | solution.py:246
  338.2 18.1 %grad_gate_up.1.refs_0_ = bf16[2,704,2048]{2,1,0:T(8,128)(2,1)} custom-call(bf16[2,704,1024]{2,1,0:T(8,128)(2,1)} %get-tuple-element.126.refs_0_, bf16[2,704,1024]{2,1,0:T(8,128)(2,1)} %collective-permute-done.25.refs_9_.refs_1_, bf16[1024,2048]{1,0:T(8,128)(2,1)} %bitcast.121, bf16[1024,2048]{1,0:T(8,128)(2,1)} %copy-done.30, ...), custom_call_target="tpu_custom_call" | custom-call | flops 118111600 | bytes 283115 | tf_op jit(solution)/shard_map/grad_gate_up/pallas_call | solution.py:196
  356.2 6.1 collective-permute-done.26.two
  363.3 3.5 join.5
  369.0 12.5 %down.1 = (bf16[2,256,1024]{2,1,0:T(8,128)(2,1)}, bf16[2,256,1024]{2,1,0:T(8,128)(2,1)}, bf16[2,256,1024]{2,1,0:T(8,128)(2,1)}, bf16[2,256,1024]{2,1,0:T(8,128)(2,1)}) custom-call(s32[2]{0:T(128)} %pad_add_fusion.1.at_ref, bf16[1024,704]{1,0:T(8,128)(2,1)} %get-tuple-element.109.refs_0_, bf16[1024,704]{1,0:T(8,128)(2,1)} %get-tuple-element.112.refs_1_, ...), custom_call_target="tpu_custom_call" | custom-call | flops 59055800 | bytes 128450 | tf_op jit(solution)/shard_map/down/pallas_call | solution.py:246
  382.6 4.8 norm_back.2
  390.5 21.7 %collective-permute-done.31.refs_2_ = bf16[256,2048]{1,0:T(8,128)(2,1)S(1)} collective-permute-done((bf16[256,2048]{1,0:T(8,128)(2,1)}, bf16[256,2048]{1,0:T(8,128)(2,1)S(1)}, u32[]{:S(2)}, u32[]{:S(2)}) %collective-permute-start.31) | collective-permute-done | bytes 1048608 | tf_op jit(solution)/shard_map/ppermute | solution.py:580
  414.8 10.0 %collective-permute-done.32.refs_3_ = bf16[256,1024]{1,0:T(8,128)(2,1)S(1)} collective-permute-done((bf16[256,1024]{1,0:T(8,128)(2,1)S(1)}, bf16[256,1024]{1,0:T(8,128)(2,1)S(1)}, u32[]{:S(2)}, u32[]{:S(2)}) %collective-permute-start.32) | collective-permute-done | bytes 524320 | tf_op jit(solution)/shard_map/ppermute | solution.py:578
  426.5 5.3 lay_rows.5
  434.4 4.5 grad_att.2
  440.0 11.2 %attend_back.2 = bf16[1,3,1024,256]{3,2,1,0:T(8,128)(2,1)S(1)} custom-call(bf16[1,1024,256]{2,1,0:T(8,128)(2,1)S(1)} %copy-done.23, bf16[1,1024,256]{2,1,0:T(8,128)(2,1)S(1)} %copy-done.25, bf16[1,1024,256]{2,1,0:T(8,128)(2,1)S(1)} %copy-done.27, bf16[1,1024,256]{2,1,0:T(8,128)(2,1)S(1)} %copy-done.11, f32[1,1024,256]{2,1,0:T(8,128)S(1)} %get-tuple-element.141.r_4_, ...), custom_call_target="tpu_custom_call" | custom-call | flops 16106127 | bytes 52428 | tf_op jit(solution)/shard_map/attend_back/pallas_call | solution.py:145
  452.3 6.7 %grad_out.1.refs_0_ = bf16[2048,256]{1,0:T(8,128)(2,1)} custom-call(bf16[1024,2048]{1,0:T(8,128)(2,1)} %bitcast.124, bf16[1024,2048]{1,0:T(8,128)(2,1)} %collective-permute-done.36.refs_1_, bf16[1024,256]{1,0:T(8,128)(2,1)} %bitcast.108, bf16[1024,256]{1,0:T(8,128)(2,1)} %copy-done.44, bf16[3,1024,256]{2,1,0:T(8,128)(2,1)} %bitcast.103), custom_call_target="tpu_custom_call" | custom-call | flops 21474836 | bytes 104857 | tf_op jit(solution)/shard_map/grad_out/pallas_call | solution.py:196
  460.1 3.7 join.6
  465.5 4.7 grad_att.3
  471.3 11.2 %attend_back.3 = bf16[1,3,1024,256]{3,2,1,0:T(8,128)(2,1)S(1)} custom-call(bf16[1,1024,256]{2,1,0:T(8,128)(2,1)S(1)} %copy-done.17, bf16[1,1024,256]{2,1,0:T(8,128)(2,1)S(1)} %copy-done.19, bf16[1,1024,256]{2,1,0:T(8,128)(2,1)S(1)} %copy-done.21, bf16[1,1024,256]{2,1,0:T(8,128)(2,1)S(1)} %copy-done.8, f32[1,1024,256]{2,1,0:T(8,128)S(1)} %copy-done.15, ...), custom_call_target="tpu_custom_call" | custom-call | flops 16106127 | bytes 52428 | tf_op jit(solution)/shard_map/attend_back/pallas_call | solution.py:145
  483.7 4.6 collective-permute-done.38.refs_3_
  489.1 3.4 add_low.1.refs_12_.refs_0_
  493.5 12.4 %grad_one.1 = (bf16[2,256,1024]{2,1,0:T(8,128)(2,1)}, bf16[2,256,1024]{2,1,0:T(8,128)(2,1)}, bf16[2,256,1024]{2,1,0:T(8,128)(2,1)}, bf16[2,256,1024]{2,1,0:T(8,128)(2,1)}) custom-call(s32[2]{0:T(128)} %pad_add_fusion.1.at_ref, bf16[3,1024,256]{2,1,0:T(8,128)(2,1)} %bitcast.98, bf16[3,1024,256]{2,1,0:T(8,128)(2,1)} %bitcast.99, ...), custom_call_target="tpu_custom_call" | custom-call | flops 64424508 | bytes 136314 | tf_op jit(solution)/shard_map/grad_one/pallas_call | solution.py:246
  507.6 10.9 %grad_qkv.1.refs_0_ = bf16[3,2048,256]{2,1,0:T(8,128)(2,1)} custom-call(bf16[1024,2048]{1,0:T(8,128)(2,1)} %bitcast.127, bf16[1024,2048]{1,0:T(8,128)(2,1)} %collective-permute-done.20.refs_6_.theirs_ref, bf16[3,1024,256]{2,1,0:T(8,128)(2,1)} %bitcast.101, bf16[3,1024,256]{2,1,0:T(8,128)(2,1)} %collective-permute-done.42.their_ref, ...), custom_call_target="tpu_custom_call" | custom-call | flops 64424508 | bytes 146800 | tf_op jit(solution)/shard_map/grad_qkv/pallas_call | solution.py:516
  521.1 3.8 collective-permute-start.49
  524.9 5.5 collective-permute-done.40.two
  531.3 3.5 join.7
  536.6 10.8 %collective-permute-done.43.refs_1_ = bf16[256,1024]{1,0:T(8,128)(2,1)} collective-permute-done((bf16[256,1024]{1,0:T(8,128)(2,1)}, bf16[256,1024]{1,0:T(8,128)(2,1)}, u32[]{:S(2)}, u32[]{:S(2)}) %collective-permute-start.43) | collective-permute-done | bytes 524320 | tf_op jit(solution)/shard_map/ppermute | solution.py:580
  547.4 5.1 collective-permute-done.44.refs_3_
  553.7 2.5 collective-permute-done.49
  559.4 4.8 norm_back.3
  564.2 3.6 collective-permute-done.53
  575.6 5.1 collective-permute-done.54
  584.0 3.4 maximum_convert_fusion.1
  588.7 2.7 collective-permute-done.62
  591.4 5.3 lay_rows.6
  596.7 5.2 turn.1
  604.8 3.1 collective-permute-start.60
  615.8 6.6 %lay_rows.7 = f32[4,256,2048]{2,1,0:T(8,128)} custom-call(s32[4]{0:T(128)} %pad_add_fusion.at_ref, bf16[256,2048]{1,0:T(8,128)(2,1)} %get-tuple-element.169.refs_0_, bf16[256,2048]{1,0:T(8,128)(2,1)} %collective-permute-done.51.refs_1_, bf16[256,2048]{1,0:T(8,128)(2,1)} %collective-permute-done.52.refs_2_, bf16[256,2048]{1,0:T(8,128)(2,1)} %collective-permute-done.56.refs_3_), custom_call_target="tpu_custom_call" | custom-call | bytes 83886 | tf_op jit(solution)/shard_map/lay_rows/pallas_call | solution.py:358
  (323 shorter events, 115.2 us)
Async XLA Ops:
  7.2 203.7 %all-gather.4.cloned.1.call-start = ((), (), s32[]{:S(2)}) async-start(), calls=%async_computation.3 | async-start | bytes 7208960 | tf_op jit(solution)/shard_map/all_gather | solution.py:903
  12.4 35.3 %collective-permute-start = (bf16[4,528,256]{2,1,0:T(8,128)(2,1)}, bf16[4,528,256]{2,1,0:T(8,128)(2,1)}, u32[]{:S(2)}, u32[]{:S(2)}) collective-permute-start(bf16[4,528,256]{2,1,0:T(8,128)(2,1)} %fusion.11), channel_id=1, source_target_pairs={{0,8},{8,16},{16,24},{24,0},{1,9},{9,17},{17,25},{25,1},{2,10},{10... | collective-permute-start | bytes 3244040 | tf_op jit(solution)/shard_map/ppermute | solution.py:575
  15.4 48.8 %collective-permute-start.1 = (bf16[4,528,256]{2,1,0:T(8,128)(2,1)}, bf16[4,528,256]{2,1,0:T(8,128)(2,1)}, u32[]{:S(2)}, u32[]{:S(2)}) collective-permute-start(bf16[4,528,256]{2,1,0:T(8,128)(2,1)} %fusion.11), channel_id=1, source_target_pairs={{0,24},{8,0},{16,8},{24,16},{1,25},{9,1},{17,9},{25,17},{2,26},{10... | collective-permute-start | bytes 3244040 | tf_op jit(solution)/shard_map/ppermute | solution.py:575
  21.3 26.4 %collective-permute-start.2 = (bf16[256,2048]{1,0:T(8,128)(2,1)}, bf16[256,2048]{1,0:T(8,128)(2,1)}, u32[]{:S(2)}, u32[]{:S(2)}) collective-permute-start(bf16[256,2048]{1,0:T(8,128)(2,1)} %get-tuple-element.195.refs_4_), channel_id=1, source_target_pairs={{0,4},{4,0},{1,5},{5,1},{2,6},{6,2},{3,7},{7,3},{8,12},{12,8},{9,1... | collective-permute-start | bytes 3145736 | tf_op jit(solution)/shard_map/ppermute | solution.py:578
  24.9 50.4 %collective-permute-start.6 = (bf16[256,2048]{1,0:T(8,128)(2,1)}, bf16[256,2048]{1,0:T(8,128)(2,1)}, u32[]{:S(2)}, u32[]{:S(2)}) collective-permute-start(bf16[256,2048]{1,0:T(8,128)(2,1)} %get-tuple-element.192.refs_5_), channel_id=1, source_target_pairs={{0,4},{4,0},{1,5},{5,1},{2,6},{6,2},{3,7},{7,3},{8,12},{12,8},{9,1... | collective-permute-start | bytes 3145736 | tf_op jit(solution)/shard_map/ppermute | solution.py:578
  65.3 26.7 %collective-permute-start.4 = (bf16[2,528,256]{2,1,0:T(8,128)(2,1)S(1)}, bf16[2,528,256]{2,1,0:T(8,128)(2,1)}, u32[]{:S(2)}, u32[]{:S(2)}) collective-permute-start(bf16[2,528,256]{2,1,0:T(8,128)(2,1)S(1)} %slice.159), channel_id=1, source_target_pairs={{0,8},{8,16},{16,24},{24,0},{1,9},{9,17},{17,25},{25,1},{2,10},{10... | collective-permute-start | bytes 1622024 | tf_op jit(solution)/shard_map/ppermute | solution.py:575
  67.6 24.4 %collective-permute-start.5 = (bf16[2,512,256]{2,1,0:T(8,128)(2,1)S(1)}, bf16[2,512,256]{2,1,0:T(8,128)(2,1)S(1)}, u32[]{:S(2)}, u32[]{:S(2)}) collective-permute-start(bf16[2,512,256]{2,1,0:T(8,128)(2,1)S(1)} %slice.160), channel_id=1, source_target_pairs={{0,24},{8,0},{16,8},{24,16},{1,25},{9,1},{17,9},{25,17},{2,26},{10... | collective-permute-start | bytes 1572872 | tf_op jit(solution)/shard_map/ppermute | solution.py:575
  73.1 24.1 %collective-permute-start.7 = (bf16[256,2048]{1,0:T(8,128)(2,1)}, bf16[256,2048]{1,0:T(8,128)(2,1)S(1)}, u32[]{:S(2)}, u32[]{:S(2)}) collective-permute-start(bf16[256,2048]{1,0:T(8,128)(2,1)} %collective-permute-done.2.refs_2_), channel_id=1, source_target_pairs={{0,2},{1,3},{2,0},{3,1},{4,6},{5,7},{6,4},{7,5},{8,10},{9,11},{10,... | collective-permute-start | bytes 3145736 | tf_op jit(solution)/shard_map/ppermute | solution.py:580
  92.0 180.6 %all-gather.6.cloned.1.call-start = ((), (), s32[]{:S(2)}) async-start(), calls=%async_computation.4 | async-start | bytes 3604480 | tf_op jit(solution)/shard_map/all_gather | solution.py:904
  115.3 18.7 %collective-permute-start.8 = (bf16[4,2048,256]{2,1,0:T(8,128)(2,1)}, bf16[4,2048,256]{2,1,0:T(8,128)(2,1)S(1)}, u32[]{:S(2)}, u32[]{:S(2)}) collective-permute-start(bf16[4,2048,256]{2,1,0:T(8,128)(2,1)} %constant_dynamic-update-slice_fusion.refs_2_.refs_1_.refs_6_.refs_7_.refs_8_), channel_id=1, source_target_pairs={{0,1},{1,0},{2,3},{3,2},{4,5},{5,4},{6,7},{7,6},{8,9},{9,8},{10,11... | collective-permute-start | bytes 12582920 | tf_op jit(solution)/shard_map/ppermute | solution.py:583
  116.0 25.8 %collective-permute-start.9 = (bf16[256,2048]{1,0:T(8,128)(2,1)}, bf16[256,2048]{1,0:T(8,128)(2,1)S(1)}, u32[]{:S(2)}, u32[]{:S(2)}) collective-permute-start(bf16[256,2048]{1,0:T(8,128)(2,1)} %collective-permute-done.6.refs_2_), channel_id=1, source_target_pairs={{0,2},{1,3},{2,0},{3,1},{4,6},{5,7},{6,4},{7,5},{8,10},{9,11},{10,... | collective-permute-start | bytes 3145736 | tf_op jit(solution)/shard_map/ppermute | solution.py:580
  161.7 25.2 %collective-permute-start.10 = (bf16[2,256,1024]{2,1,0:T(8,128)(2,1)}, bf16[2,256,1024]{2,1,0:T(8,128)(2,1)S(1)}, u32[]{:S(2)}, u32[]{:S(2)}) collective-permute-start(bf16[2,256,1024]{2,1,0:T(8,128)(2,1)} %get-tuple-element.101.refs_4_), channel_id=1, source_target_pairs={{0,4},{4,0},{1,5},{5,1},{2,6},{6,2},{3,7},{7,3},{8,12},{12,8},{9,1... | collective-permute-start | bytes 3145736 | tf_op jit(solution)/shard_map/ppermute | solution.py:578
  163.3 24.8 %collective-permute-start.11 = (bf16[2,256,1024]{2,1,0:T(8,128)(2,1)}, bf16[2,256,1024]{2,1,0:T(8,128)(2,1)S(1)}, u32[]{:S(2)}, u32[]{:S(2)}) collective-permute-start(bf16[2,256,1024]{2,1,0:T(8,128)(2,1)} %get-tuple-element.103), channel_id=1, source_target_pairs={{0,2},{1,3},{2,0},{3,1},{4,6},{5,7},{6,4},{7,5},{8,10},{9,11},{10,... | collective-permute-start | bytes 3145736 | tf_op jit(solution)/shard_map/ppermute | solution.py:580
  164.8 29.9 %collective-permute-start.14 = (bf16[1024,256]{1,0:T(8,128)(2,1)S(1)}, bf16[1024,256]{1,0:T(8,128)(2,1)S(1)}, u32[]{:S(2)}, u32[]{:S(2)}) collective-permute-start(bf16[1024,256]{1,0:T(8,128)(2,1)S(1)} %bitcast.110), channel_id=1, source_target_pairs={{0,1},{1,0},{2,3},{3,2},{4,5},{5,4},{6,7},{7,6},{8,9},{9,8},{10,11... | collective-permute-start | bytes 1572872 | tf_op jit(solution)/shard_map/ppermute | solution.py:583
  192.5 12.8 %collective-permute-start.12 = (bf16[256,1024]{1,0:T(8,128)(2,1)}, bf16[256,1024]{1,0:T(8,128)(2,1)S(1)}, u32[]{:S(2)}, u32[]{:S(2)}) collective-permute-start(bf16[256,1024]{1,0:T(8,128)(2,1)} %get-tuple-element.105), channel_id=1, source_target_pairs={{0,2},{1,3},{2,0},{3,1},{4,6},{5,7},{6,4},{7,5},{8,10},{9,11},{10,... | collective-permute-start | bytes 1572872 | tf_op jit(solution)/shard_map/ppermute | solution.py:580
  194.1 12.5 %collective-permute-start.13 = (bf16[256,1024]{1,0:T(8,128)(2,1)}, bf16[256,1024]{1,0:T(8,128)(2,1)S(1)}, u32[]{:S(2)}, u32[]{:S(2)}) collective-permute-start(bf16[256,1024]{1,0:T(8,128)(2,1)} %get-tuple-element.107), channel_id=1, source_target_pairs={{0,4},{4,0},{1,5},{5,1},{2,6},{6,2},{3,7},{7,3},{8,12},{12,8},{9,1... | collective-permute-start | bytes 1572872 | tf_op jit(solution)/shard_map/ppermute | solution.py:578
  210.9 49.8 %collective-permute-start.21 = (bf16[2,704,2048]{2,1,0:T(8,128)(2,1)}, bf16[2,704,2048]{2,1,0:T(8,128)(2,1)}, u32[]{:S(2)}, u32[]{:S(2)}) collective-permute-start(bf16[2,704,2048]{2,1,0:T(8,128)(2,1)} %all-gather.4.cloned.1.call-done.weight_ref.refs_4_.refs_5_), channel_id=1, source_target_pairs={{0,1},{1,0},{2,3},{3,2},{4,5},{5,4},{6,7},{7,6},{8,9},{9,8},{10,11... | collective-permute-start | bytes 17301512 | tf_op jit(solution)/shard_map/ppermute | solution.py:583
  210.9 31.2 %collective-permute-start.20 = (bf16[1024,2048]{1,0:T(8,128)(2,1)}, bf16[1024,2048]{1,0:T(8,128)(2,1)}, u32[]{:S(2)}, u32[]{:S(2)}) collective-permute-start(bf16[1024,2048]{1,0:T(8,128)(2,1)} %bitcast.126), channel_id=1, source_target_pairs={{0,1},{1,0},{2,3},{3,2},{4,5},{5,4},{6,7},{7,6},{8,9},{9,8},{10,11... | collective-permute-start | bytes 12582920 | tf_op jit(solution)/shard_map/ppermute | solution.py:583
  211.4 43.3 %collective-permute-start.19 = (bf16[1024,2048]{1,0:T(8,128)(2,1)}, bf16[1024,2048]{1,0:T(8,128)(2,1)}, u32[]{:S(2)}, u32[]{:S(2)}) collective-permute-start(bf16[1024,2048]{1,0:T(8,128)(2,1)} %bitcast.114), channel_id=1, source_target_pairs={{0,1},{1,0},{2,3},{3,2},{4,5},{5,4},{6,7},{7,6},{8,9},{9,8},{10,11... | collective-permute-start | bytes 12582920 | tf_op jit(solution)/shard_map/ppermute | solution.py:583
  211.5 151.4 %reduce-scatter.4.cloned.1.call-start = ((), (), s32[]{:S(2)}) async-start(), calls=%async_computation.5 | async-start | bytes 3604480 | tf_op jit(solution)/shard_map/reduce_scatter | solution.py:943
  211.6 25.8 %collective-permute-start.16 = (bf16[256,2048]{1,0:T(8,128)(2,1)}, bf16[256,2048]{1,0:T(8,128)(2,1)S(1)}, u32[]{:S(2)}, u32[]{:S(2)}) collective-permute-start(bf16[256,2048]{1,0:T(8,128)(2,1)} %get-tuple-element.108.refs_0_), channel_id=1, source_target_pairs={{0,2},{1,3},{2,0},{3,1},{4,6},{5,7},{6,4},{7,5},{8,10},{9,11},{10,... | collective-permute-start | bytes 3145736 | tf_op jit(solution)/shard_map/ppermute | solution.py:580
  212.1 27.1 %collective-permute-start.15 = (bf16[256,2048]{1,0:T(8,128)(2,1)}, bf16[256,2048]{1,0:T(8,128)(2,1)S(1)}, u32[]{:S(2)}, u32[]{:S(2)}) collective-permute-start(bf16[256,2048]{1,0:T(8,128)(2,1)} %get-tuple-element.108.refs_0_), channel_id=1, source_target_pairs={{0,4},{4,0},{1,5},{5,1},{2,6},{6,2},{3,7},{7,3},{8,12},{12,8},{9,1... | collective-permute-start | bytes 3145736 | tf_op jit(solution)/shard_map/ppermute | solution.py:578
  238.3 13.8 %collective-permute-start.17 = (bf16[256,1024]{1,0:T(8,128)(2,1)}, bf16[256,1024]{1,0:T(8,128)(2,1)S(1)}, u32[]{:S(2)}, u32[]{:S(2)}) collective-permute-start(bf16[256,1024]{1,0:T(8,128)(2,1)} %slice.215), channel_id=1, source_target_pairs={{0,4},{4,0},{1,5},{5,1},{2,6},{6,2},{3,7},{7,3},{8,12},{12,8},{9,1... | collective-permute-start | bytes 1572872 | tf_op jit(solution)/shard_map/ppermute | solution.py:578
  241.1 13.6 %collective-permute-start.18 = (bf16[256,1024]{1,0:T(8,128)(2,1)}, bf16[256,1024]{1,0:T(8,128)(2,1)}, u32[]{:S(2)}, u32[]{:S(2)}) collective-permute-start(bf16[256,1024]{1,0:T(8,128)(2,1)} %slice.216), channel_id=1, source_target_pairs={{0,2},{1,3},{2,0},{3,1},{4,6},{5,7},{6,4},{7,5},{8,10},{9,11},{10,... | collective-permute-start | bytes 1572872 | tf_op jit(solution)/shard_map/ppermute | solution.py:580
  272.7 12.5 %collective-permute-start.23 = (bf16[704,1024]{1,0:T(8,128)(2,1)}, bf16[704,1024]{1,0:T(8,128)(2,1)S(1)}, u32[]{:S(2)}, u32[]{:S(2)}) collective-permute-start(bf16[704,1024]{1,0:T(8,128)(2,1)} %get-tuple-element.114), channel_id=1, source_target_pairs={{0,1},{1,0},{2,3},{3,2},{4,5},{5,4},{6,7},{7,6},{8,9},{9,8},{10,11... | collective-permute-start | bytes 4325384 | tf_op jit(solution)/shard_map/ppermute | solution.py:583
  272.7 24.0 %collective-permute-start.22 = (bf16[704,2048]{1,0:T(8,128)(2,1)}, bf16[704,2048]{1,0:T(8,128)(2,1)}, u32[]{:S(2)}, u32[]{:S(2)}) collective-permute-start(bf16[704,2048]{1,0:T(8,128)(2,1)} %all-gather.6.cloned.1.call-done.weight_ref.refs_2_), channel_id=1, source_target_pairs={{0,1},{1,0},{2,3},{3,2},{4,5},{5,4},{6,7},{7,6},{8,9},{9,8},{10,11... | collective-permute-start | bytes 8650760 | tf_op jit(solution)/shard_map/ppermute | solution.py:583
  296.5 211.1 %reduce-scatter.6.cloned.1.call-start = ((), (), s32[]{:S(2)}) async-start(), calls=%async_computation.6 | async-start | bytes 7208960 | tf_op jit(solution)/shard_map/reduce_scatter | solution.py:966
  296.6 18.2 %collective-permute-start.24 = (bf16[1024,2048]{1,0:T(8,128)(2,1)}, bf16[1024,2048]{1,0:T(8,128)(2,1)S(1)}, u32[]{:S(2)}, u32[]{:S(2)}) collective-permute-start(bf16[1024,2048]{1,0:T(8,128)(2,1)} %bitcast.120), channel_id=1, source_target_pairs={{0,1},{1,0},{2,3},{3,2},{4,5},{5,4},{6,7},{7,6},{8,9},{9,8},{10,11... | collective-permute-start | bytes 12582920 | tf_op jit(solution)/shard_map/ppermute | solution.py:583
  305.6 9.2 %collective-permute-start.25 = (bf16[2,704,1024]{2,1,0:T(8,128)(2,1)}, bf16[2,704,1024]{2,1,0:T(8,128)(2,1)}, u32[]{:S(2)}, u32[]{:S(2)}) collective-permute-start(bf16[2,704,1024]{2,1,0:T(8,128)(2,1)} %get-tuple-element.121), channel_id=1, source_target_pairs={{0,1},{1,0},{2,3},{3,2},{4,5},{5,4},{6,7},{7,6},{8,9},{9,8},{10,11... | collective-permute-start | bytes 8650760 | tf_op jit(solution)/shard_map/ppermute | solution.py:583
  337.1 25.3 %collective-permute-start.26 = (bf16[2,256,1024]{2,1,0:T(8,128)(2,1)}, bf16[2,256,1024]{2,1,0:T(8,128)(2,1)S(1)}, u32[]{:S(2)}, u32[]{:S(2)}) collective-permute-start(bf16[2,256,1024]{2,1,0:T(8,128)(2,1)} %get-tuple-element.123.refs_4_), channel_id=1, source_target_pairs={{0,4},{4,0},{1,5},{5,1},{2,6},{6,2},{3,7},{7,3},{8,12},{12,8},{9,1... | collective-permute-start | bytes 3145736 | tf_op jit(solution)/shard_map/ppermute | solution.py:578
  337.8 25.2 %collective-permute-start.27 = (bf16[2,256,1024]{2,1,0:T(8,128)(2,1)}, bf16[2,256,1024]{2,1,0:T(8,128)(2,1)}, u32[]{:S(2)}, u32[]{:S(2)}) collective-permute-start(bf16[2,256,1024]{2,1,0:T(8,128)(2,1)} %get-tuple-element.125), channel_id=1, source_target_pairs={{0,2},{1,3},{2,0},{3,1},{4,6},{5,7},{6,4},{7,5},{8,10},{9,11},{10,... | collective-permute-start | bytes 3145736 | tf_op jit(solution)/shard_map/ppermute | solution.py:580
  366.8 216.2 %reduce-scatter.8.cloned.1.call-start = ((), (), s32[]{:S(2)}) async-start(), calls=%async_computation.8 | async-start | bytes 1310720 | tf_op jit(solution)/shard_map/reduce_scatter | solution.py:1001
  367.8 13.8 %collective-permute-start.28 = (bf16[256,1024]{1,0:T(8,128)(2,1)S(1)}, bf16[256,1024]{1,0:T(8,128)(2,1)S(1)}, u32[]{:S(2)}, u32[]{:S(2)}) collective-permute-start(bf16[256,1024]{1,0:T(8,128)(2,1)S(1)} %copy-done.64), channel_id=1, source_target_pairs={{0,2},{1,3},{2,0},{3,1},{4,6},{5,7},{6,4},{7,5},{8,10},{9,11},{10,... | collective-permute-start | bytes 1572872 | tf_op jit(solution)/shard_map/ppermute | solution.py:580
  368.0 13.6 %collective-permute-start.29 = (bf16[256,1024]{1,0:T(8,128)(2,1)S(1)}, bf16[256,1024]{1,0:T(8,128)(2,1)S(1)}, u32[]{:S(2)}, u32[]{:S(2)}) collective-permute-start(bf16[256,1024]{1,0:T(8,128)(2,1)S(1)} %copy-done.63), channel_id=1, source_target_pairs={{0,4},{4,0},{1,5},{5,1},{2,6},{6,2},{3,7},{7,3},{8,12},{12,8},{9,1... | collective-permute-start | bytes 1572872 | tf_op jit(solution)/shard_map/ppermute | solution.py:578
  387.3 24.9 %collective-permute-start.31 = (bf16[256,2048]{1,0:T(8,128)(2,1)}, bf16[256,2048]{1,0:T(8,128)(2,1)S(1)}, u32[]{:S(2)}, u32[]{:S(2)}) collective-permute-start(bf16[256,2048]{1,0:T(8,128)(2,1)} %get-tuple-element.134.refs_0_), channel_id=1, source_target_pairs={{0,2},{1,3},{2,0},{3,1},{4,6},{5,7},{6,4},{7,5},{8,10},{9,11},{10,... | collective-permute-start | bytes 3145736 | tf_op jit(solution)/shard_map/ppermute | solution.py:580
  389.2 24.3 %collective-permute-start.30 = (bf16[256,2048]{1,0:T(8,128)(2,1)}, bf16[256,2048]{1,0:T(8,128)(2,1)S(1)}, u32[]{:S(2)}, u32[]{:S(2)}) collective-permute-start(bf16[256,2048]{1,0:T(8,128)(2,1)} %get-tuple-element.134.refs_0_), channel_id=1, source_target_pairs={{0,4},{4,0},{1,5},{5,1},{2,6},{6,2},{3,7},{7,3},{8,12},{12,8},{9,1... | collective-permute-start | bytes 3145736 | tf_op jit(solution)/shard_map/ppermute | solution.py:578
  412.3 12.6 %collective-permute-start.32 = (bf16[256,1024]{1,0:T(8,128)(2,1)S(1)}, bf16[256,1024]{1,0:T(8,128)(2,1)S(1)}, u32[]{:S(2)}, u32[]{:S(2)}) collective-permute-start(bf16[256,1024]{1,0:T(8,128)(2,1)S(1)} %slice.217), channel_id=1, source_target_pairs={{0,4},{4,0},{1,5},{5,1},{2,6},{6,2},{3,7},{7,3},{8,12},{12,8},{9,1... | collective-permute-start | bytes 1572872 | tf_op jit(solution)/shard_map/ppermute | solution.py:578
  413.6 12.1 %collective-permute-start.33 = (bf16[256,1024]{1,0:T(8,128)(2,1)S(1)}, bf16[256,1024]{1,0:T(8,128)(2,1)S(1)}, u32[]{:S(2)}, u32[]{:S(2)}) collective-permute-start(bf16[256,1024]{1,0:T(8,128)(2,1)S(1)} %slice.218), channel_id=1, source_target_pairs={{0,2},{1,3},{2,0},{3,1},{4,6},{5,7},{6,4},{7,5},{8,10},{9,11},{10,... | collective-permute-start | bytes 1572872 | tf_op jit(solution)/shard_map/ppermute | solution.py:580
  431.9 19.4 %collective-permute-start.36 = (bf16[1024,2048]{1,0:T(8,128)(2,1)}, bf16[1024,2048]{1,0:T(8,128)(2,1)}, u32[]{:S(2)}, u32[]{:S(2)}) collective-permute-start(bf16[1024,2048]{1,0:T(8,128)(2,1)} %bitcast.122), channel_id=1, source_target_pairs={{0,1},{1,0},{2,3},{3,2},{4,5},{5,4},{6,7},{7,6},{8,9},{9,8},{10,11... | collective-permute-start | bytes 12582920 | tf_op jit(solution)/shard_map/ppermute | solution.py:583
  431.9 28.2 %collective-permute-start.34 = (bf16[2,256,1024]{2,1,0:T(8,128)(2,1)}, bf16[2,256,1024]{2,1,0:T(8,128)(2,1)}, u32[]{:S(2)}, u32[]{:S(2)}) collective-permute-start(bf16[2,256,1024]{2,1,0:T(8,128)(2,1)} %get-tuple-element.135.refs_7_), channel_id=1, source_target_pairs={{0,4},{4,0},{1,5},{5,1},{2,6},{6,2},{3,7},{7,3},{8,12},{12,8},{9,1... | collective-permute-start | bytes 3145736 | tf_op jit(solution)/shard_map/ppermute | solution.py:578
  433.0 27.1 %collective-permute-start.35 = (bf16[2,256,1024]{2,1,0:T(8,128)(2,1)}, bf16[2,256,1024]{2,1,0:T(8,128)(2,1)}, u32[]{:S(2)}, u32[]{:S(2)}) collective-permute-start(bf16[2,256,1024]{2,1,0:T(8,128)(2,1)} %get-tuple-element.137), channel_id=1, source_target_pairs={{0,2},{1,3},{2,0},{3,1},{4,6},{5,7},{6,4},{7,5},{8,10},{9,11},{10,... | collective-permute-start | bytes 3145736 | tf_op jit(solution)/shard_map/ppermute | solution.py:580
  451.2 56.4 %collective-permute-start.42 = (bf16[3,1024,256]{2,1,0:T(8,128)(2,1)S(1)}, bf16[3,1024,256]{2,1,0:T(8,128)(2,1)}, u32[]{:S(2)}, u32[]{:S(2)}) collective-permute-start(bf16[3,1024,256]{2,1,0:T(8,128)(2,1)S(1)} %bitcast.102), channel_id=1, source_target_pairs={{0,1},{1,0},{2,3},{3,2},{4,5},{5,4},{6,7},{7,6},{8,9},{9,8},{10,11... | collective-permute-start | bytes 4718600 | tf_op jit(solution)/shard_map/ppermute | solution.py:583
  459.0 137.7 %all-gather.8.cloned.1.call-start = ((), (), s32[]{:S(2)}) async-start(), calls=%async_computation.7 | async-start | bytes 4325376 | tf_op jit(solution)/shard_map/all_gather | solution.py:1021
  459.1 33.5 %collective-permute-start.39 = (bf16[704,512]{1,0:T(8,128)(2,1)S(1)}, bf16[704,512]{1,0:T(8,128)(2,1)S(1)}, u32[]{:S(2)}, u32[]{:S(2)}) collective-permute-start(bf16[704,512]{1,0:T(8,128)(2,1)S(1)} %copy-done.35), channel_id=1, source_target_pairs={{0,4},{4,0},{1,5},{5,1},{2,6},{6,2},{3,7},{7,3},{8,12},{12,8},{9,1... | collective-permute-start | bytes 2162696 | tf_op jit(solution)/shard_map/ppermute | solution.py:578
  463.8 19.9 %collective-permute-start.37 = (bf16[256,1024]{1,0:T(8,128)(2,1)}, bf16[256,1024]{1,0:T(8,128)(2,1)S(1)}, u32[]{:S(2)}, u32[]{:S(2)}) collective-permute-start(bf16[256,1024]{1,0:T(8,128)(2,1)} %get-tuple-element.143), channel_id=1, source_target_pairs={{0,2},{1,3},{2,0},{3,1},{4,6},{5,7},{6,4},{7,5},{8,10},{9,11},{10,... | collective-permute-start | bytes 1572872 | tf_op jit(solution)/shard_map/ppermute | solution.py:580
  464.5 23.8 %collective-permute-start.38 = (bf16[256,1024]{1,0:T(8,128)(2,1)}, bf16[256,1024]{1,0:T(8,128)(2,1)S(1)}, u32[]{:S(2)}, u32[]{:S(2)}) collective-permute-start(bf16[256,1024]{1,0:T(8,128)(2,1)} %get-tuple-element.145), channel_id=1, source_target_pairs={{0,4},{4,0},{1,5},{5,1},{2,6},{6,2},{3,7},{7,3},{8,12},{12,8},{9,1... | collective-permute-start | bytes 1572872 | tf_op jit(solution)/shard_map/ppermute | solution.py:578
  505.9 24.5 %collective-permute-start.40 = (bf16[2,256,1024]{2,1,0:T(8,128)(2,1)}, bf16[2,256,1024]{2,1,0:T(8,128)(2,1)S(1)}, u32[]{:S(2)}, u32[]{:S(2)}) collective-permute-start(bf16[2,256,1024]{2,1,0:T(8,128)(2,1)} %get-tuple-element.152.refs_0_), channel_id=1, source_target_pairs={{0,4},{4,0},{1,5},{5,1},{2,6},{6,2},{3,7},{7,3},{8,12},{12,8},{9,1... | collective-permute-start | bytes 3145736 | tf_op jit(solution)/shard_map/ppermute | solution.py:578
  506.9 24.2 %collective-permute-start.41 = (bf16[2,256,1024]{2,1,0:T(8,128)(2,1)}, bf16[2,256,1024]{2,1,0:T(8,128)(2,1)}, u32[]{:S(2)}, u32[]{:S(2)}) collective-permute-start(bf16[2,256,1024]{2,1,0:T(8,128)(2,1)} %get-tuple-element.154), channel_id=1, source_target_pairs={{0,2},{1,3},{2,0},{3,1},{4,6},{5,7},{6,4},{7,5},{8,10},{9,11},{10,... | collective-permute-start | bytes 3145736 | tf_op jit(solution)/shard_map/ppermute | solution.py:580
  520.0 33.7 %collective-permute-start.48 = (bf16[2,3,256,256]{3,2,1,0:T(8,128)(2,1)S(1)}, bf16[2,3,256,256]{3,2,1,0:T(8,128)(2,1)}, u32[]{:S(2)}, u32[]{:S(2)}) collective-permute-start(bf16[2,3,256,256]{3,2,1,0:T(8,128)(2,1)S(1)} %pad_maximum_fusion), channel_id=1, source_target_pairs={{0,8},{8,16},{16,24},{24,0},{1,9},{9,17},{17,25},{25,1},{2,10},{10... | collective-permute-start | bytes 2359304 | tf_op jit(solution)/shard_map/ppermute | solution.py:575
  521.1 35.2 %collective-permute-start.49 = (bf16[2,3,256,256]{3,2,1,0:T(8,128)(2,1)}, bf16[2,3,256,256]{3,2,1,0:T(8,128)(2,1)}, u32[]{:S(2)}, u32[]{:S(2)}) collective-permute-start(bf16[2,3,256,256]{3,2,1,0:T(8,128)(2,1)} %pad_maximum_fusion.1), channel_id=1, source_target_pairs={{0,24},{8,0},{16,8},{24,16},{1,25},{9,1},{17,9},{25,17},{2,26},{10... | collective-permute-start | bytes 2359304 | tf_op jit(solution)/shard_map/ppermute | solution.py:575
  534.9 12.5 %collective-permute-start.43 = (bf16[256,1024]{1,0:T(8,128)(2,1)}, bf16[256,1024]{1,0:T(8,128)(2,1)}, u32[]{:S(2)}, u32[]{:S(2)}) collective-permute-start(bf16[256,1024]{1,0:T(8,128)(2,1)} %get-tuple-element.156), channel_id=1, source_target_pairs={{0,2},{1,3},{2,0},{3,1},{4,6},{5,7},{6,4},{7,5},{8,10},{9,11},{10,... | collective-permute-start | bytes 1572872 | tf_op jit(solution)/shard_map/ppermute | solution.py:580
  535.6 17.0 %collective-permute-start.44 = (bf16[256,1024]{1,0:T(8,128)(2,1)}, bf16[256,1024]{1,0:T(8,128)(2,1)}, u32[]{:S(2)}, u32[]{:S(2)}) collective-permute-start(bf16[256,1024]{1,0:T(8,128)(2,1)} %get-tuple-element.157), channel_id=1, source_target_pairs={{0,4},{4,0},{1,5},{5,1},{2,6},{6,2},{3,7},{7,3},{8,12},{12,8},{9,1... | collective-permute-start | bytes 1572872 | tf_op jit(solution)/shard_map/ppermute | solution.py:578
  552.5 17.7 %collective-permute-start.46 = (bf16[256,2048]{1,0:T(8,128)(2,1)S(1)}, bf16[256,2048]{1,0:T(8,128)(2,1)}, u32[]{:S(2)}, u32[]{:S(2)}) collective-permute-start(bf16[256,2048]{1,0:T(8,128)(2,1)S(1)} %copy-done.31), channel_id=1, source_target_pairs={{0,2},{1,3},{2,0},{3,1},{4,6},{5,7},{6,4},{7,5},{8,10},{9,11},{10,... | collective-permute-start | bytes 3145736 | tf_op jit(solution)/shard_map/ppermute | solution.py:580
  557.5 10.3 %collective-permute-start.53 = (bf16[3,256,256]{2,1,0:T(8,128)(2,1)S(1)}, bf16[3,256,256]{2,1,0:T(8,128)(2,1)S(1)}, u32[]{:S(2)}, u32[]{:S(2)}) collective-permute-start(bf16[3,256,256]{2,1,0:T(8,128)(2,1)S(1)} %fusion.17.refs_8_), channel_id=1, source_target_pairs={{0,24},{8,0},{16,8},{24,16},{1,25},{9,1},{17,9},{25,17},{2,26},{10... | collective-permute-start | bytes 1179656 | tf_op jit(solution)/shard_map/ppermute | solution.py:575
  569.4 11.3 %collective-permute-start.54 = (bf16[3,256,256]{2,1,0:T(8,128)(2,1)S(1)}, bf16[3,256,256]{2,1,0:T(8,128)(2,1)S(1)}, u32[]{:S(2)}, u32[]{:S(2)}) collective-permute-start(bf16[3,256,256]{2,1,0:T(8,128)(2,1)S(1)} %get-tuple-element.197), channel_id=1, source_target_pairs={{0,8},{8,16},{16,24},{24,0},{1,9},{9,17},{17,25},{25,1},{2,10},{10... | collective-permute-start | bytes 1179656 | tf_op jit(solution)/shard_map/ppermute | solution.py:575
  572.8 18.6 %collective-permute-start.45 = (bf16[256,2048]{1,0:T(8,128)(2,1)S(1)}, bf16[256,2048]{1,0:T(8,128)(2,1)}, u32[]{:S(2)}, u32[]{:S(2)}) collective-permute-start(bf16[256,2048]{1,0:T(8,128)(2,1)S(1)} %copy-done.31), channel_id=1, source_target_pairs={{0,1},{1,0},{2,3},{3,2},{4,5},{5,4},{6,7},{7,6},{8,9},{9,8},{10,11... | collective-permute-start | bytes 3145736 | tf_op jit(solution)/shard_map/ppermute | solution.py:583
  572.8 18.6 %collective-permute-start.47 = (bf16[256,2048]{1,0:T(8,128)(2,1)}, bf16[256,2048]{1,0:T(8,128)(2,1)}, u32[]{:S(2)}, u32[]{:S(2)}) collective-permute-start(bf16[256,2048]{1,0:T(8,128)(2,1)} %collective-permute-done.46.refs_2_), channel_id=1, source_target_pairs={{0,1},{1,0},{2,3},{3,2},{4,5},{5,4},{6,7},{7,6},{8,9},{9,8},{10,11... | collective-permute-start | bytes 3145736 | tf_op jit(solution)/shard_map/ppermute | solution.py:583
  574.2 27.7 %collective-permute-start.52 = (bf16[256,2048]{1,0:T(8,128)(2,1)}, bf16[256,2048]{1,0:T(8,128)(2,1)}, u32[]{:S(2)}, u32[]{:S(2)}) collective-permute-start(bf16[256,2048]{1,0:T(8,128)(2,1)} %get-tuple-element.169.refs_0_), channel_id=1, source_target_pairs={{0,2},{1,3},{2,0},{3,1},{4,6},{5,7},{6,4},{7,5},{8,10},{9,11},{10,... | collective-permute-start | bytes 3145736 | tf_op jit(solution)/shard_map/ppermute | solution.py:580
  583.0 8.4 %collective-permute-start.62 = (bf16[512,256]{1,0:T(8,128)(2,1)}, bf16[512,256]{1,0:T(8,128)(2,1)S(1)}, u32[]{:S(2)}, u32[]{:S(2)}) collective-permute-start(bf16[512,256]{1,0:T(8,128)(2,1)} %reduce-scatter.8.cloned.1.call-done), channel_id=1, source_target_pairs={{0,4},{4,0},{1,5},{5,1},{2,6},{6,2},{3,7},{7,3},{8,12},{12,8},{9,1... | collective-permute-start | bytes 786440 | tf_op jit(solution)/shard_map/ppermute | solution.py:578
  587.6 20.3 %collective-permute-start.55 = (bf16[3,512,256]{2,1,0:T(8,128)(2,1)}, bf16[3,512,256]{2,1,0:T(8,128)(2,1)}, u32[]{:S(2)}, u32[]{:S(2)}) collective-permute-start(bf16[3,512,256]{2,1,0:T(8,128)(2,1)} %pad_maximum_fusion.2), channel_id=1, source_target_pairs={{0,4},{4,0},{1,5},{5,1},{2,6},{6,2},{3,7},{7,3},{8,12},{12,8},{9,1... | collective-permute-start | bytes 2359304 | tf_op jit(solution)/shard_map/ppermute | solution.py:578
  591.4 24.5 %collective-permute-start.51 = (bf16[256,2048]{1,0:T(8,128)(2,1)}, bf16[256,2048]{1,0:T(8,128)(2,1)}, u32[]{:S(2)}, u32[]{:S(2)}) collective-permute-start(bf16[256,2048]{1,0:T(8,128)(2,1)} %get-tuple-element.169.refs_0_), channel_id=1, source_target_pairs={{0,1},{1,0},{2,3},{3,2},{4,5},{5,4},{6,7},{7,6},{8,9},{9,8},{10,11... | collective-permute-start | bytes 3145736 | tf_op jit(solution)/shard_map/ppermute | solution.py:583
  604.0 5.5 collective-permute-start.58
  604.1 5.5 collective-permute-start.59
  609.3 6.5 %collective-permute-start.56 = (bf16[256,2048]{1,0:T(8,128)(2,1)}, bf16[256,2048]{1,0:T(8,128)(2,1)}, u32[]{:S(2)}, u32[]{:S(2)}) collective-permute-start(bf16[256,2048]{1,0:T(8,128)(2,1)} %collective-permute-done.52.refs_2_), channel_id=1, source_target_pairs={{0,1},{1,0},{2,3},{3,2},{4,5},{5,4},{6,7},{7,6},{8,9},{9,8},{10,11... | collective-permute-start | bytes 3145736 | tf_op jit(solution)/shard_map/ppermute | solution.py:583
  (70 other events, 359.5 us)
Sparse Core Ops, SparseCore 0:
  92.2 106.0 all-gather.3
  211.7 55.9 all-gather.5
  296.6 53.0 reduce-scatter.3
  366.9 98.9 reduce-scatter.5
  468.0 27.6 reduce-scatter.7
  536.7 42.0 all-gather.7
